TPU v7x, 32 devices: a whole 2x2x4 slice. The times are simulated.
32 devices in a mesh: dp: 4 (over z), ctx: 2 (over x), mp: 4 (over y, core).
Axes of the slice: x: 2, y: 2, z: 4, core: 2. Of those that a mesh axis runs over, the one named last changes fastest.
Arguments:
- block_input: bfloat16 [16384, 768], P(('dp', 'ctx', 'mp')), may hold values from -6 to 6
- cotangent: bfloat16 [16384, 768], P(('dp', 'ctx', 'mp')), may hold values from -6 to 6
- doc_lengths: int32 [8, 3], P(('dp', 'ctx')), may hold values from 1 to 1024, 1536 in all within a row
- reuse_heads: int32 [6], replicated, may hold values from 0 to 11, as said below
- norm_gain1: bfloat16 [2, 768], replicated, may hold values from 0.099609375 to 1.8984375
- norm_bias1: bfloat16 [2, 768], replicated, may hold values from -4 to 4
- projections1: bfloat16 [3, 768, 768], P(None, None, 'mp'), may hold values from -0.3125 to 0.3125
- front_bias1: bfloat16 [2, 768], P(None, 'mp'), may hold values from -4 to 4
- out_weight1: bfloat16 [768, 768], P('mp'), may hold values from -0.625 to 0.625
- out_bias1: bfloat16 [2, 768], replicated, may hold values from -4 to 4
- up_weight1: bfloat16 [768, 3072], P(None, 'mp'), may hold values from -0.21875 to 0.21875
- up_bias1: bfloat16 [3072], P('mp'), may hold values from -4 to 4
- down_weight1: bfloat16 [3072, 768], P('mp'), may hold values from -0.109375 to 0.109375
- norm_gain2: bfloat16 [2, 768], replicated, may hold values from 0.099609375 to 1.8984375
- norm_bias2: bfloat16 [2, 768], replicated, may hold values from -4 to 4
- query_key2: bfloat16 [2, 768, 768], P(None, None, 'mp'), may hold values from -0.3125 to 0.3125
- query_bias2: bfloat16 [768], P('mp'), may hold values from -4 to 4
- fresh_value2: bfloat16 [768, 384], P(None, 'mp'), may hold values from -0.3125 to 0.3125
- value_bias2: bfloat16 [384], P('mp'), may hold values from -4 to 4
- out_weight2: bfloat16 [768, 768], P('mp'), may hold values from -0.625 to 0.625
- out_bias2: bfloat16 [2, 768], replicated, may hold values from -4 to 4
- up_weight2: bfloat16 [768, 3072], P(None, 'mp'), may hold values from -0.21875 to 0.21875
- up_bias2: bfloat16 [3072], P('mp'), may hold values from -4 to 4
- down_weight2: bfloat16 [3072, 768], P('mp'), may hold values from -0.109375 to 0.109375
Outputs:
- block_output: bfloat16 [16384, 768], P(('dp', 'ctx', 'mp'))
- input_grad: bfloat16 [16384, 768], P(('dp', 'ctx', 'mp'))
- grad_norm_gain1: float32 [2, 768], replicated
- grad_norm_bias1: float32 [2, 768], replicated
- grad_projections1: float32 [3, 768, 768], P(None, None, 'mp')
- grad_front_bias1: float32 [2, 768], P(None, 'mp')
- grad_out_weight1: float32 [768, 768], P('mp')
- grad_out_bias1: float32 [2, 768], replicated
- grad_up_weight1: float32 [768, 3072], P(None, 'mp')
- grad_up_bias1: float32 [3072], P('mp')
- grad_down_weight1: float32 [3072, 768], P('mp')
- grad_norm_gain2: float32 [2, 768], replicated
- grad_norm_bias2: float32 [2, 768], replicated
- grad_query_key2: float32 [2, 768, 768], P(None, None, 'mp')
- grad_query_bias2: float32 [768], P('mp')
- grad_fresh_value2: float32 [768, 384], P(None, 'mp')
- grad_value_bias2: float32 [384], P('mp')
- grad_out_weight2: float32 [768, 768], P('mp')
- grad_out_bias2: float32 [2, 768], replicated
- grad_up_weight2: float32 [768, 3072], P(None, 'mp')
- grad_up_bias2: float32 [3072], P('mp')
- grad_down_weight2: float32 [3072, 768], P('mp')
Inputs may be any that keep to these rules, and one draw needn't show every extreme that they name: `doc_lengths`: each row lists the lengths of the 3 documents of one group; they sum to 1536 and the longest is exactly 1024. `reuse_heads`: 6 distinct head numbers.
All inputs are finite; a program needn't handle non-finite values.
Results may differ from a plain program's by a relative error of at most 0.03.
Values may be sent and summed in bfloat16 or wider, within the bound.
A program may use at most 192 MiB of HBM per device.

v0:
```python
from functools import partial

import jax
import jax.numpy as jnp
from jax import lax
from jax.sharding import PartitionSpec as P

D = 768
H = 12
HD = 64
REUSE = 6
WIN = 512
SHORT = 1536


EPS = 1e-05


def passed_along(block, axis, distance):
    devices = range(lax.axis_size(axis))
    route = [(i - distance, i) for i in devices if i - distance in devices]
    return lax.ppermute(block, axis, route)


def norm_rows(value, gain, shift):
    mean = jnp.mean(value, axis=-1, keepdims=True)
    centred = value - mean
    spread = jnp.mean(centred * centred, axis=-1, keepdims=True)
    scale = lax.rsqrt(spread + EPS)
    unit = centred * scale
    return (unit * gain + shift, unit, scale)


def norm_back(grad, unit, scale, gain):
    scaled = grad * gain
    inner = (
        scaled
        - jnp.mean(scaled, axis=-1, keepdims=True)
        - unit * jnp.mean(scaled * unit, axis=-1, keepdims=True)
    )
    return (scale * inner, jnp.sum(grad * unit, axis=0), jnp.sum(grad, axis=0))


def dot_plain(left, right):
    return jnp.dot(left, right, preferred_element_type=jnp.float32)


def dot_back(left, right):
    return lax.dot_general(
        left, right, (((1,), (1,)), ((), ())), preferred_element_type=jnp.float32
    )


def dot_rows(left, right):
    return lax.dot_general(
        left, right, (((0,), (0,)), ((), ())), preferred_element_type=jnp.float32
    )


def project(normed, weight_fn):
    gathered = lax.all_gather(normed, "mp", axis=0, tiled=True)
    return (weight_fn(gathered, 0), gathered)


def weight_grad(kept, grad_cols):
    return dot_rows(kept, grad_cols)


def branch_out(left, weight):
    return lax.psum_scatter(dot_plain(left, weight), "mp", scatter_dimension=0, tiled=True)


def spread_back(grad_cols, back_fn):
    return lax.psum_scatter(back_fn(grad_cols), "mp", scatter_dimension=0, tiled=True)


def gather_grad(share_grad):
    return lax.all_gather(share_grad.astype(jnp.bfloat16), "mp", axis=0, tiled=True)


def block_rows():
    return 512


def masked_scores(block_queries, keys, allowed):
    raw = (
        jnp.einsum("qhe,khe->hqk", block_queries, keys, preferred_element_type=jnp.float32) * 0.125
    )
    return jnp.where(allowed[None], raw, -jnp.inf)


def attend(queries, keys, values, rule):
    rows, heads, size = queries.shape
    block = block_rows()
    count = rows // block
    grouped = queries.reshape(count, block, heads, size)
    starts = jnp.arange(count, dtype=jnp.int32) * block

    def one_block(item):
        block_queries, start = item
        scores = masked_scores(block_queries, keys, rule(start, block))
        top = jnp.max(scores, axis=-1, keepdims=True)
        powers = jnp.exp(scores - top)
        total = jnp.sum(powers, axis=-1, keepdims=True)
        weights = (powers / total).astype(jnp.bfloat16)
        result = jnp.einsum("hqk,khe->qhe", weights, values, preferred_element_type=jnp.float32)
        return (result, (top + jnp.log(total))[..., 0])

    result, logsum = lax.map(one_block, (grouped, starts))
    return (result.reshape(rows, heads, size), logsum)


def attend_back(queries, keys, values, grad_out, logsum, rule):
    rows, heads, size = queries.shape
    block = block_rows()
    count = rows // block
    grouped = queries.reshape(count, block, heads, size)
    grad_grouped = grad_out.reshape(count, block, heads, size)
    starts = jnp.arange(count, dtype=jnp.int32) * block

    def one_block(carry, item):
        key_grad, value_grad = carry
        block_queries, block_grad, block_logsum, start = item
        scores = masked_scores(block_queries, keys, rule(start, block))
        weights = jnp.exp(scores - block_logsum[..., None])
        rounded = weights.astype(jnp.bfloat16)
        grad_weights = jnp.einsum(
            "qhe,khe->hqk", block_grad, values, preferred_element_type=jnp.float32
        )
        inner = jnp.sum(weights * grad_weights, axis=-1, keepdims=True)
        grad_scores = (weights * (grad_weights - inner)).astype(jnp.bfloat16)
        query_grad = (
            jnp.einsum("hqk,khe->qhe", grad_scores, keys, preferred_element_type=jnp.float32)
            * 0.125
        )
        key_grad = (
            key_grad
            + jnp.einsum(
                "hqk,qhe->khe", grad_scores, block_queries, preferred_element_type=jnp.float32
            )
            * 0.125
        )
        value_grad = value_grad + jnp.einsum(
            "hqk,qhe->khe", rounded, block_grad, preferred_element_type=jnp.float32
        )
        return ((key_grad, value_grad), query_grad)

    empty = jnp.zeros(keys.shape, jnp.float32)
    (key_grad, value_grad), query_grad = lax.scan(
        one_block, (empty, empty), (grouped, grad_grouped, logsum, starts)
    )
    return (query_grad.reshape(rows, heads, size), key_grad, value_grad)


def window_rule(has_prev):

    def allowed(start, rows):
        query_pos = start + jnp.arange(rows, dtype=jnp.int32)
        key_pos = jnp.arange(2 * WIN, dtype=jnp.int32)
        own = (key_pos[None, :] >= WIN) & (key_pos[None, :] - WIN <= query_pos[:, None])
        return own | (key_pos[None, :] < WIN) & has_prev

    return allowed


def doc_rule(lengths):
    ends = jnp.cumsum(lengths)
    place = jnp.arange(SHORT, dtype=jnp.int32)
    docs = jnp.sum((place[:, None] >= ends[None, :]).astype(jnp.int32), axis=1)

    def allowed(start, rows):
        query_pos = start + jnp.arange(rows, dtype=jnp.int32)
        query_doc = lax.dynamic_slice_in_dim(docs, start, rows, 0)
        return (query_doc[:, None] == docs[None, :]) & (query_pos[:, None] >= place[None, :])

    return allowed


def split_heads(tensor):
    return tensor.reshape(tensor.shape[0], tensor.shape[1] // HD, HD)


def flatten_heads(tensor):
    return tensor.reshape(tensor.shape[0], tensor.shape[1] * tensor.shape[2])


def mix(queries, keys, values, lengths):
    earlier = passed_along(jnp.stack([keys[:WIN], values[:WIN]]), "ctx", 1)
    has_prev = lax.axis_index("ctx") > 0
    window_keys = split_heads(jnp.concatenate([earlier[0], keys[:WIN]], axis=0))
    window_values = split_heads(jnp.concatenate([earlier[1], values[:WIN]], axis=0))
    window_out, window_sum = attend(
        split_heads(queries[:WIN]), window_keys, window_values, window_rule(has_prev)
    )
    doc_out, doc_sum = attend(
        split_heads(queries[WIN:]),
        split_heads(keys[WIN:]),
        split_heads(values[WIN:]),
        doc_rule(lengths),
    )
    heads_out = flatten_heads(jnp.concatenate([window_out, doc_out], axis=0)).astype(jnp.bfloat16)
    return (heads_out, (earlier, window_sum, doc_sum))


def mix_back(queries, keys, values, lengths, kept, grad_heads):
    earlier, window_sum, doc_sum = kept
    has_prev = lax.axis_index("ctx") > 0
    window_keys = split_heads(jnp.concatenate([earlier[0], keys[:WIN]], axis=0))
    window_values = split_heads(jnp.concatenate([earlier[1], values[:WIN]], axis=0))
    window_dq, window_dk, window_dv = attend_back(
        split_heads(queries[:WIN]),
        window_keys,
        window_values,
        split_heads(grad_heads[:WIN]),
        window_sum,
        window_rule(has_prev),
    )
    doc_dq, doc_dk, doc_dv = attend_back(
        split_heads(queries[WIN:]),
        split_heads(keys[WIN:]),
        split_heads(values[WIN:]),
        split_heads(grad_heads[WIN:]),
        doc_sum,
        doc_rule(lengths),
    )
    returned = passed_along(
        jnp.stack([flatten_heads(window_dk[:WIN]), flatten_heads(window_dv[:WIN])]), "ctx", -1
    )
    grad_query = jnp.concatenate([flatten_heads(window_dq), flatten_heads(doc_dq)], axis=0)
    grad_key = jnp.concatenate(
        [flatten_heads(window_dk[WIN:]) + returned[0], flatten_heads(doc_dk)], axis=0
    )
    grad_value = jnp.concatenate(
        [flatten_heads(window_dv[WIN:]) + returned[1], flatten_heads(doc_dv)], axis=0
    )
    return (grad_query, grad_key, grad_value)


def tail_forward(
    stream,
    queries,
    keys,
    values,
    lengths,
    out_weight,
    out_bias,
    norm_gain,
    norm_bias,
    up_weight,
    up_bias,
    down_weight,
):
    heads_out, attn_kept = mix(queries, keys, values, lengths)
    stream = stream + branch_out(heads_out, out_weight) + out_bias[0]
    normed, unit, scale = norm_rows(stream, norm_gain[1], norm_bias[1])
    hidden, kept_rows = project(
        normed.astype(jnp.bfloat16), lambda piece, start: dot_plain(piece, up_weight)
    )
    hidden = hidden + up_bias
    active = jax.nn.gelu(hidden, approximate=True).astype(jnp.bfloat16)
    stream = stream + branch_out(active, down_weight) + out_bias[1]
    return (stream, (heads_out, attn_kept, unit, scale, kept_rows, hidden, active))


def tail_backward(
    grad_stream, queries, keys, values, lengths, kept, out_weight, norm_gain, up_weight, down_weight
):
    heads_out, attn_kept, unit, scale, kept_rows, hidden, active = kept
    down_rows = gather_grad(grad_stream)
    grad_down = dot_rows(active, down_rows)
    grad_active = dot_back(down_rows, down_weight)
    unused, pull = jax.vjp(partial(jax.nn.gelu, approximate=True), hidden)
    grad_hidden = pull(grad_active)[0]
    grad_upbias = jnp.sum(grad_hidden, axis=0)
    hidden_low = grad_hidden.astype(jnp.bfloat16)
    grad_up = weight_grad(kept_rows, hidden_low)
    normed_grad = spread_back(hidden_low, lambda block: dot_back(block, up_weight))
    grad_mid, grad_gain, grad_shift = norm_back(normed_grad, unit, scale, norm_gain[1])
    grad_bias_mlp = jnp.sum(grad_stream, axis=0)
    grad_stream = grad_stream + grad_mid
    attn_rows = gather_grad(grad_stream)
    grad_out = dot_rows(heads_out, attn_rows)
    grad_heads = dot_back(attn_rows, out_weight).astype(jnp.bfloat16)
    grad_bias_attn = jnp.sum(grad_stream, axis=0)
    grad_query, grad_key, grad_value = mix_back(
        queries, keys, values, lengths, attn_kept, grad_heads
    )
    return (
        grad_stream,
        grad_query,
        grad_key,
        grad_value,
        (grad_out, grad_up, grad_upbias, grad_down),
        (grad_gain, grad_shift, grad_bias_attn, grad_bias_mlp),
    )


def shards(
    block_input,
    cotangent,
    doc_lengths,
    reuse_heads,
    norm_gain1,
    norm_bias1,
    projections1,
    front_bias1,
    out_weight1,
    out_bias1,
    up_weight1,
    up_bias1,
    down_weight1,
    norm_gain2,
    norm_bias2,
    query_key2,
    query_bias2,
    fresh_value2,
    value_bias2,
    out_weight2,
    out_bias2,
    up_weight2,
    up_bias2,
    down_weight2,
):
    lengths = doc_lengths[0]
    width = projections1.shape[2]
    heads = width // HD
    stream0 = block_input.astype(jnp.float32)
    normed1, unit1, scale1 = norm_rows(stream0, norm_gain1[0], norm_bias1[0])

    def first_fn(piece, start):
        return jnp.einsum(
            "rd,cdk->rck", piece, projections1, preferred_element_type=jnp.float32
        ).reshape(piece.shape[0], 3 * width)

    front1, kept1 = project(normed1.astype(jnp.bfloat16), first_fn)
    queries1 = (front1[:, :width] + front_bias1[0]).astype(jnp.bfloat16)
    keys1 = front1[:, width : 2 * width].astype(jnp.bfloat16)
    values1 = (front1[:, 2 * width :] + front_bias1[1]).astype(jnp.bfloat16)
    stream1, tail1 = tail_forward(
        stream0,
        queries1,
        keys1,
        values1,
        lengths,
        out_weight1,
        out_bias1,
        norm_gain1,
        norm_bias1,
        up_weight1,
        up_bias1,
        down_weight1,
    )
    normed2, unit2, scale2 = norm_rows(stream1, norm_gain2[0], norm_bias2[0])

    def second_fn(piece, start):
        paired = jnp.einsum(
            "rd,cdk->rck", piece, query_key2, preferred_element_type=jnp.float32
        ).reshape(piece.shape[0], 2 * width)
        return jnp.concatenate([paired, dot_plain(piece, fresh_value2)], axis=1)

    front2, kept2 = project(normed2.astype(jnp.bfloat16), second_fn)
    queries2 = (front2[:, :width] + query_bias2).astype(jnp.bfloat16)
    keys2 = front2[:, width : 2 * width].astype(jnp.bfloat16)
    fresh = (front2[:, 2 * width :] + value_bias2).astype(jnp.bfloat16)
    all_first, all_fresh = (
        lax.all_gather(values1, "mp", axis=1, tiled=True),
        lax.all_gather(fresh, "mp", axis=1, tiled=True),
    )
    total_rows = values1.shape[0]
    source = jnp.concatenate(
        [all_first.reshape(total_rows, H, HD), all_fresh.reshape(total_rows, H - REUSE, HD)], axis=1
    )
    mine = lax.axis_index("mp") * heads + jnp.arange(heads, dtype=jnp.int32)
    reused = jnp.sum(
        jnp.where(
            jnp.arange(REUSE, dtype=jnp.int32)[None, :] == mine[:, None], reuse_heads[None, :], 0
        ),
        axis=1,
    )
    chosen = jnp.where(mine < REUSE, reused, H + mine - REUSE)
    picker = chosen[:, None] == jnp.arange(2 * H - REUSE, dtype=jnp.int32)[None, :]
    values2 = (
        jnp.einsum(
            "rse,hs->rhe", source, picker.astype(jnp.bfloat16), preferred_element_type=jnp.float32
        )
        .astype(jnp.bfloat16)
        .reshape(total_rows, width)
    )
    stream2, tail2 = tail_forward(
        stream1,
        queries2,
        keys2,
        values2,
        lengths,
        out_weight2,
        out_bias2,
        norm_gain2,
        norm_bias2,
        up_weight2,
        up_bias2,
        down_weight2,
    )
    block_output = stream2.astype(jnp.bfloat16)
    grad_upper = cotangent.astype(jnp.float32)
    grad_upper, query_grad2, key_grad2, value_grad2, mats2, small2 = tail_backward(
        grad_upper,
        queries2,
        keys2,
        values2,
        lengths,
        tail2,
        out_weight2,
        norm_gain2,
        up_weight2,
        down_weight2,
    )
    source_grad = jnp.einsum(
        "rhe,hs->rse",
        value_grad2.reshape(total_rows, heads, HD),
        picker.astype(jnp.float32),
        precision=lax.Precision.HIGHEST,
        preferred_element_type=jnp.float32,
    )
    back_first, back_fresh = (
        lax.psum_scatter(
            source_grad[:, :H].reshape(total_rows, H * HD), "mp", scatter_dimension=1, tiled=True
        ),
        lax.psum_scatter(
            source_grad[:, H:].reshape(total_rows, (H - REUSE) * HD),
            "mp",
            scatter_dimension=1,
            tiled=True,
        ),
    )
    grad_qbias2 = jnp.sum(query_grad2, axis=0)
    grad_vbias2 = jnp.sum(back_fresh, axis=0)
    cols2 = jnp.concatenate(
        [
            query_grad2.astype(jnp.bfloat16),
            key_grad2.astype(jnp.bfloat16),
            back_fresh.astype(jnp.bfloat16),
        ],
        axis=1,
    )
    grad_front2 = weight_grad(kept2, cols2)
    grad_qk2 = jnp.transpose(grad_front2[:, : 2 * width].reshape(D, 2, width), (1, 0, 2))
    grad_fresh2 = grad_front2[:, 2 * width :]

    def second_back(block):
        paired = block[:, : 2 * width].reshape(block.shape[0], 2, width)
        return jnp.einsum(
            "rck,cdk->rd", paired, query_key2, preferred_element_type=jnp.float32
        ) + dot_back(block[:, 2 * width :], fresh_value2)

    normed_grad2 = spread_back(cols2, second_back)
    norm_input2, gain_front2, shift_front2 = norm_back(normed_grad2, unit2, scale2, norm_gain2[0])
    grad_middle = grad_upper + norm_input2
    grad_out2, grad_up2, grad_upbias2, grad_down2 = (mats2[0], mats2[1], mats2[2], mats2[3])
    grad_lower, query_grad1, key_grad1, value_grad1, mats1, small1 = tail_backward(
        grad_middle,
        queries1,
        keys1,
        values1,
        lengths,
        tail1,
        out_weight1,
        norm_gain1,
        up_weight1,
        down_weight1,
    )
    value_grad1 = value_grad1 + back_first
    grad_fbias1 = jnp.stack([jnp.sum(query_grad1, axis=0), jnp.sum(value_grad1, axis=0)])
    cols1 = jnp.concatenate(
        [
            query_grad1.astype(jnp.bfloat16),
            key_grad1.astype(jnp.bfloat16),
            value_grad1.astype(jnp.bfloat16),
        ],
        axis=1,
    )
    grad_proj1 = jnp.transpose(weight_grad(kept1, cols1).reshape(D, 3, width), (1, 0, 2))

    def first_back(block):
        return jnp.einsum(
            "rck,cdk->rd",
            block.reshape(block.shape[0], 3, width),
            projections1,
            preferred_element_type=jnp.float32,
        )

    normed_grad1 = spread_back(cols1, first_back)
    norm_input1, gain_front1, shift_front1 = norm_back(normed_grad1, unit1, scale1, norm_gain1[0])
    input_grad = (grad_lower + norm_input1).astype(jnp.bfloat16)
    (
        grad_proj1,
        grad_fbias1,
        grad_out1,
        grad_up1,
        grad_upbias1,
        grad_down1,
        grad_qk2,
        grad_qbias2,
        grad_fresh2,
        grad_vbias2,
        grad_out2,
        grad_up2,
        grad_upbias2,
        grad_down2,
    ) = lax.psum(
        (
            grad_proj1,
            grad_fbias1,
            mats1[0],
            mats1[1],
            mats1[2],
            mats1[3],
            grad_qk2,
            grad_qbias2,
            grad_fresh2,
            grad_vbias2,
            grad_out2,
            grad_up2,
            grad_upbias2,
            grad_down2,
        ),
        ("dp", "ctx"),
    )
    gains1 = jnp.stack([gain_front1, small1[0]])
    shifts1 = jnp.stack([shift_front1, small1[1]])
    biases1 = jnp.stack([small1[2], small1[3]])
    gains2 = jnp.stack([gain_front2, small2[0]])
    shifts2 = jnp.stack([shift_front2, small2[1]])
    biases2 = jnp.stack([small2[2], small2[3]])
    gains1, shifts1, biases1, gains2, shifts2, biases2 = lax.psum(
        (gains1, shifts1, biases1, gains2, shifts2, biases2), ("dp", "ctx", "mp")
    )
    return (
        block_output,
        input_grad,
        gains1,
        shifts1,
        grad_proj1,
        grad_fbias1,
        grad_out1,
        biases1,
        grad_up1,
        grad_upbias1,
        grad_down1,
        gains2,
        shifts2,
        grad_qk2,
        grad_qbias2,
        grad_fresh2,
        grad_vbias2,
        grad_out2,
        biases2,
        grad_up2,
        grad_upbias2,
        grad_down2,
    )


def solution(mesh):
    placed = (
        P(("dp", "ctx", "mp"), None),
        P(("dp", "ctx", "mp"), None),
        P(("dp", "ctx"), None),
        P(),
        P(),
        P(),
        P(None, None, "mp"),
        P(None, "mp"),
        P("mp", None),
        P(),
        P(None, "mp"),
        P("mp"),
        P("mp", None),
        P(),
        P(),
        P(None, None, "mp"),
        P("mp"),
        P(None, "mp"),
        P("mp"),
        P("mp", None),
        P(),
        P(None, "mp"),
        P("mp"),
        P("mp", None),
    )
    return jax.shard_map(
        shards,
        mesh=mesh,
        in_specs=placed,
        out_specs=(
            P(("dp", "ctx", "mp"), None),
            P(("dp", "ctx", "mp"), None),
            P(),
            P(),
            P(None, None, "mp"),
            P(None, "mp"),
            P("mp", None),
            P(),
            P(None, "mp"),
            P("mp"),
            P("mp", None),
            P(),
            P(),
            P(None, None, "mp"),
            P("mp"),
            P(None, "mp"),
            P("mp"),
            P("mp", None),
            P(),
            P(None, "mp"),
            P("mp"),
            P("mp", None),
        ),
        check_vma=False,
    )
```

profile of v0, /device:TPU:0, one launch (start us, length us, event | category | flops | bytes accessed | tf_op | source)
XLA Modules:
  0.0 1797.9 jit_solution(263428893648403092)
XLA Ops:
  17.1 28.3 %all-gather.11.cloned.1.call-done = bf16[2048,768]{1,0:T(8,128)(2,1)} async-done(((bf16[512,768]{1,0:T(8,128)(2,1)}), bf16[2048,768]{1,0:T(8,128)(2,1)}) %all-gather.11.cloned.1.call-update) | async-done | bytes 3145744 | tf_op jit(solution)/shard_map/all_gather | solution.py:61
  45.4 5.3 fusion.238
  65.2 41.6 %while.12 = (s32[]{:T(128)}, bf16[3,512,3,64]{1,3,2,0:T(8,128)(2,1)}, f32[3,3,512]{2,1,0:T(4,128)}, s32[3]{0:T(128)}, s32[1536]{0:T(1024)S(1)}, /*index=5*/bf16[...) while((s32[]{:T(128)}, ...), condition=%wide.region_9.10_spmd.clone, body=%wide.region_6.9_spmd.clone.sunk | while | flops 634649600 | bytes 38017264 | solution.py:109
  122.6 56.3 %reduce-scatter.11.cloned.1.call-done = f32[512,768]{1,0:T(8,128)} async-done(((f32[2048,768]{1,0:T(8,128)}), f32[512,768]{1,0:T(8,128)}) %reduce-scatter.11.cloned.1.call-update) | async-done | bytes 1572880 | tf_op jit(solution)/shard_map/reduce_scatter | solution.py:70
  182.8 28.2 %all-gather.13.cloned.1.call-done = bf16[2048,768]{1,0:T(8,128)(2,1)} async-done(((bf16[512,768]{1,0:T(8,128)(2,1)}), bf16[2048,768]{1,0:T(8,128)(2,1)}) %all-gather.13.cloned.1.call-update) | async-done | bytes 3145744 | tf_op jit(solution)/shard_map/all_gather | solution.py:61
  211.0 8.8 multiply_convert_fusion.5
  221.4 4.5 fusion.242
  226.7 57.8 %reduce-scatter.13.cloned.1.call-done = f32[512,768]{1,0:T(8,128)} async-done(((f32[2048,768]{1,0:T(8,128)}), f32[512,768]{1,0:T(8,128)}) %reduce-scatter.13.cloned.1.call-update) | async-done | bytes 1572880 | tf_op jit(solution)/shard_map/reduce_scatter | solution.py:70
  289.2 28.0 %all-gather.15.cloned.1.call-done = bf16[2048,768]{1,0:T(8,128)(2,1)} async-done(((bf16[512,768]{1,0:T(8,128)(2,1)}), bf16[2048,768]{1,0:T(8,128)(2,1)}) %all-gather.15.cloned.1.call-update) | async-done | bytes 3145744 | tf_op jit(solution)/shard_map/all_gather | solution.py:61
  321.2 26.5 %all-gather.17.cloned.1.call-done = bf16[2048,768]{0,1:T(8,128)(2,1)} async-done(((bf16[2048,192]{0,1:T(8,128)(2,1)}), bf16[2048,768]{0,1:T(8,128)(2,1)}) %all-gather.17.cloned.1.call-update) | async-done | bytes 3145744 | tf_op jit(solution)/shard_map/all_gather | solution.py:366
  347.7 5.9 copy.83
  360.4 9.1 all-gather.19.cloned.1.call-done
  371.9 5.1 fusion.115
  383.6 41.0 %while.13 = (s32[]{:T(128)}, bf16[3,512,3,64]{1,3,2,0:T(8,128)(2,1)S(1)}, f32[3,3,512]{2,1,0:T(4,128)}, s32[3]{0:T(128)}, s32[1536]{0:T(1024)S(1)}, /*index=5*/b...) while((s32[]{:T(128)}, ...), condition=%wide.region_22.23_spmd.clone, body=%wide.region_19.22_spmd.clone.sunk | while | flops 634649600 | bytes 33298616 | solution.py:109
  437.3 56.9 %reduce-scatter.15.cloned.1.call-done = f32[512,768]{1,0:T(8,128)} async-done(((f32[2048,768]{1,0:T(8,128)}), f32[512,768]{1,0:T(8,128)}) %reduce-scatter.15.cloned.1.call-update) | async-done | bytes 1572880 | tf_op jit(solution)/shard_map/reduce_scatter | solution.py:70
  498.9 28.0 %all-gather.21.cloned.1.call-done = bf16[2048,768]{1,0:T(8,128)(2,1)} async-done(((bf16[512,768]{1,0:T(8,128)(2,1)}), bf16[2048,768]{1,0:T(8,128)(2,1)}) %all-gather.21.cloned.1.call-update) | async-done | bytes 3145744 | tf_op jit(solution)/shard_map/all_gather | solution.py:61
  526.9 7.2 fusion.243
  534.2 22.8 %all-gather.23.cloned.1.call-done = bf16[2048,768]{1,0:T(8,128)(2,1)} async-done(((bf16[512,768]{1,0:T(8,128)(2,1)}), bf16[2048,768]{1,0:T(8,128)(2,1)}) %all-gather.23.cloned.1.call-update) | async-done | bytes 3145744 | tf_op jit(solution)/shard_map/all_gather | solution.py:78
  557.0 12.3 fusion.215
  570.9 4.6 fusion.166
  575.6 7.9 fusion.244
  583.6 50.5 %reduce-scatter.19.cloned.1.call-done = f32[512,768]{1,0:T(8,128)} async-done(((f32[2048,768]{1,0:T(8,128)}), f32[512,768]{1,0:T(8,128)}) %reduce-scatter.19.cloned.1.call-update) | async-done | bytes 1572880 | tf_op jit(solution)/shard_map/reduce_scatter | solution.py:74
  636.8 58.1 %reduce-scatter.17.cloned.1.call-done = f32[512,768]{1,0:T(8,128)} async-done(((f32[2048,768]{1,0:T(8,128)}), f32[512,768]{1,0:T(8,128)}) %reduce-scatter.17.cloned.1.call-update) | async-done | bytes 1572880 | tf_op jit(solution)/shard_map/reduce_scatter | solution.py:70
  701.7 28.2 %all-gather.25.cloned.1.call-done = bf16[2048,768]{1,0:T(8,128)(2,1)} async-done(((bf16[512,768]{1,0:T(8,128)(2,1)}), bf16[2048,768]{1,0:T(8,128)(2,1)}) %all-gather.25.cloned.1.call-update) | async-done | bytes 3145744 | tf_op jit(solution)/shard_map/all_gather | solution.py:78
  733.2 5.0 fusion.168
  743.1 5.4 multiply_convert_fusion.3
  753.5 100.8 %while.14 = (s32[]{:T(128)}, f32[1536,3,64]{0,2,1:T(8,128)}, f32[1536,3,64]{0,2,1:T(8,128)S(1)}, f32[3,512,3,64]{1,3,2,0:T(8,128)}, bf16[3,512,3,64]{1,3,2,0:T(8...) while((s32[]{:T(128)}, f32[1536,3,64]{0,2,1:T(8,128)}, ...), condition=%wide.region_33.34_spmd.clone, body=%wide.region_31.33_spmd.clone.sunk | while | flops 1535114240 | bytes 146127200 | solution.py:149
  760.7 7.2 multiply_reduce_fusion.19
  767.9 9.4 multiply_convert_fusion.8
  777.3 5.0 fusion.385
  794.2 7.2 multiply_reduce_fusion.19
  801.4 9.4 multiply_convert_fusion.8
  810.9 5.0 fusion.385
  827.8 7.2 multiply_reduce_fusion.19
  835.0 9.4 multiply_convert_fusion.8
  844.4 5.0 fusion.385
  856.6 5.5 convolution_bitcast_fusion
  862.1 4.6 copy-done.15
  880.3 31.2 %reduce-scatter.21.cloned.1.call-done = f32[2048,96]{0,1:T(8,128)} async-done(((f32[2048,384]{0,1:T(8,128)}), f32[2048,96]{0,1:T(8,128)}) %reduce-scatter.21.cloned.1.call-update) | async-done | bytes 786448 | tf_op jit(solution)/shard_map/reduce_scatter | solution.py:428
  919.3 58.4 %reduce-scatter.23.cloned.1.call-done = f32[512,768]{1,0:T(8,128)} async-done(((f32[2048,768]{1,0:T(8,128)}), f32[512,768]{1,0:T(8,128)}) %reduce-scatter.23.cloned.1.call-update) | async-done | bytes 1572880 | tf_op jit(solution)/shard_map/reduce_scatter | solution.py:74
  985.4 28.7 %all-gather.27.cloned.1.call-done = bf16[2048,768]{1,0:T(8,128)(2,1)} async-done(((bf16[512,768]{1,0:T(8,128)(2,1)}), bf16[2048,768]{1,0:T(8,128)(2,1)}) %all-gather.27.cloned.1.call-update) | async-done | bytes 3145744 | tf_op jit(solution)/shard_map/all_gather | solution.py:78
  1014.0 10.9 fusion.217
  1026.6 4.5 fusion.162
  1031.1 58.5 %reduce-scatter.25.cloned.1.call-done = f32[512,768]{1,0:T(8,128)} async-done(((f32[2048,768]{1,0:T(8,128)}), f32[512,768]{1,0:T(8,128)}) %reduce-scatter.25.cloned.1.call-update) | async-done | bytes 1572880 | tf_op jit(solution)/shard_map/reduce_scatter | solution.py:74
  1101.1 6.3 copy.102
  1107.5 18.4 %all-gather.29.cloned.1.call-done = bf16[2048,768]{1,0:T(8,128)(2,1)} async-done(((bf16[512,768]{1,0:T(8,128)(2,1)}), bf16[2048,768]{1,0:T(8,128)(2,1)}) %all-gather.29.cloned.1.call-update) | async-done | bytes 3145744 | tf_op jit(solution)/shard_map/all_gather | solution.py:78
  1130.0 4.9 fusion.171
  1134.9 4.5 multiply_reduce_fusion.2
  1143.8 5.4 multiply_convert_fusion.2
  1154.3 99.6 %while.15 = (s32[]{:T(128)}, f32[1536,3,64]{0,2,1:T(8,128)S(1)}, f32[1536,3,64]{0,2,1:T(8,128)S(1)}, f32[3,512,3,64]{1,3,2,0:T(8,128)}, bf16[3,512,3,64]{1,3,2,0...) while((s32[]{:T(128)}, f32[1536,3,64]{0,2,1:T(8,128)S(1)}, ...), condition=%wide.region_44.45_spmd.clone, body=%wide.region_42.44_spmd.clone.sunk | while | flops 1535114240 | bytes 136690080 | solution.py:149
  1161.5 7.2 multiply_reduce_fusion.20
  1168.7 9.5 multiply_convert_fusion.9
  1178.2 5.0 fusion.399
  1194.8 7.2 multiply_reduce_fusion.20
  1202.0 9.4 multiply_convert_fusion.9
  1211.4 5.0 fusion.399
  1228.0 7.2 multiply_reduce_fusion.20
  1235.2 9.4 multiply_convert_fusion.9
  1244.6 5.0 fusion.399
  1266.3 4.6 convolution_bitcast_fusion.1
  1271.2 7.1 fusion.247
  1303.9 38.7 %all-reduce.1 = (f32[2,192]{1,0:T(2,128)}, f32[768]{0:T(1024)}, f32[192]{0:T(256)}, f32[96]{0:T(128)}, f32[768]{0:T(1024)}) all-reduce(f32[2,192]{1,0:T(2,128)S(1)} %pad_maximum_fusion.27, f32[768]{0:T(1024)S(1)} %copy-done.155, f32[192]{0:T(256)S(1)} %reduce_sum.481, ...), channel_id=1, replica_groups=mesh['dp'=4,'ctx'=2,'mp'=4] {'dp','ctx'}, use_global_device_ids=true, to_apply=%region_59.60 | all-reduce | flops 2208 | bytes 17664 | tf_op jit(solution)/shard_map/psum | solution.py:509
  1344.9 43.1 %all-reduce = (f32[2,768]{1,0:T(2,128)}, f32[2,768]{1,0:T(2,128)}, f32[2,768]{1,0:T(2,128)}, f32[2,768]{1,0:T(2,128)}, f32[2,768]{1,0:T(2,128)}, /*index=5*/f32[2,768]{1,0:T(2,128)}) all-reduce(f32[2,768]{1,0:T(2,128)S(1)} %pad_maximum_fusion.21, ...), channel_id=1, replica_groups=mesh['dp'=4,'ctx'=2,'mp'=4] {'dp','ctx','mp'}, use_global_device_ids=true, to_apply=%region_51.52 | all-reduce | flops 9216 | bytes 73728 | tf_op jit(solution)/shard_map/psum | solution.py:534
  1391.0 387.1 %all-reduce.5.cloned.1.call-done = (f32[3,768,192]{1,2,0:T(8,128)}, f32[192,768]{1,0:T(8,128)}, f32[768,768]{1,0:T(8,128)}, f32[768,768]{1,0:T(8,128)}, f32[2,76...) async-done(((f32[3,768,192]{1,2,0:T(8,128)}, f32[192,768]{1,0:T(8,128)}, f32[768,768]{1,0:T(8,128)}, ...) | async-done | bytes 13860880 | tf_op jit(solution)/shard_map/psum | solution.py:509
  (772 shorter events, 353.9 us)
Async XLA Ops:
  7.2 549.8 %copy-start = (bf16[768,768]{1,0:T(8,128)(2,1)S(1)}, bf16[768,768]{1,0:T(8,128)(2,1)}, u32[]{:S(2)}) copy-start(bf16[768,768]{1,0:T(8,128)(2,1)} %param.55) | copy-start | bytes 3538948
  7.2 38.2 %copy-start.174 = (bf16[3,768,192]{1,2,0:T(8,128)(2,1)S(1)}, bf16[3,768,192]{1,2,0:T(8,128)(2,1)}, u32[]{:S(2)}) copy-start(bf16[3,768,192]{1,2,0:T(8,128)(2,1)} %param.38) | copy-start | bytes 2654212
  7.2 38.2 %all-gather.11.cloned.1.call-start = ((), (), s32[]{:S(2)}) async-start(), calls=%async_computation.10 | async-start | bytes 3932160 | tf_op jit(solution)/shard_map/all_gather | solution.py:61
  11.1 170.0 %copy-start.111 = (f32[768]{0:T(1024)}, f32[768]{0:T(1024)S(1)}, u32[]{:S(2)}) copy-start(f32[768]{0:T(1024)S(1)} %get-tuple-element.780) | copy-start | bytes 9220
  14.0 164.9 %reduce-scatter.11.cloned.1.call-start = ((), (), s32[]{:S(2)}) async-start(), calls=%async_computation.11 | async-start | bytes 7864320 | tf_op jit(solution)/shard_map/reduce_scatter | solution.py:70
  60.4 49.7 %collective-permute-start = (bf16[2,512,192]{1,2,0:T(8,128)(2,1)}, bf16[2,512,192]{1,2,0:T(8,128)(2,1)}, u32[]{:S(2)}, u32[]{:S(2)}) collective-permute-start(bf16[2,512,192]{1,2,0:T(8,128)(2,1)} %pad_maximum_fusion.10), channel_id=1, source_target_pairs={{0,4},{1,5},{2,6},{3,7},{8,12},{9,13},{10,14},{11,15},{16,20},{17,... | collective-permute-start | bytes 1179656 | tf_op jit(solution)/shard_map/ppermute | solution.py:22
  121.3 57.6 %copy-start.30 = (bf16[512,768]{1,0:T(8,128)(2,1)S(1)}, bf16[512,768]{1,0:T(8,128)(2,1)}, u32[]{:S(2)}) copy-start(bf16[512,768]{1,0:T(8,128)(2,1)} %param.32) | copy-start | bytes 2359300
  121.4 89.6 %all-gather.13.cloned.1.call-start = ((), (), s32[]{:S(2)}) async-start(), calls=%async_computation.12 | async-start | bytes 3932160 | tf_op jit(solution)/shard_map/all_gather | solution.py:61
  180.7 103.8 %copy-start.10 = (f32[512,768]{1,0:T(8,128)}, f32[512,768]{1,0:T(8,128)S(1)}, u32[]{:S(2)}) copy-start(f32[512,768]{1,0:T(8,128)S(1)} %get-tuple-element.715) | copy-start | bytes 4718596
  180.7 39.0 %copy-start.119 = (f32[512]{0:T(512)}, f32[512]{0:T(512)S(1)}, u32[]{:S(2)}) copy-start(f32[512]{0:T(512)S(1)} %broadcast_multiply_fusion.10) | copy-start | bytes 6148
  181.0 38.7 %copy-start.125 = (f32[512]{0:T(512)}, f32[512]{0:T(512)S(1)}, u32[]{:S(2)}) copy-start(f32[512]{0:T(512)S(1)} %add_rsqrt_fusion.2) | copy-start | bytes 6148
  182.3 102.2 %reduce-scatter.13.cloned.1.call-start = ((), (), s32[]{:S(2)}) async-start(), calls=%async_computation.13 | async-start | bytes 7864320 | tf_op jit(solution)/shard_map/reduce_scatter | solution.py:70
  182.7 37.0 %copy-start.156 = (f32[768]{0:T(1024)}, f32[768]{0:T(1024)S(1)}, u32[]{:S(2)}) copy-start(f32[768]{0:T(1024)S(1)} %convert_element_type.195) | copy-start | bytes 9220
  225.9 58.5 %copy-start.137 = (f32[768]{0:T(1024)S(1)}, f32[768]{0:T(1024)}, u32[]{:S(2)}) copy-start(f32[768]{0:T(1024)} %get-tuple-element.598) | copy-start | bytes 9220
  225.9 91.2 %all-gather.15.cloned.1.call-start = ((), (), s32[]{:S(2)}) async-start(), calls=%async_computation.14 | async-start | bytes 3932160 | tf_op jit(solution)/shard_map/all_gather | solution.py:61
  226.7 59.8 %copy-start.113 = (f32[768]{0:T(1024)}, f32[768]{0:T(1024)S(1)}, u32[]{:S(2)}) copy-start(f32[768]{0:T(1024)S(1)} %get-tuple-element.783) | copy-start | bytes 9220
  286.1 31.0 %copy-start.99 = (bf16[768,96]{0,1:T(8,128)(2,1)S(1)}, bf16[768,96]{0,1:T(8,128)(2,1)}, u32[]{:S(2)}) copy-start(bf16[768,96]{0,1:T(8,128)(2,1)} %param.49) | copy-start | bytes 442372
  286.2 34.7 %copy-start.121 = (f32[512]{0:T(512)}, f32[512]{0:T(512)S(1)}, u32[]{:S(2)}) copy-start(f32[512]{0:T(512)S(1)} %broadcast_multiply_fusion.9) | copy-start | bytes 6148
  286.5 34.4 %copy-start.127 = (f32[512]{0:T(512)}, f32[512]{0:T(512)S(1)}, u32[]{:S(2)}) copy-start(f32[512]{0:T(512)S(1)} %add_rsqrt_fusion.1) | copy-start | bytes 6148
  288.5 59.3 %all-gather.17.cloned.1.call-start = ((), (), s32[]{:S(2)}) async-start(), calls=%async_computation.15 | async-start | bytes 3932160 | tf_op jit(solution)/shard_map/all_gather | solution.py:366
  289.1 80.5 %all-gather.19.cloned.1.call-start = ((), (), s32[]{:S(2)}) async-start(), calls=%async_computation.16 | async-start | bytes 1966080 | tf_op jit(solution)/shard_map/all_gather | solution.py:367
  289.1 31.8 %copy-start.178 = (bf16[192]{0:T(256)(128)(2,1)S(1)}, bf16[192]{0:T(256)(128)(2,1)}, u32[]{:S(2)}) copy-start(bf16[192]{0:T(256)(128)(2,1)} %param.48) | copy-start | bytes 1156
  289.1 31.9 %copy-start.179 = (s32[6]{0:T(128)S(1)}, s32[6]{0:T(128)}, u32[]{:S(2)}) copy-start(s32[6]{0:T(128)} %param.35) | copy-start | bytes 76
  320.9 173.3 %reduce-scatter.15.cloned.1.call-start = ((), (), s32[]{:S(2)}) async-start(), calls=%async_computation.17 | async-start | bytes 7864320 | tf_op jit(solution)/shard_map/reduce_scatter | solution.py:70
  321.2 50.7 %copy-start.162 = (s32[3]{0:T(128)}, s32[3]{0:T(128)S(1)}, u32[]{:S(2)}) copy-start(s32[3]{0:T(128)S(1)} %compare_select_fusion) | copy-start | bytes 40
  378.7 46.6 %collective-permute-start.1 = (bf16[2,512,192]{1,2,0:T(8,128)(2,1)}, bf16[2,512,192]{1,2,0:T(8,128)(2,1)}, u32[]{:S(2)}, u32[]{:S(2)}) collective-permute-start(bf16[2,512,192]{1,2,0:T(8,128)(2,1)} %pad_maximum_fusion.13), channel_id=1, source_target_pairs={{0,4},{1,5},{2,6},{3,7},{8,12},{9,13},{10,14},{11,15},{16,20},{17,... | collective-permute-start | bytes 1179656 | tf_op jit(solution)/shard_map/ppermute | solution.py:22
  436.6 57.6 %copy-start.13 = (f32[512,768]{1,0:T(8,128)S(1)}, f32[512,768]{1,0:T(8,128)}, u32[]{:S(2)}) copy-start(f32[512,768]{1,0:T(8,128)} %copy-done.12) | copy-start | bytes 4718596
  436.6 90.3 %all-gather.21.cloned.1.call-start = ((), (), s32[]{:S(2)}) async-start(), calls=%async_computation.18 | async-start | bytes 3932160 | tf_op jit(solution)/shard_map/all_gather | solution.py:61
  495.9 31.0 %copy-start.170 = (bf16[768,768]{1,0:T(8,128)(2,1)S(1)}, bf16[768,768]{1,0:T(8,128)(2,1)}, u32[]{:S(2)}) copy-start(bf16[768,768]{1,0:T(8,128)(2,1)} %param.53) | copy-start | bytes 3538948
  498.2 58.8 %all-gather.23.cloned.1.call-start = ((), (), s32[]{:S(2)}) async-start(), calls=%async_computation.20 | async-start | bytes 3932160 | tf_op jit(solution)/shard_map/all_gather | solution.py:78
  498.8 135.3 %reduce-scatter.19.cloned.1.call-start = ((), (), s32[]{:S(2)}) async-start(), calls=%async_computation.21 | async-start | bytes 7864320 | tf_op jit(solution)/shard_map/reduce_scatter | solution.py:74
  575.6 119.3 %reduce-scatter.17.cloned.1.call-start = ((), (), s32[]{:S(2)}) async-start(), calls=%async_computation.19 | async-start | bytes 7864320 | tf_op jit(solution)/shard_map/reduce_scatter | solution.py:70
  583.5 50.6 %copy-start.20 = (f32[512,768]{1,0:T(8,128)S(1)}, f32[512,768]{1,0:T(8,128)}, u32[]{:S(2)}) copy-start(f32[512,768]{1,0:T(8,128)} %copy-done.19) | copy-start | bytes 4718596
  583.5 111.3 %copy-start.46 = (bf16[512,768]{1,0:T(8,128)(2,1)S(1)}, bf16[512,768]{1,0:T(8,128)(2,1)}, u32[]{:S(2)}) copy-start(bf16[512,768]{1,0:T(8,128)(2,1)} %param.33) | copy-start | bytes 2359300
  583.6 146.3 %all-gather.25.cloned.1.call-start = ((), (), s32[]{:S(2)}) async-start(), calls=%async_computation.22 | async-start | bytes 3932160 | tf_op jit(solution)/shard_map/all_gather | solution.py:78
  701.2 210.4 %reduce-scatter.21.cloned.1.call-start = ((), (), s32[]{:S(2)}) async-start(), calls=%async_computation.23 | async-start | bytes 3932160 | tf_op jit(solution)/shard_map/reduce_scatter | solution.py:428
  751.0 104.1 %collective-permute-start.2 = (f32[2,512,192]{1,2,0:T(8,128)}, f32[2,512,192]{1,2,0:T(8,128)}, u32[]{:S(2)}, u32[]{:S(2)}) collective-permute-start(f32[2,512,192]{1,2,0:T(8,128)} %pad_maximum_fusion.3), channel_id=1, source_target_pairs={{4,0},{5,1},{6,2},{7,3},{12,8},{13,9},{14,10},{15,11},{20,16},{21,... | collective-permute-start | bytes 2359304 | tf_op jit(solution)/shard_map/ppermute | solution.py:22
  871.4 106.4 %reduce-scatter.23.cloned.1.call-start = ((), (), s32[]{:S(2)}) async-start(), calls=%async_computation.24 | async-start | bytes 7864320 | tf_op jit(solution)/shard_map/reduce_scatter | solution.py:74
  872.7 42.0 %copy-start.53 = (bf16[1536,3,64]{0,2,1:T(8,128)(2,1)}, bf16[1536,3,64]{0,2,1:T(8,128)(2,1)S(1)}, u32[]{:S(2)}) copy-start(bf16[1536,3,64]{0,2,1:T(8,128)(2,1)S(1)} %convert.85) | copy-start | bytes 1769476
  874.2 39.4 %copy-start.38 = (bf16[3,512,3,64]{1,0,3,2:T(4,128)(2,1)}, bf16[3,512,3,64]{1,0,3,2:T(4,128)(2,1)S(1)}, u32[]{:S(2)}) copy-start(bf16[3,512,3,64]{1,0,3,2:T(4,128)(2,1)S(1)} %copy.95) | copy-start | bytes 1769476
  875.3 38.4 %copy-start.100 = (bf16[768,96]{0,1:T(8,128)(2,1)S(1)}, bf16[768,96]{0,1:T(8,128)(2,1)}, u32[]{:S(2)}) copy-start(bf16[768,96]{0,1:T(8,128)(2,1)} %param.49) | copy-start | bytes 442372
  879.2 35.5 %copy-start.76 = (bf16[512,3,64]{0,2,1:T(8,128)(2,1)}, bf16[512,3,64]{0,2,1:T(8,128)(2,1)S(1)}, u32[]{:S(2)}) copy-start(bf16[512,3,64]{0,2,1:T(8,128)(2,1)S(1)} %get-tuple-element.754) | copy-start | bytes 589828
  880.3 34.4 %copy-start.78 = (bf16[512,192]{0,1:T(8,128)(2,1)}, bf16[512,192]{0,1:T(8,128)(2,1)S(1)}, u32[]{:S(2)}) copy-start(bf16[512,192]{0,1:T(8,128)(2,1)S(1)} %fusion.190) | copy-start | bytes 589828
  919.2 58.5 %copy-start.14 = (f32[512,768]{1,0:T(8,128)S(1)}, f32[512,768]{1,0:T(8,128)}, u32[]{:S(2)}) copy-start(f32[512,768]{1,0:T(8,128)} %copy-done.12) | copy-start | bytes 4718596
  919.2 58.5 %copy-start.114 = (f32[768]{0:T(1024)S(1)}, f32[768]{0:T(1024)}, u32[]{:S(2)}) copy-start(f32[768]{0:T(1024)} %copy-done.113) | copy-start | bytes 9220
  919.3 58.5 %copy-start.122 = (f32[512]{0:T(512)S(1)}, f32[512]{0:T(512)}, u32[]{:S(2)}) copy-start(f32[512]{0:T(512)} %copy-done.121) | copy-start | bytes 6148
  919.3 58.5 %copy-start.128 = (f32[512]{0:T(512)S(1)}, f32[512]{0:T(512)}, u32[]{:S(2)}) copy-start(f32[512]{0:T(512)} %copy-done.127) | copy-start | bytes 6148
  919.3 94.7 %all-gather.27.cloned.1.call-start = ((), (), s32[]{:S(2)}) async-start(), calls=%async_computation.25 | async-start | bytes 3932160 | tf_op jit(solution)/shard_map/all_gather | solution.py:78
  983.2 30.8 %copy-start.172 = (bf16[768,768]{1,0:T(8,128)(2,1)S(1)}, bf16[768,768]{1,0:T(8,128)(2,1)}, u32[]{:S(2)}) copy-start(bf16[768,768]{1,0:T(8,128)(2,1)} %param.44) | copy-start | bytes 3538948
  985.3 104.3 %reduce-scatter.25.cloned.1.call-start = ((), (), s32[]{:S(2)}) async-start(), calls=%async_computation.26 | async-start | bytes 7864320 | tf_op jit(solution)/shard_map/reduce_scatter | solution.py:74
  1031.1 58.6 %copy-start.11 = (f32[512,768]{1,0:T(8,128)S(1)}, f32[512,768]{1,0:T(8,128)}, u32[]{:S(2)}) copy-start(f32[512,768]{1,0:T(8,128)} %copy-done.10) | copy-start | bytes 4718596
  1031.1 58.6 %copy-start.112 = (f32[768]{0:T(1024)S(1)}, f32[768]{0:T(1024)}, u32[]{:S(2)}) copy-start(f32[768]{0:T(1024)} %copy-done.111) | copy-start | bytes 9220
  1031.1 58.6 %copy-start.120 = (f32[512]{0:T(512)S(1)}, f32[512]{0:T(512)}, u32[]{:S(2)}) copy-start(f32[512]{0:T(512)} %copy-done.119) | copy-start | bytes 6148
  1031.1 58.6 %copy-start.126 = (f32[512]{0:T(512)S(1)}, f32[512]{0:T(512)}, u32[]{:S(2)}) copy-start(f32[512]{0:T(512)} %copy-done.125) | copy-start | bytes 6148
  1031.1 94.8 %all-gather.29.cloned.1.call-start = ((), (), s32[]{:S(2)}) async-start(), calls=%async_computation.27 | async-start | bytes 3932160 | tf_op jit(solution)/shard_map/all_gather | solution.py:78
  1097.2 164.2 %reduce-scatter.27.cloned.1.call-start = ((), (), s32[]{:S(2)}) async-start(), calls=%async_computation.28 | async-start | bytes 7864320 | tf_op jit(solution)/shard_map/reduce_scatter | solution.py:425
  1107.4 235.2 %reduce-scatter.29.cloned.1.call-start = ((), (), s32[]{:S(2)}) async-start(), calls=%async_computation.29 | async-start | bytes 7864320 | tf_op jit(solution)/shard_map/reduce_scatter | solution.py:74
  1151.7 107.8 %collective-permute-start.3 = (f32[2,512,192]{1,2,0:T(8,128)}, f32[2,512,192]{1,2,0:T(8,128)}, u32[]{:S(2)}, u32[]{:S(2)}) collective-permute-start(f32[2,512,192]{1,2,0:T(8,128)} %pad_maximum_fusion.4), channel_id=1, source_target_pairs={{4,0},{5,1},{6,2},{7,3},{12,8},{13,9},{14,10},{15,11},{20,16},{21,... | collective-permute-start | bytes 2359304 | tf_op jit(solution)/shard_map/ppermute | solution.py:22
  1270.9 507.2 %all-reduce.5.cloned.1.call-start = ((), (), s32[]{:S(2)}) async-start(), calls=%async_computation.30 | async-start | bytes 27721728 | tf_op jit(solution)/shard_map/psum | solution.py:509
  1302.8 39.8 %copy-start.31 = (bf16[512,768]{1,0:T(8,128)(2,1)S(1)}, bf16[512,768]{1,0:T(8,128)(2,1)}, u32[]{:S(2)}) copy-start(bf16[512,768]{1,0:T(8,128)(2,1)} %param.32) | copy-start | bytes 2359300
  1302.9 39.8 %copy-start.116 = (f32[768]{0:T(1024)S(1)}, f32[768]{0:T(1024)}, u32[]{:S(2)}) copy-start(f32[768]{0:T(1024)} %copy-done.115) | copy-start | bytes 9220
  1302.9 39.8 %copy-start.118 = (f32[512]{0:T(512)S(1)}, f32[512]{0:T(512)}, u32[]{:S(2)}) copy-start(f32[512]{0:T(512)} %copy-done.117) | copy-start | bytes 6148
  1302.9 39.8 %copy-start.124 = (f32[512]{0:T(512)S(1)}, f32[512]{0:T(512)}, u32[]{:S(2)}) copy-start(f32[512]{0:T(512)} %copy-done.123) | copy-start | bytes 6148
  1302.9 85.1 %copy-start.35 = (f32[512,768]{1,0:T(8,128)S(1)}, f32[512,768]{1,0:T(8,128)}, u32[]{:S(2)}) copy-start(f32[512,768]{1,0:T(8,128)} %copy-done.34) | copy-start | bytes 4718596
  (176 other events, 648.9 us)
Sparse Core Ops, SparseCore 0:
  14.2 31.2 all-gather.10
  121.5 57.4 reduce-scatter.10
  182.4 28.5 all-gather.12
  226.1 58.3 reduce-scatter.12
  288.6 28.5 all-gather.14
  319.2 28.5 all-gather.16
  349.9 19.6 all-gather.18
  436.7 57.4 reduce-scatter.14
  498.3 28.5 all-gather.20
  528.4 28.5 all-gather.22
  575.7 58.3 reduce-scatter.18
  636.5 58.3 reduce-scatter.16
  701.3 28.5 all-gather.24
  871.5 40.0 reduce-scatter.20
  919.4 58.3 reduce-scatter.22
  985.4 28.5 all-gather.26
  1031.2 58.3 reduce-scatter.24
  1097.3 28.5 all-gather.28
  1128.4 58.4 reduce-scatter.26
  1271.0 60.3 reduce-scatter.28
  1339.4 438.6 all-reduce.4
where the time goes:
time: 1800 us
  waiting for transfers between devices  1060 us (59%)
  matrix products  311 us (17%)
  other arithmetic  171 us (10%)
  local copies, waits for them, and re-layouts  117 us (6%)
  blocking collectives  81.8 us (5%)
  loops' own time  24.1 us (1%)
    psum x1, waiting for transfers between devices, shards(): lax.psum((grad_proj1, grad_fbias1, mats1[0], mats1[1], mats1[2], mats1[3]...  387 us
    reduce_scatter x4, waiting for transfers between devices, branch_out(): lax.psum_scatter(dot_plain(left, weight), 'mp', scatter_dimension=0, tile...  229 us
    reduce_scatter x4, waiting for transfers between devices, spread_back(): lax.psum_scatter(back_fn(grad_cols), 'mp', scatter_dimension=0, tiled=True)  167 us
    all_gather x4, waiting for transfers between devices, project(): gathered = lax.all_gather(normed, 'mp', axis=0, tiled=True)  113 us
    all_gather x4, waiting for transfers between devices, gather_grad(): lax.all_gather(share_grad.astype(jnp.bfloat16), 'mp', axis=0, tiled=True)  98.1 us
    convert_element_type x8, other arithmetic, one_block(): grad_scores = (weights * (grad_weights - inner)).astype(jnp.bfloat16)  67.4 us
    dot_general x14, matrix products, masked_scores(): jnp.einsum('qhe,khe->hqk', block_queries, keys, preferred_element_type=jn...  57.5 us
    unnamed x385, local copies, waits for them, and re-layouts  43.1 us
  transfers between devices with their start and end apart: 25, of which 19 were waited for; matrix products, arithmetic and copies ran while one was open for 21% of the time, Pallas kernels for 0%

commit v1 on v0

v1 whole, which is shorter than its diff:
```python
import functools

import jax
import jax.numpy as jnp
from jax import lax
from jax.experimental import pallas as pl
from jax.experimental.pallas import tpu as pltpu
from jax.sharding import PartitionSpec as P

D = 768
HD = 64
REUSE = 6
WIN = 512
GROUP = 3
BAND = GROUP * HD
TILE = 256
TILES = 3 * WIN // TILE
EPS = 1e-05
SCALE = HD**-0.5
F32 = jnp.float32
BF16 = jnp.bfloat16


def swap(value, axis, bit):
    devices = range(lax.axis_size(axis))
    return lax.ppermute(value, axis, [(i, i ^ bit) for i in devices])


def gather_shards(own):
    far = swap(own, "mp", 2)
    near = swap(own, "mp", 1)
    return [own, near, far, swap(far, "mp", 1)]


def in_order(parts):
    me = lax.axis_index("mp")
    result = jnp.zeros((4,) + parts[0].shape, parts[0].dtype)
    for distance, part in enumerate(parts):
        result = lax.dynamic_update_index_in_dim(result, part, me ^ distance, 0)
    return result


def by_distance(stacked):
    me = lax.axis_index("mp")
    return [
        lax.dynamic_index_in_dim(stacked, me ^ distance, 0, keepdims=False)
        for distance in range(4)
    ]


def dot(left, right, left_dim, right_dim):
    return lax.dot_general(
        left, right, (((left_dim,), (right_dim,)), ((), ())), preferred_element_type=F32
    )


def norm_rows(value, gain, shift):
    mean = jnp.mean(value, axis=-1, keepdims=True)
    centred = value - mean
    spread = jnp.mean(centred * centred, axis=-1, keepdims=True)
    scale = lax.rsqrt(spread + EPS)
    unit = centred * scale
    return (unit * gain + shift).astype(BF16), unit, scale


def norm_back(grad, unit, scale, gain):
    scaled = grad * gain
    inner = (
        scaled
        - jnp.mean(scaled, axis=-1, keepdims=True)
        - unit * jnp.mean(scaled * unit, axis=-1, keepdims=True)
    )
    return scale * inner, jnp.sum(grad * unit, axis=0), jnp.sum(grad, axis=0)


def attend_kernel(first_ref, lo_ref, q_ref, k0, k1, k2, v0, v1, v2, out_ref, exact_ref, sum_ref, top, total, acc):
    keys, values = (k2, k1, k0), (v2, v1, v0)
    for t in range(WIN // TILE):
        cols = slice(t * TILE, (t + 1) * TILE)
        low = lo_ref[:, cols]
        place = 2 * WIN + t * TILE + lax.broadcasted_iota(jnp.int32, (1, TILE), 1)
        last = 2 * WIN // TILE + t

        def scores(kt, j):
            rows = slice(j * HD, (j + 1) * HD)
            span = slice(kt % 2 * TILE, (kt % 2 + 1) * TILE)
            return dot(keys[kt // 2][0, rows, span], q_ref[0, rows, cols] * SCALE, 0, 0)

        def tile(kt):
            spot = kt * TILE + lax.broadcasted_iota(jnp.int32, (TILE, TILE), 0)
            keep = spot >= low
            if kt == last:
                keep = keep & (spot <= place)
            span = slice(kt % 2 * TILE, (kt % 2 + 1) * TILE)
            for j in range(GROUP):
                rows = slice(j * HD, (j + 1) * HD)
                raw = jnp.where(keep, scores(kt, j), -jnp.inf)
                peak = jnp.max(raw, axis=0, keepdims=True)
                if kt != last:
                    before = top[j]
                    peak = jnp.maximum(peak, before)
                powers = jnp.exp(raw - peak)
                added = jnp.sum(powers, axis=0, keepdims=True)
                result = dot(values[kt // 2][0, rows, span], powers.astype(BF16), 1, 0)
                if kt != last:
                    shrink = jnp.exp(before - peak)
                    added = added + total[j] * shrink
                    result = result + acc[j] * shrink
                top[j] = peak
                total[j] = added
                acc[j] = result

        tile(last)
        for kt in reversed(range(last)):
            pl.when(kt >= first_ref[t])(functools.partial(tile, kt))
        for j in range(GROUP):
            rows = slice(j * HD, (j + 1) * HD)
            result = acc[j] / total[j]
            out_ref[0, rows, cols] = result.astype(BF16)
            exact_ref[0, rows, cols] = result
            sum_ref[0, j : j + 1, cols] = top[j] + jnp.log(total[j])


def attend_back_kernel(
    first_ref, lo_ref, q_ref, k0, k1, k2, v0, v1, v2, out_ref, grad_ref, sum_ref,
    dq_ref, dk0, dk1, dk2, dv0, dv1, dv2, acc_k, acc_v, acc_q,
):
    keys, values = (k2, k1, k0), (v2, v1, v0)
    acc_k[...] = jnp.zeros_like(acc_k)
    acc_v[...] = jnp.zeros_like(acc_v)
    for t in range(WIN // TILE):
        cols = slice(t * TILE, (t + 1) * TILE)
        low = lo_ref[:, cols]
        place = 2 * WIN + t * TILE + lax.broadcasted_iota(jnp.int32, (1, TILE), 1)
        last = 2 * WIN // TILE + t

        def tile(kt):
            spot = kt * TILE + lax.broadcasted_iota(jnp.int32, (TILE, TILE), 0)
            keep = spot >= low
            if kt == last:
                keep = keep & (spot <= place)
            span = slice(kt % 2 * TILE, (kt % 2 + 1) * TILE)
            for j in range(GROUP):
                rows = slice(j * HD, (j + 1) * HD)
                key = keys[kt // 2][0, rows, span]
                query = q_ref[0, rows, cols] * SCALE
                grad = grad_ref[0, rows, cols]
                inner = jnp.sum(
                    grad.astype(F32) * out_ref[0, rows, cols], axis=0, keepdims=True
                )
                raw = jnp.where(keep, dot(key, query, 0, 0), -jnp.inf)
                weights = jnp.exp(raw - sum_ref[0, j : j + 1, cols])
                grad_weights = dot(values[kt // 2][0, rows, span], grad, 0, 0)
                low_grad = (weights * (grad_weights - inner)).astype(BF16)
                acc_v[kt, rows, :] += dot(grad, weights.astype(BF16), 1, 1)
                acc_k[kt, rows, :] += dot(query, low_grad, 1, 1)
                result = dot(key, low_grad, 1, 0)
                if kt != last:
                    result = result + acc_q[j]
                acc_q[j] = result

        tile(last)
        for kt in reversed(range(last)):
            pl.when(kt >= first_ref[t])(functools.partial(tile, kt))
        for j in range(GROUP):
            rows = slice(j * HD, (j + 1) * HD)
            dq_ref[0, rows, cols] = acc_q[j] * SCALE
    for part, (dk, dv) in enumerate(((dk2, dv2), (dk1, dv1), (dk0, dv0))):
        for half in range(2):
            span = slice(half * TILE, (half + 1) * TILE)
            dk[0, :, span] = acc_k[2 * part + half].astype(dk.dtype)
            dv[0, :, span] = acc_v[2 * part + half].astype(dv.dtype)


def band(place):
    return pl.BlockSpec((1, BAND, WIN), lambda s, *_: (s, place, 0))


LOW = pl.BlockSpec((1, WIN), lambda s, *_: (0, 0))
SUMS = pl.BlockSpec((1, 8, WIN), lambda s, *_: (s, 0, 0))


def attend(first, low, operands, places):
    return pl.pallas_call(
        attend_kernel,
        grid_spec=pltpu.PrefetchScalarGridSpec(
            num_scalar_prefetch=1,
            grid=(4,),
            in_specs=[LOW] + [band(p) for p in places],
            out_specs=[band(0), band(0), SUMS],
            scratch_shapes=[
                pltpu.VMEM((GROUP, 1, TILE), F32),
                pltpu.VMEM((GROUP, 1, TILE), F32),
                pltpu.VMEM((GROUP, HD, TILE), F32),
            ],
        ),
        out_shape=[
            jax.ShapeDtypeStruct((4, BAND, WIN), BF16),
            jax.ShapeDtypeStruct((4, BAND, WIN), F32),
            jax.ShapeDtypeStruct((4, 8, WIN), F32),
        ],
        compiler_params=pltpu.CompilerParams(vmem_limit_bytes=32 * 1024 * 1024),
        name="attend",
    )(first, low, *operands)


def attend_back(first, low, operands, places, heads, grad_heads, sums):
    kinds = (F32, F32, BF16, BF16, F32, BF16, BF16)
    return pl.pallas_call(
        attend_back_kernel,
        grid_spec=pltpu.PrefetchScalarGridSpec(
            num_scalar_prefetch=1,
            grid=(4,),
            in_specs=[LOW] + [band(p) for p in places] + [band(0), band(0), SUMS],
            out_specs=[band(0)] * 7,
            scratch_shapes=[
                pltpu.VMEM((TILES, BAND, TILE), F32),
                pltpu.VMEM((TILES, BAND, TILE), F32),
                pltpu.VMEM((GROUP, HD, TILE), F32),
            ],
        ),
        out_shape=[jax.ShapeDtypeStruct((4, BAND, WIN), kind) for kind in kinds],
        compiler_params=pltpu.CompilerParams(vmem_limit_bytes=32 * 1024 * 1024),
        name="attend_back",
    )(first, low, *operands, heads, grad_heads, sums)


def routes():
    windows, groups = lax.axis_size("ctx"), lax.axis_size("mp")
    onward = [(c * groups + m, c * groups + m + 1) for c in range(windows) for m in (1, 2)]
    onward += [(c * groups, (c + 1) * groups) for c in range(windows - 1)]
    second = [(c * groups + 2, c * groups + 3) for c in range(windows)]
    first_home = [(c * groups + 3, c * groups + 2) for c in range(windows)]
    home = [(c * groups + 2, c * groups + 1) for c in range(windows)]
    home += [((c + 1) * groups, c * groups) for c in range(windows - 1)]
    return onward, second, first_home, home


def pass_on(block):
    onward, second, _, _ = routes()
    before = lax.ppermute(block, ("ctx", "mp"), onward)
    return before, lax.ppermute(before, ("ctx", "mp"), second)


def pass_home(before, earlier):
    _, _, first_home, home = routes()
    near, far = lax.ppermute((before, earlier), ("ctx", "mp"), first_home)
    far = (before.astype(F32) + far.astype(F32)).astype(BF16)
    return near.astype(F32) + lax.ppermute(far, ("ctx", "mp"), home).astype(F32)


def row_starts(lengths):
    part = lax.axis_index("mp")
    place = (part - 1) * WIN + jnp.arange(WIN, dtype=jnp.int32)
    ends = jnp.cumsum(lengths)
    begun = jnp.max(jnp.where(place[:, None] >= ends[None, :], ends[None, :], 0), axis=1)
    document = begun - (part - 1) * WIN + 2 * WIN
    window = jnp.where(lax.axis_index("ctx") > 0, WIN, 2 * WIN)
    low = jnp.where(part == 0, window, document).astype(jnp.int32)
    return low.reshape(1, WIN), low[::TILE] // TILE


def reduce_shards(parts):
    own, near, far, last = parts
    near, last = swap(jnp.stack([near, last]), "mp", 1)
    far = (far.astype(F32) + last.astype(F32)).astype(BF16)
    far = swap(far, "mp", 2)
    total = own.astype(F32) + near.astype(F32) + far.astype(F32)
    return sum_replicas(total.astype(BF16))


def sum_replicas(value):
    steps = [("ctx", 1)]
    bit = 1
    while bit < lax.axis_size("dp"):
        steps.append(("dp", bit))
        bit *= 2
    for axis, bit in steps:
        high = (lax.axis_index(axis) // bit) % 2
        half = value.shape[0] // 2
        kept = lax.dynamic_slice_in_dim(value, high * half, half, 0)
        sent = lax.dynamic_slice_in_dim(value, (1 - high) * half, half, 0)
        value = (kept.astype(F32) + swap(sent, axis, bit).astype(F32)).astype(BF16)
    for axis, bit in reversed(steps):
        high = (lax.axis_index(axis) // bit) % 2
        half = value.shape[0]
        other = swap(value, axis, bit)
        whole = jnp.zeros((2 * half,) + value.shape[1:], BF16)
        whole = lax.dynamic_update_slice_in_dim(whole, value, high * half, 0)
        value = lax.dynamic_update_slice_in_dim(whole, other, (1 - high) * half, 0)
    return value


def sum_all(value):
    for axis in ("mp", "ctx", "dp"):
        bit = 1
        while bit < lax.axis_size(axis):
            value = value + swap(value, axis, bit)
            bit *= 2
    return value


def gelu(hidden):
    return jax.nn.gelu(hidden, approximate=True)


def tail_forward(stream, heads, out_weight, out_bias, gain, shift, ups, up_biases, downs):
    stream = stream + dot(heads, out_weight, 0, 0) + out_bias[0]
    normed, unit, scale = norm_rows(stream, gain[1], shift[1])
    hidden, active, total = [], [], out_bias[1]
    for up, bias, down in zip(ups, up_biases, downs, strict=True):
        hidden.append(dot(normed, up, 1, 0) + bias)
        active.append(gelu(hidden[-1]).astype(BF16))
        total = total + dot(active[-1], down, 1, 0)
    return stream + total, (normed, unit, scale, hidden, active)


def tail_backward(grad, kept, out_weight, gain, ups, downs):
    normed, unit, scale, hidden, active = kept
    bias_mlp = jnp.sum(grad, axis=0)
    rounded = grad.astype(BF16)
    mats, up_biases, normed_grad = [], [], 0.0
    for up, down, before, after in zip(ups, downs, hidden, active, strict=True):
        _, pull = jax.vjp(gelu, before)
        grad_hidden = pull(dot(rounded, down, 1, 1))[0]
        up_biases.append(jnp.sum(grad_hidden, axis=0))
        low = grad_hidden.astype(BF16)
        mats.append(
            jnp.concatenate(
                [dot(normed, low, 0, 0).astype(BF16), dot(after, rounded, 0, 0).astype(BF16)]
            )
        )
        normed_grad = normed_grad + dot(low, up, 1, 1)
    middle, gain_grad, shift_grad = norm_back(normed_grad, unit, scale, gain[1])
    grad = grad + middle
    bias_attn = jnp.sum(grad, axis=0)
    rounded = grad.astype(BF16)
    grad_heads = dot(out_weight, rounded, 1, 1).astype(BF16)
    return grad, rounded, grad_heads, mats, up_biases, (gain_grad, shift_grad, bias_attn, bias_mlp)


def turned(weight):
    return jnp.swapaxes(weight, -1, -2)


def shards(
    block_input, cotangent, doc_lengths, reuse_heads,
    norm_gain1, norm_bias1, projections1, front_bias1, out_weight1, out_bias1,
    up_weight1, up_bias1, down_weight1,
    norm_gain2, norm_bias2, query_key2, query_bias2, fresh_value2, value_bias2,
    out_weight2, out_bias2, up_weight2, up_bias2, down_weight2,
):
    low, first = row_starts(doc_lengths[0])

    front1 = in_order(gather_shards(turned(projections1).reshape(3 * BAND, D)))
    small = jnp.concatenate(
        [front_bias1.reshape(-1), query_bias2, value_bias2, up_bias1, up_bias2]
    )
    filler = (-small.shape[0]) % 1024
    small = gather_shards(jnp.pad(small, (0, filler)).reshape(-1, 128))
    small = [part.reshape(-1) for part in small]
    n_front, n_query, n_value, n_up = 2 * BAND, BAND, BAND // 2, D
    cuts = [n_front, n_front + n_query, n_front + n_query + n_value]
    up_biases1 = [part[cuts[2] : cuts[2] + n_up] for part in small]
    up_biases2 = [part[cuts[2] + n_up : cuts[2] + 2 * n_up] for part in small]
    ordered = in_order([part[: cuts[2]] for part in small])
    none = jnp.zeros((4, BAND), BF16)
    bias1 = jnp.concatenate([ordered[:, :BAND], none, ordered[:, BAND:n_front]], axis=1)
    bias2 = jnp.concatenate(
        [ordered[:, n_front : cuts[1]], none, ordered[:, cuts[1] : cuts[2]]], axis=1
    )
    outs1 = in_order(gather_shards(out_weight1)).reshape(D, D)
    ups1 = gather_shards(up_weight1)
    downs1 = gather_shards(down_weight1)
    front2 = in_order(
        gather_shards(
            jnp.concatenate([turned(query_key2).reshape(2 * BAND, D), turned(fresh_value2)])
        )
    )
    outs2 = in_order(gather_shards(out_weight2)).reshape(D, D)
    ups2 = gather_shards(up_weight2)
    downs2 = gather_shards(down_weight2)

    stream0 = block_input.astype(F32)
    normed1, unit1, scale1 = norm_rows(stream0, norm_gain1[0], norm_bias1[0])
    n_front1, n_front2 = front1.shape[1], front2.shape[1]
    cols1 = dot(front1.reshape(-1, D), normed1, 1, 1).reshape(4, n_front1, WIN)
    cols1 = (cols1 + bias1[:, :, None]).astype(BF16)
    before1, earlier1 = pass_on(cols1[:, BAND:])
    operands1 = (cols1, cols1, before1, earlier1, cols1, before1, earlier1)
    places1 = (0, 1, 0, 0, 2, 1, 1)
    heads1, exact1, sums1 = attend(first, low, operands1, places1)
    stream1, kept1 = tail_forward(
        stream0, heads1.reshape(D, WIN), outs1, out_bias1, norm_gain1, norm_bias1,
        ups1, up_biases1, downs1,
    )

    normed2, unit2, scale2 = norm_rows(stream1, norm_gain2[0], norm_bias2[0])
    cols2 = dot(front2.reshape(-1, D), normed2, 1, 1).reshape(4, n_front2, WIN)
    cols2 = (cols2 + bias2[:, :, None]).astype(BF16)
    before2, earlier2 = pass_on(cols2[:, BAND:])

    def mixed(first_values, fresh):
        first_values = first_values.reshape(-1, HD, WIN)
        reused = [
            lax.dynamic_index_in_dim(first_values, reuse_heads[n], 0, keepdims=True)
            for n in range(REUSE)
        ]
        return jnp.concatenate(reused + [fresh.reshape(-1, HD, WIN)]).reshape(4, BAND, WIN)

    values2 = [
        mixed(cols1[:, 2 * BAND :], cols2[:, 2 * BAND :]),
        mixed(before1[:, BAND:], before2[:, BAND:]),
        mixed(earlier1[:, BAND:], earlier2[:, BAND:]),
    ]
    operands2 = (cols2, cols2, before2, earlier2, *values2)
    places2 = (0, 1, 0, 0, 0, 0, 0)
    heads2, exact2, sums2 = attend(first, low, operands2, places2)
    stream2, kept2 = tail_forward(
        stream1, heads2.reshape(D, WIN), outs2, out_bias2, norm_gain2, norm_bias2,
        ups2, up_biases2, downs2,
    )
    block_output = stream2.astype(BF16)

    grad, rounded, grad_heads, mats2, up_grads2, small2 = tail_backward(
        cotangent.astype(F32), kept2, outs2, norm_gain2, ups2, downs2
    )
    mats2 = reduce_shards(mats2)
    dq2, dk2, dk2_before, dk2_earlier, dv2, dv2_before, dv2_earlier = attend_back(
        first, low, operands2, places2, exact2, grad_heads.reshape(4, BAND, WIN), sums2
    )
    grad_out2 = dot(heads2.reshape(D, WIN), rounded, 1, 0).astype(BF16).reshape(4, BAND, D)

    def fresh_part(grads):
        return grads[2:].reshape(4, BAND // 2, WIN)

    def join2(keys, values):
        return jnp.concatenate([keys, fresh_part(values)], axis=1)

    kv2 = join2(dk2, dv2) + pass_home(
        join2(dk2_before, dv2_before), join2(dk2_earlier, dv2_earlier)
    )
    dcols2 = jnp.concatenate([dq2, kv2], axis=1)
    bias_grad2 = jnp.sum(dcols2, axis=2)
    dcols2 = dcols2.astype(BF16)
    grad_front2 = dot(dcols2.reshape(-1, WIN), normed2, 1, 0).astype(BF16).reshape(4, n_front2, D)
    attn2 = [
        jnp.pad(jnp.concatenate(pair), ((0, D - BAND - n_front2), (0, 0)))
        for pair in zip(by_distance(grad_out2), by_distance(grad_front2), strict=True)
    ]
    attn2 = reduce_shards(attn2)
    normed_grad = dot(dcols2.reshape(-1, WIN), front2.reshape(-1, D), 0, 0)
    middle, gain_front2, shift_front2 = norm_back(normed_grad, unit2, scale2, norm_gain2[0])
    grad = grad + middle

    grad, rounded, grad_heads, mats1, up_grads1, small1 = tail_backward(
        grad, kept1, outs1, norm_gain1, ups1, downs1
    )
    mats1 = reduce_shards(mats1)
    dq1, dk1, dk1_before, dk1_earlier, dv1, dv1_before, dv1_earlier = attend_back(
        first, low, operands1, places1, exact1, grad_heads.reshape(4, BAND, WIN), sums1
    )
    grad_out1 = dot(heads1.reshape(D, WIN), rounded, 1, 0).astype(BF16).reshape(4, BAND, D)

    def reused(values, grads):
        heads = values.astype(F32).reshape(-1, HD, WIN)
        given = grads[:2].astype(F32).reshape(-1, HD, WIN)
        taken = jnp.arange(heads.shape[0])[:, None] == reuse_heads[None, :]
        for n in range(REUSE):
            heads = heads + jnp.where(taken[:, n, None, None], given[n], 0.0)
        return heads.reshape(values.shape)

    def join1(keys, values, grads):
        return jnp.concatenate([keys, reused(values, grads).astype(keys.dtype)], axis=1)

    kv1 = join1(dk1, dv1, dv2) + pass_home(
        join1(dk1_before, dv1_before, dv2_before), join1(dk1_earlier, dv1_earlier, dv2_earlier)
    )
    dcols1 = jnp.concatenate([dq1, kv1], axis=1)
    bias_grad1 = jnp.sum(dcols1, axis=2)
    dcols1 = dcols1.astype(BF16)
    grad_front1 = dot(dcols1.reshape(-1, WIN), normed1, 1, 0).astype(BF16).reshape(4, n_front1, D)
    attn1 = [
        jnp.concatenate(pair)
        for pair in zip(by_distance(grad_out1), by_distance(grad_front1), strict=True)
    ]
    attn1 = reduce_shards(attn1)
    normed_grad = dot(dcols1.reshape(-1, WIN), front1.reshape(-1, D), 0, 0)
    middle, gain_front1, shift_front1 = norm_back(normed_grad, unit1, scale1, norm_gain1[0])
    input_grad = (grad + middle).astype(BF16)

    vectors = [
        gain_front1, small1[0], shift_front1, small1[1], small1[2], small1[3],
        gain_front2, small2[0], shift_front2, small2[1], small2[2], small2[3],
        bias_grad1[:, :BAND].reshape(-1), bias_grad1[:, 2 * BAND :].reshape(-1),
        bias_grad2[:, :BAND].reshape(-1), bias_grad2[:, 2 * BAND :].reshape(-1),
        in_order(up_grads1).reshape(-1), in_order(up_grads2).reshape(-1),
    ]
    lengths = [vector.shape[0] for vector in vectors]
    packed = jnp.concatenate(vectors)
    filler = (-packed.shape[0]) % 1024
    packed = sum_all(jnp.pad(packed, (0, filler)).reshape(-1, 128)).reshape(-1)
    sums, at = [], 0
    for length in lengths:
        sums.append(packed[at : at + length])
        at += length
    me = lax.axis_index("mp")

    def mine(vector):
        return lax.dynamic_index_in_dim(vector.reshape(4, -1), me, 0, keepdims=False)

    def pair(i):
        return jnp.stack([sums[i], sums[i + 1]])

    mats1, attn1 = mats1.astype(F32), attn1.astype(F32)
    mats2, attn2 = mats2.astype(F32), attn2.astype(F32)
    return (
        block_output,
        input_grad,
        pair(0),
        pair(2),
        turned(attn1[BAND : BAND + n_front1].reshape(3, BAND, D)),
        jnp.stack([mine(sums[12]), mine(sums[13])]),
        attn1[:BAND],
        pair(4),
        mats1[:D],
        mine(sums[16]),
        mats1[D:],
        pair(6),
        pair(8),
        turned(attn2[BAND : 3 * BAND].reshape(2, BAND, D)),
        mine(sums[14]),
        turned(attn2[3 * BAND : BAND + n_front2]),
        mine(sums[15]),
        attn2[:BAND],
        pair(10),
        mats2[:D],
        mine(sums[17]),
        mats2[D:],
    )


def solution(mesh):
    rows = P(("dp", "ctx", "mp"), None)
    placed = (
        rows, rows, P(("dp", "ctx"), None), P(),
        P(), P(), P(None, None, "mp"), P(None, "mp"), P("mp", None), P(),
        P(None, "mp"), P("mp"), P("mp", None),
        P(), P(), P(None, None, "mp"), P("mp"), P(None, "mp"), P("mp"),
        P("mp", None), P(), P(None, "mp"), P("mp"), P("mp", None),
    )
    given = (
        rows, rows,
        P(), P(), P(None, None, "mp"), P(None, "mp"), P("mp", None), P(),
        P(None, "mp"), P("mp"), P("mp", None),
        P(), P(), P(None, None, "mp"), P("mp"), P(None, "mp"), P("mp"),
        P("mp", None), P(), P(None, "mp"), P("mp"), P("mp", None),
    )
    return jax.shard_map(shards, mesh=mesh, in_specs=placed, out_specs=given, check_vma=False)
```

time: 1800 us -> 820 us (0.46)
  waiting for transfers between devices: 1060 us -> 303 us
  matrix products: 311 us -> 109 us
  starting transfers between devices: 13.8 us -> 148 us
  other arithmetic: 171 us -> 81.6 us
  blocking collectives: 81.8 us -> 0 us
  Pallas kernels: 0 us -> 49.7 us
  loops' own time: 24.1 us -> 0 us
    reduce_scatter x10 -> x0, waiting for transfers between devices: 428 us -> none  [the longest x4 229 us: branch_out(): lax.psum_scatter(dot_plain(left, weight), 'mp', scatter_dimension=0, tile...]
    psum x1 -> x0, waiting for transfers between devices: 387 us -> none  [shards(): lax.psum((grad_proj1, grad_fbias1, mats1[0], mats1[1], mats1[2], mats1[3]...]
    ppermute x4 -> x74, waiting for transfers between devices: 0.01 us -> 303 us  [the longest x64 261 us: swap(): return lax.ppermute(value, axis, [(i, i ^ bit) for i in devices])]
    all_gather x10 -> x0, waiting for transfers between devices: 246 us -> none  [the longest x4 113 us: project(): gathered = lax.all_gather(normed, 'mp', axis=0, tiled=True)]
    dot_general x80 -> x60, matrix products: 303 us -> 109 us  [dot(): lax.dot_general(left, right, (((left_dim,), (right_dim,)), ((), ())), pre...]
    ppermute x4 -> x74, starting transfers between devices: 11.3 us -> 148 us  [the longest x64 122 us: swap(): return lax.ppermute(value, axis, [(i, i ^ bit) for i in devices])]
    psum x2 -> x0, blocking collectives: 81.8 us -> none  [the longest x1 43.1 us: shards(): lax.psum((gains1, shifts1, biases1, gains2, shifts2, biases2), ('dp', 'ct...]
    pallas_call x0 -> x4, Pallas kernels: none -> 49.7 us  [the longest x2 26 us: attend_back(): pl.pallas_call(attend_back_kernel, grid_spec=pltpu.PrefetchScalarGridSpec...]
  transfers between devices with their start and end apart: 25 -> 74, of which waited for: 19 -> 28; matrix products, arithmetic and copies ran while one was open for 21% -> 31% of each run, Pallas kernels for 0% -> 4%
where the time goes in v1:
time: 820 us; the launch traced here: 817 us
  waiting for transfers between devices  303 us (37%)
  starting transfers between devices  148 us (18%)
  local copies, waits for them, and re-layouts  110 us (13%)
  matrix products  109 us (13%)
  other arithmetic  81.6 us (10%)
  Pallas kernels  49.7 us (6%)
  between operations  15.8 us (2%)
    ppermute x64, waiting for transfers between devices, swap(): return lax.ppermute(value, axis, [(i, i ^ bit) for i in devices])  261 us
    ppermute x64, starting transfers between devices, swap(): return lax.ppermute(value, axis, [(i, i ^ bit) for i in devices])  122 us
    dot_general x60, matrix products, dot(): lax.dot_general(left, right, (((left_dim,), (right_dim,)), ((), ())), pre...  109 us
    unnamed x394, local copies, waits for them, and re-layouts  30.7 us
    ppermute x2, waiting for transfers between devices, pass_home(): return near.astype(F32) + lax.ppermute(far, ('ctx', 'mp'), home).astype(F32)  28.9 us
    pallas_call x2, Pallas kernels, attend_back(): pl.pallas_call(attend_back_kernel, grid_spec=pltpu.PrefetchScalarGridSpec...  26 us
    pallas_call x2, Pallas kernels, attend(): pl.pallas_call(attend_kernel, grid_spec=pltpu.PrefetchScalarGridSpec(num_...  23.8 us
  transfers between devices with their start and end apart: 74, of which 28 were waited for; matrix products, arithmetic and copies ran while one was open for 31% of the time, Pallas kernels for 4%

profile of v1, /device:TPU:0, one launch (start us, length us, event | category | flops | bytes accessed | tf_op | source)
XLA Modules:
  0.0 816.9 jit_solution(8249920214493349337)
XLA Ops:
  1.4 2.8 concatenate.108
  4.7 2.6 collective-permute-start.4
  54.3 4.2 add_convert_fusion.q_ref.k0.v0
  58.6 3.6 collective-permute-start.6
  66.5 13.6 %collective-permute-done.6.k1.v1 = bf16[4,384,512]{2,1,0:T(8,128)(2,1)S(1)} collective-permute-done((bf16[4,384,512]{2,1,0:T(8,128)(2,1)S(1)}, bf16[4,384,512]{2,1,0:T(8,128)(2,1)S(1)}, u32[]{:S(2)}, u32[]{:S(2)}) %collective-permute-start.6) | collective-permute-done | bytes 1572896 | tf_op jit(solution)/shard_map/ppermute | solution.py:241
  83.1 10.6 %collective-permute-start.10 = (bf16[192,768]{1,0:T(8,128)(2,1)}, bf16[192,768]{1,0:T(8,128)(2,1)S(1)}, u32[]{:S(2)}, u32[]{:S(2)}) collective-permute-start(bf16[192,768]{1,0:T(8,128)(2,1)} %collective-permute-done.9), channel_id=1, source_target_pairs={{0,1},{1,0},{2,3},{3,2},{4,5},{5,4},{6,7},{7,6},{8,9},{9,8},{10,11... | collective-permute-start | bytes 884744 | tf_op jit(solution)/shard_map/ppermute | solution.py:26
  93.7 3.1 collective-permute-start.13
  103.7 20.0 %collective-permute-done.13 = bf16[768,768]{1,0:T(8,128)(2,1)S(1)} collective-permute-done((bf16[768,768]{1,0:T(8,128)(2,1)S(1)}, bf16[768,768]{1,0:T(8,128)(2,1)S(1)}, u32[]{:S(2)}, u32[]{:S(2)}) %collective-permute-start.13) | collective-permute-done | bytes 1179680 | tf_op jit(solution)/shard_map/ppermute | solution.py:26
  125.6 11.9 %attend.2 = (bf16[4,192,512]{2,1,0:T(8,128)(2,1)S(1)}, f32[4,192,512]{2,1,0:T(8,128)S(1)}, f32[4,8,512]{2,1,0:T(8,128)S(1)}) custom-call(s32[2]{0:T(128)S(1)} %and_select_fusion.first_ref, s32[1,512]{1,0:T(1,128)S(1)} %bitcast.549, bf16[4,576,512]{2,1,0:T(8,128)(2,1)S(1)} %add_convert_fusion.q_ref.k0.v0, ...), custom_call_target="tpu_custom_call" | custom-call | tf_op jit(solution)/shard_map/attend/pallas_call | solution.py:184
  137.5 3.0 fusion.186
  144.9 4.0 collective-permute-done.14
  148.9 11.8 %collective-permute-start.27 = (bf16[768,768]{1,0:T(8,128)(2,1)S(1)}, bf16[768,768]{1,0:T(8,128)(2,1)}, u32[]{:S(2)}, u32[]{:S(2)}) collective-permute-start(bf16[768,768]{1,0:T(8,128)(2,1)S(1)} %copy-done.139), channel_id=1, source_target_pairs={{0,2},{1,3},{2,0},{3,1},{4,6},{5,7},{6,4},{7,5},{8,10},{9,11},{10,... | collective-permute-start | bytes 3538952 | tf_op jit(solution)/shard_map/ppermute | solution.py:26
  167.8 3.7 add_convert_fusion.1.q_ref.k0
  171.7 11.1 %collective-permute-start.20 = (bf16[4,288,512]{2,1,0:T(8,128)(2,1)S(1)}, bf16[4,288,512]{2,1,0:T(8,128)(2,1)S(1)}, u32[]{:S(2)}, u32[]{:S(2)}) collective-permute-start(bf16[4,288,512]{2,1,0:T(8,128)(2,1)S(1)} %slice.468), channel_id=1, source_target_pairs={{1,2},{2,3},{5,6},{6,7},{0,4},{9,10},{10,11},{13,14},{14,15},{8,12... | collective-permute-start | bytes 3538952 | tf_op jit(solution)/shard_map/ppermute | solution.py:241
  182.9 16.5 %collective-permute-done.27 = bf16[768,768]{1,0:T(8,128)(2,1)} collective-permute-done((bf16[768,768]{1,0:T(8,128)(2,1)S(1)}, bf16[768,768]{1,0:T(8,128)(2,1)}, u32[]{:S(2)}, u32[]{:S(2)}) %collective-permute-start.27) | collective-permute-done | bytes 1179680 | tf_op jit(solution)/shard_map/ppermute | solution.py:26
  203.1 11.9 %attend.3 = (bf16[4,192,512]{2,1,0:T(8,128)(2,1)S(1)}, f32[4,192,512]{2,1,0:T(8,128)S(1)}, f32[4,8,512]{2,1,0:T(8,128)S(1)}) custom-call(s32[2]{0:T(128)S(1)} %and_select_fusion.first_ref, s32[1,512]{1,0:T(1,128)S(1)} %bitcast.550, bf16[4,480,512]{2,1,0:T(8,128)(2,1)S(1)} %copy-done.1, bf16[4,480,512]{2,1,0:T(8,128)(2,1)S(1)} %copy-done.1, ...), custom_call_target="tpu_custom_call" | custom-call | tf_op jit(solution)/shard_map/attend/pallas_call | solution.py:184
  218.0 2.8 fusion.164
  236.3 2.5 convolution_convert_fusion.2
  249.6 13.0 %attend_back.2 = (f32[4,192,512]{2,1,0:T(8,128)S(1)}, f32[4,192,512]{2,1,0:T(8,128)S(1)}, bf16[4,192,512]{2,1,0:T(8,128)(2,1)S(1)}, bf16[4,192,512]{2,1,0:T(8,12...) custom-call(s32[2]{0:T(128)S(1)} %and_select_fusion.first_ref, ...), custom_call_target="tpu_custom_call" | custom-call | tf_op jit(solution)/shard_map/attend_back/pallas_call | solution.py:209
  273.5 2.6 convolution_convert_fusion.10
  277.8 2.6 pad_maximum_fusion.2
  280.4 11.6 %collective-permute-start.66 = (bf16[2,1536,768]{2,1,0:T(8,128)(2,1)}, bf16[2,1536,768]{2,1,0:T(8,128)(2,1)}, u32[]{:S(2)}, u32[]{:S(2)}) collective-permute-start(bf16[2,1536,768]{2,1,0:T(8,128)(2,1)} %pad_maximum_fusion.2), channel_id=1, source_target_pairs={{0,1},{1,0},{2,3},{3,2},{4,5},{5,4},{6,7},{7,6},{8,9},{9,8},{10,11... | collective-permute-start | bytes 14155784 | tf_op jit(solution)/shard_map/ppermute | solution.py:26
  307.5 27.9 %collective-permute-done.33 = bf16[4,288,512]{2,1,0:T(8,128)(2,1)S(1)} collective-permute-done((bf16[4,288,512]{2,1,0:T(8,128)(2,1)S(1)}, bf16[4,288,512]{2,1,0:T(8,128)(2,1)S(1)}, u32[]{:S(2)}, u32[]{:S(2)}) %collective-permute-start.33) | collective-permute-done | bytes 1179680 | tf_op jit(solution)/shard_map/ppermute | solution.py:249
  338.7 4.9 fusion.108
  354.9 2.2 fusion.166
  359.1 2.2 fusion.168
  367.7 2.7 convolution_convert_fusion.20
  370.6 12.9 %attend_back.3 = (f32[4,192,512]{2,1,0:T(8,128)S(1)}, f32[4,192,512]{2,1,0:T(8,128)S(1)}, bf16[4,192,512]{2,1,0:T(8,128)(2,1)S(1)}, bf16[4,192,512]{2,1,0:T(8,12...) custom-call(s32[2]{0:T(128)S(1)} %and_select_fusion.first_ref, ...), custom_call_target="tpu_custom_call" | custom-call | tf_op jit(solution)/shard_map/attend_back/pallas_call | solution.py:209
  397.0 14.8 %collective-permute-start.58 = (bf16[2,768,768]{2,1,0:T(8,128)(2,1)}, bf16[2,768,768]{2,1,0:T(8,128)(2,1)S(1)}, u32[]{:S(2)}, u32[]{:S(2)}) collective-permute-start(bf16[2,768,768]{2,1,0:T(8,128)(2,1)} %pad_maximum_fusion.5), channel_id=1, source_target_pairs={{0,1},{1,0},{2,3},{3,2},{4,5},{5,4},{6,7},{7,6},{8,9},{9,8},{10,11... | collective-permute-start | bytes 7077896 | tf_op jit(solution)/shard_map/ppermute | solution.py:26
  428.4 2.5 pad_maximum_fusion.1
  444.1 18.4 %collective-permute-start.59 = (bf16[768,768]{1,0:T(8,128)(2,1)}, bf16[768,768]{1,0:T(8,128)(2,1)}, u32[]{:S(2)}, u32[]{:S(2)}) collective-permute-start(bf16[768,768]{1,0:T(8,128)(2,1)} %fusion.18), channel_id=1, source_target_pairs={{0,2},{1,3},{2,0},{3,1},{4,6},{5,7},{6,4},{7,5},{8,10},{9,11},{10,... | collective-permute-start | bytes 3538952 | tf_op jit(solution)/shard_map/ppermute | solution.py:26
  462.4 3.8 fusion
  468.2 2.8 maximum_add_fusion
  472.6 6.1 fusion.37
  491.0 4.8 collective-permute-start.37
  495.8 2.9 convolution_convert_fusion
  501.0 44.7 %collective-permute-done.38 = f32[144,128]{1,0:T(8,128)S(1)} collective-permute-done((f32[144,128]{1,0:T(8,128)S(1)}, f32[144,128]{1,0:T(8,128)S(1)}, u32[]{:S(2)}, u32[]{:S(2)}) %collective-permute-start.38) | collective-permute-done | bytes 73760 | tf_op jit(solution)/shard_map/ppermute | solution.py:26
  545.8 14.7 %collective-permute-start.39 = (f32[144,128]{1,0:T(8,128)S(1)}, f32[144,128]{1,0:T(8,128)S(1)}, u32[]{:S(2)}, u32[]{:S(2)}) collective-permute-start(f32[144,128]{1,0:T(8,128)S(1)} %fusion.286), channel_id=1, source_target_pairs={{0,4},{4,0},{1,5},{5,1},{2,6},{6,2},{3,7},{7,3},{8,12},{12,8},{9,1... | collective-permute-start | bytes 221192 | tf_op jit(solution)/shard_map/ppermute | solution.py:26
  562.9 4.3 collective-permute-done.40
  568.9 3.9 collective-permute-done.41
  579.3 2.6 collective-permute-start.60
  587.0 5.4 collective-permute-done.60
  594.7 4.6 collective-permute-done.61
  599.5 3.9 fusion.3
  603.4 3.3 fusion.2
  613.5 5.5 collective-permute-done.62
  631.2 2.4 collective-permute-start.43
  637.3 20.6 %collective-permute-done.51 = bf16[1536,768]{1,0:T(8,128)(2,1)} collective-permute-done((bf16[1536,768]{1,0:T(8,128)(2,1)}, bf16[1536,768]{1,0:T(8,128)(2,1)}, u32[]{:S(2)}, u32[]{:S(2)}) %collective-permute-start.51) | collective-permute-done | bytes 2359328 | tf_op jit(solution)/shard_map/ppermute | solution.py:26
  657.9 3.3 fusion.5
  661.7 15.6 %collective-permute-done.43 = bf16[768,768]{1,0:T(8,128)(2,1)S(1)} collective-permute-done((bf16[768,768]{1,0:T(8,128)(2,1)S(1)}, bf16[768,768]{1,0:T(8,128)(2,1)S(1)}, u32[]{:S(2)}, u32[]{:S(2)}) %collective-permute-start.43) | collective-permute-done | bytes 1179680 | tf_op jit(solution)/shard_map/ppermute | solution.py:26
  682.7 12.7 %collective-permute-done.44 = bf16[384,768]{1,0:T(8,128)(2,1)S(1)} collective-permute-done((bf16[384,768]{1,0:T(8,128)(2,1)S(1)}, bf16[384,768]{1,0:T(8,128)(2,1)S(1)}, u32[]{:S(2)}, u32[]{:S(2)}) %collective-permute-start.44) | collective-permute-done | bytes 589856 | tf_op jit(solution)/shard_map/ppermute | solution.py:26
  698.5 11.9 %collective-permute-done.45 = bf16[192,768]{1,0:T(8,128)(2,1)S(1)} collective-permute-done((bf16[192,768]{1,0:T(8,128)(2,1)S(1)}, bf16[192,768]{1,0:T(8,128)(2,1)S(1)}, u32[]{:S(2)}, u32[]{:S(2)}) %collective-permute-start.45) | collective-permute-done | bytes 294944 | tf_op jit(solution)/shard_map/ppermute | solution.py:26
  710.6 9.5 %collective-permute-done.53 = bf16[384,768]{1,0:T(8,128)(2,1)S(1)} collective-permute-done((bf16[384,768]{1,0:T(8,128)(2,1)S(1)}, bf16[384,768]{1,0:T(8,128)(2,1)S(1)}, u32[]{:S(2)}, u32[]{:S(2)}) %collective-permute-start.53) | collective-permute-done | bytes 589856 | tf_op jit(solution)/shard_map/ppermute | solution.py:26
  720.5 5.0 collective-permute-done.46
  725.6 10.7 %collective-permute-done.54 = bf16[192,768]{1,0:T(8,128)(2,1)S(1)} collective-permute-done((bf16[192,768]{1,0:T(8,128)(2,1)S(1)}, bf16[192,768]{1,0:T(8,128)(2,1)S(1)}, u32[]{:S(2)}, u32[]{:S(2)}) %collective-permute-start.54) | collective-permute-done | bytes 294944 | tf_op jit(solution)/shard_map/ppermute | solution.py:26
  736.8 6.5 collective-permute-done.47
  743.3 3.3 collective-permute-start.48
  746.6 5.1 collective-permute-done.55
  754.3 2.5 collective-permute-done.48
  758.1 9.0 %collective-permute-done.56 = bf16[384,768]{1,0:T(8,128)(2,1)S(1)} collective-permute-done((bf16[384,768]{1,0:T(8,128)(2,1)S(1)}, bf16[384,768]{1,0:T(8,128)(2,1)S(1)}, u32[]{:S(2)}, u32[]{:S(2)}) %collective-permute-start.56) | collective-permute-done | bytes 589856 | tf_op jit(solution)/shard_map/ppermute | solution.py:26
  769.0 24.5 %collective-permute-done.49 = bf16[384,768]{1,0:T(8,128)(2,1)S(1)} collective-permute-done((bf16[384,768]{1,0:T(8,128)(2,1)S(1)}, bf16[384,768]{1,0:T(8,128)(2,1)S(1)}, u32[]{:S(2)}, u32[]{:S(2)}) %collective-permute-start.49) | collective-permute-done | bytes 589856 | tf_op jit(solution)/shard_map/ppermute | solution.py:26
  795.9 2.5 fusion.177
  798.7 15.3 %collective-permute-done.57 = bf16[768,768]{1,0:T(8,128)(2,1)S(1)} collective-permute-done((bf16[768,768]{1,0:T(8,128)(2,1)S(1)}, bf16[768,768]{1,0:T(8,128)(2,1)S(1)}, u32[]{:S(2)}, u32[]{:S(2)}) %collective-permute-start.57) | collective-permute-done | bytes 1179680 | tf_op jit(solution)/shard_map/ppermute | solution.py:26
  814.1 2.5 fusion.178
  (847 shorter events, 266.9 us)
Async XLA Ops:
  4.2 43.4 %collective-permute-start.3 = (bf16[24,128]{1,0:T(8,128)(2,1)S(1)}, bf16[24,128]{1,0:T(8,128)(2,1)S(1)}, u32[]{:S(2)}, u32[]{:S(2)}) collective-permute-start(bf16[24,128]{1,0:T(8,128)(2,1)S(1)} %pad_bitcast_fusion.1), channel_id=1, source_target_pairs={{0,1},{1,0},{2,3},{3,2},{4,5},{5,4},{6,7},{7,6},{8,9},{9,8},{10,11... | collective-permute-start | bytes 18440 | tf_op jit(solution)/shard_map/ppermute | solution.py:26
  4.7 34.0 %collective-permute-start.4 = (bf16[24,128]{1,0:T(8,128)(2,1)S(1)}, bf16[24,128]{1,0:T(8,128)(2,1)S(1)}, u32[]{:S(2)}, u32[]{:S(2)}) collective-permute-start(bf16[24,128]{1,0:T(8,128)(2,1)S(1)} %pad_bitcast_fusion.1), channel_id=1, source_target_pairs={{0,2},{1,3},{2,0},{3,1},{4,6},{5,7},{6,4},{7,5},{8,10},{9,11},{10,... | collective-permute-start | bytes 18440 | tf_op jit(solution)/shard_map/ppermute | solution.py:26
  7.3 41.1 %collective-permute-start = (bf16[576,768]{1,0:T(8,128)(2,1)}, bf16[576,768]{1,0:T(8,128)(2,1)S(1)}, u32[]{:S(2)}, u32[]{:S(2)}) collective-permute-start(bf16[576,768]{1,0:T(8,128)(2,1)} %bitcast.609), channel_id=1, source_target_pairs={{0,1},{1,0},{2,3},{3,2},{4,5},{5,4},{6,7},{7,6},{8,9},{9,8},{10,11... | collective-permute-start | bytes 2654216 | tf_op jit(solution)/shard_map/ppermute | solution.py:26
  7.5 22.2 %collective-permute-start.1 = (bf16[576,768]{1,0:T(8,128)(2,1)}, bf16[576,768]{1,0:T(8,128)(2,1)}, u32[]{:S(2)}, u32[]{:S(2)}) collective-permute-start(bf16[576,768]{1,0:T(8,128)(2,1)} %bitcast.610), channel_id=1, source_target_pairs={{0,2},{1,3},{2,0},{3,1},{4,6},{5,7},{6,4},{7,5},{8,10},{9,11},{10,... | collective-permute-start | bytes 2654216 | tf_op jit(solution)/shard_map/ppermute | solution.py:26
  7.8 57.0 %collective-permute-start.8 = (bf16[192,768]{1,0:T(8,128)(2,1)}, bf16[192,768]{1,0:T(8,128)(2,1)}, u32[]{:S(2)}, u32[]{:S(2)}) collective-permute-start(bf16[192,768]{1,0:T(8,128)(2,1)} %param.32), channel_id=1, source_target_pairs={{0,1},{1,0},{2,3},{3,2},{4,5},{5,4},{6,7},{7,6},{8,9},{9,8},{10,11... | collective-permute-start | bytes 884744 | tf_op jit(solution)/shard_map/ppermute | solution.py:26
  29.7 23.6 %collective-permute-start.2 = (bf16[576,768]{1,0:T(8,128)(2,1)}, bf16[576,768]{1,0:T(8,128)(2,1)S(1)}, u32[]{:S(2)}, u32[]{:S(2)}) collective-permute-start(bf16[576,768]{1,0:T(8,128)(2,1)} %collective-permute-done.1), channel_id=1, source_target_pairs={{0,1},{1,0},{2,3},{3,2},{4,5},{5,4},{6,7},{7,6},{8,9},{9,8},{10,11... | collective-permute-start | bytes 2654216 | tf_op jit(solution)/shard_map/ppermute | solution.py:26
  47.6 18.9 %collective-permute-start.9 = (bf16[192,768]{1,0:T(8,128)(2,1)S(1)}, bf16[192,768]{1,0:T(8,128)(2,1)}, u32[]{:S(2)}, u32[]{:S(2)}) collective-permute-start(bf16[192,768]{1,0:T(8,128)(2,1)S(1)} %copy-done.95), channel_id=1, source_target_pairs={{0,2},{1,3},{2,0},{3,1},{4,6},{5,7},{6,4},{7,5},{8,10},{9,11},{10,... | collective-permute-start | bytes 884744 | tf_op jit(solution)/shard_map/ppermute | solution.py:26
  48.1 51.1 %collective-permute-start.17 = (bf16[480,768]{1,0:T(8,128)(2,1)}, bf16[480,768]{1,0:T(8,128)(2,1)}, u32[]{:S(2)}, u32[]{:S(2)}) collective-permute-start(bf16[480,768]{1,0:T(8,128)(2,1)} %pad_maximum_fusion.10), channel_id=1, source_target_pairs={{0,1},{1,0},{2,3},{3,2},{4,5},{5,4},{6,7},{7,6},{8,9},{9,8},{10,11... | collective-permute-start | bytes 2211848 | tf_op jit(solution)/shard_map/ppermute | solution.py:26
  48.5 50.0 %collective-permute-start.18 = (bf16[480,768]{1,0:T(8,128)(2,1)}, bf16[480,768]{1,0:T(8,128)(2,1)S(1)}, u32[]{:S(2)}, u32[]{:S(2)}) collective-permute-start(bf16[480,768]{1,0:T(8,128)(2,1)} %pad_maximum_fusion.10), channel_id=1, source_target_pairs={{0,2},{1,3},{2,0},{3,1},{4,6},{5,7},{6,4},{7,5},{8,10},{9,11},{10,... | collective-permute-start | bytes 2211848 | tf_op jit(solution)/shard_map/ppermute | solution.py:26
  58.6 21.5 %collective-permute-start.6 = (bf16[4,384,512]{2,1,0:T(8,128)(2,1)S(1)}, bf16[4,384,512]{2,1,0:T(8,128)(2,1)S(1)}, u32[]{:S(2)}, u32[]{:S(2)}) collective-permute-start(bf16[4,384,512]{2,1,0:T(8,128)(2,1)S(1)} %slice.462), channel_id=1, source_target_pairs={{1,2},{2,3},{5,6},{6,7},{0,4},{9,10},{10,11},{13,14},{14,15},{8,12... | collective-permute-start | bytes 4718600 | tf_op jit(solution)/shard_map/ppermute | solution.py:241
  64.8 18.3 %collective-permute-start.22 = (bf16[192,768]{1,0:T(8,128)(2,1)S(1)}, bf16[192,768]{1,0:T(8,128)(2,1)S(1)}, u32[]{:S(2)}, u32[]{:S(2)}) collective-permute-start(bf16[192,768]{1,0:T(8,128)(2,1)S(1)} %copy-done.96), channel_id=1, source_target_pairs={{0,1},{1,0},{2,3},{3,2},{4,5},{5,4},{6,7},{7,6},{8,9},{9,8},{10,11... | collective-permute-start | bytes 884744 | tf_op jit(solution)/shard_map/ppermute | solution.py:26
  66.5 27.2 %collective-permute-start.23 = (bf16[192,768]{1,0:T(8,128)(2,1)S(1)}, bf16[192,768]{1,0:T(8,128)(2,1)S(1)}, u32[]{:S(2)}, u32[]{:S(2)}) collective-permute-start(bf16[192,768]{1,0:T(8,128)(2,1)S(1)} %copy-done.96), channel_id=1, source_target_pairs={{0,2},{1,3},{2,0},{3,1},{4,6},{5,7},{6,4},{7,5},{8,10},{9,11},{10,... | collective-permute-start | bytes 884744 | tf_op jit(solution)/shard_map/ppermute | solution.py:26
  80.1 45.5 %collective-permute-start.7 = (bf16[4,384,512]{2,1,0:T(8,128)(2,1)S(1)}, bf16[4,384,512]{2,1,0:T(8,128)(2,1)S(1)}, u32[]{:S(2)}, u32[]{:S(2)}) collective-permute-start(bf16[4,384,512]{2,1,0:T(8,128)(2,1)S(1)} %collective-permute-done.6.k1.v1), channel_id=1, source_target_pairs={{2,3},{6,7},{10,11},{14,15},{18,19},{22,23},{26,27},{30,31}} | collective-permute-start | bytes 4718600 | tf_op jit(solution)/shard_map/ppermute | solution.py:242
  83.1 13.7 %collective-permute-start.10 = (bf16[192,768]{1,0:T(8,128)(2,1)}, bf16[192,768]{1,0:T(8,128)(2,1)S(1)}, u32[]{:S(2)}, u32[]{:S(2)}) collective-permute-start(bf16[192,768]{1,0:T(8,128)(2,1)} %collective-permute-done.9), channel_id=1, source_target_pairs={{0,1},{1,0},{2,3},{3,2},{4,5},{5,4},{6,7},{7,6},{8,9},{9,8},{10,11... | collective-permute-start | bytes 884744 | tf_op jit(solution)/shard_map/ppermute | solution.py:26
  93.7 29.9 %collective-permute-start.13 = (bf16[768,768]{1,0:T(8,128)(2,1)S(1)}, bf16[768,768]{1,0:T(8,128)(2,1)S(1)}, u32[]{:S(2)}, u32[]{:S(2)}) collective-permute-start(bf16[768,768]{1,0:T(8,128)(2,1)S(1)} %copy-done.144), channel_id=1, source_target_pairs={{0,2},{1,3},{2,0},{3,1},{4,6},{5,7},{6,4},{7,5},{8,10},{9,11},{10,... | collective-permute-start | bytes 3538952 | tf_op jit(solution)/shard_map/ppermute | solution.py:26
  96.8 52.1 %collective-permute-start.14 = (bf16[768,768]{1,0:T(8,128)(2,1)S(1)}, bf16[768,768]{1,0:T(8,128)(2,1)S(1)}, u32[]{:S(2)}, u32[]{:S(2)}) collective-permute-start(bf16[768,768]{1,0:T(8,128)(2,1)S(1)} %copy-done.142), channel_id=1, source_target_pairs={{0,2},{1,3},{2,0},{3,1},{4,6},{5,7},{6,4},{7,5},{8,10},{9,11},{10,... | collective-permute-start | bytes 3538952 | tf_op jit(solution)/shard_map/ppermute | solution.py:26
  99.2 64.7 %collective-permute-start.12 = (bf16[768,768]{1,0:T(8,128)(2,1)S(1)}, bf16[768,768]{1,0:T(8,128)(2,1)S(1)}, u32[]{:S(2)}, u32[]{:S(2)}) collective-permute-start(bf16[768,768]{1,0:T(8,128)(2,1)S(1)} %copy-done.142), channel_id=1, source_target_pairs={{0,1},{1,0},{2,3},{3,2},{4,5},{5,4},{6,7},{7,6},{8,9},{9,8},{10,11... | collective-permute-start | bytes 3538952 | tf_op jit(solution)/shard_map/ppermute | solution.py:26
  102.7 58.0 %collective-permute-start.11 = (bf16[768,768]{1,0:T(8,128)(2,1)S(1)}, bf16[768,768]{1,0:T(8,128)(2,1)S(1)}, u32[]{:S(2)}, u32[]{:S(2)}) collective-permute-start(bf16[768,768]{1,0:T(8,128)(2,1)S(1)} %copy-done.144), channel_id=1, source_target_pairs={{0,1},{1,0},{2,3},{3,2},{4,5},{5,4},{6,7},{7,6},{8,9},{9,8},{10,11... | collective-permute-start | bytes 3538952 | tf_op jit(solution)/shard_map/ppermute | solution.py:26
  123.6 59.2 %collective-permute-start.28 = (bf16[768,768]{1,0:T(8,128)(2,1)S(1)}, bf16[768,768]{1,0:T(8,128)(2,1)S(1)}, u32[]{:S(2)}, u32[]{:S(2)}) collective-permute-start(bf16[768,768]{1,0:T(8,128)(2,1)S(1)} %copy-done.140), channel_id=1, source_target_pairs={{0,2},{1,3},{2,0},{3,1},{4,6},{5,7},{6,4},{7,5},{8,10},{9,11},{10,... | collective-permute-start | bytes 3538952 | tf_op jit(solution)/shard_map/ppermute | solution.py:26
  125.6 17.7 %collective-permute-start.15 = (bf16[768,768]{1,0:T(8,128)(2,1)S(1)}, bf16[768,768]{1,0:T(8,128)(2,1)S(1)}, u32[]{:S(2)}, u32[]{:S(2)}) collective-permute-start(bf16[768,768]{1,0:T(8,128)(2,1)S(1)} %collective-permute-done.13), channel_id=1, source_target_pairs={{0,1},{1,0},{2,3},{3,2},{4,5},{5,4},{6,7},{7,6},{8,9},{9,8},{10,11... | collective-permute-start | bytes 3538952 | tf_op jit(solution)/shard_map/ppermute | solution.py:26
  143.2 79.3 %collective-permute-start.26 = (bf16[768,768]{1,0:T(8,128)(2,1)S(1)}, bf16[768,768]{1,0:T(8,128)(2,1)S(1)}, u32[]{:S(2)}, u32[]{:S(2)}) collective-permute-start(bf16[768,768]{1,0:T(8,128)(2,1)S(1)} %copy-done.140), channel_id=1, source_target_pairs={{0,1},{1,0},{2,3},{3,2},{4,5},{5,4},{6,7},{7,6},{8,9},{9,8},{10,11... | collective-permute-start | bytes 3538952 | tf_op jit(solution)/shard_map/ppermute | solution.py:26
  148.9 50.5 %collective-permute-start.27 = (bf16[768,768]{1,0:T(8,128)(2,1)S(1)}, bf16[768,768]{1,0:T(8,128)(2,1)}, u32[]{:S(2)}, u32[]{:S(2)}) collective-permute-start(bf16[768,768]{1,0:T(8,128)(2,1)S(1)} %copy-done.139), channel_id=1, source_target_pairs={{0,2},{1,3},{2,0},{3,1},{4,6},{5,7},{6,4},{7,5},{8,10},{9,11},{10,... | collective-permute-start | bytes 3538952 | tf_op jit(solution)/shard_map/ppermute | solution.py:26
  164.0 57.7 %collective-permute-start.25 = (bf16[768,768]{1,0:T(8,128)(2,1)S(1)}, bf16[768,768]{1,0:T(8,128)(2,1)S(1)}, u32[]{:S(2)}, u32[]{:S(2)}) collective-permute-start(bf16[768,768]{1,0:T(8,128)(2,1)S(1)} %copy-done.139), channel_id=1, source_target_pairs={{0,1},{1,0},{2,3},{3,2},{4,5},{5,4},{6,7},{7,6},{8,9},{9,8},{10,11... | collective-permute-start | bytes 3538952 | tf_op jit(solution)/shard_map/ppermute | solution.py:26
  171.7 28.0 %collective-permute-start.20 = (bf16[4,288,512]{2,1,0:T(8,128)(2,1)S(1)}, bf16[4,288,512]{2,1,0:T(8,128)(2,1)S(1)}, u32[]{:S(2)}, u32[]{:S(2)}) collective-permute-start(bf16[4,288,512]{2,1,0:T(8,128)(2,1)S(1)} %slice.468), channel_id=1, source_target_pairs={{1,2},{2,3},{5,6},{6,7},{0,4},{9,10},{10,11},{13,14},{14,15},{8,12... | collective-permute-start | bytes 3538952 | tf_op jit(solution)/shard_map/ppermute | solution.py:241
  182.8 47.9 %collective-permute-start.30 = (bf16[768,768]{1,0:T(8,128)(2,1)S(1)}, bf16[768,768]{1,0:T(8,128)(2,1)S(1)}, u32[]{:S(2)}, u32[]{:S(2)}) collective-permute-start(bf16[768,768]{1,0:T(8,128)(2,1)S(1)} %collective-permute-done.28), channel_id=1, source_target_pairs={{0,1},{1,0},{2,3},{3,2},{4,5},{5,4},{6,7},{7,6},{8,9},{9,8},{10,11... | collective-permute-start | bytes 3538952 | tf_op jit(solution)/shard_map/ppermute | solution.py:26
  199.4 26.6 %collective-permute-start.29 = (bf16[768,768]{1,0:T(8,128)(2,1)}, bf16[768,768]{1,0:T(8,128)(2,1)S(1)}, u32[]{:S(2)}, u32[]{:S(2)}) collective-permute-start(bf16[768,768]{1,0:T(8,128)(2,1)} %collective-permute-done.27), channel_id=1, source_target_pairs={{0,1},{1,0},{2,3},{3,2},{4,5},{5,4},{6,7},{7,6},{8,9},{9,8},{10,11... | collective-permute-start | bytes 3538952 | tf_op jit(solution)/shard_map/ppermute | solution.py:26
  265.8 31.8 %collective-permute-start.32 = (bf16[4,288,512]{2,1,0:T(8,128)(2,1)}, bf16[4,288,512]{2,1,0:T(8,128)(2,1)}, u32[]{:S(2)}, u32[]{:S(2)}) collective-permute-start(bf16[4,288,512]{2,1,0:T(8,128)(2,1)} %pad_maximum_fusion.9), channel_id=1, source_target_pairs={{3,2},{7,6},{11,10},{15,14},{19,18},{23,22},{27,26},{31,30}} | collective-permute-start | bytes 3538952 | tf_op jit(solution)/shard_map/ppermute | solution.py:247
  268.7 38.8 %collective-permute-start.31 = (bf16[4,288,512]{2,1,0:T(8,128)(2,1)}, bf16[4,288,512]{2,1,0:T(8,128)(2,1)}, u32[]{:S(2)}, u32[]{:S(2)}) collective-permute-start(bf16[4,288,512]{2,1,0:T(8,128)(2,1)} %pad_maximum_fusion.8), channel_id=1, source_target_pairs={{3,2},{7,6},{11,10},{15,14},{19,18},{23,22},{27,26},{31,30}} | collective-permute-start | bytes 3538952 | tf_op jit(solution)/shard_map/ppermute | solution.py:247
  280.4 182.0 %collective-permute-start.66 = (bf16[2,1536,768]{2,1,0:T(8,128)(2,1)}, bf16[2,1536,768]{2,1,0:T(8,128)(2,1)}, u32[]{:S(2)}, u32[]{:S(2)}) collective-permute-start(bf16[2,1536,768]{2,1,0:T(8,128)(2,1)} %pad_maximum_fusion.2), channel_id=1, source_target_pairs={{0,1},{1,0},{2,3},{3,2},{4,5},{5,4},{6,7},{7,6},{8,9},{9,8},{10,11... | collective-permute-start | bytes 14155784 | tf_op jit(solution)/shard_map/ppermute | solution.py:26
  299.3 36.1 %collective-permute-start.33 = (bf16[4,288,512]{2,1,0:T(8,128)(2,1)S(1)}, bf16[4,288,512]{2,1,0:T(8,128)(2,1)S(1)}, u32[]{:S(2)}, u32[]{:S(2)}) collective-permute-start(bf16[4,288,512]{2,1,0:T(8,128)(2,1)S(1)} %add_convert_fusion.5), channel_id=1, source_target_pairs={{2,1},{6,5},{4,0},{10,9},{14,13},{12,8},{18,17},{22,21},{20,16},{2... | collective-permute-start | bytes 3538952 | tf_op jit(solution)/shard_map/ppermute | solution.py:249
  388.9 41.9 %collective-permute-start.35 = (bf16[4,384,512]{2,1,0:T(8,128)(2,1)S(1)}, bf16[4,384,512]{2,1,0:T(8,128)(2,1)S(1)}, u32[]{:S(2)}, u32[]{:S(2)}) collective-permute-start(bf16[4,384,512]{2,1,0:T(8,128)(2,1)S(1)} %pad_maximum_fusion.7), channel_id=1, source_target_pairs={{3,2},{7,6},{11,10},{15,14},{19,18},{23,22},{27,26},{31,30}} | collective-permute-start | bytes 4718600 | tf_op jit(solution)/shard_map/ppermute | solution.py:247
  397.0 45.3 %collective-permute-start.58 = (bf16[2,768,768]{2,1,0:T(8,128)(2,1)}, bf16[2,768,768]{2,1,0:T(8,128)(2,1)S(1)}, u32[]{:S(2)}, u32[]{:S(2)}) collective-permute-start(bf16[2,768,768]{2,1,0:T(8,128)(2,1)} %pad_maximum_fusion.5), channel_id=1, source_target_pairs={{0,1},{1,0},{2,3},{3,2},{4,5},{5,4},{6,7},{7,6},{8,9},{9,8},{10,11... | collective-permute-start | bytes 7077896 | tf_op jit(solution)/shard_map/ppermute | solution.py:26
  422.0 45.3 %collective-permute-start.34 = (bf16[4,384,512]{2,1,0:T(8,128)(2,1)}, bf16[4,384,512]{2,1,0:T(8,128)(2,1)}, u32[]{:S(2)}, u32[]{:S(2)}) collective-permute-start(bf16[4,384,512]{2,1,0:T(8,128)(2,1)} %pad_maximum_fusion.6), channel_id=1, source_target_pairs={{3,2},{7,6},{11,10},{15,14},{19,18},{23,22},{27,26},{31,30}} | collective-permute-start | bytes 4718600 | tf_op jit(solution)/shard_map/ppermute | solution.py:247
  432.5 35.7 %collective-permute-start.36 = (bf16[4,384,512]{2,1,0:T(8,128)(2,1)}, bf16[4,384,512]{2,1,0:T(8,128)(2,1)}, u32[]{:S(2)}, u32[]{:S(2)}) collective-permute-start(bf16[4,384,512]{2,1,0:T(8,128)(2,1)} %add_convert_fusion.2), channel_id=1, source_target_pairs={{2,1},{6,5},{4,0},{10,9},{14,13},{12,8},{18,17},{22,21},{20,16},{2... | collective-permute-start | bytes 4718600 | tf_op jit(solution)/shard_map/ppermute | solution.py:249
  436.0 163.5 %collective-permute-start.50 = (bf16[2,1536,768]{2,1,0:T(8,128)(2,1)}, bf16[2,1536,768]{2,1,0:T(8,128)(2,1)}, u32[]{:S(2)}, u32[]{:S(2)}) collective-permute-start(bf16[2,1536,768]{2,1,0:T(8,128)(2,1)} %pad_maximum_fusion.1), channel_id=1, source_target_pairs={{0,1},{1,0},{2,3},{3,2},{4,5},{5,4},{6,7},{7,6},{8,9},{9,8},{10,11... | collective-permute-start | bytes 14155784 | tf_op jit(solution)/shard_map/ppermute | solution.py:26
  444.1 133.1 %collective-permute-start.59 = (bf16[768,768]{1,0:T(8,128)(2,1)}, bf16[768,768]{1,0:T(8,128)(2,1)}, u32[]{:S(2)}, u32[]{:S(2)}) collective-permute-start(bf16[768,768]{1,0:T(8,128)(2,1)} %fusion.18), channel_id=1, source_target_pairs={{0,2},{1,3},{2,0},{3,1},{4,6},{5,7},{6,4},{7,5},{8,10},{9,11},{10,... | collective-permute-start | bytes 3538952 | tf_op jit(solution)/shard_map/ppermute | solution.py:26
  466.2 137.2 %collective-permute-start.67 = (bf16[1536,768]{1,0:T(8,128)(2,1)}, bf16[1536,768]{1,0:T(8,128)(2,1)}, u32[]{:S(2)}, u32[]{:S(2)}) collective-permute-start(bf16[1536,768]{1,0:T(8,128)(2,1)} %fusion), channel_id=1, source_target_pairs={{0,2},{1,3},{2,0},{3,1},{4,6},{5,7},{6,4},{7,5},{8,10},{9,11},{10,... | collective-permute-start | bytes 7077896 | tf_op jit(solution)/shard_map/ppermute | solution.py:26
  500.8 44.9 %collective-permute-start.38 = (f32[144,128]{1,0:T(8,128)S(1)}, f32[144,128]{1,0:T(8,128)S(1)}, u32[]{:S(2)}, u32[]{:S(2)}) collective-permute-start(f32[144,128]{1,0:T(8,128)S(1)} %fusion.149), channel_id=1, source_target_pairs={{0,2},{1,3},{2,0},{3,1},{4,6},{5,7},{6,4},{7,5},{8,10},{9,11},{10,... | collective-permute-start | bytes 221192 | tf_op jit(solution)/shard_map/ppermute | solution.py:26
  545.8 17.0 %collective-permute-start.39 = (f32[144,128]{1,0:T(8,128)S(1)}, f32[144,128]{1,0:T(8,128)S(1)}, u32[]{:S(2)}, u32[]{:S(2)}) collective-permute-start(f32[144,128]{1,0:T(8,128)S(1)} %fusion.286), channel_id=1, source_target_pairs={{0,4},{4,0},{1,5},{5,1},{2,6},{6,2},{3,7},{7,3},{8,12},{12,8},{9,1... | collective-permute-start | bytes 221192 | tf_op jit(solution)/shard_map/ppermute | solution.py:26
  562.1 67.5 %collective-permute-start.42 = (bf16[2,768,768]{2,1,0:T(8,128)(2,1)}, bf16[2,768,768]{2,1,0:T(8,128)(2,1)}, u32[]{:S(2)}, u32[]{:S(2)}) collective-permute-start(bf16[2,768,768]{2,1,0:T(8,128)(2,1)} %pad_maximum_fusion.4), channel_id=1, source_target_pairs={{0,1},{1,0},{2,3},{3,2},{4,5},{5,4},{6,7},{7,6},{8,9},{9,8},{10,11... | collective-permute-start | bytes 7077896 | tf_op jit(solution)/shard_map/ppermute | solution.py:26
  579.3 13.1 %collective-permute-start.60 = (bf16[384,768]{1,0:T(8,128)(2,1)S(1)}, bf16[384,768]{1,0:T(8,128)(2,1)S(1)}, u32[]{:S(2)}, u32[]{:S(2)}) collective-permute-start(bf16[384,768]{1,0:T(8,128)(2,1)S(1)} %constant_dynamic-slice_fusion.8), channel_id=1, source_target_pairs={{0,4},{4,0},{1,5},{5,1},{2,6},{6,2},{3,7},{7,3},{8,12},{12,8},{9,1... | collective-permute-start | bytes 1769480 | tf_op jit(solution)/shard_map/ppermute | solution.py:26
  603.4 54.5 %collective-permute-start.51 = (bf16[1536,768]{1,0:T(8,128)(2,1)}, bf16[1536,768]{1,0:T(8,128)(2,1)}, u32[]{:S(2)}, u32[]{:S(2)}) collective-permute-start(bf16[1536,768]{1,0:T(8,128)(2,1)} %fusion.3), channel_id=1, source_target_pairs={{0,2},{1,3},{2,0},{3,1},{4,6},{5,7},{6,4},{7,5},{8,10},{9,11},{10,... | collective-permute-start | bytes 7077896 | tf_op jit(solution)/shard_map/ppermute | solution.py:26
  607.8 25.8 %collective-permute-start.68 = (bf16[768,768]{1,0:T(8,128)(2,1)}, bf16[768,768]{1,0:T(8,128)(2,1)}, u32[]{:S(2)}, u32[]{:S(2)}) collective-permute-start(bf16[768,768]{1,0:T(8,128)(2,1)} %constant_dynamic-slice_fusion.3), channel_id=1, source_target_pairs={{0,4},{4,0},{1,5},{5,1},{2,6},{6,2},{3,7},{7,3},{8,12},{12,8},{9,1... | collective-permute-start | bytes 3538952 | tf_op jit(solution)/shard_map/ppermute | solution.py:26
  609.0 10.0 %collective-permute-start.62 = (bf16[96,768]{1,0:T(8,128)(2,1)}, bf16[96,768]{1,0:T(8,128)(2,1)}, u32[]{:S(2)}, u32[]{:S(2)}) collective-permute-start(bf16[96,768]{1,0:T(8,128)(2,1)} %constant_dynamic-slice_fusion.6), channel_id=1, source_target_pairs={{0,16},{8,24},{16,0},{24,8},{1,17},{9,25},{17,1},{25,9},{2,18},{10... | collective-permute-start | bytes 442376 | tf_op jit(solution)/shard_map/ppermute | solution.py:26
  629.6 50.6 %collective-permute-start.64 = (bf16[192,768]{1,0:T(8,128)(2,1)}, bf16[192,768]{1,0:T(8,128)(2,1)S(1)}, u32[]{:S(2)}, u32[]{:S(2)}) collective-permute-start(bf16[192,768]{1,0:T(8,128)(2,1)} %constant_dynamic-update-slice_fusion.14), channel_id=1, source_target_pairs={{0,8},{8,0},{16,24},{24,16},{1,9},{9,1},{17,25},{25,17},{2,10},{10... | collective-permute-start | bytes 884744 | tf_op jit(solution)/shard_map/ppermute | solution.py:26
  631.2 46.0 %collective-permute-start.43 = (bf16[768,768]{1,0:T(8,128)(2,1)S(1)}, bf16[768,768]{1,0:T(8,128)(2,1)S(1)}, u32[]{:S(2)}, u32[]{:S(2)}) collective-permute-start(bf16[768,768]{1,0:T(8,128)(2,1)S(1)} %fusion.21), channel_id=1, source_target_pairs={{0,2},{1,3},{2,0},{3,1},{4,6},{5,7},{6,4},{7,5},{8,10},{9,11},{10,... | collective-permute-start | bytes 3538952 | tf_op jit(solution)/shard_map/ppermute | solution.py:26
  635.2 47.1 %collective-permute-start.69 = (bf16[384,768]{1,0:T(8,128)(2,1)S(1)}, bf16[384,768]{1,0:T(8,128)(2,1)S(1)}, u32[]{:S(2)}, u32[]{:S(2)}) collective-permute-start(bf16[384,768]{1,0:T(8,128)(2,1)S(1)} %constant_dynamic-slice_fusion.2), channel_id=1, source_target_pairs={{0,8},{8,0},{16,24},{24,16},{1,9},{9,1},{17,25},{25,17},{2,10},{10... | collective-permute-start | bytes 1769480 | tf_op jit(solution)/shard_map/ppermute | solution.py:26
  661.3 34.7 %collective-permute-start.52 = (bf16[768,768]{1,0:T(8,128)(2,1)S(1)}, bf16[768,768]{1,0:T(8,128)(2,1)S(1)}, u32[]{:S(2)}, u32[]{:S(2)}) collective-permute-start(bf16[768,768]{1,0:T(8,128)(2,1)S(1)} %constant_dynamic-slice_fusion.12), channel_id=1, source_target_pairs={{0,4},{4,0},{1,5},{5,1},{2,6},{6,2},{3,7},{7,3},{8,12},{12,8},{9,1... | collective-permute-start | bytes 3538952 | tf_op jit(solution)/shard_map/ppermute | solution.py:26
  679.1 16.3 %collective-permute-start.44 = (bf16[384,768]{1,0:T(8,128)(2,1)S(1)}, bf16[384,768]{1,0:T(8,128)(2,1)S(1)}, u32[]{:S(2)}, u32[]{:S(2)}) collective-permute-start(bf16[384,768]{1,0:T(8,128)(2,1)S(1)} %constant_dynamic-slice_fusion.17), channel_id=1, source_target_pairs={{0,4},{4,0},{1,5},{5,1},{2,6},{6,2},{3,7},{7,3},{8,12},{12,8},{9,1... | collective-permute-start | bytes 1769480 | tf_op jit(solution)/shard_map/ppermute | solution.py:26
  680.3 71.8 %collective-permute-start.65 = (bf16[384,768]{1,0:T(8,128)(2,1)S(1)}, bf16[384,768]{1,0:T(8,128)(2,1)S(1)}, u32[]{:S(2)}, u32[]{:S(2)}) collective-permute-start(bf16[384,768]{1,0:T(8,128)(2,1)S(1)} %constant_dynamic-update-slice_fusion.12), channel_id=1, source_target_pairs={{0,4},{4,0},{1,5},{5,1},{2,6},{6,2},{3,7},{7,3},{8,12},{12,8},{9,1... | collective-permute-start | bytes 1769480 | tf_op jit(solution)/shard_map/ppermute | solution.py:26
  682.5 15.6 %collective-permute-start.70 = (bf16[192,768]{1,0:T(8,128)(2,1)S(1)}, bf16[192,768]{1,0:T(8,128)(2,1)S(1)}, u32[]{:S(2)}, u32[]{:S(2)}) collective-permute-start(bf16[192,768]{1,0:T(8,128)(2,1)S(1)} %constant_dynamic-slice_fusion.1), channel_id=1, source_target_pairs={{0,16},{8,24},{16,0},{24,8},{1,17},{9,25},{17,1},{25,9},{2,18},{10... | collective-permute-start | bytes 884744 | tf_op jit(solution)/shard_map/ppermute | solution.py:26
  695.7 14.7 %collective-permute-start.45 = (bf16[192,768]{1,0:T(8,128)(2,1)S(1)}, bf16[192,768]{1,0:T(8,128)(2,1)S(1)}, u32[]{:S(2)}, u32[]{:S(2)}) collective-permute-start(bf16[192,768]{1,0:T(8,128)(2,1)S(1)} %constant_dynamic-slice_fusion.16), channel_id=1, source_target_pairs={{0,8},{8,0},{16,24},{24,16},{1,9},{9,1},{17,25},{25,17},{2,10},{10... | collective-permute-start | bytes 884744 | tf_op jit(solution)/shard_map/ppermute | solution.py:26
  696.4 23.7 %collective-permute-start.53 = (bf16[384,768]{1,0:T(8,128)(2,1)S(1)}, bf16[384,768]{1,0:T(8,128)(2,1)S(1)}, u32[]{:S(2)}, u32[]{:S(2)}) collective-permute-start(bf16[384,768]{1,0:T(8,128)(2,1)S(1)} %constant_dynamic-slice_fusion.11), channel_id=1, source_target_pairs={{0,8},{8,0},{16,24},{24,16},{1,9},{9,1},{17,25},{25,17},{2,10},{10... | collective-permute-start | bytes 1769480 | tf_op jit(solution)/shard_map/ppermute | solution.py:26
  698.3 22.0 %collective-permute-start.71 = (bf16[192,768]{1,0:T(8,128)(2,1)S(1)}, bf16[192,768]{1,0:T(8,128)(2,1)S(1)}, u32[]{:S(2)}, u32[]{:S(2)}) collective-permute-start(bf16[192,768]{1,0:T(8,128)(2,1)S(1)} %get-tuple-element.97), channel_id=1, source_target_pairs={{0,16},{8,24},{16,0},{24,8},{1,17},{9,25},{17,1},{25,9},{2,18},{10... | collective-permute-start | bytes 884744 | tf_op jit(solution)/shard_map/ppermute | solution.py:26
  710.5 14.9 %collective-permute-start.46 = (bf16[96,768]{1,0:T(8,128)(2,1)S(1)}, bf16[96,768]{1,0:T(8,128)(2,1)S(1)}, u32[]{:S(2)}, u32[]{:S(2)}) collective-permute-start(bf16[96,768]{1,0:T(8,128)(2,1)S(1)} %constant_dynamic-slice_fusion.15), channel_id=1, source_target_pairs={{0,16},{8,24},{16,0},{24,8},{1,17},{9,25},{17,1},{25,9},{2,18},{10... | collective-permute-start | bytes 442376 | tf_op jit(solution)/shard_map/ppermute | solution.py:26
  720.3 16.0 %collective-permute-start.54 = (bf16[192,768]{1,0:T(8,128)(2,1)S(1)}, bf16[192,768]{1,0:T(8,128)(2,1)S(1)}, u32[]{:S(2)}, u32[]{:S(2)}) collective-permute-start(bf16[192,768]{1,0:T(8,128)(2,1)S(1)} %constant_dynamic-slice_fusion.10), channel_id=1, source_target_pairs={{0,16},{8,24},{16,0},{24,8},{1,17},{9,25},{17,1},{25,9},{2,18},{10... | collective-permute-start | bytes 884744 | tf_op jit(solution)/shard_map/ppermute | solution.py:26
  720.4 31.4 %collective-permute-start.72 = (bf16[384,768]{1,0:T(8,128)(2,1)S(1)}, bf16[384,768]{1,0:T(8,128)(2,1)S(1)}, u32[]{:S(2)}, u32[]{:S(2)}) collective-permute-start(bf16[384,768]{1,0:T(8,128)(2,1)S(1)} %constant_dynamic-update-slice_fusion.8), channel_id=1, source_target_pairs={{0,8},{8,0},{16,24},{24,16},{1,9},{9,1},{17,25},{25,17},{2,10},{10... | collective-permute-start | bytes 1769480 | tf_op jit(solution)/shard_map/ppermute | solution.py:26
  725.5 17.8 %collective-permute-start.47 = (bf16[96,768]{1,0:T(8,128)(2,1)S(1)}, bf16[96,768]{1,0:T(8,128)(2,1)S(1)}, u32[]{:S(2)}, u32[]{:S(2)}) collective-permute-start(bf16[96,768]{1,0:T(8,128)(2,1)S(1)} %get-tuple-element.103), channel_id=1, source_target_pairs={{0,16},{8,24},{16,0},{24,8},{1,17},{9,25},{17,1},{25,9},{2,18},{10... | collective-permute-start | bytes 442376 | tf_op jit(solution)/shard_map/ppermute | solution.py:26
  736.4 15.3 %collective-permute-start.55 = (bf16[192,768]{1,0:T(8,128)(2,1)S(1)}, bf16[192,768]{1,0:T(8,128)(2,1)S(1)}, u32[]{:S(2)}, u32[]{:S(2)}) collective-permute-start(bf16[192,768]{1,0:T(8,128)(2,1)S(1)} %get-tuple-element.101), channel_id=1, source_target_pairs={{0,16},{8,24},{16,0},{24,8},{1,17},{9,25},{17,1},{25,9},{2,18},{10... | collective-permute-start | bytes 884744 | tf_op jit(solution)/shard_map/ppermute | solution.py:26
  743.3 13.4 %collective-permute-start.48 = (bf16[192,768]{1,0:T(8,128)(2,1)S(1)}, bf16[192,768]{1,0:T(8,128)(2,1)S(1)}, u32[]{:S(2)}, u32[]{:S(2)}) collective-permute-start(bf16[192,768]{1,0:T(8,128)(2,1)S(1)} %constant_dynamic-update-slice_fusion.26), channel_id=1, source_target_pairs={{0,8},{8,0},{16,24},{24,16},{1,9},{9,1},{17,25},{25,17},{2,10},{10... | collective-permute-start | bytes 884744 | tf_op jit(solution)/shard_map/ppermute | solution.py:26
  751.7 15.4 %collective-permute-start.56 = (bf16[384,768]{1,0:T(8,128)(2,1)S(1)}, bf16[384,768]{1,0:T(8,128)(2,1)S(1)}, u32[]{:S(2)}, u32[]{:S(2)}) collective-permute-start(bf16[384,768]{1,0:T(8,128)(2,1)S(1)} %constant_dynamic-update-slice_fusion.20), channel_id=1, source_target_pairs={{0,8},{8,0},{16,24},{24,16},{1,9},{9,1},{17,25},{25,17},{2,10},{10... | collective-permute-start | bytes 1769480 | tf_op jit(solution)/shard_map/ppermute | solution.py:26
  751.9 43.8 %collective-permute-start.73 = (bf16[768,768]{1,0:T(8,128)(2,1)S(1)}, bf16[768,768]{1,0:T(8,128)(2,1)S(1)}, u32[]{:S(2)}, u32[]{:S(2)}) collective-permute-start(bf16[768,768]{1,0:T(8,128)(2,1)S(1)} %constant_dynamic-update-slice_fusion.6), channel_id=1, source_target_pairs={{0,4},{4,0},{1,5},{5,1},{2,6},{6,2},{3,7},{7,3},{8,12},{12,8},{9,1... | collective-permute-start | bytes 3538952 | tf_op jit(solution)/shard_map/ppermute | solution.py:26
  756.8 36.7 %collective-permute-start.49 = (bf16[384,768]{1,0:T(8,128)(2,1)S(1)}, bf16[384,768]{1,0:T(8,128)(2,1)S(1)}, u32[]{:S(2)}, u32[]{:S(2)}) collective-permute-start(bf16[384,768]{1,0:T(8,128)(2,1)S(1)} %constant_dynamic-update-slice_fusion.24), channel_id=1, source_target_pairs={{0,4},{4,0},{1,5},{5,1},{2,6},{6,2},{3,7},{7,3},{8,12},{12,8},{9,1... | collective-permute-start | bytes 1769480 | tf_op jit(solution)/shard_map/ppermute | solution.py:26
  767.2 46.8 %collective-permute-start.57 = (bf16[768,768]{1,0:T(8,128)(2,1)S(1)}, bf16[768,768]{1,0:T(8,128)(2,1)S(1)}, u32[]{:S(2)}, u32[]{:S(2)}) collective-permute-start(bf16[768,768]{1,0:T(8,128)(2,1)S(1)} %constant_dynamic-update-slice_fusion.18), channel_id=1, source_target_pairs={{0,4},{4,0},{1,5},{5,1},{2,6},{6,2},{3,7},{7,3},{8,12},{12,8},{9,1... | collective-permute-start | bytes 3538952 | tf_op jit(solution)/shard_map/ppermute | solution.py:26
  (190 other events, 1822.2 us)

commit v2 on v1

--- a/solution.py
+++ b/solution.py
@@ -11,6 +11,7 @@
 HD = 64
 REUSE = 6
 WIN = 512
+EARLY = 2
 GROUP = 3
 BAND = GROUP * HD
 TILE = 256
@@ -26,18 +27,8 @@
     return lax.ppermute(value, axis, [(i, i ^ bit) for i in devices])
 
 
-def gather_shards(own):
-    far = swap(own, "mp", 2)
-    near = swap(own, "mp", 1)
-    return [own, near, far, swap(far, "mp", 1)]
-
-
 def in_order(parts):
-    me = lax.axis_index("mp")
-    result = jnp.zeros((4,) + parts[0].shape, parts[0].dtype)
-    for distance, part in enumerate(parts):
-        result = lax.dynamic_update_index_in_dim(result, part, me ^ distance, 0)
-    return result
+    return jnp.concatenate(by_distance(jnp.stack(parts)))
 
 
 def by_distance(stacked):
@@ -46,6 +37,24 @@
         lax.dynamic_index_in_dim(stacked, me ^ distance, 0, keepdims=False)
         for distance in range(4)
     ]
+
+
+def flip(position, bit):
+    return position + bit * (1 - 2 * ((position // bit) % 2))
+
+
+def remote(source, target, sent, received, device):
+    return pltpu.make_async_remote_copy(
+        src_ref=source, dst_ref=target, send_sem=sent, recv_sem=received,
+        device_id=device, device_id_type=pl.DeviceIdType.MESH,
+    )
+
+
+def meet(devices):
+    barrier = pltpu.get_barrier_semaphore()
+    for device in devices:
+        pl.semaphore_signal(barrier, inc=1, device_id=device, device_id_type=pl.DeviceIdType.MESH)
+    pl.semaphore_wait(barrier, len(devices))
 
 
 def dot(left, right, left_dim, right_dim):
@@ -225,25 +234,206 @@
     )(first, low, *operands, heads, grad_heads, sums)
 
 
+def front_kernel(n_more, *refs):
+    refs = list(refs)
+
+    def take(count):
+        taken = refs[:count]
+        del refs[:count]
+        return taken
+
+    ctx, dp, mp = (lax.axis_index(axis) for axis in ("ctx", "dp", "mp"))
+    (normed,) = take(1)
+    near, far, last = {"mp": flip(mp, 1)}, {"mp": flip(mp, 2)}, {"mp": 3 - mp}
+    window = {"ctx": 1 - ctx}
+    order = (mp, flip(mp, 1), flip(mp, 2), 3 - mp)
+    if n_more:
+        fixed_own = take(3)
+        more_own = take(n_more)
+        cols, before, earlier = take(3)
+        fixed = take(3)
+        more = take(n_more)
+        kv_out, kv_in, on_out, on_in, f_out, f_in, m_out, m_in = refs
+        front, bias, _ = fixed
+        meet([near, far, last, window, {"dp": flip(dp, 1)}])
+    else:
+        front, bias = take(2)
+        cols, before, earlier = take(3)
+        kv_out, kv_in, on_out, on_in = refs
+        meet([near, last, window])
+
+    if n_more:
+        def whole(k, way, device):
+            return remote(fixed_own[k], fixed[k].at[mp], f_out.at[k, way], f_in.at[k, way], device)
+
+        def onward():
+            there = front.at[flip(mp, 2)]
+            return remote(there, there, f_out.at[0, 2], f_in.at[0, 2], near)
+
+        whole(0, 1, far).start()
+        whole(0, 0, near).start()
+        for k in (1, 2):
+            for way, device in enumerate((near, far, last)):
+                whole(k, way, device).start()
+
+        bit = lax.rem(dp, 2)
+        first = [(bit, {"dp": flip(dp, 1)}), (ctx, window)]
+
+        def sizes(a):
+            rows = more_own[a].shape[0]
+            (low, low_device), (high, high_device) = first if a % 2 else first[::-1]
+            return rows, rows // 4, rows // 2, low, low_device, high, high_device
+
+        def beside(a):
+            return remote(more_own[a], more[a].at[mp], m_out.at[a, 0], m_in.at[a, 0], near)
+
+        def across(a):
+            rows, quarter, half, low, _, high, _ = sizes(a)
+            here = pl.ds(pl.multiple_of(high * half + low * quarter, 16), quarter)
+            return remote(
+                more_own[a].at[here], more[a].at[mp, here], m_out.at[a, 1], m_in.at[a, 1], far
+            )
+
+        def widen(a):
+            rows, quarter, half, low, device, high, _ = sizes(a)
+            here = pl.ds(pl.multiple_of(high * half + low * quarter, 16), quarter)
+            there = more[a].at[flip(mp, 2), here]
+            return remote(there, there, m_out.at[a, 2], m_in.at[a, 2], device)
+
+        def complete(a):
+            rows, quarter, half, low, _, high, device = sizes(a)
+            here = pl.ds(pl.multiple_of(high * half, 16), half)
+            there = more[a].at[flip(mp, 2), here]
+            return remote(there, there, m_out.at[a, 3], m_in.at[a, 3], device)
+
+        def hand_on(a):
+            there = more[a].at[flip(mp, 2)]
+            return remote(there, there, m_out.at[a, 4], m_in.at[a, 4], near)
+
+        for a in range(EARLY):
+            across(a).start()
+        for a in range(n_more):
+            beside(a).start()
+        for k in range(3):
+            fixed[k][mp] = fixed_own[k][...]
+
+    kv_rows = before.shape[1]
+    from_row = cols.shape[1] - kv_rows
+    sends_on = (mp == 1) | (mp == 2)
+    sends_window = (mp == 0) & (ctx == 0)
+    receives = (mp >= 2) | ((mp == 0) & (ctx == 1))
+
+    def pass_on(slot, device):
+        source = cols.at[slot, pl.ds(from_row, kv_rows)]
+        return remote(source, before.at[slot], kv_out.at[slot], kv_in.at[slot], device)
+
+    def pass_again(slot):
+        return remote(before.at[slot], earlier.at[slot], on_out.at[slot], on_in.at[slot], {"mp": 3})
+
+    for k, slot in enumerate(order):
+        if n_more and k == 1:
+            for vector in (1, 2):
+                for way, device in enumerate((near, far, last)):
+                    whole(vector, way, device).wait_recv()
+            whole(0, 0, near).wait_recv()
+        if n_more and k == 2:
+            whole(0, 1, far).wait_recv()
+            onward().start()
+        if n_more and k == 3:
+            onward().wait_recv()
+        column = jnp.transpose(bias[slot])[: cols.shape[1], 0:1]
+        cols[slot] = (dot(front[slot, : cols.shape[1]], normed[...], 1, 1) + column).astype(BF16)
+        pl.when(sends_on)(lambda: pass_on(slot, {"mp": mp + 1}).start())
+        pl.when(sends_window)(lambda: pass_on(slot, window).start())
+
+    for a in range(EARLY, n_more):
+        across(a).start()
+    for a in range(n_more + 2 if n_more else 0):
+        if a < n_more:
+            across(a).wait_recv()
+            widen(a).start()
+        if 1 <= a <= n_more:
+            widen(a - 1).wait_recv()
+            complete(a - 1).start()
+        if a >= 2:
+            complete(a - 2).wait_recv()
+            hand_on(a - 2).start()
+
+    def received():
+        for slot in range(4):
+            pass_on(slot, window).wait_recv()
+            pl.when(mp == 2)(lambda: pass_again(slot).start())
+
+    pl.when(receives)(received)
+
+    def sent(device):
+        for slot in range(4):
+            pass_on(slot, device).wait_send()
+
+    pl.when(sends_on)(lambda: sent({"mp": mp + 1}))
+    pl.when(sends_window)(lambda: sent(window))
+
+    def again_sent():
+        for slot in range(4):
+            pass_again(slot).wait_send()
+
+    def again_received():
+        for slot in range(4):
+            pass_again(slot).wait_recv()
+
+    pl.when(mp == 2)(again_sent)
+    pl.when(mp == 3)(again_received)
+    if n_more:
+        for k in range(3):
+            for way, device in enumerate((near, far, last)):
+                if k or way < 2:
+                    whole(k, way, device).wait_send()
+        onward().wait_send()
+        for a in range(n_more):
+            beside(a).wait()
+            across(a).wait_send()
+            widen(a).wait_send()
+            complete(a).wait_send()
+            hand_on(a).wait()
+
+
+def project(normed, front, bias, n_cols, kv_rows, small=None, more=()):
+    place = pl.BlockSpec(memory_space=pltpu.VMEM)
+    far = pl.BlockSpec(memory_space=pl.ANY)
+    dma = pltpu.SemaphoreType.DMA
+    fixed = [front, bias] + ([small] if more else [])
+    made = [(4, n_cols, WIN), (4, kv_rows, WIN), (4, kv_rows, WIN)]
+    made = [jax.ShapeDtypeStruct(shape, BF16) for shape in made]
+    scratch = [dma((4,))] * 4
+    gathered = []
+    if more:
+        gathered = [jax.ShapeDtypeStruct((4,) + v.shape, v.dtype) for v in fixed + list(more)]
+        scratch += [dma((3, 3))] * 2 + [dma((len(more), 5))] * 2
+    return pl.pallas_call(
+        functools.partial(front_kernel, len(more)),
+        out_shape=made + gathered,
+        in_specs=[place] * (1 + len(fixed)) + [far] * len(more),
+        out_specs=[place] * (3 + (3 if more else 0)) + [far] * len(more),
+        scratch_shapes=scratch,
+        compiler_params=pltpu.CompilerParams(
+            collective_id=1 if more else 2,
+            has_side_effects=True,
+            vmem_limit_bytes=48 * 1024 * 1024,
+        ),
+        name="front_gather" if more else "front",
+    )(normed, *fixed, *more)
+
+
 def routes():
     windows, groups = lax.axis_size("ctx"), lax.axis_size("mp")
-    onward = [(c * groups + m, c * groups + m + 1) for c in range(windows) for m in (1, 2)]
-    onward += [(c * groups, (c + 1) * groups) for c in range(windows - 1)]
-    second = [(c * groups + 2, c * groups + 3) for c in range(windows)]
     first_home = [(c * groups + 3, c * groups + 2) for c in range(windows)]
     home = [(c * groups + 2, c * groups + 1) for c in range(windows)]
     home += [((c + 1) * groups, c * groups) for c in range(windows - 1)]
-    return onward, second, first_home, home
-
-
-def pass_on(block):
-    onward, second, _, _ = routes()
-    before = lax.ppermute(block, ("ctx", "mp"), onward)
-    return before, lax.ppermute(before, ("ctx", "mp"), second)
+    return first_home, home
 
 
 def pass_home(before, earlier):
-    _, _, first_home, home = routes()
+    first_home, home = routes()
     near, far = lax.ppermute((before, earlier), ("ctx", "mp"), first_home)
     far = (before.astype(F32) + far.astype(F32)).astype(BF16)
     return near.astype(F32) + lax.ppermute(far, ("ctx", "mp"), home).astype(F32)
@@ -260,44 +450,171 @@
     return low.reshape(1, WIN), low[::TILE] // TILE
 
 
-def reduce_shards(parts):
+def sum_cores(parts):
     own, near, far, last = parts
     near, last = swap(jnp.stack([near, last]), "mp", 1)
-    far = (far.astype(F32) + last.astype(F32)).astype(BF16)
-    far = swap(far, "mp", 2)
-    total = own.astype(F32) + near.astype(F32) + far.astype(F32)
-    return sum_replicas(total.astype(BF16))
-
-
-def sum_replicas(value):
-    steps = [("ctx", 1)]
+    return (
+        (own.astype(F32) + near.astype(F32)).astype(BF16),
+        (far.astype(F32) + last.astype(F32)).astype(BF16),
+    )
+
+
+def sum_chips(own, far):
+    total = own.astype(F32) + swap(far, "mp", 2).astype(F32)
+    return lax.psum(total.astype(BF16), ("dp", "ctx"))
+
+
+def sum_kernel(
+    parts, rows, own, far, vec_in, out, vec, from_y, mine, from_x, kept, from_z, from_vec,
+    y_out, y_in, x_out, x_in, z_out, z_in, g_out, g_in, h_out, h_in, v_out, v_in,
+):
+    ctx, dp, mp = (lax.axis_index(axis) for axis in ("ctx", "dp", "mp"))
+    n_dp = lax.axis_size("dp")
+    half = rows // 2
+    piece = half // n_dp
+    other_chip, other_window = {"mp": flip(mp, 2)}, {"ctx": 1 - ctx}
+    partners = [other_chip, other_window, {"mp": flip(mp, 1)}]
     bit = 1
-    while bit < lax.axis_size("dp"):
-        steps.append(("dp", bit))
+    while bit < n_dp:
+        partners.append({"dp": flip(dp, bit)})
         bit *= 2
-    for axis, bit in steps:
-        high = (lax.axis_index(axis) // bit) % 2
-        half = value.shape[0] // 2
-        kept = lax.dynamic_slice_in_dim(value, high * half, half, 0)
-        sent = lax.dynamic_slice_in_dim(value, (1 - high) * half, half, 0)
-        value = (kept.astype(F32) + swap(sent, axis, bit).astype(F32)).astype(BF16)
-    for axis, bit in reversed(steps):
-        high = (lax.axis_index(axis) // bit) % 2
-        half = value.shape[0]
-        other = swap(value, axis, bit)
-        whole = jnp.zeros((2 * half,) + value.shape[1:], BF16)
-        whole = lax.dynamic_update_slice_in_dim(whole, value, high * half, 0)
-        value = lax.dynamic_update_slice_in_dim(whole, other, (1 - high) * half, 0)
-    return value
-
-
-def sum_all(value):
-    for axis in ("mp", "ctx", "dp"):
-        bit = 1
-        while bit < lax.axis_size(axis):
-            value = value + swap(value, axis, bit)
-            bit *= 2
-    return value
+
+    def along(k):
+        return {"dp": lax.rem(dp + k, n_dp)}
+
+    def ds(start, size):
+        return pl.ds(pl.multiple_of(start, 16), size)
+
+    def span(i, high, at=0, size=half):
+        return ds(i * rows + high * half + at * piece, size)
+
+    def to_y(i):
+        here = ds(i * rows, rows)
+        return remote(far.at[here], from_y.at[here], y_out.at[i], y_in.at[i], other_chip)
+
+    def to_x(i):
+        target = from_x.at[ds(i * half, half)]
+        return remote(mine.at[span(i, 1 - ctx)], target, x_out.at[i], x_in.at[i], other_window)
+
+    def to_z(i, k):
+        other = lax.rem(dp + k, n_dp)
+        source = kept.at[ds(i * half + other * piece, piece)]
+        target = from_z.at[ds((i * n_dp + k) * piece, piece)]
+        return remote(source, target, z_out.at[i, k], z_in.at[i, k], along(k))
+
+    def round_z(i, k):
+        here = out.at[span(i, ctx, dp, piece)]
+        return remote(here, here, g_out.at[i, k], g_in.at[i, k], along(k))
+
+    def back_x(i):
+        here = out.at[span(i, ctx)]
+        return remote(here, here, h_out.at[i], h_in.at[i], other_window)
+
+    def each(count, step):
+        lax.fori_loop(0, count, lambda i, _: (step(i), 0)[1], 0)
+
+    barrier = pltpu.get_barrier_semaphore()
+
+    def greet(device):
+        pl.semaphore_signal(barrier, inc=1, device_id=device, device_id_type=pl.DeviceIdType.MESH)
+
+    for partner in partners[:3]:
+        greet(partner)
+    each(n_dp - 1, lambda k: greet(along(k + 1)))
+    pl.semaphore_wait(barrier, n_dp + 2)
+
+    vec[...] = vec_in[...]
+    for hop, partner in enumerate(partners):
+        copy = remote(vec, from_vec.at[hop], v_out.at[hop], v_in.at[hop], partner)
+        copy.start()
+        if hop == 0:
+            each(parts, lambda i: to_y(i).start())
+        copy.wait()
+        vec[...] = vec[...] + from_vec[hop]
+
+    def join(i):
+        to_y(i).wait_recv()
+        here = ds(i * rows, rows)
+        mine[here, :] = (own[here, :].astype(F32) + from_y[here, :].astype(F32)).astype(BF16)
+        to_x(i).start()
+
+    def spread(i):
+        to_x(i).wait_recv()
+        there = ds(i * half, half)
+        total = mine[span(i, ctx), :].astype(F32) + from_x[there, :].astype(F32)
+        kept[there, :] = total.astype(BF16)
+        each(n_dp - 1, lambda k: to_z(i, k + 1).start())
+
+    def gather(i):
+        def add(k, total):
+            to_z(i, k).wait_recv()
+            return total + from_z[ds((i * n_dp + k) * piece, piece), :].astype(F32)
+
+        total = kept[ds(i * half + dp * piece, piece), :].astype(F32)
+        out[span(i, ctx, dp, piece), :] = lax.fori_loop(1, n_dp, add, total).astype(BF16)
+        each(n_dp - 1, lambda k: round_z(i, k + 1).start())
+
+    def give(i):
+        each(n_dp - 1, lambda k: round_z(i, k + 1).wait_recv())
+        back_x(i).start()
+
+    def step(i):
+        for late, stage in enumerate((join, spread, gather, give)):
+            pl.when((i >= late) & (i < parts + late))(functools.partial(stage, i - late))
+
+    each(parts + 3, step)
+
+    def finish(i):
+        to_y(i).wait_send()
+        to_x(i).wait_send()
+        back_x(i).wait()
+
+        def sent(k):
+            to_z(i, k + 1).wait_send()
+            round_z(i, k + 1).wait_send()
+
+        each(n_dp - 1, sent)
+
+    each(parts, finish)
+
+
+def sum_replicas(own, far, vectors):
+    n_dp = lax.axis_size("dp")
+    rows = max(256, 32 * n_dp)
+    parts = -(-own.shape[0] // rows)
+    total = parts * rows
+    hops = 3 + (n_dp - 1).bit_length()
+    lanes = own.shape[1]
+    own, far = (jnp.pad(v, ((0, total - v.shape[0]), (0, 0))) for v in (own, far))
+    place = pl.BlockSpec(memory_space=pltpu.VMEM)
+    dma = pltpu.SemaphoreType.DMA
+    return pl.pallas_call(
+        functools.partial(sum_kernel, parts, rows),
+        out_shape=[
+            jax.ShapeDtypeStruct((total, lanes), BF16),
+            jax.ShapeDtypeStruct(vectors.shape, F32),
+        ],
+        in_specs=[place, place, place],
+        out_specs=[place, place],
+        scratch_shapes=[
+            pltpu.VMEM((total, lanes), BF16),
+            pltpu.VMEM((total, lanes), BF16),
+            pltpu.VMEM((total // 2, lanes), BF16),
+            pltpu.VMEM((total // 2, lanes), BF16),
+            pltpu.VMEM((total // 2, lanes), BF16),
+            pltpu.VMEM((hops,) + vectors.shape, F32),
+            dma((parts,)), dma((parts,)),
+            dma((parts,)), dma((parts,)),
+            dma((parts, n_dp)), dma((parts, n_dp)),
+            dma((parts, n_dp)), dma((parts, n_dp)),
+            dma((parts,)), dma((parts,)),
+            dma((hops,)), dma((hops,)),
+        ],
+        compiler_params=pltpu.CompilerParams(
+            collective_id=0, has_side_effects=True, vmem_limit_bytes=56 * 1024 * 1024
+        ),
+        name="sum_replicas",
+    )(own, far, vectors)
 
 
 def gelu(hidden):
@@ -352,41 +669,44 @@
 ):
     low, first = row_starts(doc_lengths[0])
 
-    front1 = in_order(gather_shards(turned(projections1).reshape(3 * BAND, D)))
-    small = jnp.concatenate(
-        [front_bias1.reshape(-1), query_bias2, value_bias2, up_bias1, up_bias2]
-    )
-    filler = (-small.shape[0]) % 1024
-    small = gather_shards(jnp.pad(small, (0, filler)).reshape(-1, 128))
-    small = [part.reshape(-1) for part in small]
-    n_front, n_query, n_value, n_up = 2 * BAND, BAND, BAND // 2, D
-    cuts = [n_front, n_front + n_query, n_front + n_query + n_value]
-    up_biases1 = [part[cuts[2] : cuts[2] + n_up] for part in small]
-    up_biases2 = [part[cuts[2] + n_up : cuts[2] + 2 * n_up] for part in small]
-    ordered = in_order([part[: cuts[2]] for part in small])
-    none = jnp.zeros((4, BAND), BF16)
-    bias1 = jnp.concatenate([ordered[:, :BAND], none, ordered[:, BAND:n_front]], axis=1)
-    bias2 = jnp.concatenate(
-        [ordered[:, n_front : cuts[1]], none, ordered[:, cuts[1] : cuts[2]]], axis=1
-    )
-    outs1 = in_order(gather_shards(out_weight1)).reshape(D, D)
-    ups1 = gather_shards(up_weight1)
-    downs1 = gather_shards(down_weight1)
-    front2 = in_order(
-        gather_shards(
-            jnp.concatenate([turned(query_key2).reshape(2 * BAND, D), turned(fresh_value2)])
-        )
-    )
-    outs2 = in_order(gather_shards(out_weight2)).reshape(D, D)
-    ups2 = gather_shards(up_weight2)
-    downs2 = gather_shards(down_weight2)
-
     stream0 = block_input.astype(F32)
     normed1, unit1, scale1 = norm_rows(stream0, norm_gain1[0], norm_bias1[0])
-    n_front1, n_front2 = front1.shape[1], front2.shape[1]
-    cols1 = dot(front1.reshape(-1, D), normed1, 1, 1).reshape(4, n_front1, WIN)
-    cols1 = (cols1 + bias1[:, :, None]).astype(BF16)
-    before1, earlier1 = pass_on(cols1[:, BAND:])
+    n_front1, n_front2 = 3 * BAND, 2 * BAND + BAND // 2
+    none = jnp.zeros((BAND,), BF16)
+
+    def as_row(pieces):
+        row = jnp.concatenate(pieces).astype(F32)
+        return jnp.pad(row[None, :], ((0, 7), (0, -row.shape[0] % 128)))
+
+    small = jnp.concatenate([query_bias2, value_bias2, up_bias1, up_bias2])
+    small = jnp.pad(small, (0, 16 * 128 - small.shape[0])).reshape(16, 128)
+    own_front2 = jnp.concatenate([turned(query_key2).reshape(2 * BAND, D), turned(fresh_value2)])
+    own_front2 = jnp.pad(own_front2, ((0, -n_front2 % 64), (0, 0)))
+    (
+        cols1, before1, earlier1, front1, _, small,
+        up1, down1, up2, down2, front2, outs1, outs2,
+    ) = project(
+        normed1, turned(projections1).reshape(n_front1, D),
+        as_row([front_bias1[0], none, front_bias1[1]]), n_front1, 2 * BAND, small,
+        (up_weight1, down_weight1, up_weight2, down_weight2, own_front2, out_weight1, out_weight2),
+    )
+    ups1, downs1, ups2, downs2 = (
+        [own] + by_distance(w)[1:]
+        for own, w in (
+            (up_weight1, up1), (down_weight1, down1), (up_weight2, up2), (down_weight2, down2)
+        )
+    )
+    front2, outs1, outs2 = (
+        lax.dynamic_update_index_in_dim(w, own, lax.axis_index("mp"), 0)
+        for own, w in ((own_front2, front2), (out_weight1, outs1), (out_weight2, outs2))
+    )
+    outs1, outs2 = outs1.reshape(D, D), outs2.reshape(D, D)
+    small = small.reshape(4, -1)
+    at = BAND + BAND // 2
+    bias2 = jnp.stack([as_row([small[s, :BAND], none, small[s, BAND:at]]) for s in range(4)])
+    up_biases1 = by_distance(small[:, at : at + D])
+    up_biases2 = by_distance(small[:, at + D : at + 2 * D])
+
     operands1 = (cols1, cols1, before1, earlier1, cols1, before1, earlier1)
     places1 = (0, 1, 0, 0, 2, 1, 1)
     heads1, exact1, sums1 = attend(first, low, operands1, places1)
@@ -396,9 +716,8 @@
     )
 
     normed2, unit2, scale2 = norm_rows(stream1, norm_gain2[0], norm_bias2[0])
-    cols2 = dot(front2.reshape(-1, D), normed2, 1, 1).reshape(4, n_front2, WIN)
-    cols2 = (cols2 + bias2[:, :, None]).astype(BF16)
-    before2, earlier2 = pass_on(cols2[:, BAND:])
+    cols2, before2, earlier2 = project(normed2, front2, bias2, n_front2, n_front2 - BAND)
+    front2 = front2[:, :n_front2]
 
     def mixed(first_values, fresh):
         first_values = first_values.reshape(-1, HD, WIN)
@@ -425,7 +744,7 @@
     grad, rounded, grad_heads, mats2, up_grads2, small2 = tail_backward(
         cotangent.astype(F32), kept2, outs2, norm_gain2, ups2, downs2
     )
-    mats2 = reduce_shards(mats2)
+    mats2 = sum_chips(*sum_cores(mats2))
     dq2, dk2, dk2_before, dk2_earlier, dv2, dv2_before, dv2_earlier = attend_back(
         first, low, operands2, places2, exact2, grad_heads.reshape(4, BAND, WIN), sums2
     )
@@ -445,10 +764,10 @@
     dcols2 = dcols2.astype(BF16)
     grad_front2 = dot(dcols2.reshape(-1, WIN), normed2, 1, 0).astype(BF16).reshape(4, n_front2, D)
     attn2 = [
-        jnp.pad(jnp.concatenate(pair), ((0, D - BAND - n_front2), (0, 0)))
+        jnp.concatenate(pair)
         for pair in zip(by_distance(grad_out2), by_distance(grad_front2), strict=True)
     ]
-    attn2 = reduce_shards(attn2)
+    attn2 = sum_cores(attn2)
     normed_grad = dot(dcols2.reshape(-1, WIN), front2.reshape(-1, D), 0, 0)
     middle, gain_front2, shift_front2 = norm_back(normed_grad, unit2, scale2, norm_gain2[0])
     grad = grad + middle
@@ -456,7 +775,7 @@
     grad, rounded, grad_heads, mats1, up_grads1, small1 = tail_backward(
         grad, kept1, outs1, norm_gain1, ups1, downs1
     )
-    mats1 = reduce_shards(mats1)
+    mats1 = sum_cores(mats1)
     dq1, dk1, dk1_before, dk1_earlier, dv1, dv1_before, dv1_earlier = attend_back(
         first, low, operands1, places1, exact1, grad_heads.reshape(4, BAND, WIN), sums1
     )
@@ -484,7 +803,7 @@
         jnp.concatenate(pair)
         for pair in zip(by_distance(grad_out1), by_distance(grad_front1), strict=True)
     ]
-    attn1 = reduce_shards(attn1)
+    attn1 = sum_cores(attn1)
     normed_grad = dot(dcols1.reshape(-1, WIN), front1.reshape(-1, D), 0, 0)
     middle, gain_front1, shift_front1 = norm_back(normed_grad, unit1, scale1, norm_gain1[0])
     input_grad = (grad + middle).astype(BF16)
@@ -494,12 +813,16 @@
         gain_front2, small2[0], shift_front2, small2[1], small2[2], small2[3],
         bias_grad1[:, :BAND].reshape(-1), bias_grad1[:, 2 * BAND :].reshape(-1),
         bias_grad2[:, :BAND].reshape(-1), bias_grad2[:, 2 * BAND :].reshape(-1),
-        in_order(up_grads1).reshape(-1), in_order(up_grads2).reshape(-1),
+        in_order(up_grads1), in_order(up_grads2),
     ]
     lengths = [vector.shape[0] for vector in vectors]
     packed = jnp.concatenate(vectors)
     filler = (-packed.shape[0]) % 1024
-    packed = sum_all(jnp.pad(packed, (0, filler)).reshape(-1, 128)).reshape(-1)
+    stack, packed = sum_replicas(
+        *(jnp.concatenate(three) for three in zip(attn2, mats1, attn1, strict=True)),
+        jnp.pad(packed, (0, filler)).reshape(-1, 128),
+    )
+    packed = packed.reshape(-1)
     sums, at = [], 0
     for length in lengths:
         sums.append(packed[at : at + length])
@@ -512,8 +835,11 @@
     def pair(i):
         return jnp.stack([sums[i], sums[i + 1]])
 
-    mats1, attn1 = mats1.astype(F32), attn1.astype(F32)
-    mats2, attn2 = mats2.astype(F32), attn2.astype(F32)
+    mats2, stack = mats2.astype(F32), stack.astype(F32)
+    rows2, rows1 = BAND + n_front2, BAND + n_front1
+    attn2, mats1, attn1 = (
+        stack[at : at + size] for at, size in ((0, rows2), (rows2, 2 * D), (rows2 + 2 * D, rows1))
+    )
     return (
         block_output,
         input_grad,

time: 820 us -> 815 us (level)
  Pallas kernels: 49.7 us -> 392 us
  waiting for transfers between devices: 303 us -> 48.8 us
  starting transfers between devices: 148 us -> 60.1 us
  matrix products: 109 us -> 92.4 us
  between operations: 15.8 us -> 29 us
  other arithmetic: 81.6 us -> 72 us
    pallas_call x0 -> x3, Pallas kernels: none -> 330 us  [the longest x1 195 us: sum_replicas(): pl.pallas_call(functools.partial(sum_kernel, parts, rows), out_shape=[jax...]
    ppermute x64 -> x5, waiting for transfers between devices: 261 us -> 28.6 us  [swap(): return lax.ppermute(value, axis, [(i, i ^ bit) for i in devices])]
    ppermute x64 -> x5, starting transfers between devices: 122 us -> 50.1 us  [swap(): return lax.ppermute(value, axis, [(i, i ^ bit) for i in devices])]
    unnamed x394 -> x457, local copies, waits for them, and re-layouts: 30.7 us -> 60.6 us
    ppermute x4 -> x0, starting transfers between devices: 16.7 us -> none  [the longest x2 14.7 us: pass_on(): before = lax.ppermute(block, ('ctx', 'mp'), onward)]
    dynamic_update_slice x47 -> x2, local copies, waits for them, and re-layouts: 18.1 us -> 1.53 us  [shards(): lax.dynamic_update_index_in_dim(w, own, lax.axis_index('mp'), 0)]
    dot_general x60 -> x58, matrix products: 109 us -> 92.4 us  [dot(): lax.dot_general(left, right, (((left_dim,), (right_dim,)), ((), ())), pre...]
    ppermute x4 -> x0, waiting for transfers between devices: 13.6 us -> none  [the longest x2 13.6 us: pass_on(): before = lax.ppermute(block, ('ctx', 'mp'), onward)]
  transfers between devices with their start and end apart: 74 -> 12, of which waited for: 28 -> 2; matrix products, arithmetic and copies ran while one was open for 31% -> 20% of each run, Pallas kernels for 4% -> 26%
where the time goes in v2:
time: 815 us; the launch traced here: 811 us
  Pallas kernels  392 us (48%)
  local copies, waits for them, and re-layouts  117 us (14%)
  matrix products  92.4 us (11%)
  other arithmetic  72 us (9%)
  starting transfers between devices  60.1 us (7%)
  waiting for transfers between devices  48.8 us (6%)
  between operations  29 us (4%)
    pallas_call x1, Pallas kernels, sum_replicas(): pl.pallas_call(functools.partial(sum_kernel, parts, rows), out_shape=[jax...  195 us
    pallas_call x2, Pallas kernels, project(): pl.pallas_call(functools.partial(front_kernel, len(more)), out_shape=made...  135 us
    dot_general x58, matrix products, dot(): lax.dot_general(left, right, (((left_dim,), (right_dim,)), ((), ())), pre...  92.4 us
    unnamed x457, local copies, waits for them, and re-layouts  60.6 us
    ppermute x5, starting transfers between devices, swap(): return lax.ppermute(value, axis, [(i, i ^ bit) for i in devices])  50.1 us
    pallas_call x2, Pallas kernels, attend(): pl.pallas_call(attend_kernel, grid_spec=pltpu.PrefetchScalarGridSpec(num_...  35.4 us
    ppermute x5, waiting for transfers between devices, swap(): return lax.ppermute(value, axis, [(i, i ^ bit) for i in devices])  28.6 us
    pallas_call x2, Pallas kernels, attend_back(): pl.pallas_call(attend_back_kernel, grid_spec=pltpu.PrefetchScalarGridSpec...  26.1 us
  transfers between devices with their start and end apart: 12, of which 2 were waited for; matrix products, arithmetic and copies ran while one was open for 20% of the time, Pallas kernels for 26%

profile of v2, /device:TPU:0, one launch (start us, length us, event | category | flops | bytes accessed | tf_op | source)
XLA Modules:
  0.0 811.0 jit_solution(16119387798567073933)
XLA Ops:
  11.9 100.2 %front_gather.1 = (bf16[4,576,512]{2,1,0:T(8,128)(2,1)}, bf16[4,384,512]{2,1,0:T(8,128)(2,1)}, bf16[4,384,512]{2,1,0:T(8,128)(2,1)}, bf16[4,576,768]{2,1,0:T(8,1...) custom-call(bf16[512,768]{1,0:T(8,128)(2,1)S(1)} %fusion.31.refs_0_,, ...), custom_call_target="tpu_custom_call" | custom-call | tf_op jit(solution)/shard_map/front_gather/pallas_call | solution.py:412
  124.4 2.2 slice.373
  127.6 2.2 slice.383
  131.2 23.3 %attend.2 = (bf16[4,192,512]{2,1,0:T(8,128)(2,1)S(1)}, f32[4,192,512]{2,1,0:T(8,128)S(1)}, f32[4,8,512]{2,1,0:T(8,128)S(1)}) custom-call(s32[2]{0:T(128)S(1)} %and_select_fusion.first_ref, s32[1,512]{1,0:T(1,128)S(1)} %bitcast.632, bf16[4,576,512]{2,1,0:T(8,128)(2,1)S(1)} %copy-done, bf16[4,576,512]{2,1,0:T(8,128)(2,1)S(1)} %copy-done, ...), custom_call_target="tpu_custom_call" | custom-call | tf_op jit(solution)/shard_map/attend/pallas_call | solution.py:193
  157.1 2.4 fusion.298
  161.0 1.7 add_convert_fusion.6
  162.8 2.3 convolution_add_fusion.4
  165.2 2.6 convolution_add_fusion.5
  167.8 2.6 convolution_add_fusion.6
  181.4 34.7 %front.1 = (bf16[4,480,512]{2,1,0:T(8,128)(2,1)S(1)}, bf16[4,288,512]{2,1,0:T(8,128)(2,1)S(1)}, bf16[4,288,512]{2,1,0:T(8,128)(2,1)S(1)}) custom-call(bf16[512,768]{1,0:T(8,128)(2,1)S(1)} %add_convert_fusion.5.refs_0_, bf16[4,512,768]{2,1,0:T(8,128)(2,1)} %bitcast_dynamic-update-slice_fusion.refs_1_, f32[4,8,512]{2,1,0:T(8,128)S(1)} %maximum_convert_fusion.refs_2_), custom_call_target="tpu_custom_call" | custom-call | tf_op jit(solution)/shard_map/front/pallas_call | solution.py:412
  247.9 12.1 %attend.3 = (bf16[4,192,512]{2,1,0:T(8,128)(2,1)S(1)}, f32[4,192,512]{2,1,0:T(8,128)S(1)}, f32[4,8,512]{2,1,0:T(8,128)S(1)}) custom-call(s32[2]{0:T(128)S(1)} %and_select_fusion.first_ref, s32[1,512]{1,0:T(1,128)S(1)} %bitcast.633, bf16[4,480,512]{2,1,0:T(8,128)(2,1)S(1)} %copy-done.2, bf16[4,480,512]{2,1,0:T(8,128)(2,1)S(1)} %copy-done.2, ...), custom_call_target="tpu_custom_call" | custom-call | tf_op jit(solution)/shard_map/attend/pallas_call | solution.py:193
  271.5 2.8 fusion.278
  277.5 2.1 multiply_reduce_fusion
  281.8 12.9 %attend_back.2 = (f32[4,192,512]{2,1,0:T(8,128)S(1)}, f32[4,192,512]{2,1,0:T(8,128)S(1)}, bf16[4,192,512]{2,1,0:T(8,128)(2,1)S(1)}, bf16[4,192,512]{2,1,0:T(8,12...) custom-call(s32[2]{0:T(128)S(1)} %and_select_fusion.first_ref, ...), custom_call_target="tpu_custom_call" | custom-call | tf_op jit(solution)/shard_map/attend_back/pallas_call | solution.py:218
  298.3 1.9 collective-permute-start
  304.7 2.6 pad_maximum_fusion.2
  307.2 5.7 collective-permute-start.9
  313.0 1.9 convolution_convert_fusion.3
  314.9 1.8 convolution_convert_fusion.9
  322.1 3.5 fusion.128
  325.6 2.0 convolution_convert_fusion.2
  327.6 2.0 convolution_convert_fusion.8
  331.0 1.7 collective-permute-start.2
  344.5 3.0 fusion.134
  349.9 3.5 add_convert_fusion.3
  353.4 20.2 %collective-permute-done.2 = bf16[4,288,512]{2,1,0:T(8,128)(2,1)} collective-permute-done((bf16[4,288,512]{2,1,0:T(8,128)(2,1)}, bf16[4,288,512]{2,1,0:T(8,128)(2,1)}, u32[]{:S(2)}, u32[]{:S(2)}) %collective-permute-start.2) | collective-permute-done | bytes 1179680 | tf_op jit(solution)/shard_map/ppermute | solution.py:439
  373.6 2.2 maximum_add_fusion.1
  378.2 2.8 fusion.110
  383.6 2.1 fusion.301
  385.8 2.1 fusion.302
  387.9 2.2 fusion.280
  390.1 2.3 fusion.303
  404.9 13.2 %attend_back.3 = (f32[4,192,512]{2,1,0:T(8,128)S(1)}, f32[4,192,512]{2,1,0:T(8,128)S(1)}, bf16[4,192,512]{2,1,0:T(8,128)(2,1)S(1)}, bf16[4,192,512]{2,1,0:T(8,12...) custom-call(s32[2]{0:T(128)S(1)} %and_select_fusion.first_ref, ...), custom_call_target="tpu_custom_call" | custom-call | tf_op jit(solution)/shard_map/attend_back/pallas_call | solution.py:218
  424.9 1.9 collective-permute-start.4
  431.5 2.2 collective-permute-start.3
  434.9 2.5 pad_maximum_fusion.1
  437.5 9.4 %collective-permute-start.7 = (bf16[2,1536,768]{2,1,0:T(8,128)(2,1)}, bf16[2,1536,768]{2,1,0:T(8,128)(2,1)}, u32[]{:S(2)}, u32[]{:S(2)}) collective-permute-start(bf16[2,1536,768]{2,1,0:T(8,128)(2,1)} %pad_maximum_fusion.1), channel_id=1, source_target_pairs={{0,1},{1,0},{2,3},{3,2},{4,5},{5,4},{6,7},{7,6},{8,9},{9,8},{10,11... | collective-permute-start | bytes 14155784 | tf_op jit(solution)/shard_map/ppermute | solution.py:27
  446.9 1.7 convolution_convert_fusion.1
  453.1 1.8 convolution_convert_fusion.11
  455.0 1.8 convolution_convert_fusion.18
  459.1 2.0 convolution_convert_fusion.10
  461.1 2.0 convolution_convert_fusion.17
  463.0 1.8 add_convert_fusion.1
  472.0 3.2 fusion.22
  475.2 3.9 fusion.10
  479.1 25.1 %collective-permute-start.10 = (bf16[1536,768]{1,0:T(8,128)(2,1)}, bf16[1536,768]{1,0:T(8,128)(2,1)}, u32[]{:S(2)}, u32[]{:S(2)}) collective-permute-start(bf16[1536,768]{1,0:T(8,128)(2,1)} %fusion.10), channel_id=1, source_target_pairs={{0,2},{1,3},{2,0},{3,1},{4,6},{5,7},{6,4},{7,5},{8,10},{9,11},{10,... | collective-permute-start | bytes 7077896 | tf_op jit(solution)/shard_map/ppermute | solution.py:27
  504.2 2.3 maximum_add_fusion
  508.5 2.0 convolution_convert_fusion
  513.8 9.9 %collective-permute-start.8 = (bf16[2,768,768]{2,1,0:T(8,128)(2,1)}, bf16[2,768,768]{2,1,0:T(8,128)(2,1)}, u32[]{:S(2)}, u32[]{:S(2)}) collective-permute-start(bf16[2,768,768]{2,1,0:T(8,128)(2,1)} %pad_maximum_fusion.4), channel_id=1, source_target_pairs={{0,1},{1,0},{2,3},{3,2},{4,5},{5,4},{6,7},{7,6},{8,9},{9,8},{10,11... | collective-permute-start | bytes 7077896 | tf_op jit(solution)/shard_map/ppermute | solution.py:27
  524.0 5.2 fusion.37
  531.8 28.6 %collective-permute-done.10 = bf16[1536,768]{1,0:T(8,128)(2,1)} collective-permute-done((bf16[1536,768]{1,0:T(8,128)(2,1)}, bf16[1536,768]{1,0:T(8,128)(2,1)}, u32[]{:S(2)}, u32[]{:S(2)}) %collective-permute-start.10) | collective-permute-done | bytes 2359328 | tf_op jit(solution)/shard_map/ppermute | solution.py:27
  560.4 4.7 add_convert_fusion
  566.7 3.6 fusion.12
  570.4 2.3 fusion.20
  572.7 2.7 fusion.7.own
  575.3 2.8 fusion.9.far
  578.2 195.1 %sum_replicas.1 = (bf16[3072,768]{1,0:T(8,128)(2,1)}, f32[144,128]{1,0:T(8,128)}) custom-call(bf16[3072,768]{1,0:T(8,128)(2,1)} %fusion.7.own, bf16[3072,768]{1,0:T(8,128)(2,1)} %fusion.9.far, f32[144,128]{1,0:T(8,128)} %pad_bitcast_fusion.vec_in), custom_call_target="tpu_custom_call" | custom-call | tf_op jit(solution)/shard_map/sum_replicas/pallas_call | solution.py:591
  774.2 2.7 slice.485
  776.8 2.2 slice.489
  779.0 4.4 convert_element_type.500
  791.8 1.7 slice_bitcast_fusion.8
  793.5 2.1 fusion.285
  795.6 4.2 fusion.286
  799.8 4.2 fusion.287
  (695 shorter events, 161.1 us)
Async XLA Ops:
  7.3 792.5 %all-reduce.12.cloned.1.call-start = ((), (), s32[]{:S(2)}) async-start(), calls=%async_computation | async-start | bytes 4718592 | tf_op jit(solution)/shard_map/psum | solution.py:464
  11.1 101.1 %copy-start.15 = (bf16[512,768]{1,0:T(8,128)(2,1)}, bf16[512,768]{1,0:T(8,128)(2,1)S(1)}, u32[]{:S(2)}) copy-start(bf16[512,768]{1,0:T(8,128)(2,1)S(1)} %fusion.31.refs_0_) | copy-start | bytes 2359300
  11.9 103.1 %copy-start.132 = (s32[6]{0:T(128)S(1)}, s32[6]{0:T(128)}, u32[]{:S(2)}) copy-start(s32[6]{0:T(128)} %param.27) | copy-start | bytes 76
  11.9 111.4 %copy-start.153 = (bf16[2,768]{1,0:T(2,128)(2,1)S(1)}, bf16[2,768]{1,0:T(2,128)(2,1)}, u32[]{:S(2)}) copy-start(bf16[2,768]{1,0:T(2,128)(2,1)} %param.44) | copy-start | bytes 9220
  11.9 112.1 %copy-start.154 = (bf16[2,768]{1,0:T(2,128)(2,1)S(1)}, bf16[2,768]{1,0:T(2,128)(2,1)}, u32[]{:S(2)}) copy-start(bf16[2,768]{1,0:T(2,128)(2,1)} %param.33) | copy-start | bytes 9220
  11.9 112.1 %copy-start.170 = (s32[1,3]{1,0:T(1,128)S(1)}, s32[1,3]{1,0:T(1,128)}, u32[]{:S(2)}) copy-start(s32[1,3]{1,0:T(1,128)} %param.26) | copy-start | bytes 40
  162.8 10.0 %copy-start.88 = (bf16[512,768]{1,0:T(8,128)(2,1)}, bf16[512,768]{1,0:T(8,128)(2,1)S(1)}, u32[]{:S(2)}) copy-start(bf16[512,768]{1,0:T(8,128)(2,1)S(1)} %add_convert_fusion.6) | copy-start | bytes 2359300
  162.8 7.7 slice-start.8
  165.2 10.2 %copy-start.67 = (f32[512,768]{1,0:T(8,128)}, f32[512,768]{1,0:T(8,128)S(1)}, u32[]{:S(2)}) copy-start(f32[512,768]{1,0:T(8,128)S(1)} %convolution_add_fusion.4) | copy-start | bytes 4718596
  181.4 34.8 %copy-start.17 = (bf16[512,768]{1,0:T(8,128)(2,1)}, bf16[512,768]{1,0:T(8,128)(2,1)S(1)}, u32[]{:S(2)}) copy-start(bf16[512,768]{1,0:T(8,128)(2,1)S(1)} %add_convert_fusion.5.refs_0_) | copy-start | bytes 2359300
  237.9 8.4 %copy-start.8 = (bf16[4,288,512]{2,1,0:T(8,128)(2,1)S(1)}, bf16[4,288,512]{2,1,0:T(8,128)(2,1)}, u32[]{:S(2)}) copy-start(bf16[4,288,512]{2,1,0:T(8,128)(2,1)} %copy-done.7) | copy-start | bytes 3538948
  237.9 8.4 %copy-start.29 = (bf16[192,768]{1,0:T(8,128)(2,1)S(1)}, bf16[192,768]{1,0:T(8,128)(2,1)}, u32[]{:S(2)}) copy-start(bf16[192,768]{1,0:T(8,128)(2,1)} %refs_10_.1) | copy-start | bytes 884740
  239.5 7.5 copy-start.14
  239.5 7.5 copy-start.66
  241.1 6.0 copy-start.13
  247.9 12.1 %copy-start.36 = (bf16[4,192,768]{2,1,0:T(8,128)(2,1)S(1)}, bf16[4,192,768]{2,1,0:T(8,128)(2,1)}, u32[]{:S(2)}) copy-start(bf16[4,192,768]{2,1,0:T(8,128)(2,1)} %bitcast_dynamic-update-slice_fusion.1) | copy-start | bytes 3538948
  247.9 12.1 %copy-start.46 = (f32[512,768]{1,0:T(8,128)S(1)}, f32[512,768]{1,0:T(8,128)}, u32[]{:S(2)}) copy-start(f32[512,768]{1,0:T(8,128)} %copy-done.45) | copy-start | bytes 4718596
  247.9 12.1 %copy-start.158 = (f32[768]{0:T(1024)S(1)}, f32[768]{0:T(1024)}, u32[]{:S(2)}) copy-start(f32[768]{0:T(1024)} %get-tuple-element.129) | copy-start | bytes 9220
  247.9 14.1 %slice-start.4 = ((s8[4718592]{0:T(1024)(128)(4,1)}), s8[4194304]{0:T(1024)(128)(4,1)S(1)}, s32[]{:S(2)}) async-start(s8[4718592]{0:T(1024)(128)(4,1)} %bitcast.701), calls=%async_computation.5 | async-start | bytes 8388608
  261.0 18.7 %copy-start.39 = (f32[512,768]{1,0:T(8,128)}, f32[512,768]{1,0:T(8,128)S(1)}, u32[]{:S(2)}) copy-start(f32[512,768]{1,0:T(8,128)S(1)} %get-tuple-element.255) | copy-start | bytes 4718596
  262.9 5.7 copy-start.187
  265.0 10.1 %copy-start.185 = (f32[512,768]{1,0:T(8,128)}, f32[512,768]{1,0:T(8,128)S(1)}, u32[]{:S(2)}) copy-start(f32[512,768]{1,0:T(8,128)S(1)} %convolution_add_fusion.2) | copy-start | bytes 4718596
  266.6 33.6 %copy-start.63 = (f32[512,768]{1,0:T(8,128)}, f32[512,768]{1,0:T(8,128)S(1)}, u32[]{:S(2)}) copy-start(f32[512,768]{1,0:T(8,128)S(1)} %convolution_add_fusion) | copy-start | bytes 4718596
  281.0 38.4 %copy-start.50 = (f32[512,768]{1,0:T(8,128)}, f32[512,768]{1,0:T(8,128)S(1)}, u32[]{:S(2)}) copy-start(f32[512,768]{1,0:T(8,128)S(1)} %get-tuple-element.151) | copy-start | bytes 4718596
  296.4 33.2 %collective-permute-start.1 = (bf16[4,288,512]{2,1,0:T(8,128)(2,1)S(1)}, bf16[4,288,512]{2,1,0:T(8,128)(2,1)S(1)}, u32[]{:S(2)}, u32[]{:S(2)}) collective-permute-start(bf16[4,288,512]{2,1,0:T(8,128)(2,1)S(1)} %pad_maximum_fusion.9), channel_id=1, source_target_pairs={{3,2},{7,6},{11,10},{15,14},{19,18},{23,22},{27,26},{31,30}} | collective-permute-start | bytes 3538952 | tf_op jit(solution)/shard_map/ppermute | solution.py:437
  298.3 55.1 %collective-permute-start = (bf16[4,288,512]{2,1,0:T(8,128)(2,1)}, bf16[4,288,512]{2,1,0:T(8,128)(2,1)}, u32[]{:S(2)}, u32[]{:S(2)}) collective-permute-start(bf16[4,288,512]{2,1,0:T(8,128)(2,1)} %pad_maximum_fusion.8), channel_id=1, source_target_pairs={{3,2},{7,6},{11,10},{15,14},{19,18},{23,22},{27,26},{31,30}} | collective-permute-start | bytes 3538952 | tf_op jit(solution)/shard_map/ppermute | solution.py:437
  304.6 8.3 %copy-start.133 = (s32[6]{0:T(128)S(1)}, s32[6]{0:T(128)}, u32[]{:S(2)}) copy-start(s32[6]{0:T(128)} %param.27) | copy-start | bytes 76
  307.2 167.9 %collective-permute-start.9 = (bf16[2,1536,768]{2,1,0:T(8,128)(2,1)}, bf16[2,1536,768]{2,1,0:T(8,128)(2,1)}, u32[]{:S(2)}, u32[]{:S(2)}) collective-permute-start(bf16[2,1536,768]{2,1,0:T(8,128)(2,1)} %pad_maximum_fusion.2), channel_id=1, source_target_pairs={{0,1},{1,0},{2,3},{3,2},{4,5},{5,4},{6,7},{7,6},{8,9},{9,8},{10,11... | collective-permute-start | bytes 14155784 | tf_op jit(solution)/shard_map/ppermute | solution.py:27
  331.0 42.6 %collective-permute-start.2 = (bf16[4,288,512]{2,1,0:T(8,128)(2,1)}, bf16[4,288,512]{2,1,0:T(8,128)(2,1)}, u32[]{:S(2)}, u32[]{:S(2)}) collective-permute-start(bf16[4,288,512]{2,1,0:T(8,128)(2,1)} %add_convert_fusion.2), channel_id=1, source_target_pairs={{2,1},{6,5},{4,0},{10,9},{14,13},{12,8},{18,17},{22,21},{20,16},{2... | collective-permute-start | bytes 3538952 | tf_op jit(solution)/shard_map/ppermute | solution.py:439
  349.9 23.7 %copy-start.24 = (f32[4,192,512]{2,1,0:T(8,128)S(1)}, f32[4,192,512]{2,1,0:T(8,128)}, u32[]{:S(2)}) copy-start(f32[4,192,512]{2,1,0:T(8,128)} %copy-done.23) | copy-start | bytes 4718596
  375.9 6.4 slice-start.10
  383.6 9.7 %copy-start.92 = (bf16[512,768]{1,0:T(8,128)(2,1)}, bf16[512,768]{1,0:T(8,128)(2,1)S(1)}, u32[]{:S(2)}) copy-start(bf16[512,768]{1,0:T(8,128)(2,1)S(1)} %convert_element_type.444) | copy-start | bytes 2359300
  387.9 6.8 copy-start.173
  390.1 5.7 copy-start.171
  404.9 14.3 %copy-start.110 = (f32[64,512]{1,0:T(8,128)S(1)}, f32[64,512]{1,0:T(8,128)}, u32[]{:S(2)}) copy-start(f32[64,512]{1,0:T(8,128)} %get-tuple-element.196) | copy-start | bytes 393220
  424.9 38.1 %collective-permute-start.4 = (bf16[4,384,512]{2,1,0:T(8,128)(2,1)}, bf16[4,384,512]{2,1,0:T(8,128)(2,1)}, u32[]{:S(2)}, u32[]{:S(2)}) collective-permute-start(bf16[4,384,512]{2,1,0:T(8,128)(2,1)} %pad_maximum_fusion.7), channel_id=1, source_target_pairs={{3,2},{7,6},{11,10},{15,14},{19,18},{23,22},{27,26},{31,30}} | collective-permute-start | bytes 4718600 | tf_op jit(solution)/shard_map/ppermute | solution.py:437
  431.5 72.6 %collective-permute-start.3 = (bf16[4,384,512]{2,1,0:T(8,128)(2,1)}, bf16[4,384,512]{2,1,0:T(8,128)(2,1)}, u32[]{:S(2)}, u32[]{:S(2)}) collective-permute-start(bf16[4,384,512]{2,1,0:T(8,128)(2,1)} %pad_maximum_fusion.6), channel_id=1, source_target_pairs={{3,2},{7,6},{11,10},{15,14},{19,18},{23,22},{27,26},{31,30}} | collective-permute-start | bytes 4718600 | tf_op jit(solution)/shard_map/ppermute | solution.py:437
  434.9 12.0 %copy-start.18 = (bf16[512,768]{1,0:T(8,128)(2,1)S(1)}, bf16[512,768]{1,0:T(8,128)(2,1)}, u32[]{:S(2)}) copy-start(bf16[512,768]{1,0:T(8,128)(2,1)} %copy-done.17) | copy-start | bytes 2359300
  437.5 127.7 %collective-permute-start.7 = (bf16[2,1536,768]{2,1,0:T(8,128)(2,1)}, bf16[2,1536,768]{2,1,0:T(8,128)(2,1)}, u32[]{:S(2)}, u32[]{:S(2)}) collective-permute-start(bf16[2,1536,768]{2,1,0:T(8,128)(2,1)} %pad_maximum_fusion.1), channel_id=1, source_target_pairs={{0,1},{1,0},{2,3},{3,2},{4,5},{5,4},{6,7},{7,6},{8,9},{9,8},{10,11... | collective-permute-start | bytes 14155784 | tf_op jit(solution)/shard_map/ppermute | solution.py:27
  451.7 20.1 %collective-permute-start.6 = (bf16[2,672,768]{2,1,0:T(8,128)(2,1)}, bf16[2,672,768]{2,1,0:T(8,128)(2,1)}, u32[]{:S(2)}, u32[]{:S(2)}) collective-permute-start(bf16[2,672,768]{2,1,0:T(8,128)(2,1)} %pad_maximum_fusion.5), channel_id=1, source_target_pairs={{0,1},{1,0},{2,3},{3,2},{4,5},{5,4},{6,7},{7,6},{8,9},{9,8},{10,11... | collective-permute-start | bytes 6193160 | tf_op jit(solution)/shard_map/ppermute | solution.py:27
  464.9 39.3 %collective-permute-start.5 = (bf16[4,384,512]{2,1,0:T(8,128)(2,1)S(1)}, bf16[4,384,512]{2,1,0:T(8,128)(2,1)S(1)}, u32[]{:S(2)}, u32[]{:S(2)}) collective-permute-start(bf16[4,384,512]{2,1,0:T(8,128)(2,1)S(1)} %add_convert_fusion.1), channel_id=1, source_target_pairs={{2,1},{6,5},{4,0},{10,9},{14,13},{12,8},{18,17},{22,21},{20,16},{2... | collective-permute-start | bytes 4718600 | tf_op jit(solution)/shard_map/ppermute | solution.py:439
  475.2 29.0 %copy-start.22 = (f32[4,192,512]{2,1,0:T(8,128)S(1)}, f32[4,192,512]{2,1,0:T(8,128)}, u32[]{:S(2)}) copy-start(f32[4,192,512]{2,1,0:T(8,128)} %copy-done.21) | copy-start | bytes 4718596
  479.1 81.3 %collective-permute-start.10 = (bf16[1536,768]{1,0:T(8,128)(2,1)}, bf16[1536,768]{1,0:T(8,128)(2,1)}, u32[]{:S(2)}, u32[]{:S(2)}) collective-permute-start(bf16[1536,768]{1,0:T(8,128)(2,1)} %fusion.10), channel_id=1, source_target_pairs={{0,2},{1,3},{2,0},{3,1},{4,6},{5,7},{6,4},{7,5},{8,10},{9,11},{10,... | collective-permute-start | bytes 7077896 | tf_op jit(solution)/shard_map/ppermute | solution.py:27
  512.1 11.7 %copy-start.53 = (bf16[512,768]{1,0:T(8,128)(2,1)S(1)}, bf16[512,768]{1,0:T(8,128)(2,1)}, u32[]{:S(2)}) copy-start(bf16[512,768]{1,0:T(8,128)(2,1)} %param.24) | copy-start | bytes 2359300
  512.1 11.7 %copy-start.120 = (f32[768]{0:T(1024)S(1)}, f32[768]{0:T(1024)}, u32[]{:S(2)}) copy-start(f32[768]{0:T(1024)} %copy-done.119) | copy-start | bytes 9220
  512.1 11.7 %copy-start.122 = (f32[512]{0:T(512)S(1)}, f32[512]{0:T(512)}, u32[]{:S(2)}) copy-start(f32[512]{0:T(512)} %copy-done.121) | copy-start | bytes 6148
  512.1 11.7 %copy-start.129 = (f32[512]{0:T(512)S(1)}, f32[512]{0:T(512)}, u32[]{:S(2)}) copy-start(f32[512]{0:T(512)} %copy-done.128) | copy-start | bytes 6148
  513.8 56.5 %collective-permute-start.8 = (bf16[2,768,768]{2,1,0:T(8,128)(2,1)}, bf16[2,768,768]{2,1,0:T(8,128)(2,1)}, u32[]{:S(2)}, u32[]{:S(2)}) collective-permute-start(bf16[2,768,768]{2,1,0:T(8,128)(2,1)} %pad_maximum_fusion.4), channel_id=1, source_target_pairs={{0,1},{1,0},{2,3},{3,2},{4,5},{5,4},{6,7},{7,6},{8,9},{9,8},{10,11... | collective-permute-start | bytes 7077896 | tf_op jit(solution)/shard_map/ppermute | solution.py:27
  523.8 5.5 copy-start.143
  523.9 5.5 copy-start.164
  523.9 5.5 copy-start.141
  523.9 5.5 copy-start.163
  523.9 5.5 copy-start.139
  523.9 5.5 copy-start.142
  523.9 5.5 copy-start.140
  523.9 5.6 copy-start.150
  523.9 5.6 copy-start.157
  524.0 5.6 copy-start.149
  524.0 5.7 copy-start.148
  524.0 5.7 copy-start.147
  524.0 5.7 copy-start.146
  524.0 5.7 copy-start.145
  530.4 30.0 %copy-start.69 = (bf16[768,768]{1,0:T(8,128)(2,1)S(1)}, bf16[768,768]{1,0:T(8,128)(2,1)}, u32[]{:S(2)}) copy-start(bf16[768,768]{1,0:T(8,128)(2,1)} %convolution_convert_fusion.9) | copy-start | bytes 3538948
  530.4 30.0 %copy-start.70 = (bf16[768,768]{1,0:T(8,128)(2,1)S(1)}, bf16[768,768]{1,0:T(8,128)(2,1)}, u32[]{:S(2)}) copy-start(bf16[768,768]{1,0:T(8,128)(2,1)} %convolution_convert_fusion.8) | copy-start | bytes 3538948
  (151 other events, 313.2 us)
Sparse Core Ops, SparseCore 0:
  565.2 160.8 all-reduce.11

commit v3 on v2

--- a/solution.py
+++ b/solution.py
@@ -14,6 +14,9 @@
 EARLY = 2
 GROUP = 3
 BAND = GROUP * HD
+AT_REUSE = 2
+AT_FLAG = AT_REUSE + REUSE
+AT_GIVEN = AT_FLAG + 4 * GROUP
 TILE = 256
 TILES = 3 * WIN // TILE
 EPS = 1e-05
@@ -82,20 +85,38 @@
     return scale * inner, jnp.sum(grad * unit, axis=0), jnp.sum(grad, axis=0)
 
 
-def attend_kernel(first_ref, lo_ref, q_ref, k0, k1, k2, v0, v1, v2, out_ref, exact_ref, sum_ref, top, total, acc):
-    keys, values = (k2, k1, k0), (v2, v1, v0)
+def place_values(refs, values):
+    if len(refs) == 3:
+        for part, ref in enumerate(reversed(refs)):
+            values[part] = ref[0]
+        return
+    group = pl.program_id(0)
+
+    def reused():
+        for part in range(3):
+            for j in range(GROUP):
+                values[part, j * HD : (j + 1) * HD, :] = refs[4 * (2 - part) + j][0]
+
+    def fresh():
+        for part in range(3):
+            values[part] = refs[4 * (2 - part) + GROUP][0]
+
+    pl.when(group < 2)(reused)
+    pl.when(group >= 2)(fresh)
+
+
+def attend_kernel(n_values, first_ref, lo_ref, q_ref, k0, k1, k2, *refs):
+    v_refs = refs[:n_values]
+    out_ref, exact_ref, sum_ref, values, raw, top, total, acc = refs[n_values:]
+    keys = (k2, k1, k0)
+    place_values(v_refs, values)
     for t in range(WIN // TILE):
         cols = slice(t * TILE, (t + 1) * TILE)
         low = lo_ref[:, cols]
         place = 2 * WIN + t * TILE + lax.broadcasted_iota(jnp.int32, (1, TILE), 1)
         last = 2 * WIN // TILE + t
 
-        def scores(kt, j):
-            rows = slice(j * HD, (j + 1) * HD)
-            span = slice(kt % 2 * TILE, (kt % 2 + 1) * TILE)
-            return dot(keys[kt // 2][0, rows, span], q_ref[0, rows, cols] * SCALE, 0, 0)
-
-        def tile(kt):
+        def score(kt):
             spot = kt * TILE + lax.broadcasted_iota(jnp.int32, (TILE, TILE), 0)
             keep = spot >= low
             if kt == last:
@@ -103,40 +124,59 @@
             span = slice(kt % 2 * TILE, (kt % 2 + 1) * TILE)
             for j in range(GROUP):
                 rows = slice(j * HD, (j + 1) * HD)
-                raw = jnp.where(keep, scores(kt, j), -jnp.inf)
-                peak = jnp.max(raw, axis=0, keepdims=True)
-                if kt != last:
-                    before = top[j]
-                    peak = jnp.maximum(peak, before)
-                powers = jnp.exp(raw - peak)
-                added = jnp.sum(powers, axis=0, keepdims=True)
-                result = dot(values[kt // 2][0, rows, span], powers.astype(BF16), 1, 0)
-                if kt != last:
-                    shrink = jnp.exp(before - peak)
-                    added = added + total[j] * shrink
-                    result = result + acc[j] * shrink
-                top[j] = peak
-                total[j] = added
-                acc[j] = result
-
-        tile(last)
-        for kt in reversed(range(last)):
-            pl.when(kt >= first_ref[t])(functools.partial(tile, kt))
+                found = dot(keys[kt // 2][0, rows, span], q_ref[0, rows, cols] * SCALE, 0, 0)
+                found = jnp.where(keep, found, -jnp.inf)
+                raw[j, kt] = found
+                peak = jnp.max(found.reshape(TILE // 8, 8, TILE), axis=0)
+                top[j] = peak if kt == last else jnp.maximum(top[j], peak)
+
+        def weigh(kt):
+            span = slice(kt % 2 * TILE, (kt % 2 + 1) * TILE)
+            for j in range(GROUP):
+                rows = slice(j * HD, (j + 1) * HD)
+                powers = jnp.exp(raw[j, kt] - top[j, 0:1])
+                added = jnp.sum(powers.reshape(TILE // 8, 8, TILE), axis=0)
+                result = dot(values[kt // 2, rows, span], powers.astype(BF16), 1, 0)
+                total[j] = added if kt == last else total[j] + added
+                acc[j] = result if kt == last else acc[j] + result
+
+        for stage in (score, weigh):
+            stage(last)
+            for kt in reversed(range(last)):
+                pl.when(kt >= first_ref[t])(functools.partial(stage, kt))
+            if stage is score:
+                for j in range(GROUP):
+                    top[j] = jnp.broadcast_to(jnp.max(top[j], axis=0, keepdims=True), (8, TILE))
         for j in range(GROUP):
             rows = slice(j * HD, (j + 1) * HD)
-            result = acc[j] / total[j]
+            whole = jnp.sum(total[j], axis=0, keepdims=True)
+            result = acc[j] / whole
             out_ref[0, rows, cols] = result.astype(BF16)
             exact_ref[0, rows, cols] = result
-            sum_ref[0, j : j + 1, cols] = top[j] + jnp.log(total[j])
-
-
-def attend_back_kernel(
-    first_ref, lo_ref, q_ref, k0, k1, k2, v0, v1, v2, out_ref, grad_ref, sum_ref,
-    dq_ref, dk0, dk1, dk2, dv0, dv1, dv2, acc_k, acc_v, acc_q,
-):
-    keys, values = (k2, k1, k0), (v2, v1, v0)
+            sum_ref[0, j : j + 1, cols] = top[j, 0:1] + jnp.log(whole)
+
+
+def attend_back_kernel(n_values, n_given, first_ref, lo_ref, _, q_ref, k0, k1, k2, *refs):
+    v_refs, refs = refs[:n_values], refs[n_values:]
+    given, refs = refs[:n_given], refs[n_given:]
+    (
+        out_ref, grad_ref, sum_ref, dq_ref, dk0, dk1, dk2, dv0, dv1, dv2,
+        values, acc_k, acc_v, acc_q,
+    ) = refs
+    keys = (k2, k1, k0)
+    place_values(v_refs, values)
     acc_k[...] = jnp.zeros_like(acc_k)
     acc_v[...] = jnp.zeros_like(acc_v)
+    for i, ref in enumerate(given):
+        part, j = 2 - i // GROUP, i % GROUP
+        head = GROUP * pl.program_id(0) + j
+
+        def add(part=part, j=j, ref=ref):
+            for half in range(2):
+                span = slice(half * TILE, (half + 1) * TILE)
+                acc_v[2 * part + half, j * HD : (j + 1) * HD, :] = ref[0, :, span].astype(F32)
+
+        pl.when(first_ref[AT_FLAG + head] == 1)(add)
     for t in range(WIN // TILE):
         cols = slice(t * TILE, (t + 1) * TILE)
         low = lo_ref[:, cols]
@@ -159,7 +199,7 @@
                 )
                 raw = jnp.where(keep, dot(key, query, 0, 0), -jnp.inf)
                 weights = jnp.exp(raw - sum_ref[0, j : j + 1, cols])
-                grad_weights = dot(values[kt // 2][0, rows, span], grad, 0, 0)
+                grad_weights = dot(values[kt // 2, rows, span], grad, 0, 0)
                 low_grad = (weights * (grad_weights - inner)).astype(BF16)
                 acc_v[kt, rows, :] += dot(grad, weights.astype(BF16), 1, 1)
                 acc_k[kt, rows, :] += dot(query, low_grad, 1, 1)
@@ -189,17 +229,50 @@
 SUMS = pl.BlockSpec((1, 8, WIN), lambda s, *_: (s, 0, 0))
 
 
-def attend(first, low, operands, places):
+def head_block(stride, offset, j):
+    def at(s, scalars):
+        head = scalars[AT_REUSE + jnp.minimum(GROUP * s + j, REUSE - 1)]
+        return (head // GROUP * stride + offset + head % GROUP, 0, 0)
+
+    return pl.BlockSpec((1, HD, WIN), at)
+
+
+def given_block(j):
+    return pl.BlockSpec(
+        (1, HD, WIN), lambda s, scalars: (scalars[AT_GIVEN + GROUP * s + j], 0, 0)
+    )
+
+
+FRESH = pl.BlockSpec((1, BAND, WIN), lambda s, *_: (jnp.maximum(s - 2, 0), 0, 0))
+
+
+def values_of(cols, before, earlier):
+    return [cols, before, earlier], [band(2), band(1), band(1)]
+
+
+def values_mixed(firsts, freshes):
+    arrays, specs = [], []
+    for k, (first, fresh) in enumerate(zip(firsts, freshes, strict=True)):
+        stride, offset = (3 * GROUP, 2 * GROUP) if k == 0 else (2 * GROUP, GROUP)
+        arrays += [first.reshape(-1, HD, WIN)] * GROUP + [fresh]
+        specs += [head_block(stride, offset, j) for j in range(GROUP)] + [FRESH]
+    return arrays, specs
+
+
+def attend(scalars, low, front, values):
+    arrays, specs = values
     return pl.pallas_call(
-        attend_kernel,
+        functools.partial(attend_kernel, len(arrays)),
         grid_spec=pltpu.PrefetchScalarGridSpec(
             num_scalar_prefetch=1,
             grid=(4,),
-            in_specs=[LOW] + [band(p) for p in places],
+            in_specs=[LOW, band(0), band(1), band(0), band(0)] + specs,
             out_specs=[band(0), band(0), SUMS],
             scratch_shapes=[
-                pltpu.VMEM((GROUP, 1, TILE), F32),
-                pltpu.VMEM((GROUP, 1, TILE), F32),
+                pltpu.VMEM((3, BAND, WIN), BF16),
+                pltpu.VMEM((GROUP, TILES, TILE, TILE), F32),
+                pltpu.VMEM((GROUP, 8, TILE), F32),
+                pltpu.VMEM((GROUP, 8, TILE), F32),
                 pltpu.VMEM((GROUP, HD, TILE), F32),
             ],
         ),
@@ -210,19 +283,25 @@
         ],
         compiler_params=pltpu.CompilerParams(vmem_limit_bytes=32 * 1024 * 1024),
         name="attend",
-    )(first, low, *operands)
-
-
-def attend_back(first, low, operands, places, heads, grad_heads, sums):
+    )(scalars, low, front[0], *front, *arrays)
+
+
+def attend_back(after, scalars, low, front, values, given, heads, grad_heads, sums):
     kinds = (F32, F32, BF16, BF16, F32, BF16, BF16)
+    arrays, specs = values
+    given_arrays = [v.reshape(-1, HD, WIN) for v in given for _ in range(GROUP)]
+    given_specs = [given_block(j) for _ in given for j in range(GROUP)]
     return pl.pallas_call(
-        attend_back_kernel,
+        functools.partial(attend_back_kernel, len(arrays), len(given_arrays)),
         grid_spec=pltpu.PrefetchScalarGridSpec(
             num_scalar_prefetch=1,
             grid=(4,),
-            in_specs=[LOW] + [band(p) for p in places] + [band(0), band(0), SUMS],
+            in_specs=[LOW, pl.BlockSpec(memory_space=pl.ANY)]
+            + [band(0), band(1), band(0), band(0)] + specs + given_specs
+            + [band(0), band(0), SUMS],
             out_specs=[band(0)] * 7,
             scratch_shapes=[
+                pltpu.VMEM((3, BAND, WIN), BF16),
                 pltpu.VMEM((TILES, BAND, TILE), F32),
                 pltpu.VMEM((TILES, BAND, TILE), F32),
                 pltpu.VMEM((GROUP, HD, TILE), F32),
@@ -231,7 +310,7 @@
         out_shape=[jax.ShapeDtypeStruct((4, BAND, WIN), kind) for kind in kinds],
         compiler_params=pltpu.CompilerParams(vmem_limit_bytes=32 * 1024 * 1024),
         name="attend_back",
-    )(first, low, *operands, heads, grad_heads, sums)
+    )(scalars, low, after, front[0], *front, *arrays, *given_arrays, heads, grad_heads, sums)
 
 
 def front_kernel(n_more, *refs):
@@ -459,142 +538,167 @@
     )
 
 
-def sum_chips(own, far):
-    total = own.astype(F32) + swap(far, "mp", 2).astype(F32)
-    return lax.psum(total.astype(BF16), ("dp", "ctx"))
-
-
-def sum_kernel(
-    parts, rows, own, far, vec_in, out, vec, from_y, mine, from_x, kept, from_z, from_vec,
-    y_out, y_in, x_out, x_in, z_out, z_in, g_out, g_in, h_out, h_in, v_out, v_in,
-):
+def sum_kernel(counts, rows, *refs):
+    refs = list(refs)
+
+    def take(count):
+        taken = refs[:count]
+        del refs[:count]
+        return taken
+
+    owns, fars = take(len(counts)), take(len(counts))
+    vec_in, out, vec, from_y, mine, from_x, kept, from_z, from_vec = take(9)
+    y_out, y_in, x_out, x_in, z_out, z_in, g_out, g_in, h_out, h_in, v_out, v_in = refs
+    parts = sum(counts)
+    firsts = [sum(counts[:k]) for k in range(len(counts))]
     ctx, dp, mp = (lax.axis_index(axis) for axis in ("ctx", "dp", "mp"))
-    n_dp = lax.axis_size("dp")
     half = rows // 2
-    piece = half // n_dp
+    bits = [1 << k for k in range((lax.axis_size("dp") - 1).bit_length())]
+    highs = [(dp // bit) % 2 for bit in bits]
     other_chip, other_window = {"mp": flip(mp, 2)}, {"ctx": 1 - ctx}
-    partners = [other_chip, other_window, {"mp": flip(mp, 1)}]
-    bit = 1
-    while bit < n_dp:
-        partners.append({"dp": flip(dp, bit)})
-        bit *= 2
-
-    def along(k):
-        return {"dp": lax.rem(dp + k, n_dp)}
+    beside = [{"dp": flip(dp, bit)} for bit in bits]
+    partners = [other_chip, other_window, {"mp": flip(mp, 1)}] + beside
 
     def ds(start, size):
         return pl.ds(pl.multiple_of(start, 16), size)
 
-    def span(i, high, at=0, size=half):
-        return ds(i * rows + high * half + at * piece, size)
-
-    def to_y(i):
-        here = ds(i * rows, rows)
-        return remote(far.at[here], from_y.at[here], y_out.at[i], y_in.at[i], other_chip)
+    def segment(i, k, sent=False):
+        start, size = 0, half
+        for high in highs[:k]:
+            size //= 2
+            start = start + high * size
+        if sent:
+            size //= 2
+            start = start + (1 - highs[k]) * size
+        return start, size
+
+    def to_y(array, i):
+        here = ds((firsts[array] + i) * rows, rows)
+        source = fars[array].at[ds(i * rows, rows)]
+        place = firsts[array] + i
+        return remote(source, from_y.at[here], y_out.at[place], y_in.at[place], other_chip)
 
     def to_x(i):
+        source = mine.at[ds(i * rows + (1 - ctx) * half, half)]
         target = from_x.at[ds(i * half, half)]
-        return remote(mine.at[span(i, 1 - ctx)], target, x_out.at[i], x_in.at[i], other_window)
+        return remote(source, target, x_out.at[i], x_in.at[i], other_window)
 
     def to_z(i, k):
-        other = lax.rem(dp + k, n_dp)
-        source = kept.at[ds(i * half + other * piece, piece)]
-        target = from_z.at[ds((i * n_dp + k) * piece, piece)]
-        return remote(source, target, z_out.at[i, k], z_in.at[i, k], along(k))
-
-    def round_z(i, k):
-        here = out.at[span(i, ctx, dp, piece)]
-        return remote(here, here, g_out.at[i, k], g_in.at[i, k], along(k))
+        start, size = segment(i, k, True)
+        target = from_z.at[ds(i * half + half - 2 * size, size)]
+        source = kept.at[ds(i * half + start, size)]
+        return remote(source, target, z_out.at[i, k], z_in.at[i, k], beside[k])
+
+    def back_z(i, k):
+        start, size = segment(i, k + 1)
+        here = out.at[ds(i * rows + ctx * half + start, size)]
+        return remote(here, here, g_out.at[i, k], g_in.at[i, k], beside[k])
 
     def back_x(i):
-        here = out.at[span(i, ctx)]
+        here = out.at[ds(i * rows + ctx * half, half)]
         return remote(here, here, h_out.at[i], h_in.at[i], other_window)
 
     def each(count, step):
         lax.fori_loop(0, count, lambda i, _: (step(i), 0)[1], 0)
 
-    barrier = pltpu.get_barrier_semaphore()
-
-    def greet(device):
-        pl.semaphore_signal(barrier, inc=1, device_id=device, device_id_type=pl.DeviceIdType.MESH)
-
-    for partner in partners[:3]:
-        greet(partner)
-    each(n_dp - 1, lambda k: greet(along(k + 1)))
-    pl.semaphore_wait(barrier, n_dp + 2)
-
+    meet(partners)
     vec[...] = vec_in[...]
     for hop, partner in enumerate(partners):
         copy = remote(vec, from_vec.at[hop], v_out.at[hop], v_in.at[hop], partner)
         copy.start()
         if hop == 0:
-            each(parts, lambda i: to_y(i).start())
+            for array, count in enumerate(counts):
+                each(count, lambda i, array=array: to_y(array, i).start())
         copy.wait()
         vec[...] = vec[...] + from_vec[hop]
 
     def join(i):
-        to_y(i).wait_recv()
         here = ds(i * rows, rows)
-        mine[here, :] = (own[here, :].astype(F32) + from_y[here, :].astype(F32)).astype(BF16)
+        for array, count in enumerate(counts):
+
+            def add(array=array):
+                to_y(array, i - firsts[array]).wait_recv()
+                term = owns[array][ds((i - firsts[array]) * rows, rows), :]
+                mine[here, :] = (term.astype(F32) + from_y[here, :].astype(F32)).astype(BF16)
+
+            pl.when((i >= firsts[array]) & (i < firsts[array] + count))(add)
         to_x(i).start()
 
     def spread(i):
         to_x(i).wait_recv()
         there = ds(i * half, half)
-        total = mine[span(i, ctx), :].astype(F32) + from_x[there, :].astype(F32)
+        total = mine[ds(i * rows + ctx * half, half), :].astype(F32) + from_x[there, :].astype(F32)
         kept[there, :] = total.astype(BF16)
-        each(n_dp - 1, lambda k: to_z(i, k + 1).start())
-
-    def gather(i):
-        def add(k, total):
-            to_z(i, k).wait_recv()
-            return total + from_z[ds((i * n_dp + k) * piece, piece), :].astype(F32)
-
-        total = kept[ds(i * half + dp * piece, piece), :].astype(F32)
-        out[span(i, ctx, dp, piece), :] = lax.fori_loop(1, n_dp, add, total).astype(BF16)
-        each(n_dp - 1, lambda k: round_z(i, k + 1).start())
-
-    def give(i):
-        each(n_dp - 1, lambda k: round_z(i, k + 1).wait_recv())
-        back_x(i).start()
+        to_z(i, 0).start()
+
+    def narrow(k, i):
+        to_z(i, k).wait_recv()
+        start, size = segment(i, k + 1)
+        here = ds(i * half + start, size)
+        there = ds(i * half + half - 2 * size, size)
+        total = (kept[here, :].astype(F32) + from_z[there, :].astype(F32)).astype(BF16)
+        if k + 1 < len(bits):
+            kept[here, :] = total
+            to_z(i, k + 1).start()
+        else:
+            out[ds(i * rows + ctx * half + start, size), :] = total
+            back_z(i, k).start()
+
+    def widen(k, i):
+        back_z(i, k).wait_recv()
+        if k:
+            back_z(i, k - 1).start()
+        else:
+            back_x(i).start()
+
+    stages = [join, spread]
+    stages += [functools.partial(narrow, k) for k in range(len(bits))]
+    stages += [functools.partial(widen, k) for k in reversed(range(len(bits)))]
 
     def step(i):
-        for late, stage in enumerate((join, spread, gather, give)):
+        for late, stage in enumerate(stages):
             pl.when((i >= late) & (i < parts + late))(functools.partial(stage, i - late))
 
-    each(parts + 3, step)
+    each(parts + len(stages) - 1, step)
+    for array, count in enumerate(counts):
+        each(count, lambda i, array=array: to_y(array, i).wait_send())
 
     def finish(i):
-        to_y(i).wait_send()
         to_x(i).wait_send()
         back_x(i).wait()
-
-        def sent(k):
-            to_z(i, k + 1).wait_send()
-            round_z(i, k + 1).wait_send()
-
-        each(n_dp - 1, sent)
+        for k in range(len(bits)):
+            to_z(i, k).wait_send()
+            back_z(i, k).wait_send()
 
     each(parts, finish)
 
 
-def sum_replicas(own, far, vectors):
-    n_dp = lax.axis_size("dp")
-    rows = max(256, 32 * n_dp)
-    parts = -(-own.shape[0] // rows)
+def rows_of_part():
+    return max(256, 32 * lax.axis_size("dp"))
+
+
+def sum_replicas(pairs, vectors):
+    rows = rows_of_part()
+    bits = (lax.axis_size("dp") - 1).bit_length()
+    hops = 3 + bits
+    lanes = pairs[0][0].shape[1]
+    owns, fars = (
+        [jnp.pad(v, ((0, -v.shape[0] % rows), (0, 0))) for v in half] for half in zip(*pairs)
+    )
+    counts = [v.shape[0] // rows for v in owns]
+    parts = sum(counts)
     total = parts * rows
-    hops = 3 + (n_dp - 1).bit_length()
-    lanes = own.shape[1]
-    own, far = (jnp.pad(v, ((0, total - v.shape[0]), (0, 0))) for v in (own, far))
     place = pl.BlockSpec(memory_space=pltpu.VMEM)
     dma = pltpu.SemaphoreType.DMA
     return pl.pallas_call(
-        functools.partial(sum_kernel, parts, rows),
+        functools.partial(sum_kernel, counts, rows),
         out_shape=[
             jax.ShapeDtypeStruct((total, lanes), BF16),
             jax.ShapeDtypeStruct(vectors.shape, F32),
         ],
-        in_specs=[place, place, place],
+        in_specs=[place] * len(counts)
+        + [pl.BlockSpec(memory_space=pl.ANY)] * len(counts)
+        + [place],
         out_specs=[place, place],
         scratch_shapes=[
             pltpu.VMEM((total, lanes), BF16),
@@ -605,8 +709,8 @@
             pltpu.VMEM((hops,) + vectors.shape, F32),
             dma((parts,)), dma((parts,)),
             dma((parts,)), dma((parts,)),
-            dma((parts, n_dp)), dma((parts, n_dp)),
-            dma((parts, n_dp)), dma((parts, n_dp)),
+            dma((parts, bits)), dma((parts, bits)),
+            dma((parts, bits)), dma((parts, bits)),
             dma((parts,)), dma((parts,)),
             dma((hops,)), dma((hops,)),
         ],
@@ -614,7 +718,7 @@
             collective_id=0, has_side_effects=True, vmem_limit_bytes=56 * 1024 * 1024
         ),
         name="sum_replicas",
-    )(own, far, vectors)
+    )(*owns, *fars, vectors)
 
 
 def gelu(hidden):
@@ -668,6 +772,9 @@
     out_weight2, out_bias2, up_weight2, up_bias2, down_weight2,
 ):
     low, first = row_starts(doc_lengths[0])
+    taken = jnp.arange(4 * GROUP, dtype=jnp.int32)[:, None] == reuse_heads[None, :]
+    taker = jnp.sum(jnp.where(taken, jnp.arange(REUSE, dtype=jnp.int32)[None, :], 0), axis=1)
+    scalars = jnp.concatenate([first, reuse_heads, jnp.any(taken, axis=1).astype(jnp.int32), taker])
 
     stream0 = block_input.astype(F32)
     normed1, unit1, scale1 = norm_rows(stream0, norm_gain1[0], norm_bias1[0])
@@ -707,9 +814,9 @@
     up_biases1 = by_distance(small[:, at : at + D])
     up_biases2 = by_distance(small[:, at + D : at + 2 * D])
 
-    operands1 = (cols1, cols1, before1, earlier1, cols1, before1, earlier1)
-    places1 = (0, 1, 0, 0, 2, 1, 1)
-    heads1, exact1, sums1 = attend(first, low, operands1, places1)
+    front_kv1 = (cols1, before1, earlier1)
+    values1 = values_of(cols1, before1, earlier1)
+    heads1, exact1, sums1 = attend(scalars, low, front_kv1, values1)
     stream1, kept1 = tail_forward(
         stream0, heads1.reshape(D, WIN), outs1, out_bias1, norm_gain1, norm_bias1,
         ups1, up_biases1, downs1,
@@ -719,22 +826,10 @@
     cols2, before2, earlier2 = project(normed2, front2, bias2, n_front2, n_front2 - BAND)
     front2 = front2[:, :n_front2]
 
-    def mixed(first_values, fresh):
-        first_values = first_values.reshape(-1, HD, WIN)
-        reused = [
-            lax.dynamic_index_in_dim(first_values, reuse_heads[n], 0, keepdims=True)
-            for n in range(REUSE)
-        ]
-        return jnp.concatenate(reused + [fresh.reshape(-1, HD, WIN)]).reshape(4, BAND, WIN)
-
-    values2 = [
-        mixed(cols1[:, 2 * BAND :], cols2[:, 2 * BAND :]),
-        mixed(before1[:, BAND:], before2[:, BAND:]),
-        mixed(earlier1[:, BAND:], earlier2[:, BAND:]),
-    ]
-    operands2 = (cols2, cols2, before2, earlier2, *values2)
-    places2 = (0, 1, 0, 0, 0, 0, 0)
-    heads2, exact2, sums2 = attend(first, low, operands2, places2)
+    front_kv2 = (cols2, before2, earlier2)
+    fresh2 = [v[:, -(BAND // 2) :].reshape(2, BAND, WIN) for v in front_kv2]
+    values2 = values_mixed(front_kv1, fresh2)
+    heads2, exact2, sums2 = attend(scalars, low, front_kv2, values2)
     stream2, kept2 = tail_forward(
         stream1, heads2.reshape(D, WIN), outs2, out_bias2, norm_gain2, norm_bias2,
         ups2, up_biases2, downs2,
@@ -744,9 +839,9 @@
     grad, rounded, grad_heads, mats2, up_grads2, small2 = tail_backward(
         cotangent.astype(F32), kept2, outs2, norm_gain2, ups2, downs2
     )
-    mats2 = sum_chips(*sum_cores(mats2))
+    own2, far2 = sum_cores(mats2)
     dq2, dk2, dk2_before, dk2_earlier, dv2, dv2_before, dv2_earlier = attend_back(
-        first, low, operands2, places2, exact2, grad_heads.reshape(4, BAND, WIN), sums2
+        far2, scalars, low, front_kv2, values2, (), exact2, grad_heads.reshape(4, BAND, WIN), sums2
     )
     grad_out2 = dot(heads2.reshape(D, WIN), rounded, 1, 0).astype(BF16).reshape(4, BAND, D)
 
@@ -777,23 +872,16 @@
     )
     mats1 = sum_cores(mats1)
     dq1, dk1, dk1_before, dk1_earlier, dv1, dv1_before, dv1_earlier = attend_back(
-        first, low, operands1, places1, exact1, grad_heads.reshape(4, BAND, WIN), sums1
+        far2, scalars, low, front_kv1, values1, (dv2, dv2_before, dv2_earlier), exact1,
+        grad_heads.reshape(4, BAND, WIN), sums1,
     )
     grad_out1 = dot(heads1.reshape(D, WIN), rounded, 1, 0).astype(BF16).reshape(4, BAND, D)
 
-    def reused(values, grads):
-        heads = values.astype(F32).reshape(-1, HD, WIN)
-        given = grads[:2].astype(F32).reshape(-1, HD, WIN)
-        taken = jnp.arange(heads.shape[0])[:, None] == reuse_heads[None, :]
-        for n in range(REUSE):
-            heads = heads + jnp.where(taken[:, n, None, None], given[n], 0.0)
-        return heads.reshape(values.shape)
-
-    def join1(keys, values, grads):
-        return jnp.concatenate([keys, reused(values, grads).astype(keys.dtype)], axis=1)
-
-    kv1 = join1(dk1, dv1, dv2) + pass_home(
-        join1(dk1_before, dv1_before, dv2_before), join1(dk1_earlier, dv1_earlier, dv2_earlier)
+    def join1(keys, values):
+        return jnp.concatenate([keys, values], axis=1)
+
+    kv1 = join1(dk1, dv1) + pass_home(
+        join1(dk1_before, dv1_before), join1(dk1_earlier, dv1_earlier)
     )
     dcols1 = jnp.concatenate([dq1, kv1], axis=1)
     bias_grad1 = jnp.sum(dcols1, axis=2)
@@ -818,10 +906,8 @@
     lengths = [vector.shape[0] for vector in vectors]
     packed = jnp.concatenate(vectors)
     filler = (-packed.shape[0]) % 1024
-    stack, packed = sum_replicas(
-        *(jnp.concatenate(three) for three in zip(attn2, mats1, attn1, strict=True)),
-        jnp.pad(packed, (0, filler)).reshape(-1, 128),
-    )
+    pairs = ((own2, far2), attn2, mats1, attn1)
+    stack, packed = sum_replicas(pairs, jnp.pad(packed, (0, filler)).reshape(-1, 128))
     packed = packed.reshape(-1)
     sums, at = [], 0
     for length in lengths:
@@ -835,34 +921,35 @@
     def pair(i):
         return jnp.stack([sums[i], sums[i + 1]])
 
-    mats2, stack = mats2.astype(F32), stack.astype(F32)
-    rows2, rows1 = BAND + n_front2, BAND + n_front1
-    attn2, mats1, attn1 = (
-        stack[at : at + size] for at, size in ((0, rows2), (rows2, 2 * D), (rows2 + 2 * D, rows1))
-    )
+    shares, at = [], 0
+    for own, _ in pairs:
+        shares.append(stack[at : at + own.shape[0]])
+        at += own.shape[0] + -own.shape[0] % rows_of_part()
+    mats2, attn2, mats1, attn1 = shares
+
     return (
         block_output,
         input_grad,
         pair(0),
         pair(2),
-        turned(attn1[BAND : BAND + n_front1].reshape(3, BAND, D)),
+        turned(attn1[BAND : BAND + n_front1].reshape(3, BAND, D)).astype(F32),
         jnp.stack([mine(sums[12]), mine(sums[13])]),
-        attn1[:BAND],
+        attn1[:BAND].astype(F32),
         pair(4),
-        mats1[:D],
+        mats1[:D].astype(F32),
         mine(sums[16]),
-        mats1[D:],
+        mats1[D:].astype(F32),
         pair(6),
         pair(8),
-        turned(attn2[BAND : 3 * BAND].reshape(2, BAND, D)),
+        turned(attn2[BAND : 3 * BAND].reshape(2, BAND, D)).astype(F32),
         mine(sums[14]),
-        turned(attn2[3 * BAND : BAND + n_front2]),
+        turned(attn2[3 * BAND : BAND + n_front2]).astype(F32),
         mine(sums[15]),
-        attn2[:BAND],
+        attn2[:BAND].astype(F32),
         pair(10),
-        mats2[:D],
+        mats2[:D].astype(F32),
         mine(sums[17]),
-        mats2[D:],
+        mats2[D:].astype(F32),
     )
 
 

time: 815 us -> 666 us (0.82)
  local copies, waits for them, and re-layouts: 117 us -> 46.7 us
  starting transfers between devices: 60.1 us -> 20.8 us
  between operations: 29 us -> 3.61 us
  other arithmetic: 72 us -> 59.2 us
  Pallas kernels: 392 us -> 381 us
    ppermute x5 -> x4, starting transfers between devices: 50.1 us -> 12.5 us  [swap(): return lax.ppermute(value, axis, [(i, i ^ bit) for i in devices])]
    ppermute x2, waiting for transfers between devices: 20.2 us -> 49.1 us  [pass_home(): return near.astype(F32) + lax.ppermute(far, ('ctx', 'mp'), home).astype(F32)]
    ppermute x5 -> x4, waiting for transfers between devices: 28.6 us -> 0.01 us  [swap(): return lax.ppermute(value, axis, [(i, i ^ bit) for i in devices])]
    unnamed x457 -> x340, local copies, waits for them, and re-layouts: 60.6 us -> 34.8 us
    slice x14 -> x6, local copies, waits for them, and re-layouts: 18.1 us -> 0.19 us  [the longest x3 0.1 us: fresh_part(): return grads[2:].reshape(4, BAND // 2, WIN)]
    pallas_call x5, Pallas kernels: 257 us -> 242 us  [the longest x1 197 us: sum_replicas(): pl.pallas_call(functools.partial(sum_kernel, counts, rows), out_shape=[ja...]
    broadcast_in_dim x36 -> x0, local copies, waits for them, and re-layouts: 14.4 us -> none  [reused(): heads = heads + jnp.where(taken[:, n, None, None], given[n], 0.0)]
  transfers between devices with their start and end apart: 12 -> 10, of which waited for: 2 -> 2; matrix products, arithmetic and copies ran while one was open for 20% -> 12% of each run, Pallas kernels for 26% -> 0%
where the time goes in v3:
time: 666 us; the launch traced here: 657 us
  Pallas kernels  381 us (57%)
  matrix products  97.1 us (15%)
  other arithmetic  59.2 us (9%)
  waiting for transfers between devices  49.1 us (7%)
  local copies, waits for them, and re-layouts  46.7 us (7%)
  starting transfers between devices  20.8 us (3%)
    pallas_call x1, Pallas kernels, sum_replicas(): pl.pallas_call(functools.partial(sum_kernel, counts, rows), out_shape=[ja...  197 us
    pallas_call x2, Pallas kernels, project(): pl.pallas_call(functools.partial(front_kernel, len(more)), out_shape=made...  139 us
    dot_general x58, matrix products, dot(): lax.dot_general(left, right, (((left_dim,), (right_dim,)), ((), ())), pre...  97.1 us
    ppermute x2, waiting for transfers between devices, pass_home(): return near.astype(F32) + lax.ppermute(far, ('ctx', 'mp'), home).astype(F32)  49.1 us
    unnamed x340, local copies, waits for them, and re-layouts  34.8 us
    pallas_call x2, Pallas kernels, attend_back(): pl.pallas_call(functools.partial(attend_back_kernel, len(arrays), len(giv...  28.6 us
    pallas_call x2, Pallas kernels, attend(): pl.pallas_call(functools.partial(attend_kernel, len(arrays)), grid_spec=p...  16.5 us
  transfers between devices with their start and end apart: 10, of which 2 were waited for; matrix products, arithmetic and copies ran while one was open for 12% of the time, Pallas kernels for 0%

profile of v3, /device:TPU:0, one launch (start us, length us, event | category | flops | bytes accessed | tf_op | source)
XLA Modules:
  0.0 657.2 jit_solution(9228940732169975391)
XLA Ops:
  3.7 1.5 fusion.28
  6.8 100.2 %front_gather.1 = (bf16[4,576,512]{2,1,0:T(8,128)(2,1)}, bf16[4,384,512]{2,1,0:T(8,128)(2,1)}, bf16[4,384,512]{2,1,0:T(8,128)(2,1)}, bf16[4,576,768]{2,1,0:T(8,1...) custom-call(bf16[512,768]{1,0:T(8,128)(2,1)S(1)} %fusion.21.refs_0_,, ...), custom_call_target="tpu_custom_call" | custom-call | tf_op jit(solution)/shard_map/front_gather/pallas_call | solution.py:491
  107.9 2.0 copy-done
  109.9 1.4 copy-done.3
  111.3 1.4 copy-done.6
  112.7 7.9 %attend.2 = (bf16[4,192,512]{2,1,0:T(8,128)(2,1)S(1)}, f32[4,192,512]{2,1,0:T(8,128)S(1)}, f32[4,8,512]{2,1,0:T(8,128)S(1)}) custom-call(s32[32]{0:T(128)S(1)} %pad_add_fusion.first_ref, s32[1,512]{1,0:T(1,128)S(1)} %bitcast.490, bf16[4,576,512]{2,1,0:T(8,128)(2,1)S(1)} %copy-done, bf16[4,576,512]{2,1,0:T(8,128)(2,1)S(1)} %copy-done, ...), custom_call_target="tpu_custom_call" | custom-call | tf_op jit(solution)/shard_map/attend/pallas_call | solution.py:264
  122.8 2.3 convolution_add_fusion.4
  125.2 2.6 convolution_add_fusion.5
  127.8 2.6 convolution_add_fusion.6
  139.9 38.3 %front.1 = (bf16[4,480,512]{2,1,0:T(8,128)(2,1)S(1)}, bf16[4,288,512]{2,1,0:T(8,128)(2,1)S(1)}, bf16[4,288,512]{2,1,0:T(8,128)(2,1)S(1)}) custom-call(bf16[512,768]{1,0:T(8,128)(2,1)S(1)} %add_convert_fusion.4.refs_0_, bf16[4,512,768]{2,1,0:T(8,128)(2,1)} %bitcast_dynamic-update-slice_fusion.refs_1_, f32[4,8,512]{2,1,0:T(8,128)S(1)} %maximum_convert_fusion.refs_2_), custom_call_target="tpu_custom_call" | custom-call | tf_op jit(solution)/shard_map/front/pallas_call | solution.py:491
  178.4 1.5 copy-done.1
  179.9 8.6 %attend.3 = (bf16[4,192,512]{2,1,0:T(8,128)(2,1)S(1)}, f32[4,192,512]{2,1,0:T(8,128)S(1)}, f32[4,8,512]{2,1,0:T(8,128)S(1)}) custom-call(s32[32]{0:T(128)S(1)} %pad_add_fusion.first_ref, s32[1,512]{1,0:T(1,128)S(1)} %bitcast.491, bf16[4,480,512]{2,1,0:T(8,128)(2,1)S(1)} %get-tuple-element.68.q_ref.k0, bf16[4,480,512]{2,1,0:T(8,128)(2,1)S(1)} %get-tuple-element.68.q_ref.k0, ...), custom_call_target="tpu_custom_call" | custom-call | tf_op jit(solution)/shard_map/attend/pallas_call | solution.py:264
  190.2 2.2 convolution_add_fusion.2
  192.4 2.6 convolution_add_fusion
  196.3 1.6 fusion.268
  197.8 1.6 fusion.270
  202.9 2.1 convolution_add_fusion.1
  205.0 2.7 fusion.106
  207.7 3.1 fusion.269
  214.2 2.8 fusion.249
  217.8 2.0 multiply_reduce_fusion
  227.4 2.3 fusion.2
  229.8 15.0 %attend_back.2 = (f32[4,192,512]{2,1,0:T(8,128)S(1)}, f32[4,192,512]{2,1,0:T(8,128)S(1)}, bf16[4,192,512]{2,1,0:T(8,128)(2,1)S(1)}, bf16[4,192,512]{2,1,0:T(8,12...) custom-call(s32[32]{0:T(128)S(1)} %pad_add_fusion.first_ref, ...), custom_call_target="tpu_custom_call" | custom-call | tf_op jit(solution)/shard_map/attend_back/pallas_call | solution.py:294
  251.0 3.5 fusion.98
  255.6 1.7 collective-permute-start.1
  258.6 1.7 collective-permute-start.3
  261.0 3.0 fusion.104
  266.4 3.5 add_convert_fusion.2
  270.0 30.3 %collective-permute-done.3 = bf16[4,288,512]{2,1,0:T(8,128)(2,1)} collective-permute-done((bf16[4,288,512]{2,1,0:T(8,128)(2,1)}, bf16[4,288,512]{2,1,0:T(8,128)(2,1)}, u32[]{:S(2)}, u32[]{:S(2)}) %collective-permute-start.3) | collective-permute-done | bytes 1179680 | tf_op jit(solution)/shard_map/ppermute | solution.py:518
  300.3 2.2 maximum_add_fusion.1
  305.0 2.8 fusion.80
  309.7 1.6 fusion.265
  311.4 1.6 fusion.266
  313.2 1.6 fusion.251
  314.9 1.7 fusion.267
  316.6 2.0 convolution_convert_fusion.5
  319.7 1.8 convolution_convert_fusion.8
  323.7 1.8 convolution_convert_fusion.6
  325.5 1.4 multiply_reduce_fusion.1
  331.2 13.7 %attend_back.3 = (f32[4,192,512]{2,1,0:T(8,128)S(1)}, f32[4,192,512]{2,1,0:T(8,128)S(1)}, bf16[4,192,512]{2,1,0:T(8,128)(2,1)S(1)}, bf16[4,192,512]{2,1,0:T(8,12...) custom-call(s32[32]{0:T(128)S(1)} %pad_add_fusion.first_ref, ...), custom_call_target="tpu_custom_call" | custom-call | tf_op jit(solution)/shard_map/attend_back/pallas_call | solution.py:294
  348.6 2.0 collective-permute-start.4
  350.6 1.7 convolution_convert_fusion.1
  353.6 1.5 pad_maximum_fusion.5
  358.3 2.5 pad_maximum_fusion.2
  362.7 1.6 add_convert_fusion
  364.3 1.5 collective-permute-start.6
  366.4 3.4 convolution_convert_fusion.3
  369.8 1.8 convolution_convert_fusion.10
  371.6 2.1 convolution_convert_fusion.2
  373.7 2.1 convolution_convert_fusion.9
  375.7 2.0 fusion.12
  380.0 18.8 %collective-permute-done.6 = bf16[4,384,512]{2,1,0:T(8,128)(2,1)} collective-permute-done((bf16[4,384,512]{2,1,0:T(8,128)(2,1)}, bf16[4,384,512]{2,1,0:T(8,128)(2,1)}, u32[]{:S(2)}, u32[]{:S(2)}) %collective-permute-start.6) | collective-permute-done | bytes 1572896 | tf_op jit(solution)/shard_map/ppermute | solution.py:518
  398.7 2.8 maximum_add_fusion
  402.7 2.0 convolution_convert_fusion
  406.0 1.6 pad_maximum_fusion.4
  407.6 12.4 %collective-permute-start.9 = (bf16[2,768,768]{2,1,0:T(8,128)(2,1)}, bf16[2,768,768]{2,1,0:T(8,128)(2,1)}, u32[]{:S(2)}, u32[]{:S(2)}) collective-permute-start(bf16[2,768,768]{2,1,0:T(8,128)(2,1)} %pad_maximum_fusion.4), channel_id=1, source_target_pairs={{0,1},{1,0},{2,3},{3,2},{4,5},{5,4},{6,7},{7,6},{8,9},{9,8},{10,11... | collective-permute-start | bytes 7077896 | tf_op jit(solution)/shard_map/ppermute | solution.py:30
  420.8 5.4 fusion.27
  427.2 1.5 fusion.26
  429.8 4.6 fusion
  434.5 3.6 fusion.10
  438.0 196.9 %sum_replicas.1 = (bf16[4608,768]{1,0:T(8,128)(2,1)}, f32[144,128]{1,0:T(8,128)}) custom-call(bf16[1536,768]{1,0:T(8,128)(2,1)} %get-tuple-element.158.refs_0_, bf16[768,768]{1,0:T(8,128)(2,1)} %pad.50.refs_1_, bf16[1536,768]{1,0:T(8,128)(2,1)} %get-tuple-element.157.refs_2_, bf16[768,768]{1,0:T(8,128)(2,1)} %get-tuple-element.169.refs_3_, ...), custom_call_target="tpu_custom_call" | custom-call | tf_op jit(solution)/shard_map/sum_replicas/pallas_call | solution.py:693
  636.2 2.1 slice_convert_fusion.4
  638.3 6.2 slice_convert_fusion
  645.7 1.6 convert_bitcast_fusion.2
  (520 shorter events, 87.7 us)
Async XLA Ops:
  0.7 4.7 copy-start.108
  0.7 4.8 copy-start.90
  0.7 4.8 copy-start.55
  6.0 101.1 %copy-start.18 = (bf16[512,768]{1,0:T(8,128)(2,1)}, bf16[512,768]{1,0:T(8,128)(2,1)S(1)}, u32[]{:S(2)}) copy-start(bf16[512,768]{1,0:T(8,128)(2,1)S(1)} %fusion.21.refs_0_) | copy-start | bytes 2359300
  6.8 100.4 %copy-start.110 = (bf16[2,768]{1,0:T(2,128)(2,1)S(1)}, bf16[2,768]{1,0:T(2,128)(2,1)}, u32[]{:S(2)}) copy-start(bf16[2,768]{1,0:T(2,128)(2,1)} %param.44) | copy-start | bytes 9220
  6.8 100.5 %copy-start.111 = (bf16[2,768]{1,0:T(2,128)(2,1)S(1)}, bf16[2,768]{1,0:T(2,128)(2,1)}, u32[]{:S(2)}) copy-start(bf16[2,768]{1,0:T(2,128)(2,1)} %param.33) | copy-start | bytes 9220
  6.8 100.5 %copy-start.121 = (s32[1,3]{1,0:T(1,128)S(1)}, s32[1,3]{1,0:T(1,128)}, u32[]{:S(2)}) copy-start(s32[1,3]{1,0:T(1,128)} %param.26) | copy-start | bytes 40
  6.8 100.9 %copy-start.120 = (s32[6]{0:T(128)S(1)}, s32[6]{0:T(128)}, u32[]{:S(2)}) copy-start(s32[6]{0:T(128)} %param.27) | copy-start | bytes 76
  107.0 13.6 %copy-start.35 = (bf16[4,192,768]{2,1,0:T(8,128)(2,1)}, bf16[4,192,768]{2,1,0:T(8,128)(2,1)S(1)}, u32[]{:S(2)}) copy-start(bf16[4,192,768]{2,1,0:T(8,128)(2,1)S(1)} %get-tuple-element.72) | copy-start | bytes 3538948
  107.8 12.9 %copy-start.37 = (bf16[4,192,768]{2,1,0:T(8,128)(2,1)}, bf16[4,192,768]{2,1,0:T(8,128)(2,1)S(1)}, u32[]{:S(2)}) copy-start(bf16[4,192,768]{2,1,0:T(8,128)(2,1)S(1)} %bitcast_dynamic-update-slice_fusion.2) | copy-start | bytes 3538948
  112.7 8.0 %copy-start.51 = (bf16[512,768]{1,0:T(8,128)(2,1)S(1)}, bf16[512,768]{1,0:T(8,128)(2,1)}, u32[]{:S(2)}) copy-start(bf16[512,768]{1,0:T(8,128)(2,1)} %param.24) | copy-start | bytes 2359300
  122.1 13.3 %copy-start.41 = (f32[512,768]{1,0:T(8,128)}, f32[512,768]{1,0:T(8,128)S(1)}, u32[]{:S(2)}) copy-start(f32[512,768]{1,0:T(8,128)S(1)} %get-tuple-element.217) | copy-start | bytes 4718596
  122.7 10.0 %copy-start.84 = (bf16[512,768]{1,0:T(8,128)(2,1)}, bf16[512,768]{1,0:T(8,128)(2,1)S(1)}, u32[]{:S(2)}) copy-start(bf16[512,768]{1,0:T(8,128)(2,1)S(1)} %add_convert_fusion.5) | copy-start | bytes 2359300
  122.8 7.7 %slice-start.6 = ((s8[4718592]{0:T(1024)(128)(4,1)}), s8[4194304]{0:T(1024)(128)(4,1)S(1)}, s32[]{:S(2)}) async-start(s8[4718592]{0:T(1024)(128)(4,1)} %bitcast.519), calls=%async_computation.6 | async-start | bytes 8388608
  125.1 10.3 %copy-start.60 = (f32[512,768]{1,0:T(8,128)}, f32[512,768]{1,0:T(8,128)S(1)}, u32[]{:S(2)}) copy-start(f32[512,768]{1,0:T(8,128)S(1)} %convolution_add_fusion.4) | copy-start | bytes 4718596
  125.2 5.3 slice-start.7
  139.9 38.4 %copy-start.20 = (bf16[512,768]{1,0:T(8,128)(2,1)}, bf16[512,768]{1,0:T(8,128)(2,1)S(1)}, u32[]{:S(2)}) copy-start(bf16[512,768]{1,0:T(8,128)(2,1)S(1)} %add_convert_fusion.4.refs_0_) | copy-start | bytes 2359300
  139.9 38.5 %copy-start.36 = (bf16[4,192,768]{2,1,0:T(8,128)(2,1)S(1)}, bf16[4,192,768]{2,1,0:T(8,128)(2,1)}, u32[]{:S(2)}) copy-start(bf16[4,192,768]{2,1,0:T(8,128)(2,1)} %copy-done.35) | copy-start | bytes 3538948
  139.9 38.5 %copy-start.4 = (bf16[4,384,512]{2,1,0:T(8,128)(2,1)S(1)}, bf16[4,384,512]{2,1,0:T(8,128)(2,1)}, u32[]{:S(2)}) copy-start(bf16[4,384,512]{2,1,0:T(8,128)(2,1)} %get-tuple-element.60.k1.refs_1_) | copy-start | bytes 4718596
  139.9 38.5 %copy-start.7 = (bf16[4,384,512]{2,1,0:T(8,128)(2,1)S(1)}, bf16[4,384,512]{2,1,0:T(8,128)(2,1)}, u32[]{:S(2)}) copy-start(bf16[4,384,512]{2,1,0:T(8,128)(2,1)} %get-tuple-element.61.k2.refs_2_) | copy-start | bytes 4718596
  179.9 8.6 %copy-start.44 = (f32[512,768]{1,0:T(8,128)S(1)}, f32[512,768]{1,0:T(8,128)}, u32[]{:S(2)}) copy-start(f32[512,768]{1,0:T(8,128)} %copy-done.43) | copy-start | bytes 4718596
  189.5 32.3 %copy-start.39 = (f32[512,768]{1,0:T(8,128)}, f32[512,768]{1,0:T(8,128)S(1)}, u32[]{:S(2)}) copy-start(f32[512,768]{1,0:T(8,128)S(1)} %get-tuple-element.221) | copy-start | bytes 4718596
  190.2 6.1 slice-start.2
  192.4 7.0 %copy-start.138 = (f32[512,768]{1,0:T(8,128)}, f32[512,768]{1,0:T(8,128)S(1)}, u32[]{:S(2)}) copy-start(f32[512,768]{1,0:T(8,128)S(1)} %convolution_add_fusion.2) | copy-start | bytes 4718596
  202.8 24.6 %collective-permute-start = (bf16[2,1536,768]{2,1,0:T(8,128)(2,1)S(1)}, bf16[2,1536,768]{2,1,0:T(8,128)(2,1)S(1)}, u32[]{:S(2)}, u32[]{:S(2)}) collective-permute-start(bf16[2,1536,768]{2,1,0:T(8,128)(2,1)S(1)} %pad_maximum_fusion), channel_id=1, source_target_pairs={{0,1},{1,0},{2,3},{3,2},{4,5},{5,4},{6,7},{7,6},{8,9},{9,8},{10,11... | collective-permute-start | bytes 14155784 | tf_op jit(solution)/shard_map/ppermute | solution.py:30
  205.0 6.7 %slice-start.4 = ((s8[4718592]{0:T(1024)(128)(4,1)}), s8[4194304]{0:T(1024)(128)(4,1)S(1)}, s32[]{:S(2)}) async-start(s8[4718592]{0:T(1024)(128)(4,1)} %bitcast.517), calls=%async_computation.4 | async-start | bytes 8388608
  223.1 26.2 %copy-start.48 = (f32[512,768]{1,0:T(8,128)}, f32[512,768]{1,0:T(8,128)S(1)}, u32[]{:S(2)}) copy-start(f32[512,768]{1,0:T(8,128)S(1)} %get-tuple-element.145) | copy-start | bytes 4718596
  229.7 99.3 %copy-start.9 = (bf16[1536,768]{1,0:T(8,128)(2,1)}, bf16[1536,768]{1,0:T(8,128)(2,1)S(1)}, u32[]{:S(2)}) copy-start(bf16[1536,768]{1,0:T(8,128)(2,1)S(1)} %get-tuple-element.159._.refs_4_) | copy-start | bytes 7077892
  248.4 8.8 %collective-permute-start.2 = (bf16[4,288,512]{2,1,0:T(8,128)(2,1)S(1)}, bf16[4,288,512]{2,1,0:T(8,128)(2,1)S(1)}, u32[]{:S(2)}, u32[]{:S(2)}) collective-permute-start(bf16[4,288,512]{2,1,0:T(8,128)(2,1)S(1)} %pad_maximum_fusion.8), channel_id=1, source_target_pairs={{3,2},{7,6},{11,10},{15,14},{19,18},{23,22},{27,26},{31,30}} | collective-permute-start | bytes 3538952 | tf_op jit(solution)/shard_map/ppermute | solution.py:516
  255.6 14.4 %collective-permute-start.1 = (bf16[4,288,512]{2,1,0:T(8,128)(2,1)}, bf16[4,288,512]{2,1,0:T(8,128)(2,1)}, u32[]{:S(2)}, u32[]{:S(2)}) collective-permute-start(bf16[4,288,512]{2,1,0:T(8,128)(2,1)} %pad_maximum_fusion.7), channel_id=1, source_target_pairs={{3,2},{7,6},{11,10},{15,14},{19,18},{23,22},{27,26},{31,30}} | collective-permute-start | bytes 3538952 | tf_op jit(solution)/shard_map/ppermute | solution.py:516
  258.6 41.7 %collective-permute-start.3 = (bf16[4,288,512]{2,1,0:T(8,128)(2,1)}, bf16[4,288,512]{2,1,0:T(8,128)(2,1)}, u32[]{:S(2)}, u32[]{:S(2)}) collective-permute-start(bf16[4,288,512]{2,1,0:T(8,128)(2,1)} %add_convert_fusion.1), channel_id=1, source_target_pairs={{2,1},{6,5},{4,0},{10,9},{14,13},{12,8},{18,17},{22,21},{20,16},{2... | collective-permute-start | bytes 3538952 | tf_op jit(solution)/shard_map/ppermute | solution.py:518
  269.9 30.4 %copy-start.29 = (f32[4,192,512]{2,1,0:T(8,128)S(1)}, f32[4,192,512]{2,1,0:T(8,128)}, u32[]{:S(2)}) copy-start(f32[4,192,512]{2,1,0:T(8,128)} %copy-done.28) | copy-start | bytes 4718596
  302.6 5.8 slice-start.8
  309.7 6.9 %copy-start.87 = (bf16[512,768]{1,0:T(8,128)(2,1)}, bf16[512,768]{1,0:T(8,128)(2,1)S(1)}, u32[]{:S(2)}) copy-start(bf16[512,768]{1,0:T(8,128)(2,1)S(1)} %convert_element_type.471) | copy-start | bytes 2359300
  313.2 8.4 %copy-start.124 = (bf16[512,768]{1,0:T(8,128)(2,1)}, bf16[512,768]{1,0:T(8,128)(2,1)S(1)}, u32[]{:S(2)}) copy-start(bf16[512,768]{1,0:T(8,128)(2,1)S(1)} %get-tuple-element.230) | copy-start | bytes 2359300
  313.2 5.4 slice-start
  314.9 7.5 %copy-start.122 = (bf16[512,768]{1,0:T(8,128)(2,1)}, bf16[512,768]{1,0:T(8,128)(2,1)S(1)}, u32[]{:S(2)}) copy-start(bf16[512,768]{1,0:T(8,128)(2,1)S(1)} %get-tuple-element.143) | copy-start | bytes 2359300
  327.6 33.2 %copy-start.46 = (f32[512,768]{1,0:T(8,128)}, f32[512,768]{1,0:T(8,128)S(1)}, u32[]{:S(2)}) copy-start(f32[512,768]{1,0:T(8,128)S(1)} %get-tuple-element.149) | copy-start | bytes 4718596
  347.7 15.0 %collective-permute-start.5 = (bf16[4,384,512]{2,1,0:T(8,128)(2,1)S(1)}, bf16[4,384,512]{2,1,0:T(8,128)(2,1)S(1)}, u32[]{:S(2)}, u32[]{:S(2)}) collective-permute-start(bf16[4,384,512]{2,1,0:T(8,128)(2,1)S(1)} %pad_maximum_fusion.6), channel_id=1, source_target_pairs={{3,2},{7,6},{11,10},{15,14},{19,18},{23,22},{27,26},{31,30}} | collective-permute-start | bytes 4718600 | tf_op jit(solution)/shard_map/ppermute | solution.py:516
  348.6 31.4 %collective-permute-start.4 = (bf16[4,384,512]{2,1,0:T(8,128)(2,1)S(1)}, bf16[4,384,512]{2,1,0:T(8,128)(2,1)}, u32[]{:S(2)}, u32[]{:S(2)}) collective-permute-start(bf16[4,384,512]{2,1,0:T(8,128)(2,1)S(1)} %constant_dynamic-update-slice_fusion), channel_id=1, source_target_pairs={{3,2},{7,6},{11,10},{15,14},{19,18},{23,22},{27,26},{31,30}} | collective-permute-start | bytes 4718600 | tf_op jit(solution)/shard_map/ppermute | solution.py:516
  355.1 20.7 %collective-permute-start.7 = (bf16[2,672,768]{2,1,0:T(8,128)(2,1)}, bf16[2,672,768]{2,1,0:T(8,128)(2,1)}, u32[]{:S(2)}, u32[]{:S(2)}) collective-permute-start(bf16[2,672,768]{2,1,0:T(8,128)(2,1)} %pad_maximum_fusion.5), channel_id=1, source_target_pairs={{0,1},{1,0},{2,3},{3,2},{4,5},{5,4},{6,7},{7,6},{8,9},{9,8},{10,11... | collective-permute-start | bytes 6193160 | tf_op jit(solution)/shard_map/ppermute | solution.py:30
  360.8 67.9 %collective-permute-start.8 = (bf16[2,1536,768]{2,1,0:T(8,128)(2,1)}, bf16[2,1536,768]{2,1,0:T(8,128)(2,1)}, u32[]{:S(2)}, u32[]{:S(2)}) collective-permute-start(bf16[2,1536,768]{2,1,0:T(8,128)(2,1)} %pad_maximum_fusion.2), channel_id=1, source_target_pairs={{0,1},{1,0},{2,3},{3,2},{4,5},{5,4},{6,7},{7,6},{8,9},{9,8},{10,11... | collective-permute-start | bytes 14155784 | tf_op jit(solution)/shard_map/ppermute | solution.py:30
  364.3 34.4 %collective-permute-start.6 = (bf16[4,384,512]{2,1,0:T(8,128)(2,1)}, bf16[4,384,512]{2,1,0:T(8,128)(2,1)}, u32[]{:S(2)}, u32[]{:S(2)}) collective-permute-start(bf16[4,384,512]{2,1,0:T(8,128)(2,1)} %add_convert_fusion), channel_id=1, source_target_pairs={{2,1},{6,5},{4,0},{10,9},{14,13},{12,8},{18,17},{22,21},{20,16},{2... | collective-permute-start | bytes 4718600 | tf_op jit(solution)/shard_map/ppermute | solution.py:518
  377.8 20.9 %copy-start.27 = (f32[4,192,512]{2,1,0:T(8,128)S(1)}, f32[4,192,512]{2,1,0:T(8,128)}, u32[]{:S(2)}) copy-start(f32[4,192,512]{2,1,0:T(8,128)} %copy-done.26) | copy-start | bytes 4718596
  378.9 19.8 %copy-start.25 = (f32[4,192,512]{2,1,0:T(8,128)S(1)}, f32[4,192,512]{2,1,0:T(8,128)}, u32[]{:S(2)}) copy-start(f32[4,192,512]{2,1,0:T(8,128)} %copy-done.24) | copy-start | bytes 4718596
  407.6 13.0 %copy-start.52 = (bf16[512,768]{1,0:T(8,128)(2,1)S(1)}, bf16[512,768]{1,0:T(8,128)(2,1)}, u32[]{:S(2)}) copy-start(bf16[512,768]{1,0:T(8,128)(2,1)} %param.24) | copy-start | bytes 2359300
  407.6 13.0 %copy-start.95 = (f32[768]{0:T(1024)S(1)}, f32[768]{0:T(1024)}, u32[]{:S(2)}) copy-start(f32[768]{0:T(1024)} %copy-done.94) | copy-start | bytes 9220
  407.6 13.0 %copy-start.97 = (f32[512]{0:T(512)S(1)}, f32[512]{0:T(512)}, u32[]{:S(2)}) copy-start(f32[512]{0:T(512)} %copy-done.96) | copy-start | bytes 6148
  407.6 13.0 %copy-start.99 = (f32[512]{0:T(512)S(1)}, f32[512]{0:T(512)}, u32[]{:S(2)}) copy-start(f32[512]{0:T(512)} %copy-done.98) | copy-start | bytes 6148
  407.6 26.8 %collective-permute-start.9 = (bf16[2,768,768]{2,1,0:T(8,128)(2,1)}, bf16[2,768,768]{2,1,0:T(8,128)(2,1)}, u32[]{:S(2)}, u32[]{:S(2)}) collective-permute-start(bf16[2,768,768]{2,1,0:T(8,128)(2,1)} %pad_maximum_fusion.4), channel_id=1, source_target_pairs={{0,1},{1,0},{2,3},{3,2},{4,5},{5,4},{6,7},{7,6},{8,9},{9,8},{10,11... | collective-permute-start | bytes 7077896 | tf_op jit(solution)/shard_map/ppermute | solution.py:30
  420.7 5.5 copy-start.93
  420.7 5.6 copy-start.114
  420.7 5.6 copy-start.101
  420.7 5.6 copy-start.100
  420.7 5.6 copy-start.103
  420.7 5.6 copy-start.102
  420.7 5.7 copy-start.107
  420.7 5.8 copy-start.106
  420.7 5.8 copy-start.105
  420.8 5.8 copy-start.104
  420.8 6.4 copy-start.47
  428.7 5.7 copy-start.67
  428.7 5.7 copy-start.68
  638.3 6.2 copy-start.92
  (97 other events, 202.1 us)

commit v4 on v3

--- a/solution.py
+++ b/solution.py
@@ -15,8 +15,6 @@
 GROUP = 3
 BAND = GROUP * HD
 AT_REUSE = 2
-AT_FLAG = AT_REUSE + REUSE
-AT_GIVEN = AT_FLAG + 4 * GROUP
 TILE = 256
 TILES = 3 * WIN // TILE
 EPS = 1e-05
@@ -156,71 +154,6 @@
             sum_ref[0, j : j + 1, cols] = top[j, 0:1] + jnp.log(whole)
 
 
-def attend_back_kernel(n_values, n_given, first_ref, lo_ref, _, q_ref, k0, k1, k2, *refs):
-    v_refs, refs = refs[:n_values], refs[n_values:]
-    given, refs = refs[:n_given], refs[n_given:]
-    (
-        out_ref, grad_ref, sum_ref, dq_ref, dk0, dk1, dk2, dv0, dv1, dv2,
-        values, acc_k, acc_v, acc_q,
-    ) = refs
-    keys = (k2, k1, k0)
-    place_values(v_refs, values)
-    acc_k[...] = jnp.zeros_like(acc_k)
-    acc_v[...] = jnp.zeros_like(acc_v)
-    for i, ref in enumerate(given):
-        part, j = 2 - i // GROUP, i % GROUP
-        head = GROUP * pl.program_id(0) + j
-
-        def add(part=part, j=j, ref=ref):
-            for half in range(2):
-                span = slice(half * TILE, (half + 1) * TILE)
-                acc_v[2 * part + half, j * HD : (j + 1) * HD, :] = ref[0, :, span].astype(F32)
-
-        pl.when(first_ref[AT_FLAG + head] == 1)(add)
-    for t in range(WIN // TILE):
-        cols = slice(t * TILE, (t + 1) * TILE)
-        low = lo_ref[:, cols]
-        place = 2 * WIN + t * TILE + lax.broadcasted_iota(jnp.int32, (1, TILE), 1)
-        last = 2 * WIN // TILE + t
-
-        def tile(kt):
-            spot = kt * TILE + lax.broadcasted_iota(jnp.int32, (TILE, TILE), 0)
-            keep = spot >= low
-            if kt == last:
-                keep = keep & (spot <= place)
-            span = slice(kt % 2 * TILE, (kt % 2 + 1) * TILE)
-            for j in range(GROUP):
-                rows = slice(j * HD, (j + 1) * HD)
-                key = keys[kt // 2][0, rows, span]
-                query = q_ref[0, rows, cols] * SCALE
-                grad = grad_ref[0, rows, cols]
-                inner = jnp.sum(
-                    grad.astype(F32) * out_ref[0, rows, cols], axis=0, keepdims=True
-                )
-                raw = jnp.where(keep, dot(key, query, 0, 0), -jnp.inf)
-                weights = jnp.exp(raw - sum_ref[0, j : j + 1, cols])
-                grad_weights = dot(values[kt // 2, rows, span], grad, 0, 0)
-                low_grad = (weights * (grad_weights - inner)).astype(BF16)
-                acc_v[kt, rows, :] += dot(grad, weights.astype(BF16), 1, 1)
-                acc_k[kt, rows, :] += dot(query, low_grad, 1, 1)
-                result = dot(key, low_grad, 1, 0)
-                if kt != last:
-                    result = result + acc_q[j]
-                acc_q[j] = result
-
-        tile(last)
-        for kt in reversed(range(last)):
-            pl.when(kt >= first_ref[t])(functools.partial(tile, kt))
-        for j in range(GROUP):
-            rows = slice(j * HD, (j + 1) * HD)
-            dq_ref[0, rows, cols] = acc_q[j] * SCALE
-    for part, (dk, dv) in enumerate(((dk2, dv2), (dk1, dv1), (dk0, dv0))):
-        for half in range(2):
-            span = slice(half * TILE, (half + 1) * TILE)
-            dk[0, :, span] = acc_k[2 * part + half].astype(dk.dtype)
-            dv[0, :, span] = acc_v[2 * part + half].astype(dv.dtype)
-
-
 def band(place):
     return pl.BlockSpec((1, BAND, WIN), lambda s, *_: (s, place, 0))
 
@@ -235,12 +168,6 @@
         return (head // GROUP * stride + offset + head % GROUP, 0, 0)
 
     return pl.BlockSpec((1, HD, WIN), at)
-
-
-def given_block(j):
-    return pl.BlockSpec(
-        (1, HD, WIN), lambda s, scalars: (scalars[AT_GIVEN + GROUP * s + j], 0, 0)
-    )
 
 
 FRESH = pl.BlockSpec((1, BAND, WIN), lambda s, *_: (jnp.maximum(s - 2, 0), 0, 0))
@@ -286,33 +213,6 @@
     )(scalars, low, front[0], *front, *arrays)
 
 
-def attend_back(after, scalars, low, front, values, given, heads, grad_heads, sums):
-    kinds = (F32, F32, BF16, BF16, F32, BF16, BF16)
-    arrays, specs = values
-    given_arrays = [v.reshape(-1, HD, WIN) for v in given for _ in range(GROUP)]
-    given_specs = [given_block(j) for _ in given for j in range(GROUP)]
-    return pl.pallas_call(
-        functools.partial(attend_back_kernel, len(arrays), len(given_arrays)),
-        grid_spec=pltpu.PrefetchScalarGridSpec(
-            num_scalar_prefetch=1,
-            grid=(4,),
-            in_specs=[LOW, pl.BlockSpec(memory_space=pl.ANY)]
-            + [band(0), band(1), band(0), band(0)] + specs + given_specs
-            + [band(0), band(0), SUMS],
-            out_specs=[band(0)] * 7,
-            scratch_shapes=[
-                pltpu.VMEM((3, BAND, WIN), BF16),
-                pltpu.VMEM((TILES, BAND, TILE), F32),
-                pltpu.VMEM((TILES, BAND, TILE), F32),
-                pltpu.VMEM((GROUP, HD, TILE), F32),
-            ],
-        ),
-        out_shape=[jax.ShapeDtypeStruct((4, BAND, WIN), kind) for kind in kinds],
-        compiler_params=pltpu.CompilerParams(vmem_limit_bytes=32 * 1024 * 1024),
-        name="attend_back",
-    )(scalars, low, after, front[0], *front, *arrays, *given_arrays, heads, grad_heads, sums)
-
-
 def front_kernel(n_more, *refs):
     refs = list(refs)
 
@@ -503,21 +403,6 @@
     )(normed, *fixed, *more)
 
 
-def routes():
-    windows, groups = lax.axis_size("ctx"), lax.axis_size("mp")
-    first_home = [(c * groups + 3, c * groups + 2) for c in range(windows)]
-    home = [(c * groups + 2, c * groups + 1) for c in range(windows)]
-    home += [((c + 1) * groups, c * groups) for c in range(windows - 1)]
-    return first_home, home
-
-
-def pass_home(before, earlier):
-    first_home, home = routes()
-    near, far = lax.ppermute((before, earlier), ("ctx", "mp"), first_home)
-    far = (before.astype(F32) + far.astype(F32)).astype(BF16)
-    return near.astype(F32) + lax.ppermute(far, ("ctx", "mp"), home).astype(F32)
-
-
 def row_starts(lengths):
     part = lax.axis_index("mp")
     place = (part - 1) * WIN + jnp.arange(WIN, dtype=jnp.int32)
@@ -538,187 +423,438 @@
     )
 
 
-def sum_kernel(counts, rows, *refs):
-    refs = list(refs)
-
-    def take(count):
-        taken = refs[:count]
-        del refs[:count]
-        return taken
-
-    owns, fars = take(len(counts)), take(len(counts))
-    vec_in, out, vec, from_y, mine, from_x, kept, from_z, from_vec = take(9)
-    y_out, y_in, x_out, x_in, z_out, z_in, g_out, g_in, h_out, h_in, v_out, v_in = refs
-    parts = sum(counts)
-    firsts = [sum(counts[:k]) for k in range(len(counts))]
-    ctx, dp, mp = (lax.axis_index(axis) for axis in ("ctx", "dp", "mp"))
-    half = rows // 2
-    bits = [1 << k for k in range((lax.axis_size("dp") - 1).bit_length())]
-    highs = [(dp // bit) % 2 for bit in bits]
-    other_chip, other_window = {"mp": flip(mp, 2)}, {"ctx": 1 - ctx}
-    beside = [{"dp": flip(dp, bit)} for bit in bits]
-    partners = [other_chip, other_window, {"mp": flip(mp, 1)}] + beside
-
-    def ds(start, size):
-        return pl.ds(pl.multiple_of(start, 16), size)
-
-    def segment(i, k, sent=False):
-        start, size = 0, half
-        for high in highs[:k]:
-            size //= 2
-            start = start + high * size
-        if sent:
-            size //= 2
-            start = start + (1 - highs[k]) * size
-        return start, size
-
-    def to_y(array, i):
-        here = ds((firsts[array] + i) * rows, rows)
-        source = fars[array].at[ds(i * rows, rows)]
-        place = firsts[array] + i
-        return remote(source, from_y.at[here], y_out.at[place], y_in.at[place], other_chip)
-
-    def to_x(i):
-        source = mine.at[ds(i * rows + (1 - ctx) * half, half)]
-        target = from_x.at[ds(i * half, half)]
-        return remote(source, target, x_out.at[i], x_in.at[i], other_window)
-
-    def to_z(i, k):
-        start, size = segment(i, k, True)
-        target = from_z.at[ds(i * half + half - 2 * size, size)]
-        source = kept.at[ds(i * half + start, size)]
-        return remote(source, target, z_out.at[i, k], z_in.at[i, k], beside[k])
-
-    def back_z(i, k):
-        start, size = segment(i, k + 1)
-        here = out.at[ds(i * rows + ctx * half + start, size)]
-        return remote(here, here, g_out.at[i, k], g_in.at[i, k], beside[k])
-
-    def back_x(i):
-        here = out.at[ds(i * rows + ctx * half, half)]
-        return remote(here, here, h_out.at[i], h_in.at[i], other_window)
-
-    def each(count, step):
-        lax.fori_loop(0, count, lambda i, _: (step(i), 0)[1], 0)
-
-    meet(partners)
-    vec[...] = vec_in[...]
-    for hop, partner in enumerate(partners):
-        copy = remote(vec, from_vec.at[hop], v_out.at[hop], v_in.at[hop], partner)
-        copy.start()
-        if hop == 0:
-            for array, count in enumerate(counts):
-                each(count, lambda i, array=array: to_y(array, i).start())
-        copy.wait()
-        vec[...] = vec[...] + from_vec[hop]
-
-    def join(i):
-        here = ds(i * rows, rows)
-        for array, count in enumerate(counts):
-
-            def add(array=array):
-                to_y(array, i - firsts[array]).wait_recv()
-                term = owns[array][ds((i - firsts[array]) * rows, rows), :]
-                mine[here, :] = (term.astype(F32) + from_y[here, :].astype(F32)).astype(BF16)
-
-            pl.when((i >= firsts[array]) & (i < firsts[array] + count))(add)
-        to_x(i).start()
-
-    def spread(i):
-        to_x(i).wait_recv()
-        there = ds(i * half, half)
-        total = mine[ds(i * rows + ctx * half, half), :].astype(F32) + from_x[there, :].astype(F32)
-        kept[there, :] = total.astype(BF16)
-        to_z(i, 0).start()
-
-    def narrow(k, i):
-        to_z(i, k).wait_recv()
-        start, size = segment(i, k + 1)
-        here = ds(i * half + start, size)
-        there = ds(i * half + half - 2 * size, size)
-        total = (kept[here, :].astype(F32) + from_z[there, :].astype(F32)).astype(BF16)
-        if k + 1 < len(bits):
-            kept[here, :] = total
-            to_z(i, k + 1).start()
-        else:
-            out[ds(i * rows + ctx * half + start, size), :] = total
-            back_z(i, k).start()
-
-    def widen(k, i):
-        back_z(i, k).wait_recv()
-        if k:
-            back_z(i, k - 1).start()
-        else:
-            back_x(i).start()
-
-    stages = [join, spread]
-    stages += [functools.partial(narrow, k) for k in range(len(bits))]
-    stages += [functools.partial(widen, k) for k in reversed(range(len(bits)))]
-
-    def step(i):
-        for late, stage in enumerate(stages):
-            pl.when((i >= late) & (i < parts + late))(functools.partial(stage, i - late))
-
-    each(parts + len(stages) - 1, step)
-    for array, count in enumerate(counts):
-        each(count, lambda i, array=array: to_y(array, i).wait_send())
-
-    def finish(i):
-        to_x(i).wait_send()
-        back_x(i).wait()
-        for k in range(len(bits)):
-            to_z(i, k).wait_send()
-            back_z(i, k).wait_send()
-
-    each(parts, finish)
-
-
-def rows_of_part():
-    return max(256, 32 * lax.axis_size("dp"))
-
-
-def sum_replicas(pairs, vectors):
-    rows = rows_of_part()
-    bits = (lax.axis_size("dp") - 1).bit_length()
-    hops = 3 + bits
-    lanes = pairs[0][0].shape[1]
-    owns, fars = (
-        [jnp.pad(v, ((0, -v.shape[0] % rows), (0, 0))) for v in half] for half in zip(*pairs)
-    )
-    counts = [v.shape[0] // rows for v in owns]
-    parts = sum(counts)
-    total = parts * rows
-    place = pl.BlockSpec(memory_space=pltpu.VMEM)
-    dma = pltpu.SemaphoreType.DMA
-    return pl.pallas_call(
-        functools.partial(sum_kernel, counts, rows),
-        out_shape=[
-            jax.ShapeDtypeStruct((total, lanes), BF16),
-            jax.ShapeDtypeStruct(vectors.shape, F32),
-        ],
-        in_specs=[place] * len(counts)
-        + [pl.BlockSpec(memory_space=pl.ANY)] * len(counts)
-        + [place],
-        out_specs=[place, place],
-        scratch_shapes=[
+class Sums:
+    def __init__(self, counts, rows, owns, fars, out, refs):
+        self.counts, self.rows, self.owns, self.fars, self.out = counts, rows, owns, fars, out
+        self.from_y, self.mine, self.from_x, self.kept, self.from_z = refs[:5]
+        self.sems = refs[5:]
+        self.parts = sum(counts)
+        self.firsts = [sum(counts[:k]) for k in range(len(counts))]
+        self.ctx, self.dp, mp = (lax.axis_index(axis) for axis in ("ctx", "dp", "mp"))
+        self.half = rows // 2
+        self.bits = [1 << k for k in range((lax.axis_size("dp") - 1).bit_length())]
+        self.highs = [(self.dp // bit) % 2 for bit in self.bits]
+        self.other_chip, self.other_window = {"mp": flip(mp, 2)}, {"ctx": 1 - self.ctx}
+        self.beside = [{"dp": flip(self.dp, bit)} for bit in self.bits]
+        self.partners = [self.other_chip, self.other_window, {"mp": flip(mp, 1)}] + self.beside
+        self.stages = [self.join, self.spread]
+        self.stages += [functools.partial(self.narrow, k) for k in range(len(self.bits))]
+        self.stages += [functools.partial(self.widen, k) for k in reversed(range(len(self.bits)))]
+        self.steps = self.parts + len(self.stages) - 1
+
+    @staticmethod
+    def scratch(total, parts, bits, lanes):
+        dma = pltpu.SemaphoreType.DMA
+        return [
             pltpu.VMEM((total, lanes), BF16),
             pltpu.VMEM((total, lanes), BF16),
             pltpu.VMEM((total // 2, lanes), BF16),
             pltpu.VMEM((total // 2, lanes), BF16),
             pltpu.VMEM((total // 2, lanes), BF16),
-            pltpu.VMEM((hops,) + vectors.shape, F32),
             dma((parts,)), dma((parts,)),
             dma((parts,)), dma((parts,)),
             dma((parts, bits)), dma((parts, bits)),
             dma((parts, bits)), dma((parts, bits)),
             dma((parts,)), dma((parts,)),
-            dma((hops,)), dma((hops,)),
-        ],
+        ]
+
+    def segment(self, k, sent=False):
+        start, size = 0, self.half
+        for high in self.highs[:k]:
+            size //= 2
+            start = start + high * size
+        if sent:
+            size //= 2
+            start = start + (1 - self.highs[k]) * size
+        return start, size
+
+    def to_y(self, array, i):
+        place = self.firsts[array] + i
+        source = self.fars[array].at[ds(i * self.rows, self.rows)]
+        target = self.from_y.at[ds(place * self.rows, self.rows)]
+        return remote(
+            source, target, self.sems[0].at[place], self.sems[1].at[place], self.other_chip
+        )
+
+    def to_x(self, i):
+        source = self.mine.at[ds(i * self.rows + (1 - self.ctx) * self.half, self.half)]
+        target = self.from_x.at[ds(i * self.half, self.half)]
+        return remote(source, target, self.sems[2].at[i], self.sems[3].at[i], self.other_window)
+
+    def to_z(self, i, k):
+        start, size = self.segment(k, True)
+        source = self.kept.at[ds(i * self.half + start, size)]
+        target = self.from_z.at[ds(i * self.half + self.half - 2 * size, size)]
+        return remote(source, target, self.sems[4].at[i, k], self.sems[5].at[i, k], self.beside[k])
+
+    def back_z(self, i, k):
+        start, size = self.segment(k + 1)
+        here = self.out.at[ds(i * self.rows + self.ctx * self.half + start, size)]
+        return remote(here, here, self.sems[6].at[i, k], self.sems[7].at[i, k], self.beside[k])
+
+    def back_x(self, i):
+        here = self.out.at[ds(i * self.rows + self.ctx * self.half, self.half)]
+        return remote(here, here, self.sems[8].at[i], self.sems[9].at[i], self.other_window)
+
+    def start(self):
+        for array, count in enumerate(self.counts):
+            each(count, lambda i, array=array: self.to_y(array, i).start())
+
+    def join(self, i):
+        here = ds(i * self.rows, self.rows)
+        for array, count in enumerate(self.counts):
+            first = self.firsts[array]
+
+            def add(array=array, first=first):
+                self.to_y(array, i - first).wait_recv()
+                term = self.owns[array][ds((i - first) * self.rows, self.rows), :]
+                total = term.astype(F32) + self.from_y[here, :].astype(F32)
+                self.mine[here, :] = total.astype(BF16)
+
+            pl.when((i >= first) & (i < first + count))(add)
+        self.to_x(i).start()
+
+    def spread(self, i):
+        self.to_x(i).wait_recv()
+        there = ds(i * self.half, self.half)
+        term = self.mine[ds(i * self.rows + self.ctx * self.half, self.half), :]
+        total = term.astype(F32) + self.from_x[there, :].astype(F32)
+        self.kept[there, :] = total.astype(BF16)
+        self.to_z(i, 0).start()
+
+    def narrow(self, k, i):
+        self.to_z(i, k).wait_recv()
+        start, size = self.segment(k + 1)
+        here = ds(i * self.half + start, size)
+        there = ds(i * self.half + self.half - 2 * size, size)
+        total = self.kept[here, :].astype(F32) + self.from_z[there, :].astype(F32)
+        if k + 1 < len(self.bits):
+            self.kept[here, :] = total.astype(BF16)
+            self.to_z(i, k + 1).start()
+        else:
+            place = ds(i * self.rows + self.ctx * self.half + start, size)
+            self.out[place, :] = total.astype(BF16)
+            self.back_z(i, k).start()
+
+    def widen(self, k, i):
+        self.back_z(i, k).wait_recv()
+        if k:
+            self.back_z(i, k - 1).start()
+        else:
+            self.back_x(i).start()
+
+    def step(self, i):
+        for late, stage in enumerate(self.stages):
+            pl.when((i >= late) & (i < self.parts + late))(functools.partial(stage, i - late))
+
+    def finish(self):
+        for array, count in enumerate(self.counts):
+            each(count, lambda i, array=array: self.to_y(array, i).wait_send())
+
+        def end(i):
+            self.to_x(i).wait_send()
+            self.back_x(i).wait()
+            for k in range(len(self.bits)):
+                self.to_z(i, k).wait_send()
+                self.back_z(i, k).wait_send()
+
+        each(self.parts, end)
+
+
+def ds(start, size):
+    return pl.ds(pl.multiple_of(start, 16), size)
+
+
+def each(count, step):
+    lax.fori_loop(0, count, lambda i, _: (step(i), 0)[1], 0)
+
+
+def sum_kernel(counts, n_vectors, rows, *refs):
+    n = len(counts)
+    owns, fars, terms = refs[:n], refs[n : 2 * n], refs[2 * n : 2 * n + n_vectors]
+    refs = refs[2 * n + n_vectors :]
+    out, vec = refs[:2]
+    from_vec, v_out, v_in = refs[-3:]
+    sums = Sums(counts, rows, owns, fars, out, refs[2:-3])
+    meet(sums.partners)
+    at = 0
+    for term in terms:
+        vec[at : at + term.shape[0], : term.shape[1]] = term[...]
+        at += term.shape[0]
+    for hop, partner in enumerate(sums.partners):
+        copy = remote(vec, from_vec.at[hop], v_out.at[hop], v_in.at[hop], partner)
+        copy.start()
+        if hop == 0:
+            sums.start()
+        copy.wait()
+        vec[...] = vec[...] + from_vec[hop]
+    each(sums.steps, sums.step)
+    sums.finish()
+
+
+def rows_of_part():
+    return max(256, 32 * lax.axis_size("dp"))
+
+
+def padded(pairs):
+    rows = rows_of_part()
+    owns, fars = (
+        [jnp.pad(v, ((0, -v.shape[0] % rows), (0, 0))) for v in half] for half in zip(*pairs)
+    )
+    counts = [v.shape[0] // rows for v in owns]
+    bits = (lax.axis_size("dp") - 1).bit_length()
+    total = sum(counts) * rows
+    shape = jax.ShapeDtypeStruct((total, owns[0].shape[1]), BF16)
+    return owns, fars, counts, bits, shape, Sums.scratch(total, sum(counts), bits, shape.shape[1])
+
+
+def unpadded(stack, pairs):
+    shares, at = [], 0
+    for own, _ in pairs:
+        shares.append(stack[at : at + own.shape[0]])
+        at += own.shape[0] + -own.shape[0] % rows_of_part()
+    return shares
+
+
+def sum_replicas(pairs, vectors):
+    owns, fars, counts, bits, shape, scratch = padded(pairs)
+    place = pl.BlockSpec(memory_space=pltpu.VMEM)
+    away = pl.BlockSpec(memory_space=pl.ANY)
+    dma = pltpu.SemaphoreType.DMA
+    rows = sum(v.shape[0] for v in vectors)
+    stack, summed = pl.pallas_call(
+        functools.partial(sum_kernel, counts, len(vectors), rows_of_part()),
+        out_shape=[shape, jax.ShapeDtypeStruct((rows, D), F32)],
+        in_specs=[place] * len(counts) + [away] * len(counts) + [place] * len(vectors),
+        out_specs=[place, place],
+        scratch_shapes=scratch
+        + [pltpu.VMEM((3 + bits, rows, D), F32), dma((3 + bits,)), dma((3 + bits,))],
         compiler_params=pltpu.CompilerParams(
             collective_id=0, has_side_effects=True, vmem_limit_bytes=56 * 1024 * 1024
         ),
         name="sum_replicas",
-    )(*owns, *fars, vectors)
+    )(*owns, *fars, *vectors)
+    return unpadded(stack, pairs), summed
+
+
+def back_kernel(mixed, counts, rows, *refs):
+    refs = list(refs)
+
+    def take(count):
+        taken = refs[:count]
+        del refs[:count]
+        return taken
+
+    places, flags, lo_ref, cols, before, earlier = take(6)
+    first_values, fresh = (take(3), take(3)) if mixed else ((), ())
+    given = () if mixed else take(3)
+    exact, grad_ref, sum_ref = take(3)
+    owns, fars = take(len(counts)), take(len(counts))
+    dq_ref, dk_ref, dv_ref = take(3)
+    if mixed:
+        dv_before, dv_earlier = take(2)
+    (out,) = take(1)
+    if not mixed:
+        dv_before, dv_earlier = take(2)
+    dk_before, dk_earlier = take(2)
+    near_k, near_v, far_k, far_v, home_k, home_v = take(6)
+    values, acc_k, acc_v, acc_q = take(4)
+    kv_out, kv_in = take(2)
+    sums = Sums(counts, rows, owns, fars, out, refs)
+
+    ctx, mp = lax.axis_index("ctx"), lax.axis_index("mp")
+    sees_one = (mp >= 2) | ((mp == 0) & (ctx == 1))
+    sees_two = mp == 3
+    meet(sums.partners + [{"mp": 3 - mp}])
+    sums.start()
+    keys = ((earlier, 0), (before, 0), (cols, BAND))
+
+    def home(which, source, target, g, device):
+        return remote(
+            source.at[g], target.at[g], kv_out.at[which, g], kv_in.at[which, g], device
+        )
+
+    def pair(g, act, step):
+        act(step)
+        if mixed:
+            pl.when(g >= 2)(lambda: act(step + 1))
+        else:
+            act(step + 1)
+
+    def from_last(g, step):
+        source, target = (
+            (dk_before, near_k), (dv_before, near_v), (dk_earlier, far_k), (dv_earlier, far_v),
+        )[step]
+        return home(step, source, target, g, {"mp": 2})
+
+    def from_next(g, step, device):
+        source, target = ((dk_before, home_k), (dv_before, home_v))[step]
+        return home(4 + step, source, target, g, device)
+
+    def group(g, _):
+        if mixed:
+
+            def reused():
+                for part in range(3):
+                    for j in range(GROUP):
+                        at = places[(0 if part == 2 else REUSE) + GROUP * g + j]
+                        values[part, j * HD : (j + 1) * HD, :] = first_values[part][at]
+
+            def own():
+                for part in range(3):
+                    values[part] = fresh[part][g - 2]
+
+            pl.when(g < 2)(reused)
+            pl.when(g >= 2)(own)
+        else:
+            for part, (ref, at) in enumerate(keys):
+                values[part] = ref[g, at + BAND : at + 2 * BAND, :]
+        acc_k[...] = jnp.zeros_like(acc_k)
+        if mixed:
+            acc_v[...] = jnp.zeros_like(acc_v)
+        else:
+            for part in range(3):
+                for j in range(GROUP):
+                    head = GROUP * g + j
+                    term = given[part][places[head]].astype(F32) * flags[head]
+                    for side in range(2):
+                        acc_v[2 * part + side, j * HD : (j + 1) * HD, :] = term[
+                            :, side * TILE : (side + 1) * TILE
+                        ]
+        for t in range(WIN // TILE):
+            tokens = slice(t * TILE, (t + 1) * TILE)
+            low = lo_ref[:, tokens]
+            place = 2 * WIN + t * TILE + lax.broadcasted_iota(jnp.int32, (1, TILE), 1)
+            last = 2 * WIN // TILE + t
+
+            def tile(kt, tokens=tokens, low=low, place=place, last=last):
+                spot = kt * TILE + lax.broadcasted_iota(jnp.int32, (TILE, TILE), 0)
+                keep = spot >= low
+                if kt == last:
+                    keep = keep & (spot <= place)
+                span = slice(kt % 2 * TILE, (kt % 2 + 1) * TILE)
+                key_ref, at = keys[kt // 2]
+                for j in range(GROUP):
+                    rows_j = slice(j * HD, (j + 1) * HD)
+                    key = key_ref[g, at + j * HD : at + (j + 1) * HD, span]
+                    query = cols[g, rows_j, tokens] * SCALE
+                    grad = grad_ref[g, rows_j, tokens]
+                    inner = jnp.sum(
+                        grad.astype(F32) * exact[g, rows_j, tokens], axis=0, keepdims=True
+                    )
+                    raw = jnp.where(keep, dot(key, query, 0, 0), -jnp.inf)
+                    weights = jnp.exp(raw - sum_ref[g, j : j + 1, tokens])
+                    grad_weights = dot(values[kt // 2, rows_j, span], grad, 0, 0)
+                    low_grad = (weights * (grad_weights - inner)).astype(BF16)
+                    acc_v[kt, rows_j, :] += dot(grad, weights.astype(BF16), 1, 1)
+                    acc_k[kt, rows_j, :] += dot(query, low_grad, 1, 1)
+                    result = dot(key, low_grad, 1, 0)
+                    acc_q[j] = result if kt == last else result + acc_q[j]
+
+            for kt in reversed(range(last + 1)):
+                if kt >= 4:
+                    tile(kt)
+                else:
+                    pl.when(sees_one if kt >= 2 else sees_two)(functools.partial(tile, kt))
+            for j in range(GROUP):
+                dq_ref[g, j * HD : (j + 1) * HD, tokens] = acc_q[j] * SCALE
+            sums.step(2 * g + t)
+        results = ((dk_earlier, dv_earlier), (dk_before, dv_before), (dk_ref, dv_ref))
+        for part, (dk, dv) in enumerate(results):
+            for side in range(2):
+                span = slice(side * TILE, (side + 1) * TILE)
+                dk[g, :, span] = acc_k[2 * part + side].astype(dk.dtype)
+                dv[g, :, span] = acc_v[2 * part + side].astype(dv.dtype)
+
+        def send_last():
+            pair(g, lambda step: from_last(g, step).start(), 0)
+            pair(g, lambda step: from_last(g, step).start(), 2)
+
+        pl.when(mp == 3)(send_last)
+        pl.when((mp == 0) & (ctx == 1))(
+            lambda: pair(g, lambda step: from_next(g, step, sums.other_window).start(), 0)
+        )
+        return 0
+
+    lax.fori_loop(0, 4, group, 0)
+
+    def relay(g):
+        def one(step):
+            near, far, source, total = (
+                (near_k, far_k, dk_before, dk_ref), (near_v, far_v, dv_before, dv_ref),
+            )[step]
+            from_last(g, step).wait_recv()
+            from_last(g, step + 2).wait_recv()
+            source[g] = (source[g].astype(F32) + far[g].astype(F32)).astype(BF16)
+            from_next(g, step, {"mp": 1}).start()
+            total[g] += near[g].astype(F32)
+
+        pair(g, one, 0)
+
+    pl.when(mp == 2)(lambda: each(4, relay))
+    for i in range(8, sums.steps):
+        sums.step(i)
+
+    def arrive(g):
+        def one(step):
+            arrived, total = ((home_k, dk_ref), (home_v, dv_ref))[step]
+            from_next(g, step, sums.other_window).wait_recv()
+            total[g] += arrived[g].astype(F32)
+
+        pair(g, one, 0)
+
+    pl.when((mp == 1) | ((mp == 0) & (ctx == 0)))(lambda: each(4, arrive))
+
+    def sent_last(g):
+        pair(g, lambda step: from_last(g, step).wait_send(), 0)
+        pair(g, lambda step: from_last(g, step).wait_send(), 2)
+
+    def sent_next(device):
+        each(4, lambda g: pair(g, lambda step: from_next(g, step, device).wait_send(), 0))
+
+    pl.when(mp == 3)(lambda: each(4, sent_last))
+    pl.when(mp == 2)(lambda: sent_next({"mp": 1}))
+    pl.when((mp == 0) & (ctx == 1))(lambda: sent_next(sums.other_window))
+    sums.finish()
+
+
+def attend_back(places, flags, low, front, firsts, freshes, given, exact, grad_heads, lse, pairs):
+    mixed = bool(firsts)
+    owns, fars, counts, bits, shape, scratch = padded(pairs)
+    place = pl.BlockSpec(memory_space=pltpu.VMEM)
+    away = pl.BlockSpec(memory_space=pl.ANY)
+    scalar = pl.BlockSpec(memory_space=pltpu.SMEM)
+    dma = pltpu.SemaphoreType.DMA
+    by_head = [v.reshape(-1, HD, WIN) for v in firsts[::-1]] + list(freshes[::-1])
+    by_head += [v.reshape(-1, HD, WIN) for v in given[::-1]]
+    local = [low, *front, *by_head, exact, grad_heads, lse, *owns]
+    wide = jax.ShapeDtypeStruct((4, BAND, WIN), F32)
+    slim = jax.ShapeDtypeStruct((4, BAND, WIN), BF16)
+    outs = [wide] * 3 + ([slim] * 2 if mixed else []) + [shape]
+    block = pltpu.VMEM((4, BAND, WIN), BF16)
+    results = pl.pallas_call(
+        functools.partial(back_kernel, mixed, counts, rows_of_part()),
+        out_shape=outs,
+        in_specs=[scalar, scalar] + [place] * len(local) + [away] * len(fars),
+        out_specs=[place] * len(outs),
+        scratch_shapes=[block] * (8 if mixed else 10)
+        + [
+            pltpu.VMEM((3, BAND, WIN), BF16),
+            pltpu.VMEM((TILES, BAND, TILE), F32),
+            pltpu.VMEM((TILES, BAND, TILE), F32),
+            pltpu.VMEM((GROUP, HD, TILE), F32),
+            dma((6, 4)),
+            dma((6, 4)),
+        ]
+        + scratch,
+        compiler_params=pltpu.CompilerParams(
+            collective_id=3 if mixed else 4,
+            has_side_effects=True,
+            vmem_limit_bytes=56 * 1024 * 1024,
+        ),
+        name="attend_back",
+    )(places, flags, *local, *fars)
+    return results[:-1], unpadded(results[-1], pairs)
 
 
 def gelu(hidden):
@@ -774,7 +910,12 @@
     low, first = row_starts(doc_lengths[0])
     taken = jnp.arange(4 * GROUP, dtype=jnp.int32)[:, None] == reuse_heads[None, :]
     taker = jnp.sum(jnp.where(taken, jnp.arange(REUSE, dtype=jnp.int32)[None, :], 0), axis=1)
-    scalars = jnp.concatenate([first, reuse_heads, jnp.any(taken, axis=1).astype(jnp.int32), taker])
+    flags = jnp.any(taken, axis=1).astype(F32)
+    scalars = jnp.concatenate([first, reuse_heads])
+    band_of, in_band = reuse_heads // GROUP, reuse_heads % GROUP
+    places2 = jnp.concatenate(
+        [band_of * 3 * GROUP + 2 * GROUP + in_band, band_of * 2 * GROUP + GROUP + in_band]
+    )
 
     stream0 = block_input.astype(F32)
     normed1, unit1, scale1 = norm_rows(stream0, norm_gain1[0], norm_bias1[0])
@@ -840,21 +981,13 @@
         cotangent.astype(F32), kept2, outs2, norm_gain2, ups2, downs2
     )
     own2, far2 = sum_cores(mats2)
-    dq2, dk2, dk2_before, dk2_earlier, dv2, dv2_before, dv2_earlier = attend_back(
-        far2, scalars, low, front_kv2, values2, (), exact2, grad_heads.reshape(4, BAND, WIN), sums2
+    (dq2, dk2, dv2, dv2_before, dv2_earlier), (mats2,) = attend_back(
+        places2, flags, low, front_kv2, front_kv1, fresh2, (), exact2,
+        grad_heads.reshape(4, BAND, WIN), sums2, [(own2, far2)],
     )
     grad_out2 = dot(heads2.reshape(D, WIN), rounded, 1, 0).astype(BF16).reshape(4, BAND, D)
 
-    def fresh_part(grads):
-        return grads[2:].reshape(4, BAND // 2, WIN)
-
-    def join2(keys, values):
-        return jnp.concatenate([keys, fresh_part(values)], axis=1)
-
-    kv2 = join2(dk2, dv2) + pass_home(
-        join2(dk2_before, dv2_before), join2(dk2_earlier, dv2_earlier)
-    )
-    dcols2 = jnp.concatenate([dq2, kv2], axis=1)
+    dcols2 = jnp.concatenate([dq2, dk2, dv2[2:].reshape(4, BAND // 2, WIN)], axis=1)
     bias_grad2 = jnp.sum(dcols2, axis=2)
     dcols2 = dcols2.astype(BF16)
     grad_front2 = dot(dcols2.reshape(-1, WIN), normed2, 1, 0).astype(BF16).reshape(4, n_front2, D)
@@ -870,20 +1003,14 @@
     grad, rounded, grad_heads, mats1, up_grads1, small1 = tail_backward(
         grad, kept1, outs1, norm_gain1, ups1, downs1
     )
-    mats1 = sum_cores(mats1)
-    dq1, dk1, dk1_before, dk1_earlier, dv1, dv1_before, dv1_earlier = attend_back(
-        far2, scalars, low, front_kv1, values1, (dv2, dv2_before, dv2_earlier), exact1,
-        grad_heads.reshape(4, BAND, WIN), sums1,
+    pairs = [attn2, sum_cores(mats1)]
+    (dq1, dk1, dv1), (attn2, mats1) = attend_back(
+        taker, flags, low, front_kv1, (), (), (dv2, dv2_before, dv2_earlier), exact1,
+        grad_heads.reshape(4, BAND, WIN), sums1, pairs,
     )
     grad_out1 = dot(heads1.reshape(D, WIN), rounded, 1, 0).astype(BF16).reshape(4, BAND, D)
 
-    def join1(keys, values):
-        return jnp.concatenate([keys, values], axis=1)
-
-    kv1 = join1(dk1, dv1) + pass_home(
-        join1(dk1_before, dv1_before), join1(dk1_earlier, dv1_earlier)
-    )
-    dcols1 = jnp.concatenate([dq1, kv1], axis=1)
+    dcols1 = jnp.concatenate([dq1, dk1, dv1], axis=1)
     bias_grad1 = jnp.sum(dcols1, axis=2)
     dcols1 = dcols1.astype(BF16)
     grad_front1 = dot(dcols1.reshape(-1, WIN), normed1, 1, 0).astype(BF16).reshape(4, n_front1, D)
@@ -903,16 +1030,12 @@
         bias_grad2[:, :BAND].reshape(-1), bias_grad2[:, 2 * BAND :].reshape(-1),
         in_order(up_grads1), in_order(up_grads2),
     ]
-    lengths = [vector.shape[0] for vector in vectors]
-    packed = jnp.concatenate(vectors)
-    filler = (-packed.shape[0]) % 1024
-    pairs = ((own2, far2), attn2, mats1, attn1)
-    stack, packed = sum_replicas(pairs, jnp.pad(packed, (0, filler)).reshape(-1, 128))
-    packed = packed.reshape(-1)
+    vectors = [vector.reshape(-1, min(D, vector.size)) for vector in vectors]
+    (attn1,), packed = sum_replicas([attn1], vectors)
     sums, at = [], 0
-    for length in lengths:
-        sums.append(packed[at : at + length])
-        at += length
+    for vector in vectors:
+        sums.append(packed[at : at + vector.shape[0]].reshape(-1)[: vector.size])
+        at += vector.shape[0]
     me = lax.axis_index("mp")
 
     def mine(vector):
@@ -920,12 +1043,6 @@
 
     def pair(i):
         return jnp.stack([sums[i], sums[i + 1]])
-
-    shares, at = [], 0
-    for own, _ in pairs:
-        shares.append(stack[at : at + own.shape[0]])
-        at += own.shape[0] + -own.shape[0] % rows_of_part()
-    mats2, attn2, mats1, attn1 = shares
 
     return (
         block_output,

time: 666 us -> 663 us (level)
  Pallas kernels: 381 us -> 458 us
  waiting for transfers between devices: 49.1 us -> 0.01 us
  starting transfers between devices: 20.8 us -> 0.51 us
  matrix products: 97.1 us -> 77.3 us
  local copies, waits for them, and re-layouts: 46.7 us -> 61.7 us
    pallas_call x3, Pallas kernels: 226 us -> 308 us  [the longest x2 245 us: attend_back(): pl.pallas_call(functools.partial(back_kernel, mixed, counts, rows_of_part...]
    ppermute x6 -> x0, waiting for transfers between devices: 49.1 us -> none  [the longest x2 49.1 us: pass_home(): return near.astype(F32) + lax.ppermute(far, ('ctx', 'mp'), home).astype(F32)]
    dot_general x58, matrix products: 97.1 us -> 77.3 us  [dot(): lax.dot_general(left, right, (((left_dim,), (right_dim,)), ((), ())), pre...]
    ppermute x4, starting transfers between devices: 12.5 us -> 0.51 us  [swap(): return lax.ppermute(value, axis, [(i, i ^ bit) for i in devices])]
    ppermute x6 -> x0, starting transfers between devices: 8.36 us -> none  [the longest x4 5.12 us: pass_home(): near, far = lax.ppermute((before, earlier), ('ctx', 'mp'), first_home)]
    reshape x5 -> x14, local copies, waits for them, and re-layouts: 0.96 us -> 8.2 us  [shards(): vectors = [vector.reshape(-1, min(D, vector.size)) for vector in vectors]]
    convert_element_type x3 -> x4, other arithmetic: 10.2 us -> 14.4 us  [sum_cores(): (far.astype(F32) + last.astype(F32)).astype(BF16)]
    unnamed x340 -> x277, local copies, waits for them, and re-layouts: 34.8 us -> 33.5 us
  transfers between devices with their start and end apart: 10 -> 4, of which waited for: 2 -> 0; matrix products, arithmetic and copies ran while one was open for 12% -> 11% of each run, Pallas kernels for 0% -> 0%
where the time goes in v4:
time: 663 us; the launch traced here: 655 us
  Pallas kernels  458 us (69%)
  matrix products  77.3 us (12%)
  local copies, waits for them, and re-layouts  61.7 us (9%)
  other arithmetic  53.4 us (8%)
    pallas_call x2, Pallas kernels, attend_back(): pl.pallas_call(functools.partial(back_kernel, mixed, counts, rows_of_part...  245 us
    pallas_call x2, Pallas kernels, project(): pl.pallas_call(functools.partial(front_kernel, len(more)), out_shape=made...  134 us
    dot_general x58, matrix products, dot(): lax.dot_general(left, right, (((left_dim,), (right_dim,)), ((), ())), pre...  77.3 us
    pallas_call x1, Pallas kernels, sum_replicas(): pl.pallas_call(functools.partial(sum_kernel, counts, len(vectors), rows_o...  62.2 us
    unnamed x277, local copies, waits for them, and re-layouts  33.5 us
    pallas_call x2, Pallas kernels, attend(): pl.pallas_call(functools.partial(attend_kernel, len(arrays)), grid_spec=p...  16.5 us
    convert_element_type x4, other arithmetic, sum_cores(): (far.astype(F32) + last.astype(F32)).astype(BF16)  14.4 us
  transfers between devices with their start and end apart: 4, of which 0 were waited for; matrix products, arithmetic and copies ran while one was open for 11% of the time, Pallas kernels for 0%

profile of v4, /device:TPU:0, one launch (start us, length us, event | category | flops | bytes accessed | tf_op | source)
XLA Modules:
  0.0 654.5 jit_solution(18007044456232570933)
XLA Ops:
  0.8 1.4 convert_reduce_fusion
  2.2 1.5 fusion.26
  5.3 100.2 %front_gather.1 = (bf16[4,576,512]{2,1,0:T(8,128)(2,1)}, bf16[4,384,512]{2,1,0:T(8,128)(2,1)}, bf16[4,384,512]{2,1,0:T(8,128)(2,1)}, bf16[4,576,768]{2,1,0:T(8,1...) custom-call(bf16[512,768]{1,0:T(8,128)(2,1)S(1)} %fusion.19.refs_0_,, ...), custom_call_target="tpu_custom_call" | custom-call | tf_op jit(solution)/shard_map/front_gather/pallas_call | solution.py:391
  107.4 2.1 copy-done
  109.5 1.4 copy-done.2
  110.9 1.4 copy-done.4
  112.3 7.9 %attend.2 = (bf16[4,192,512]{2,1,0:T(8,128)(2,1)S(1)}, f32[4,192,512]{2,1,0:T(8,128)S(1)}, f32[4,8,512]{2,1,0:T(8,128)S(1)}) custom-call(s32[8]{0:T(128)S(1)} %pad_add_fusion.first_ref, s32[1,512]{1,0:T(1,128)S(1)} %bitcast.397, bf16[4,576,512]{2,1,0:T(8,128)(2,1)S(1)} %copy-done, bf16[4,576,512]{2,1,0:T(8,128)(2,1)S(1)} %copy-done, ...), custom_call_target="tpu_custom_call" | custom-call | tf_op jit(solution)/shard_map/attend/pallas_call | solution.py:191
  122.4 2.3 convolution_add_fusion.4
  124.7 2.6 convolution_add_fusion.5
  127.4 2.6 convolution_add_fusion.6
  134.8 1.3 fusion.263
  139.2 34.1 %front.1 = (bf16[4,480,512]{2,1,0:T(8,128)(2,1)S(1)}, bf16[4,288,512]{2,1,0:T(8,128)(2,1)S(1)}, bf16[4,288,512]{2,1,0:T(8,128)(2,1)S(1)}) custom-call(bf16[512,768]{1,0:T(8,128)(2,1)S(1)} %add_convert_fusion.2.refs_0_, bf16[4,512,768]{2,1,0:T(8,128)(2,1)} %bitcast_dynamic-update-slice_fusion.refs_1_, f32[4,8,512]{2,1,0:T(8,128)S(1)} %maximum_convert_fusion.refs_2_), custom_call_target="tpu_custom_call" | custom-call | tf_op jit(solution)/shard_map/front/pallas_call | solution.py:391
  173.5 3.2 copy-done.1
  176.7 8.6 %attend.3 = (bf16[4,192,512]{2,1,0:T(8,128)(2,1)S(1)}, f32[4,192,512]{2,1,0:T(8,128)S(1)}, f32[4,8,512]{2,1,0:T(8,128)S(1)}) custom-call(s32[8]{0:T(128)S(1)} %pad_add_fusion.first_ref, s32[1,512]{1,0:T(1,128)S(1)} %bitcast.398, bf16[4,480,512]{2,1,0:T(8,128)(2,1)S(1)} %get-tuple-element.64.q_ref.k0.refs_3_, ...), custom_call_target="tpu_custom_call" | custom-call | tf_op jit(solution)/shard_map/attend/pallas_call | solution.py:191
  189.2 1.6 copy-done.71
  191.9 1.6 fusion.268
  193.5 1.6 fusion.270
  198.0 2.8 pad_maximum_fusion
  203.9 1.8 fusion.269
  207.2 2.8 fusion.247
  211.0 1.4 multiply_reduce_fusion
  214.1 1.8 fusion.251
  219.1 2.2 convolution_convert_fusion.11
  225.0 2.7 fusion.96
  229.5 1.7 convolution_convert_fusion.21
  232.6 1.2 convolution_convert_fusion.18
  235.3 2.1 add_convert_fusion
  237.5 4.4 fusion.2
  241.8 116.4 %attend_back.2 = (f32[4,192,512]{2,1,0:T(8,128)}, f32[4,192,512]{2,1,0:T(8,128)}, f32[4,192,512]{2,1,0:T(8,128)}, bf16[4,192,512]{2,1,0:T(8,128)(2,1)}, bf16[4,1...) custom-call(s32[12]{0:T(128)} %pad_add_fusion.1.refs_0_, f32[12]{0:T(128)} %convert_element_type.420.refs_1_, ...), custom_call_target="tpu_custom_call" | custom-call | tf_op jit(solution)/shard_map/attend_back/pallas_call | solution.py:835
  358.3 1.3 slice.207
  359.9 1.8 fusion.7
  362.8 2.4 fusion.78
  365.8 1.3 copy-done.58
  367.1 1.6 fusion.265
  368.8 1.6 fusion.266
  370.6 1.6 fusion.249
  372.3 1.6 fusion.267
  379.5 1.7 convolution_convert_fusion.1
  383.4 1.5 pad_maximum_fusion.4
  386.0 2.5 pad_maximum_fusion.1
  391.7 1.4 multiply_reduce_fusion.1
  404.1 1.7 convolution_convert_fusion.20
  407.2 1.2 convolution_convert_fusion.9
  408.9 2.5 slice_convert_fusion
  411.4 2.0 fusion.10
  415.6 4.4 fusion
  420.0 128.9 %attend_back.3 = (f32[4,192,512]{2,1,0:T(8,128)}, f32[4,192,512]{2,1,0:T(8,128)}, f32[4,192,512]{2,1,0:T(8,128)}, bf16[2304,768]{1,0:T(8,128)(2,1)}) custom-call(s32[12]{0:T(128)} %select_reduce_fusion.1.refs_0_, f32[12]{0:T(128)} %convert_element_type.420.refs_1_, s32[1,512]{1,0:T(1,128)} %bitcast.400, ...), custom_call_target="tpu_custom_call" | custom-call | tf_op jit(solution)/shard_map/attend_back/pallas_call | solution.py:835
  549.0 1.7 constant_dynamic-update-slice_fusion.2
  551.0 1.3 copy-done.54
  553.5 2.0 convolution_convert_fusion
  555.5 1.2 dynamic-slice_bitcast_fusion
  556.9 1.6 pad_maximum_fusion.3
  558.6 1.4 copy-done.99
  560.0 3.5 fusion.25
  567.2 1.8 convert_bitcast_fusion.2
  569.0 1.8 slice_convert_fusion.4
  571.9 1.4 fusion.24
  574.2 2.5 slice_convert_fusion.2
  576.7 3.6 fusion.8
  580.3 62.2 %sum_replicas.1 = (bf16[768,768]{1,0:T(8,128)(2,1)}, f32[24,768]{1,0:T(8,128)}) custom-call(bf16[768,768]{1,0:T(8,128)(2,1)} %get-tuple-element.166.refs_0_, bf16[768,768]{1,0:T(8,128)(2,1)} %get-tuple-element.165.refs_1_, f32[1,768]{1,0:T(1,128)} %reshape.517.refs_2_, f32[1,768]{1,0:T(1,128)} %reshape.518.refs_3_, f32[1,768]{1,0:T(1,128)} %reshape.519.refs_4_, ...), custom_call_target="tpu_custom_call" | custom-call | tf_op jit(solution)/shard_map/sum_replicas/pallas_call | solution.py:625
  642.6 1.5 fusion.256
  644.9 1.2 slice.213
  646.2 1.8 slice_convert_fusion.5
  649.5 1.3 convert_bitcast_fusion
  (451 shorter events, 81.6 us)
Async XLA Ops:
  0.7 3.1 copy-start.94
  0.7 3.1 copy-start.97
  0.7 3.1 copy-start.98
  0.7 3.1 copy-start.95
  0.7 3.1 copy-start.96
  0.7 3.2 copy-start.88
  0.7 3.2 copy-start.89
  0.7 3.3 copy-start.80
  0.7 3.3 copy-start.50
  0.8 3.3 copy-start.40
  4.5 101.0 %copy-start.12 = (bf16[512,768]{1,0:T(8,128)(2,1)}, bf16[512,768]{1,0:T(8,128)(2,1)S(1)}, u32[]{:S(2)}) copy-start(bf16[512,768]{1,0:T(8,128)(2,1)S(1)} %fusion.19.refs_0_) | copy-start | bytes 2359300
  5.3 101.4 %copy-start.90 = (bf16[2,768]{1,0:T(2,128)(2,1)S(1)}, bf16[2,768]{1,0:T(2,128)(2,1)}, u32[]{:S(2)}) copy-start(bf16[2,768]{1,0:T(2,128)(2,1)} %param.44) | copy-start | bytes 9220
  5.3 101.4 %copy-start.91 = (bf16[2,768]{1,0:T(2,128)(2,1)S(1)}, bf16[2,768]{1,0:T(2,128)(2,1)}, u32[]{:S(2)}) copy-start(bf16[2,768]{1,0:T(2,128)(2,1)} %param.33) | copy-start | bytes 9220
  5.3 101.5 %copy-start.100 = (s32[1,3]{1,0:T(1,128)S(1)}, s32[1,3]{1,0:T(1,128)}, u32[]{:S(2)}) copy-start(s32[1,3]{1,0:T(1,128)} %param.26) | copy-start | bytes 40
  5.3 101.9 %copy-start.101 = (s32[6]{0:T(128)S(1)}, s32[6]{0:T(128)}, u32[]{:S(2)}) copy-start(s32[6]{0:T(128)} %param.27) | copy-start | bytes 76
  107.1 66.4 %copy-start.28 = (s32[512]{0:T(512)}, s32[512]{0:T(512)S(1)}, u32[]{:S(2)}) copy-start(s32[512]{0:T(512)S(1)} %add_select_fusion) | copy-start | bytes 6148
  107.3 12.9 %copy-start.33 = (bf16[4,192,768]{2,1,0:T(8,128)(2,1)}, bf16[4,192,768]{2,1,0:T(8,128)(2,1)S(1)}, u32[]{:S(2)}) copy-start(bf16[4,192,768]{2,1,0:T(8,128)(2,1)S(1)} %bitcast_dynamic-update-slice_fusion.2) | copy-start | bytes 3538948
  112.3 8.0 %copy-start.41 = (bf16[512,768]{1,0:T(8,128)(2,1)S(1)}, bf16[512,768]{1,0:T(8,128)(2,1)}, u32[]{:S(2)}) copy-start(bf16[512,768]{1,0:T(8,128)(2,1)} %param.24) | copy-start | bytes 2359300
  121.7 13.2 %copy-start.35 = (f32[512,768]{1,0:T(8,128)}, f32[512,768]{1,0:T(8,128)S(1)}, u32[]{:S(2)}) copy-start(f32[512,768]{1,0:T(8,128)S(1)} %get-tuple-element.205) | copy-start | bytes 4718596
  122.3 9.9 %copy-start.73 = (bf16[512,768]{1,0:T(8,128)(2,1)}, bf16[512,768]{1,0:T(8,128)(2,1)S(1)}, u32[]{:S(2)}) copy-start(bf16[512,768]{1,0:T(8,128)(2,1)S(1)} %add_convert_fusion.3) | copy-start | bytes 2359300
  122.4 7.7 %slice-start.10 = ((s8[4718592]{0:T(1024)(128)(4,1)}), s8[4194304]{0:T(1024)(128)(4,1)S(1)}, s32[]{:S(2)}) async-start(s8[4718592]{0:T(1024)(128)(4,1)} %bitcast.433), calls=%async_computation.10 | async-start | bytes 8388608
  124.7 10.1 %copy-start.57 = (f32[512,768]{1,0:T(8,128)}, f32[512,768]{1,0:T(8,128)S(1)}, u32[]{:S(2)}) copy-start(f32[512,768]{1,0:T(8,128)S(1)} %convolution_add_fusion.4) | copy-start | bytes 4718596
  124.7 5.3 slice-start.11
  136.2 49.3 %copy-start.37 = (f32[512,768]{1,0:T(8,128)}, f32[512,768]{1,0:T(8,128)S(1)}, u32[]{:S(2)}) copy-start(f32[512,768]{1,0:T(8,128)S(1)} %get-tuple-element.207) | copy-start | bytes 4718596
  139.1 34.1 %copy-start.14 = (bf16[512,768]{1,0:T(8,128)(2,1)}, bf16[512,768]{1,0:T(8,128)(2,1)S(1)}, u32[]{:S(2)}) copy-start(bf16[512,768]{1,0:T(8,128)(2,1)S(1)} %add_convert_fusion.2.refs_0_) | copy-start | bytes 2359300
  139.1 34.3 %copy-start.30 = (bf16[4,192,768]{2,1,0:T(8,128)(2,1)S(1)}, bf16[4,192,768]{2,1,0:T(8,128)(2,1)}, u32[]{:S(2)}) copy-start(bf16[4,192,768]{2,1,0:T(8,128)(2,1)} %copy-done.29) | copy-start | bytes 3538948
  139.1 34.3 %copy-start.20 = (bf16[192,768]{1,0:T(8,128)(2,1)S(1)}, bf16[192,768]{1,0:T(8,128)(2,1)}, u32[]{:S(2)}) copy-start(bf16[192,768]{1,0:T(8,128)(2,1)} %refs_10_.1) | copy-start | bytes 884740
  139.2 34.4 %copy-start.3 = (bf16[4,384,512]{2,1,0:T(8,128)(2,1)S(1)}, bf16[4,384,512]{2,1,0:T(8,128)(2,1)}, u32[]{:S(2)}) copy-start(bf16[4,384,512]{2,1,0:T(8,128)(2,1)} %get-tuple-element.56.k1.refs_1_.refs_4_) | copy-start | bytes 4718596
  139.2 34.4 %copy-start.5 = (bf16[4,384,512]{2,1,0:T(8,128)(2,1)S(1)}, bf16[4,384,512]{2,1,0:T(8,128)(2,1)}, u32[]{:S(2)}) copy-start(bf16[4,384,512]{2,1,0:T(8,128)(2,1)} %get-tuple-element.57.k2.refs_2_.refs_5_) | copy-start | bytes 4718596
  173.3 12.1 %copy-start.6 = (bf16[4,480,512]{2,1,0:T(8,128)(2,1)}, bf16[4,480,512]{2,1,0:T(8,128)(2,1)S(1)}, u32[]{:S(2)}) copy-start(bf16[4,480,512]{2,1,0:T(8,128)(2,1)S(1)} %get-tuple-element.64.q_ref.k0.refs_3_) | copy-start | bytes 5898244
  173.3 12.1 %copy-start.7 = (bf16[4,288,512]{2,1,0:T(8,128)(2,1)}, bf16[4,288,512]{2,1,0:T(8,128)(2,1)S(1)}, u32[]{:S(2)}) copy-start(bf16[4,288,512]{2,1,0:T(8,128)(2,1)S(1)} %get-tuple-element.65.k1.refs_4_) | copy-start | bytes 3538948
  173.3 12.1 %copy-start.8 = (bf16[4,288,512]{2,1,0:T(8,128)(2,1)}, bf16[4,288,512]{2,1,0:T(8,128)(2,1)S(1)}, u32[]{:S(2)}) copy-start(bf16[4,288,512]{2,1,0:T(8,128)(2,1)S(1)} %get-tuple-element.66.k2.refs_5_) | copy-start | bytes 3538948
  173.3 3.4 copy-start.1
  173.3 12.0 %copy-start.9 = (bf16[4,96,512]{2,1,0:T(8,128)(2,1)}, bf16[4,96,512]{2,1,0:T(8,128)(2,1)S(1)}, u32[]{:S(2)}) copy-start(bf16[4,96,512]{2,1,0:T(8,128)(2,1)S(1)} %slice.199) | copy-start | bytes 1179652
  173.4 12.0 %copy-start.10 = (bf16[4,96,512]{2,1,0:T(8,128)(2,1)}, bf16[4,96,512]{2,1,0:T(8,128)(2,1)S(1)}, u32[]{:S(2)}) copy-start(bf16[4,96,512]{2,1,0:T(8,128)(2,1)S(1)} %slice.200) | copy-start | bytes 1179652
  173.4 14.1 %slice-start.6 = ((s8[4718592]{0:T(1024)(128)(4,1)}), s8[4194304]{0:T(1024)(128)(4,1)S(1)}, s32[]{:S(2)}) async-start(s8[4718592]{0:T(1024)(128)(4,1)} %bitcast.429), calls=%async_computation.6 | async-start | bytes 8388608
  173.4 11.9 %copy-start.11 = (bf16[4,96,512]{2,1,0:T(8,128)(2,1)}, bf16[4,96,512]{2,1,0:T(8,128)(2,1)S(1)}, u32[]{:S(2)}) copy-start(bf16[4,96,512]{2,1,0:T(8,128)(2,1)S(1)} %slice.201) | copy-start | bytes 1179652
  173.5 11.9 %copy-start.31 = (bf16[4,192,768]{2,1,0:T(8,128)(2,1)}, bf16[4,192,768]{2,1,0:T(8,128)(2,1)S(1)}, u32[]{:S(2)}) copy-start(bf16[4,192,768]{2,1,0:T(8,128)(2,1)S(1)} %bitcast_dynamic-update-slice_fusion.1) | copy-start | bytes 3538948
  176.7 10.8 %slice-start.7 = ((s8[4718592]{0:T(1024)(128)(4,1)}), s8[524288]{0:T(1024)(128)(4,1)S(1)}, s32[]{:S(2)}) async-start(s8[4718592]{0:T(1024)(128)(4,1)} %bitcast.429), calls=%async_computation.7 | async-start | bytes 1048576
  187.5 19.1 %copy-start.78 = (bf16[512,768]{1,0:T(8,128)(2,1)}, bf16[512,768]{1,0:T(8,128)(2,1)S(1)}, u32[]{:S(2)}) copy-start(bf16[512,768]{1,0:T(8,128)(2,1)S(1)} %add_convert_fusion.1) | copy-start | bytes 2359300
  187.5 4.3 slice-start.2
  188.4 6.7 %copy-start.119 = (f32[512,768]{1,0:T(8,128)}, f32[512,768]{1,0:T(8,128)S(1)}, u32[]{:S(2)}) copy-start(f32[512,768]{1,0:T(8,128)S(1)} %convolution_add_fusion.2) | copy-start | bytes 4718596
  188.4 3.5 slice-start.3
  197.8 4.2 slice-start.8
  198.0 2.8 copy-start.63
  198.0 4.2 slice-start.9
  200.8 36.6 %collective-permute-start = (bf16[2,1536,768]{2,1,0:T(8,128)(2,1)}, bf16[2,1536,768]{2,1,0:T(8,128)(2,1)}, u32[]{:S(2)}, u32[]{:S(2)}) collective-permute-start(bf16[2,1536,768]{2,1,0:T(8,128)(2,1)} %pad_maximum_fusion), channel_id=1, source_target_pairs={{0,1},{1,0},{2,3},{3,2},{4,5},{5,4},{6,7},{7,6},{8,9},{9,8},{10,11... | collective-permute-start | bytes 14155784 | tf_op jit(solution)/shard_map/ppermute | solution.py:28
  214.1 5.0 copy-start.25
  224.1 3.6 slice-start.4
  359.9 2.8 copy-start.47
  359.9 5.9 slice-start.12
  362.8 3.1 slice-start.13
  367.1 7.7 %copy-start.76 = (bf16[512,768]{1,0:T(8,128)(2,1)}, bf16[512,768]{1,0:T(8,128)(2,1)S(1)}, u32[]{:S(2)}) copy-start(bf16[512,768]{1,0:T(8,128)(2,1)S(1)} %convert_element_type.440) | copy-start | bytes 2359300
  370.6 18.4 %copy-start.106 = (bf16[512,768]{1,0:T(8,128)(2,1)}, bf16[512,768]{1,0:T(8,128)(2,1)S(1)}, u32[]{:S(2)}) copy-start(bf16[512,768]{1,0:T(8,128)(2,1)S(1)} %get-tuple-element.218) | copy-start | bytes 2359300
  372.3 17.6 %copy-start.102 = (bf16[512,768]{1,0:T(8,128)(2,1)}, bf16[512,768]{1,0:T(8,128)(2,1)S(1)}, u32[]{:S(2)}) copy-start(bf16[512,768]{1,0:T(8,128)(2,1)S(1)} %get-tuple-element.138) | copy-start | bytes 2359300
  372.3 3.5 slice-start
  384.8 26.6 %collective-permute-start.1 = (bf16[2,672,768]{2,1,0:T(8,128)(2,1)}, bf16[2,672,768]{2,1,0:T(8,128)(2,1)}, u32[]{:S(2)}, u32[]{:S(2)}) collective-permute-start(bf16[2,672,768]{2,1,0:T(8,128)(2,1)} %pad_maximum_fusion.4), channel_id=1, source_target_pairs={{0,1},{1,0},{2,3},{3,2},{4,5},{5,4},{6,7},{7,6},{8,9},{9,8},{10,11... | collective-permute-start | bytes 6193160 | tf_op jit(solution)/shard_map/ppermute | solution.py:28
  388.5 27.1 %collective-permute-start.2 = (bf16[2,1536,768]{2,1,0:T(8,128)(2,1)}, bf16[2,1536,768]{2,1,0:T(8,128)(2,1)}, u32[]{:S(2)}, u32[]{:S(2)}) collective-permute-start(bf16[2,1536,768]{2,1,0:T(8,128)(2,1)} %pad_maximum_fusion.1), channel_id=1, source_target_pairs={{0,1},{1,0},{2,3},{3,2},{4,5},{5,4},{6,7},{7,6},{8,9},{9,8},{10,11... | collective-permute-start | bytes 14155784 | tf_op jit(solution)/shard_map/ppermute | solution.py:28
  394.3 2.9 slice-start.14
  394.3 3.6 slice-start.15
  394.3 5.0 copy-start.23
  556.9 3.1 copy-start.99
  558.6 18.2 %collective-permute-start.3 = (bf16[2,768,768]{2,1,0:T(8,128)(2,1)}, bf16[2,768,768]{2,1,0:T(8,128)(2,1)}, u32[]{:S(2)}, u32[]{:S(2)}) collective-permute-start(bf16[2,768,768]{2,1,0:T(8,128)(2,1)} %pad_maximum_fusion.3), channel_id=1, source_target_pairs={{0,1},{1,0},{2,3},{3,2},{4,5},{5,4},{6,7},{7,6},{8,9},{9,8},{10,11... | collective-permute-start | bytes 7077896 | tf_op jit(solution)/shard_map/ppermute | solution.py:28
  567.2 4.7 copy-start.56
  (79 other events, 126.5 us)

commit v5 on v4

v5 whole, which is shorter than its diff:
```python
import functools

import jax
import jax.numpy as jnp
from jax import lax
from jax.experimental import pallas as pl
from jax.experimental.pallas import tpu as pltpu
from jax.sharding import PartitionSpec as P

D = 768
HD = 64
REUSE = 6
WIN = 512
EARLY = 4
CHUNK = 256
LAG = 2
HOOK_FIRST, HOOK_SECOND = -3, 0
GROUP = 3
BAND = GROUP * HD
TILE = 256
TILES = 3 * WIN // TILE
EPS = 1e-05
SCALE = HD**-0.5
F32 = jnp.float32
BF16 = jnp.bfloat16


def swap(value, axis, bit):
    devices = range(lax.axis_size(axis))
    return lax.ppermute(value, axis, [(i, i ^ bit) for i in devices])


def in_order(parts):
    return jnp.concatenate(by_distance(jnp.stack(parts)))


def by_distance(stacked):
    me = lax.axis_index("mp")
    return [
        lax.dynamic_index_in_dim(stacked, me ^ distance, 0, keepdims=False)
        for distance in range(4)
    ]


def flip(position, bit):
    return position + bit * (1 - 2 * ((position // bit) % 2))


def remote(source, target, sent, received, device):
    return pltpu.make_async_remote_copy(
        src_ref=source, dst_ref=target, send_sem=sent, recv_sem=received,
        device_id=device, device_id_type=pl.DeviceIdType.MESH,
    )


def meet(devices):
    barrier = pltpu.get_barrier_semaphore()
    for device in devices:
        pl.semaphore_signal(barrier, inc=1, device_id=device, device_id_type=pl.DeviceIdType.MESH)
    pl.semaphore_wait(barrier, len(devices))


def dot(left, right, left_dim, right_dim):
    return lax.dot_general(
        left, right, (((left_dim,), (right_dim,)), ((), ())), preferred_element_type=F32
    )


def norm_rows(value, gain, shift):
    mean = jnp.mean(value, axis=-1, keepdims=True)
    centred = value - mean
    spread = jnp.mean(centred * centred, axis=-1, keepdims=True)
    scale = lax.rsqrt(spread + EPS)
    unit = centred * scale
    return (unit * gain + shift).astype(BF16), unit, scale


def norm_back(grad, unit, scale, gain):
    scaled = grad * gain
    inner = (
        scaled
        - jnp.mean(scaled, axis=-1, keepdims=True)
        - unit * jnp.mean(scaled * unit, axis=-1, keepdims=True)
    )
    return scale * inner, jnp.sum(grad * unit, axis=0), jnp.sum(grad, axis=0)


def front_kernel(more_rows, lead, mixed, *refs):
    refs = list(refs)

    def take(count):
        taken = refs[:count]
        del refs[:count]
        return taken

    ctx, dp, mp = (lax.axis_index(axis) for axis in ("ctx", "dp", "mp"))
    near, far, last = {"mp": flip(mp, 1)}, {"mp": flip(mp, 2)}, {"mp": 3 - mp}
    window = {"ctx": 1 - ctx}
    chunks = chunks_of(lead, more_rows)
    n_chunks, n_more = len(chunks), len(more_rows)
    n_arrays = n_more + lead
    early, offset = (EARLY, HOOK_FIRST) if lead else (2, HOOK_SECOND)
    places, lo_ref, normed = take(3)
    first_values = take(3) if mixed else ()
    front, bias = (None, None) if lead else take(2)
    vectors_own = take(2 * lead)
    arrays_own = take(n_arrays)
    cols, before, earlier, out_ref, exact_ref, sum_ref = take(6)
    vectors = take(2 * lead)
    arrays = take(n_arrays)
    if lead:
        front, bias = arrays[0], vectors[0]
    values, raw, top, total, acc, kv_out, kv_in, on_out, on_in = take(9)
    m_out, m_in = take(2)
    if lead:
        f_out, f_in = take(2)
    meet([near, far, last, window, {"dp": flip(dp, 1)}])
    directions = (near, far, last)
    if True:

        def whole(k, way):
            return remote(
                vectors_own[k], vectors[k].at[mp], f_out.at[k, way], f_in.at[k, way],
                directions[way],
            )

        bit = lax.rem(dp, 2)
        first = [(bit, {"dp": flip(dp, 1)}), (ctx, window)]

        def quarters(c):
            a, start, rows = chunks[c]
            (low, low_device), (high, high_device) = first if c % 2 else first[::-1]
            return a, start, rows // 4, rows // 2, low, low_device, high, high_device

        def copy(c, way, source, target, device):
            return remote(source, target, m_out.at[c, way], m_in.at[c, way], device)

        def beside(c):
            a, start, rows = chunks[c]
            here = pl.ds(start, rows)
            return copy(c, 0, arrays_own[a].at[here], arrays[a].at[mp, here], near)

        def across(c):
            a, start, quarter, half, low, _, high, _ = quarters(c)
            here = ds(start + high * half + low * quarter, quarter)
            return copy(c, 1, arrays_own[a].at[here], arrays[a].at[mp, here], far)

        def widen(c):
            a, start, quarter, half, low, device, high, _ = quarters(c)
            there = arrays[a].at[flip(mp, 2), ds(start + high * half + low * quarter, quarter)]
            return copy(c, 2, there, there, device)

        def complete(c):
            a, start, _, half, _, _, high, device = quarters(c)
            there = arrays[a].at[flip(mp, 2), ds(start + high * half, half)]
            return copy(c, 3, there, there, device)

        def hand_on(c):
            a, start, rows = chunks[c]
            there = arrays[a].at[flip(mp, 2), pl.ds(start, rows)]
            return copy(c, 4, there, there, near)

        across(0).start()
        beside(0).start()
        for k in range(2 * lead):
            for way in range(3):
                whole(k, way).start()
        for c in range(1, early):
            across(c).start()
        for c in range(1, n_chunks):
            beside(c).start()
        if lead:
            arrays[0][mp] = arrays_own[0][...]
        for k in range(2 * lead):
            vectors[k][mp] = vectors_own[k][...]

    def gather(step):
        for late, stage in enumerate(
            ((across, widen), (widen, complete), (complete, hand_on))
        ):
            a = step + lead - LAG * late
            if lead <= a < n_chunks:
                stage[0](a).wait_recv()
                stage[1](a).start()

    kv_rows = before.shape[1]
    from_row = cols.shape[1] - kv_rows
    sends_on = (mp == 1) | (mp == 2)
    sends_window = (mp == 0) & (ctx == 0)
    receives = (mp >= 2) | ((mp == 0) & (ctx == 1))

    def pass_on(slot, device):
        source = cols.at[slot, pl.ds(from_row, kv_rows)]
        return remote(source, before.at[slot], kv_out.at[slot], kv_in.at[slot], device)

    def pass_again(slot):
        return remote(before.at[slot], earlier.at[slot], on_out.at[slot], on_in.at[slot], {"mp": 3})

    order = (mp, flip(mp, 1), flip(mp, 2), 3 - mp) if lead else range(4)
    for k, slot in enumerate(order):
        if lead and k == 1:
            for vector in range(2):
                for way in range(3):
                    whole(vector, way).wait_recv()
            beside(0).wait_recv()
        if lead and k == 2:
            across(0).wait_recv()
            widen(0).start()
            widen(0).wait_recv()
            complete(0).start()
            complete(0).wait_recv()
            hand_on(0).start()
        if lead and k == 3:
            hand_on(0).wait_recv()
        column = jnp.transpose(bias[slot])[: cols.shape[1], 0:1]
        cols[slot] = (dot(front[slot, : cols.shape[1]], normed[...], 1, 1) + column).astype(BF16)
        pl.when(sends_on)(lambda: pass_on(slot, {"mp": mp + 1}).start())
        pl.when(sends_window)(lambda: pass_on(slot, window).start())
    for c in range(early, n_chunks):
        across(c).start()
    steps = n_chunks - lead + 2 * LAG
    for step in range(steps):
        if step + offset < 0:
            gather(step)

    def arrive(slot):
        def from_next():
            pass_on(slot, window).wait_recv()
            pl.when(mp == 2)(lambda: pass_again(slot).start())
            pl.when(mp == 3)(lambda: pass_again(slot).wait_recv())

        pl.when(receives)(from_next)

    keys = ((earlier, 0), (before, 0), (cols, BAND))
    sees_one, sees_two = receives, mp == 3
    sender = lax.max(mp - 1, 0)

    def group(k, _):
        if mixed:
            g = k
            pl.when(k < 2)(lambda: arrive(k))

            def rest():
                arrive(2)
                arrive(3)

            pl.when(k == 2)(rest)
        else:
            g = (sender % 2 + k) % 2 + 2 * ((sender // 2 + k // 2) % 2)
            arrive(g)
        place_values(mixed, g, places, first_values, keys, values)
        for t in range(WIN // TILE):
            tokens = slice(t * TILE, (t + 1) * TILE)
            low = lo_ref[:, tokens]
            place = 2 * WIN + t * TILE + lax.broadcasted_iota(jnp.int32, (1, TILE), 1)
            end = 2 * WIN // TILE + t

            def score(kt, tokens=tokens, low=low, place=place, end=end):
                spot = kt * TILE + lax.broadcasted_iota(jnp.int32, (TILE, TILE), 0)
                keep = spot >= low
                if kt == end:
                    keep = keep & (spot <= place)
                span = slice(kt % 2 * TILE, (kt % 2 + 1) * TILE)
                key_ref, at = keys[kt // 2]
                for j in range(GROUP):
                    rows = slice(j * HD, (j + 1) * HD)
                    key = key_ref[g, at + j * HD : at + (j + 1) * HD, span]
                    found = dot(key, cols[g, rows, tokens] * SCALE, 0, 0)
                    found = jnp.where(keep, found, -jnp.inf)
                    raw[j, kt] = found
                    peak = jnp.max(found.reshape(TILE // 8, 8, TILE), axis=0)
                    top[j] = peak if kt == end else jnp.maximum(top[j], peak)

            def weigh(kt, end=end):
                span = slice(kt % 2 * TILE, (kt % 2 + 1) * TILE)
                for j in range(GROUP):
                    rows = slice(j * HD, (j + 1) * HD)
                    powers = jnp.exp(raw[j, kt] - top[j, 0:1])
                    added = jnp.sum(powers.reshape(TILE // 8, 8, TILE), axis=0)
                    result = dot(values[kt // 2, rows, span], powers.astype(BF16), 1, 0)
                    total[j] = added if kt == end else total[j] + added
                    acc[j] = result if kt == end else acc[j] + result

            for stage in (score, weigh):
                for kt in reversed(range(end + 1)):
                    if kt >= 4:
                        stage(kt)
                    else:
                        pl.when(sees_one if kt >= 2 else sees_two)(functools.partial(stage, kt))
                if stage is score:
                    for j in range(GROUP):
                        top[j] = jnp.broadcast_to(jnp.max(top[j], axis=0, keepdims=True), (8, TILE))
            for j in range(GROUP):
                rows = slice(j * HD, (j + 1) * HD)
                whole_sum = jnp.sum(total[j], axis=0, keepdims=True)
                result = acc[j] / whole_sum
                out_ref[g, rows, tokens] = result.astype(BF16)
                exact_ref[g, rows, tokens] = result
                sum_ref[g, j : j + 1, tokens] = top[j, 0:1] + jnp.log(whole_sum)
            for step in range(steps):
                if (step + offset) % 2 == t and 0 <= step + offset < 8:
                    pl.when(k == (step + offset) // 2)(functools.partial(gather, step))
        return 0

    lax.fori_loop(0, 4, group, 0)
    for step in range(steps):
        if step + offset >= 8:
            gather(step)

    def sent(device):
        each(4, lambda slot: pass_on(slot, device).wait_send())

    pl.when(sends_on)(lambda: sent({"mp": mp + 1}))
    pl.when(sends_window)(lambda: sent(window))
    pl.when(mp == 2)(lambda: each(4, lambda slot: pass_again(slot).wait_send()))
    for k in range(2 * lead):
        for way in range(3):
            whole(k, way).wait_send()
    for a in range(n_chunks):
        beside(a).wait_send()
        if a >= lead:
            beside(a).wait_recv()
            hand_on(a).wait_recv()
        across(a).wait_send()
        widen(a).wait_send()
        complete(a).wait_send()
        hand_on(a).wait_send()


def place_values(mixed, g, places, first_values, keys, values):
    if not mixed:
        for part, (ref, at) in enumerate(keys):
            values[part] = ref[g, at + BAND : at + 2 * BAND, :]
        return

    def reused():
        for part in range(3):
            for j in range(GROUP):
                at = places[(0 if part == 2 else REUSE) + GROUP * g + j]
                values[part, j * HD : (j + 1) * HD, :] = first_values[part][at]

    def own():
        wide = BAND // 2
        for part, (ref, at) in enumerate(keys):
            for side in range(2):
                values[part, side * wide : (side + 1) * wide, :] = ref[
                    2 * (g - 2) + side, at + BAND : at + BAND + wide, :
                ]

    pl.when(g < 2)(reused)
    pl.when(g >= 2)(own)


def chunks_of(lead, more_rows):
    chunks = [(0, 0, 3 * BAND)] * lead
    for array, rows in enumerate(more_rows):
        size = CHUNK if rows % CHUNK == 0 else rows
        chunks += [(array + lead, start, size) for start in range(0, rows, size)]
    return chunks


def project(places, low, normed, front, bias, n_cols, kv_rows, firsts=(), small=None, more=()):
    place = pl.BlockSpec(memory_space=pltpu.VMEM)
    away = pl.BlockSpec(memory_space=pl.ANY)
    dma = pltpu.SemaphoreType.DMA
    given = [low, normed] + [v.reshape(-1, HD, WIN) for v in firsts[::-1]]
    lead = small is not None
    given += [bias, small, front] if lead else [front, bias]
    made = [(4, n_cols, WIN), (4, kv_rows, WIN), (4, kv_rows, WIN), (4, BAND, WIN)]
    made = [jax.ShapeDtypeStruct(shape, BF16) for shape in made]
    made += [jax.ShapeDtypeStruct((4, rows, WIN), F32) for rows in (BAND, 8)]
    scratch = [
        pltpu.VMEM((3, BAND, WIN), BF16),
        pltpu.VMEM((GROUP, TILES, TILE, TILE), F32),
        pltpu.VMEM((GROUP, 8, TILE), F32),
        pltpu.VMEM((GROUP, 8, TILE), F32),
        pltpu.VMEM((GROUP, HD, TILE), F32),
    ] + [dma((4,))] * 4
    gathered = ([bias, small, front] if lead else []) + list(more)
    gathered = [jax.ShapeDtypeStruct((4,) + v.shape, v.dtype) for v in gathered]
    rows = [v.shape[0] for v in more]
    scratch += [dma((len(chunks_of(lead, rows)), 5))] * 2 + ([dma((2, 3))] * 2 if lead else [])
    return pl.pallas_call(
        functools.partial(front_kernel, rows, int(lead), bool(firsts)),
        out_shape=made + gathered,
        in_specs=[pl.BlockSpec(memory_space=pltpu.SMEM)]
        + [place] * len(given) + [away] * len(more),
        out_specs=[place] * (len(made) + 3 * lead) + [away] * len(more),
        scratch_shapes=scratch,
        compiler_params=pltpu.CompilerParams(
            collective_id=1 if lead else 2,
            has_side_effects=True,
            vmem_limit_bytes=48 * 1024 * 1024,
        ),
        name="front_first" if lead else "front_second",
    )(places, *given, *more)


def row_starts(lengths):
    part = lax.axis_index("mp")
    place = (part - 1) * WIN + jnp.arange(WIN, dtype=jnp.int32)
    ends = jnp.cumsum(lengths)
    begun = jnp.max(jnp.where(place[:, None] >= ends[None, :], ends[None, :], 0), axis=1)
    document = begun - (part - 1) * WIN + 2 * WIN
    window = jnp.where(lax.axis_index("ctx") > 0, WIN, 2 * WIN)
    low = jnp.where(part == 0, window, document).astype(jnp.int32)
    return low.reshape(1, WIN)


class Sums:
    def __init__(self, counts, rows, terms, out, refs):
        n = len(counts)
        self.counts, self.rows, self.out = counts, rows, out
        self.owns, self.fars, self.nears, self.lasts = (terms[k * n : k * n + n] for k in range(4))
        self.from_near, self.from_last = refs[:2]
        self.mine = self.from_near
        self.from_y, self.from_x, self.kept, self.from_z = refs[2:6]
        self.sems = refs[6:]
        self.parts = sum(counts)
        self.firsts = [sum(counts[:k]) for k in range(len(counts))]
        self.ctx, self.dp, mp = (lax.axis_index(axis) for axis in ("ctx", "dp", "mp"))
        self.half = rows // 2
        self.bits = [1 << k for k in range((lax.axis_size("dp") - 1).bit_length())]
        self.highs = [(self.dp // bit) % 2 for bit in self.bits]
        self.other_chip, self.other_window = {"mp": flip(mp, 2)}, {"ctx": 1 - self.ctx}
        self.other_core = {"mp": flip(mp, 1)}
        self.beside = [{"dp": flip(self.dp, bit)} for bit in self.bits]
        self.partners = [self.other_chip, self.other_window, self.other_core] + self.beside
        self.stages = [self.join, self.spread]
        self.stages += [functools.partial(self.narrow, k) for k in range(len(self.bits))]
        self.stages += [functools.partial(self.widen, k) for k in reversed(range(len(self.bits)))]
        self.steps = self.parts + len(self.stages) - 1

    @staticmethod
    def scratch(total, parts, bits, lanes):
        dma = pltpu.SemaphoreType.DMA
        return [
            pltpu.VMEM((total, lanes), BF16),
            pltpu.VMEM((total, lanes), BF16),
            pltpu.VMEM((total, lanes), BF16),
            pltpu.VMEM((total // 2, lanes), BF16),
            pltpu.VMEM((total // 2, lanes), BF16),
            pltpu.VMEM((total // 2, lanes), BF16),
            dma((parts,)), dma((parts,)),
            dma((parts,)), dma((parts,)),
            dma((parts, bits)), dma((parts, bits)),
            dma((parts, bits)), dma((parts, bits)),
            dma((parts,)), dma((parts,)),
            dma((parts, 2)), dma((parts, 2)),
        ]

    def segment(self, k, sent=False):
        start, size = 0, self.half
        for high in self.highs[:k]:
            size //= 2
            start = start + high * size
        if sent:
            size //= 2
            start = start + (1 - self.highs[k]) * size
        return start, size

    def to_core(self, array, i, which):
        place = self.firsts[array] + i
        source = (self.nears, self.lasts)[which][array].at[ds(i * self.rows, self.rows)]
        target = (self.from_near, self.from_last)[which].at[ds(place * self.rows, self.rows)]
        sent, received = (sem.at[place, which] for sem in self.sems[10:12])
        return remote(source, target, sent, received, self.other_core)

    def to_y(self, i):
        here = ds(i * self.rows, self.rows)
        source, target = self.from_last.at[here], self.from_y.at[here]
        return remote(source, target, self.sems[0].at[i], self.sems[1].at[i], self.other_chip)

    def to_x(self, i):
        source = self.mine.at[ds(i * self.rows + (1 - self.ctx) * self.half, self.half)]
        target = self.from_x.at[ds(i * self.half, self.half)]
        return remote(source, target, self.sems[2].at[i], self.sems[3].at[i], self.other_window)

    def to_z(self, i, k):
        start, size = self.segment(k, True)
        source = self.kept.at[ds(i * self.half + start, size)]
        target = self.from_z.at[ds(i * self.half + self.half - 2 * size, size)]
        return remote(source, target, self.sems[4].at[i, k], self.sems[5].at[i, k], self.beside[k])

    def back_z(self, i, k):
        start, size = self.segment(k + 1)
        here = self.out.at[ds(i * self.rows + self.ctx * self.half + start, size)]
        return remote(here, here, self.sems[6].at[i, k], self.sems[7].at[i, k], self.beside[k])

    def back_x(self, i):
        here = self.out.at[ds(i * self.rows + self.ctx * self.half, self.half)]
        return remote(here, here, self.sems[8].at[i], self.sems[9].at[i], self.other_window)

    def start(self):
        for array, count in enumerate(self.counts):

            def send(i, array=array):
                self.to_core(array, i, 1).start()
                self.to_core(array, i, 0).start()

            each(count, send)
        for array, count in enumerate(self.counts):

            def fold(i, array=array):
                place = self.firsts[array] + i
                self.to_core(array, i, 1).wait_recv()
                here = ds(place * self.rows, self.rows)
                term = self.fars[array][ds(i * self.rows, self.rows), :]
                total = term.astype(F32) + self.from_last[here, :].astype(F32)
                self.from_last[here, :] = total.astype(BF16)
                self.to_y(place).start()

            each(count, fold)

    def join(self, i):
        here = ds(i * self.rows, self.rows)
        self.to_y(i).wait_recv()
        for array, count in enumerate(self.counts):
            first = self.firsts[array]

            def add(array=array, first=first):
                self.to_core(array, i - first, 0).wait_recv()
                term = self.owns[array][ds((i - first) * self.rows, self.rows), :]
                total = term.astype(F32) + self.from_near[here, :].astype(F32)
                self.mine[here, :] = (total + self.from_y[here, :].astype(F32)).astype(BF16)

            pl.when((i >= first) & (i < first + count))(add)
        self.to_x(i).start()

    def spread(self, i):
        self.to_x(i).wait_recv()
        there = ds(i * self.half, self.half)
        term = self.mine[ds(i * self.rows + self.ctx * self.half, self.half), :]
        total = term.astype(F32) + self.from_x[there, :].astype(F32)
        self.kept[there, :] = total.astype(BF16)
        self.to_z(i, 0).start()

    def narrow(self, k, i):
        self.to_z(i, k).wait_recv()
        start, size = self.segment(k + 1)
        here = ds(i * self.half + start, size)
        there = ds(i * self.half + self.half - 2 * size, size)
        total = self.kept[here, :].astype(F32) + self.from_z[there, :].astype(F32)
        if k + 1 < len(self.bits):
            self.kept[here, :] = total.astype(BF16)
            self.to_z(i, k + 1).start()
        else:
            place = ds(i * self.rows + self.ctx * self.half + start, size)
            self.out[place, :] = total.astype(BF16)
            self.back_z(i, k).start()

    def widen(self, k, i):
        self.back_z(i, k).wait_recv()
        if k:
            self.back_z(i, k - 1).start()
        else:
            self.back_x(i).start()

    def step(self, i):
        for late, stage in enumerate(self.stages):
            pl.when((i >= late) & (i < self.parts + late))(functools.partial(stage, i - late))

    def finish(self):
        for array, count in enumerate(self.counts):

            def sent(i, array=array):
                self.to_core(array, i, 0).wait_send()
                self.to_core(array, i, 1).wait_send()

            each(count, sent)

        def end(i):
            self.to_y(i).wait_send()
            self.to_x(i).wait_send()
            self.back_x(i).wait()
            for k in range(len(self.bits)):
                self.to_z(i, k).wait_send()
                self.back_z(i, k).wait_send()

        each(self.parts, end)


def ds(start, size):
    return pl.ds(pl.multiple_of(start, 16), size)


def each(count, step):
    lax.fori_loop(0, count, lambda i, _: (step(i), 0)[1], 0)


def sum_kernel(counts, n_vectors, rows, *refs):
    n = 4 * len(counts)
    shares, terms = refs[:n], refs[n : n + n_vectors]
    refs = refs[n + n_vectors :]
    out, vec = refs[:2]
    from_vec, v_out, v_in = refs[-3:]
    sums = Sums(counts, rows, shares, out, refs[2:-3])
    meet(sums.partners)
    at = 0
    for term in terms:
        vec[at : at + term.shape[0], : term.shape[1]] = term[...]
        at += term.shape[0]
    for hop, partner in enumerate(sums.partners):
        copy = remote(vec, from_vec.at[hop], v_out.at[hop], v_in.at[hop], partner)
        copy.start()
        if hop == 0:
            sums.start()
        copy.wait()
        vec[...] = vec[...] + from_vec[hop]
    each(sums.steps, sums.step)
    sums.finish()


def rows_of_part():
    return max(128, 32 * lax.axis_size("dp"))


def padded(arrays):
    rows = rows_of_part()
    terms = [
        [jnp.pad(v, ((0, -v.shape[0] % rows), (0, 0))) for v in part]
        for part in zip(*arrays, strict=True)
    ]
    own, near, far, last = terms
    counts = [v.shape[0] // rows for v in own]
    bits = (lax.axis_size("dp") - 1).bit_length()
    total = sum(counts) * rows
    shape = jax.ShapeDtypeStruct((total, own[0].shape[1]), BF16)
    scratch = Sums.scratch(total, sum(counts), bits, shape.shape[1])
    return own + far, near + last, counts, bits, shape, scratch


def unpadded(stack, arrays):
    shares, at = [], 0
    for own, *_ in arrays:
        shares.append(stack[at : at + own.shape[0]])
        at += own.shape[0] + -own.shape[0] % rows_of_part()
    return shares


def sum_replicas(arrays, vectors):
    here, there, counts, bits, shape, scratch = padded(arrays)
    place = pl.BlockSpec(memory_space=pltpu.VMEM)
    away = pl.BlockSpec(memory_space=pl.ANY)
    dma = pltpu.SemaphoreType.DMA
    rows = sum(v.shape[0] for v in vectors)
    stack, summed = pl.pallas_call(
        functools.partial(sum_kernel, counts, len(vectors), rows_of_part()),
        out_shape=[shape, jax.ShapeDtypeStruct((rows, D), F32)],
        in_specs=[place] * len(here) + [away] * len(there) + [place] * len(vectors),
        out_specs=[place, place],
        scratch_shapes=scratch
        + [pltpu.VMEM((3 + bits, rows, D), F32), dma((3 + bits,)), dma((3 + bits,))],
        compiler_params=pltpu.CompilerParams(
            collective_id=0, has_side_effects=True, vmem_limit_bytes=56 * 1024 * 1024
        ),
        name="sum_replicas",
    )(*here, *there, *vectors)
    return unpadded(stack, arrays), summed


def back_kernel(mixed, counts, rows, *refs):
    refs = list(refs)

    def take(count):
        taken = refs[:count]
        del refs[:count]
        return taken

    places, flags, lo_ref = take(3)
    shares, away = take(4 * len(counts)), take(9)
    dq_ref, dk_ref, dv_ref = take(3)
    if mixed:
        dv_before, dv_earlier = take(2)
    (out,) = take(1)
    if not mixed:
        dv_before, dv_earlier = take(2)
    dk_before, dk_earlier = take(2)
    near_k, near_v, far_k, far_v, home_k, home_v = take(6)
    values, acc_k, acc_v, acc_q = take(4)
    kv_out, kv_in = take(2)
    fetched, loaded = take(9), take(1)[0]
    loads = [
        pltpu.make_async_copy(source, target, loaded.at[k])
        for k, (source, target) in enumerate(zip(away, fetched, strict=True))
    ]
    for load in loads:
        load.start()
    cols, before, earlier, *others, exact, grad_ref, sum_ref = fetched
    first_values, given = (others, ()) if mixed else ((), others)
    sums = Sums(counts, rows, shares, out, refs)

    ctx, mp = lax.axis_index("ctx"), lax.axis_index("mp")
    sees_one = (mp >= 2) | ((mp == 0) & (ctx == 1))
    sees_two = mp == 3
    meet(sums.partners + [{"mp": 3 - mp}])
    sums.start()
    keys = ((earlier, 0), (before, 0), (cols, BAND))

    def home(which, source, target, g, device):
        return remote(
            source.at[g], target.at[g], kv_out.at[which, g], kv_in.at[which, g], device
        )

    def pair(g, act, step):
        act(step)
        if mixed:
            pl.when(g >= 2)(lambda: act(step + 1))
        else:
            act(step + 1)

    def from_last(g, step):
        source, target = (
            (dk_before, near_k), (dv_before, near_v), (dk_earlier, far_k), (dv_earlier, far_v),
        )[step]
        return home(step, source, target, g, {"mp": 2})

    def from_next(g, step, device):
        source, target = ((dk_before, home_k), (dv_before, home_v))[step]
        return home(4 + step, source, target, g, device)

    def group(g, _):
        place_values(mixed, g, places, first_values, keys, values)
        acc_k[...] = jnp.zeros_like(acc_k)
        if mixed:
            acc_v[...] = jnp.zeros_like(acc_v)
        else:
            for part in range(3):
                for j in range(GROUP):
                    head = GROUP * g + j
                    term = given[part][places[head]].astype(F32) * flags[head]
                    for side in range(2):
                        acc_v[2 * part + side, j * HD : (j + 1) * HD, :] = term[
                            :, side * TILE : (side + 1) * TILE
                        ]
        for t in range(WIN // TILE):
            tokens = slice(t * TILE, (t + 1) * TILE)
            low = lo_ref[:, tokens]
            place = 2 * WIN + t * TILE + lax.broadcasted_iota(jnp.int32, (1, TILE), 1)
            last = 2 * WIN // TILE + t

            def tile(kt, tokens=tokens, low=low, place=place, last=last):
                spot = kt * TILE + lax.broadcasted_iota(jnp.int32, (TILE, TILE), 0)
                keep = spot >= low
                if kt == last:
                    keep = keep & (spot <= place)
                span = slice(kt % 2 * TILE, (kt % 2 + 1) * TILE)
                key_ref, at = keys[kt // 2]
                for j in range(GROUP):
                    rows_j = slice(j * HD, (j + 1) * HD)
                    key = key_ref[g, at + j * HD : at + (j + 1) * HD, span]
                    query = cols[g, rows_j, tokens] * SCALE
                    grad = grad_ref[g, rows_j, tokens]
                    inner = jnp.sum(
                        grad.astype(F32) * exact[g, rows_j, tokens], axis=0, keepdims=True
                    )
                    raw = jnp.where(keep, dot(key, query, 0, 0), -jnp.inf)
                    weights = jnp.exp(raw - sum_ref[g, j : j + 1, tokens])
                    grad_weights = dot(values[kt // 2, rows_j, span], grad, 0, 0)
                    low_grad = (weights * (grad_weights - inner)).astype(BF16)
                    acc_v[kt, rows_j, :] += dot(grad, weights.astype(BF16), 1, 1)
                    acc_k[kt, rows_j, :] += dot(query, low_grad, 1, 1)
                    result = dot(key, low_grad, 1, 0)
                    acc_q[j] = result if kt == last else result + acc_q[j]

            for kt in reversed(range(last + 1)):
                if kt >= 4:
                    tile(kt)
                else:
                    pl.when(sees_one if kt >= 2 else sees_two)(functools.partial(tile, kt))
            for j in range(GROUP):
                dq_ref[g, j * HD : (j + 1) * HD, tokens] = acc_q[j] * SCALE
            sums.step(2 * g + t)
        results = ((dk_earlier, dv_earlier), (dk_before, dv_before), (dk_ref, dv_ref))
        for part, (dk, dv) in enumerate(results):
            for side in range(2):
                span = slice(side * TILE, (side + 1) * TILE)
                dk[g, :, span] = acc_k[2 * part + side].astype(dk.dtype)
                dv[g, :, span] = acc_v[2 * part + side].astype(dv.dtype)

        def send_last():
            pair(g, lambda step: from_last(g, step).start(), 0)
            pair(g, lambda step: from_last(g, step).start(), 2)

        pl.when(mp == 3)(send_last)
        pl.when((mp == 0) & (ctx == 1))(
            lambda: pair(g, lambda step: from_next(g, step, sums.other_window).start(), 0)
        )
        return 0

    for load in loads:
        load.wait()
    lax.fori_loop(0, 4, group, 0)

    def relay(g):
        def one(step):
            near, far, source, total = (
                (near_k, far_k, dk_before, dk_ref), (near_v, far_v, dv_before, dv_ref),
            )[step]
            from_last(g, step).wait_recv()
            from_last(g, step + 2).wait_recv()
            source[g] = (source[g].astype(F32) + far[g].astype(F32)).astype(BF16)
            from_next(g, step, {"mp": 1}).start()
            total[g] += near[g].astype(F32)

        pair(g, one, 0)

    pl.when(mp == 2)(lambda: each(4, relay))
    for i in range(8, sums.steps):
        sums.step(i)

    def arrive(g):
        def one(step):
            arrived, total = ((home_k, dk_ref), (home_v, dv_ref))[step]
            from_next(g, step, sums.other_window).wait_recv()
            total[g] += arrived[g].astype(F32)

        pair(g, one, 0)

    pl.when((mp == 1) | ((mp == 0) & (ctx == 0)))(lambda: each(4, arrive))

    def sent_last(g):
        pair(g, lambda step: from_last(g, step).wait_send(), 0)
        pair(g, lambda step: from_last(g, step).wait_send(), 2)

    def sent_next(device):
        each(4, lambda g: pair(g, lambda step: from_next(g, step, device).wait_send(), 0))

    pl.when(mp == 3)(lambda: each(4, sent_last))
    pl.when(mp == 2)(lambda: sent_next({"mp": 1}))
    pl.when((mp == 0) & (ctx == 1))(lambda: sent_next(sums.other_window))
    sums.finish()


def attend_back(places, flags, low, front, firsts, given, exact, grad_heads, lse, arrays):
    mixed = bool(firsts)
    here, there, counts, bits, shape, scratch = padded(arrays)
    place = pl.BlockSpec(memory_space=pltpu.VMEM)
    away = pl.BlockSpec(memory_space=pl.ANY)
    scalar = pl.BlockSpec(memory_space=pltpu.SMEM)
    dma = pltpu.SemaphoreType.DMA
    by_head = [v.reshape(-1, HD, WIN) for v in firsts[::-1] + given[::-1]]
    fetched = [*front, *by_head, exact, grad_heads, lse]
    wide = jax.ShapeDtypeStruct((4, BAND, WIN), F32)
    slim = jax.ShapeDtypeStruct((4, BAND, WIN), BF16)
    outs = [wide] * 3 + ([slim] * 2 if mixed else []) + [shape]
    block = pltpu.VMEM((4, BAND, WIN), BF16)
    results = pl.pallas_call(
        functools.partial(back_kernel, mixed, counts, rows_of_part()),
        out_shape=outs,
        in_specs=[scalar, scalar, place]
        + [place] * len(here)
        + [away] * (len(there) + len(fetched)),
        out_specs=[place] * len(outs),
        scratch_shapes=[block] * (8 if mixed else 10)
        + [
            pltpu.VMEM((3, BAND, WIN), BF16),
            pltpu.VMEM((TILES, BAND, TILE), F32),
            pltpu.VMEM((TILES, BAND, TILE), F32),
            pltpu.VMEM((GROUP, HD, TILE), F32),
            dma((6, 4)),
            dma((6, 4)),
        ]
        + [pltpu.VMEM(v.shape, v.dtype) for v in fetched]
        + [dma((len(fetched),))]
        + scratch,
        compiler_params=pltpu.CompilerParams(
            collective_id=3 if mixed else 4,
            has_side_effects=True,
            vmem_limit_bytes=60 * 1024 * 1024,
        ),
        name="attend_back",
    )(places, flags, low, *here, *there, *fetched)
    return results[:-1], unpadded(results[-1], arrays)


def gelu(hidden):
    return jax.nn.gelu(hidden, approximate=True)


def tail_forward(stream, heads, out_weight, out_bias, gain, shift, ups, up_biases, downs):
    stream = stream + dot(heads, out_weight, 0, 0) + out_bias[0]
    normed, unit, scale = norm_rows(stream, gain[1], shift[1])
    hidden, active, total = [], [], out_bias[1]
    for up, bias, down in zip(ups, up_biases, downs, strict=True):
        hidden.append(dot(normed, up, 1, 0) + bias)
        active.append(gelu(hidden[-1]).astype(BF16))
        total = total + dot(active[-1], down, 1, 0)
    return stream + total, (normed, unit, scale, hidden, active)


def tail_backward(grad, kept, out_weight, gain, ups, downs):
    normed, unit, scale, hidden, active = kept
    bias_mlp = jnp.sum(grad, axis=0)
    rounded = grad.astype(BF16)
    mats, up_biases, normed_grad = [], [], 0.0
    for up, down, before, after in zip(ups, downs, hidden, active, strict=True):
        _, pull = jax.vjp(gelu, before)
        grad_hidden = pull(dot(rounded, down, 1, 1))[0]
        up_biases.append(jnp.sum(grad_hidden, axis=0))
        low = grad_hidden.astype(BF16)
        mats.append((dot(normed, low, 0, 0).astype(BF16), dot(after, rounded, 0, 0).astype(BF16)))
        normed_grad = normed_grad + dot(low, up, 1, 1)
    middle, gain_grad, shift_grad = norm_back(normed_grad, unit, scale, gain[1])
    grad = grad + middle
    bias_attn = jnp.sum(grad, axis=0)
    rounded = grad.astype(BF16)
    grad_heads = dot(out_weight, rounded, 1, 1).astype(BF16)
    return grad, rounded, grad_heads, mats, up_biases, (gain_grad, shift_grad, bias_attn, bias_mlp)


def turned(weight):
    return jnp.swapaxes(weight, -1, -2)


def shards(
    block_input, cotangent, doc_lengths, reuse_heads,
    norm_gain1, norm_bias1, projections1, front_bias1, out_weight1, out_bias1,
    up_weight1, up_bias1, down_weight1,
    norm_gain2, norm_bias2, query_key2, query_bias2, fresh_value2, value_bias2,
    out_weight2, out_bias2, up_weight2, up_bias2, down_weight2,
):
    low = row_starts(doc_lengths[0])
    taken = jnp.arange(4 * GROUP, dtype=jnp.int32)[:, None] == reuse_heads[None, :]
    taker = jnp.sum(jnp.where(taken, jnp.arange(REUSE, dtype=jnp.int32)[None, :], 0), axis=1)
    flags = jnp.any(taken, axis=1).astype(F32)
    band_of, in_band = reuse_heads // GROUP, reuse_heads % GROUP
    places2 = jnp.concatenate(
        [band_of * 3 * GROUP + 2 * GROUP + in_band, band_of * 2 * GROUP + GROUP + in_band]
    )

    stream0 = block_input.astype(F32)
    normed1, unit1, scale1 = norm_rows(stream0, norm_gain1[0], norm_bias1[0])
    n_front1, n_front2 = 3 * BAND, 2 * BAND + BAND // 2
    none = jnp.zeros((BAND,), BF16)

    def as_row(pieces):
        row = jnp.concatenate(pieces).astype(F32)
        return jnp.pad(row[None, :], ((0, 7), (0, -row.shape[0] % 128)))

    small = jnp.concatenate([query_bias2, value_bias2, up_bias1, up_bias2])
    small = jnp.pad(small, (0, 16 * 128 - small.shape[0])).reshape(16, 128)
    own_front2 = jnp.concatenate([turned(query_key2).reshape(2 * BAND, D), turned(fresh_value2)])
    own_front2 = jnp.pad(own_front2, ((0, -n_front2 % 64), (0, 0)))
    (
        cols1, before1, earlier1, heads1, exact1, sums1, _, small, front1,
        up1, down1, front2, outs1,
    ) = project(
        places2, low, normed1, turned(projections1).reshape(n_front1, D),
        as_row([front_bias1[0], none, front_bias1[1]]), n_front1, 2 * BAND, (), small,
        (up_weight1, down_weight1, own_front2, out_weight1),
    )
    me = lax.axis_index("mp")
    ups1, downs1 = ([up_weight1] + by_distance(up1)[1:], [down_weight1] + by_distance(down1)[1:])
    front2 = lax.dynamic_update_index_in_dim(front2, own_front2, me, 0)
    outs1 = lax.dynamic_update_index_in_dim(outs1, out_weight1, me, 0).reshape(D, D)
    small = small.reshape(4, -1)
    at = BAND + BAND // 2
    bias2 = jnp.stack([as_row([small[s, :BAND], none, small[s, BAND:at]]) for s in range(4)])
    up_biases1 = by_distance(small[:, at : at + D])
    up_biases2 = by_distance(small[:, at + D : at + 2 * D])

    front_kv1 = (cols1, before1, earlier1)
    stream1, kept1 = tail_forward(
        stream0, heads1.reshape(D, WIN), outs1, out_bias1, norm_gain1, norm_bias1,
        ups1, up_biases1, downs1,
    )

    normed2, unit2, scale2 = norm_rows(stream1, norm_gain2[0], norm_bias2[0])
    front_kv1 = (cols1, before1, earlier1)
    cols2, before2, earlier2, heads2, exact2, sums2, up2, down2, outs2 = project(
        places2, low, normed2, front2, bias2, n_front2, n_front2 - BAND, front_kv1, None,
        (up_weight2, down_weight2, out_weight2),
    )
    ups2, downs2 = ([up_weight2] + by_distance(up2)[1:], [down_weight2] + by_distance(down2)[1:])
    outs2 = lax.dynamic_update_index_in_dim(outs2, out_weight2, me, 0).reshape(D, D)
    front2 = front2[:, :n_front2]

    front_kv2 = (cols2, before2, earlier2)
    stream2, kept2 = tail_forward(
        stream1, heads2.reshape(D, WIN), outs2, out_bias2, norm_gain2, norm_bias2,
        ups2, up_biases2, downs2,
    )
    block_output = stream2.astype(BF16)

    grad, rounded, grad_heads, mats2, up_grads2, small2 = tail_backward(
        cotangent.astype(F32), kept2, outs2, norm_gain2, ups2, downs2
    )
    (dq2, dk2, dv2, dv2_before, dv2_earlier), mats2 = attend_back(
        places2, flags, low, front_kv2, front_kv1, (), exact2,
        grad_heads.reshape(4, BAND, WIN), sums2, list(zip(*mats2, strict=True)),
    )
    grad_out2 = dot(heads2.reshape(D, WIN), rounded, 1, 0).astype(BF16).reshape(4, BAND, D)

    dcols2 = jnp.concatenate([dq2, dk2, dv2[2:].reshape(4, BAND // 2, WIN)], axis=1)
    bias_grad2 = jnp.sum(dcols2, axis=2)
    dcols2 = dcols2.astype(BF16)
    grad_front2 = dot(dcols2.reshape(-1, WIN), normed2, 1, 0).astype(BF16).reshape(4, n_front2, D)
    attn2 = [
        jnp.concatenate(pair)
        for pair in zip(by_distance(grad_out2), by_distance(grad_front2), strict=True)
    ]
    normed_grad = dot(dcols2.reshape(-1, WIN), front2.reshape(-1, D), 0, 0)
    middle, gain_front2, shift_front2 = norm_back(normed_grad, unit2, scale2, norm_gain2[0])
    grad = grad + middle

    grad, rounded, grad_heads, mats1, up_grads1, small1 = tail_backward(
        grad, kept1, outs1, norm_gain1, ups1, downs1
    )
    arrays = [attn2] + list(zip(*mats1, strict=True))
    (dq1, dk1, dv1), (attn2, *mats1) = attend_back(
        taker, flags, low, front_kv1, (), (dv2, dv2_before, dv2_earlier), exact1,
        grad_heads.reshape(4, BAND, WIN), sums1, arrays,
    )
    grad_out1 = dot(heads1.reshape(D, WIN), rounded, 1, 0).astype(BF16).reshape(4, BAND, D)

    dcols1 = jnp.concatenate([dq1, dk1, dv1], axis=1)
    bias_grad1 = jnp.sum(dcols1, axis=2)
    dcols1 = dcols1.astype(BF16)
    grad_front1 = dot(dcols1.reshape(-1, WIN), normed1, 1, 0).astype(BF16).reshape(4, n_front1, D)
    attn1 = [
        jnp.concatenate(pair)
        for pair in zip(by_distance(grad_out1), by_distance(grad_front1), strict=True)
    ]
    normed_grad = dot(dcols1.reshape(-1, WIN), front1.reshape(-1, D), 0, 0)
    middle, gain_front1, shift_front1 = norm_back(normed_grad, unit1, scale1, norm_gain1[0])
    input_grad = (grad + middle).astype(BF16)

    vectors = [
        gain_front1, small1[0], shift_front1, small1[1], small1[2], small1[3],
        gain_front2, small2[0], shift_front2, small2[1], small2[2], small2[3],
        bias_grad1[:, :BAND].reshape(-1), bias_grad1[:, 2 * BAND :].reshape(-1),
        bias_grad2[:, :BAND].reshape(-1), bias_grad2[:, 2 * BAND :].reshape(-1),
        in_order(up_grads1), in_order(up_grads2),
    ]
    vectors = [vector.reshape(-1, min(D, vector.size)) for vector in vectors]
    (attn1,), packed = sum_replicas([attn1], vectors)
    sums, at = [], 0
    for vector in vectors:
        sums.append(packed[at : at + vector.shape[0]].reshape(-1)[: vector.size])
        at += vector.shape[0]
    me = lax.axis_index("mp")

    def mine(vector):
        return lax.dynamic_index_in_dim(vector.reshape(4, -1), me, 0, keepdims=False)

    def pair(i):
        return jnp.stack([sums[i], sums[i + 1]])

    return (
        block_output,
        input_grad,
        pair(0),
        pair(2),
        turned(attn1[BAND : BAND + n_front1].reshape(3, BAND, D)).astype(F32),
        jnp.stack([mine(sums[12]), mine(sums[13])]),
        attn1[:BAND].astype(F32),
        pair(4),
        mats1[0].astype(F32),
        mine(sums[16]),
        mats1[1].astype(F32),
        pair(6),
        pair(8),
        turned(attn2[BAND : 3 * BAND].reshape(2, BAND, D)).astype(F32),
        mine(sums[14]),
        turned(attn2[3 * BAND : BAND + n_front2]).astype(F32),
        mine(sums[15]),
        attn2[:BAND].astype(F32),
        pair(10),
        mats2[0].astype(F32),
        mine(sums[17]),
        mats2[1].astype(F32),
    )


def solution(mesh):
    rows = P(("dp", "ctx", "mp"), None)
    placed = (
        rows, rows, P(("dp", "ctx"), None), P(),
        P(), P(), P(None, None, "mp"), P(None, "mp"), P("mp", None), P(),
        P(None, "mp"), P("mp"), P("mp", None),
        P(), P(), P(None, None, "mp"), P("mp"), P(None, "mp"), P("mp"),
        P("mp", None), P(), P(None, "mp"), P("mp"), P("mp", None),
    )
    given = (
        rows, rows,
        P(), P(), P(None, None, "mp"), P(None, "mp"), P("mp", None), P(),
        P(None, "mp"), P("mp"), P("mp", None),
        P(), P(), P(None, None, "mp"), P("mp"), P(None, "mp"), P("mp"),
        P("mp", None), P(), P(None, "mp"), P("mp"), P("mp", None),
    )
    return jax.shard_map(shards, mesh=mesh, in_specs=placed, out_specs=given, check_vma=False)
```

time: 663 us -> 626 us (0.944)
  Pallas kernels: 458 us -> 427 us
  matrix products: 77.3 us -> 96.5 us
  local copies, waits for them, and re-layouts: 61.7 us -> 47.1 us
  other arithmetic: 53.4 us -> 46.1 us
    dot_general x58, matrix products: 77.3 us -> 96.5 us  [dot(): lax.dot_general(left, right, (((left_dim,), (right_dim,)), ((), ())), pre...]
    pallas_call x4 -> x2, Pallas kernels: 151 us -> 135 us  [project(): pl.pallas_call(functools.partial(front_kernel, rows, int(lead), bool(firs...]
    unnamed x277 -> x187, local copies, waits for them, and re-layouts: 33.5 us -> 19.5 us
    convert_element_type x6 -> x2, other arithmetic: 19.5 us -> 6.71 us  [the longest x1 4.17 us: shards(): mats2[1].astype(F32)]
    pallas_call x2, Pallas kernels: 245 us -> 233 us  [attend_back(): pl.pallas_call(functools.partial(back_kernel, mixed, counts, rows_of_part...]
    concatenate x1 -> x8, other arithmetic: 0.08 us -> 8.86 us  [shards(): jnp.concatenate(pair)]
    another operation x13 -> x1, other arithmetic: 9.52 us -> 0.82 us  [the longest x12 9.34 us: sum_cores(): near, last = swap(jnp.stack([near, last]), 'mp', 1)]
  transfers between devices with their start and end apart: 4 -> 0, of which waited for: 0 -> 0; matrix products, arithmetic and copies ran while one was open for 11% -> 0% of each run, Pallas kernels for 0% -> 0%
where the time goes in v5:
time: 626 us; the launch traced here: 619 us
  Pallas kernels  427 us (68%)
  matrix products  96.5 us (15%)
  local copies, waits for them, and re-layouts  47.1 us (8%)
  other arithmetic  46.1 us (7%)
    pallas_call x2, Pallas kernels, attend_back(): pl.pallas_call(functools.partial(back_kernel, mixed, counts, rows_of_part...  233 us
    pallas_call x2, Pallas kernels, project(): pl.pallas_call(functools.partial(front_kernel, rows, int(lead), bool(firs...  135 us
    dot_general x58, matrix products, dot(): lax.dot_general(left, right, (((left_dim,), (right_dim,)), ((), ())), pre...  96.5 us
    pallas_call x1, Pallas kernels, sum_replicas(): pl.pallas_call(functools.partial(sum_kernel, counts, len(vectors), rows_o...  59.4 us
    unnamed x187, local copies, waits for them, and re-layouts  19.5 us

profile of v5, /device:TPU:0, one launch (start us, length us, event | category | flops | bytes accessed | tf_op | source)
XLA Modules:
  0.0 619.4 jit_solution(18006934769301630846)
XLA Ops:
  0.7 1.4 convert_reduce_fusion.4
  6.1 1.3 convert_reduce_fusion
  7.5 1.5 fusion.26
  12.5 79.8 %front_first.1 = (bf16[4,576,512]{2,1,0:T(8,128)(2,1)}, bf16[4,384,512]{2,1,0:T(8,128)(2,1)}, bf16[4,384,512]{2,1,0:T(8,128)(2,1)}, bf16[4,192,512]{2,1,0:T(8,12...) custom-call(s32[12]{0:T(128)S(1)} %pad_add_fusion.refs_0_, ...), custom_call_target="tpu_custom_call" | custom-call | tf_op jit(solution)/shard_map/front_first/pallas_call | solution.py:383
  94.1 3.5 fusion.266
  97.6 1.8 multiply_reduce_fusion.7
  100.8 2.1 convolution_add_fusion.4
  102.9 2.7 convolution_add_fusion.5
  105.6 2.9 fusion.120
  108.5 2.1 convolution_add_fusion.6
  115.0 1.3 fusion.267
  120.8 54.8 %front_second.1 = (bf16[4,480,512]{2,1,0:T(8,128)(2,1)}, bf16[4,288,512]{2,1,0:T(8,128)(2,1)S(1)}, bf16[4,288,512]{2,1,0:T(8,128)(2,1)S(1)}, bf16[4,192,512]{2,1...) custom-call(s32[12]{0:T(128)S(1)} %pad_add_fusion.refs_0_, ...), custom_call_target="tpu_custom_call" | custom-call | tf_op jit(solution)/shard_map/front_second/pallas_call | solution.py:383
  185.0 2.3 fusion.251
  189.1 2.1 add_convert_fusion
  191.2 2.2 fusion.272
  193.4 2.4 fusion.273
  197.4 2.2 fusion.274
  200.4 1.3 multiply_reduce_fusion
  203.1 1.9 convolution_convert_fusion.19.refs_3_
  205.0 2.0 convolution_convert_fusion.18.refs_4_
  207.0 1.9 convolution_convert_fusion.17.refs_5_
  208.9 2.0 convolution_convert_fusion.16.refs_6_
  210.9 1.8 convolution_convert_fusion.15.refs_7_
  212.8 2.0 convolution_convert_fusion.14.refs_8_
  214.7 1.8 convolution_convert_fusion.13.refs_9_
  216.6 2.2 convolution_convert_fusion.12.refs_10_
  218.7 1.7 convolution_convert_fusion.21
  220.4 102.7 %attend_back.2 = (f32[4,192,512]{2,1,0:T(8,128)}, f32[4,192,512]{2,1,0:T(8,128)}, f32[4,192,512]{2,1,0:T(8,128)}, bf16[4,192,512]{2,1,0:T(8,128)(2,1)}, bf16[4,1...) custom-call(s32[12]{0:T(128)} %copy-done.11, f32[12]{0:T(128)} %convert_element_type.326.refs_1_, s32[1,512]{1,0:T(1,128)} %bitcast.322, ...), custom_call_target="tpu_custom_call" | custom-call | tf_op jit(solution)/shard_map/attend_back/pallas_call | solution.py:848
  323.1 1.3 slice.188
  324.7 1.8 fusion.3
  327.6 2.4 fusion.78
  330.7 1.3 copy-done.35
  332.0 2.2 fusion.269
  334.2 2.2 fusion.270
  338.1 2.2 fusion.253
  341.7 2.2 fusion.271
  345.3 1.6 multiply_reduce_fusion.1
  348.2 1.7 convolution_convert_fusion.1
  352.5 1.8 convolution_convert_fusion.10.refs_4_
  354.3 2.0 convolution_convert_fusion.9.refs_5_
  357.4 1.8 convolution_convert_fusion.8.refs_7_
  359.2 2.0 convolution_convert_fusion.7.refs_8_
  362.3 1.8 convolution_convert_fusion.6.refs_10_
  364.2 2.0 convolution_convert_fusion.5.refs_11_
  367.3 1.9 convolution_convert_fusion.4.refs_13_
  369.2 1.9 convolution_convert_fusion.3.refs_14_
  371.2 1.7 convolution_convert_fusion.20
  372.8 130.4 %attend_back.3 = (f32[4,192,512]{2,1,0:T(8,128)}, f32[4,192,512]{2,1,0:T(8,128)}, f32[4,192,512]{2,1,0:T(8,128)}, bf16[2304,768]{1,0:T(8,128)(2,1)}) custom-call(s32[12]{0:T(128)} %select_reduce_fusion.1.refs_0_, f32[12]{0:T(128)} %convert_element_type.326.refs_1_, s32[1,512]{1,0:T(1,128)} %bitcast.323, bf16[768,768]{1,0:T(8,128)(2,1)} %fusion.91.refs_3_, ...), custom_call_target="tpu_custom_call" | custom-call | tf_op jit(solution)/shard_map/attend_back/pallas_call | solution.py:848
  503.3 1.7 constant_dynamic-update-slice_fusion.2
  505.3 1.3 copy-done.32
  509.0 2.5 fusion.25
  511.5 1.5 fusion.24
  512.9 2.0 convolution_convert_fusion
  529.8 1.8 fusion.2
  534.5 59.4 %sum_replicas.1 = (bf16[768,768]{1,0:T(8,128)(2,1)}, f32[24,768]{1,0:T(8,128)}) custom-call(bf16[768,768]{1,0:T(8,128)(2,1)} %pad_maximum_fusion.1.refs_0_, bf16[768,768]{1,0:T(8,128)(2,1)} %pad_maximum_fusion.2.refs_1_, bf16[768,768]{1,0:T(8,128)(2,1)} %pad_maximum_fusion.3.refs_2_, bf16[768,768]{1,0:T(8,128)(2,1)} %pad_maximum_fusion.4.refs_3_, ...), custom_call_target="tpu_custom_call" | custom-call | tf_op jit(solution)/shard_map/sum_replicas/pallas_call | solution.py:647
  593.9 1.5 fusion.260
  595.4 1.2 slice.194
  596.6 1.4 convert_bitcast_fusion
  599.9 1.3 pad_maximum_fusion.13
  601.1 1.8 slice_convert_fusion.5
  603.0 2.5 slice_convert_fusion.2
  608.7 1.3 constant_dynamic-slice_fusion.2
  612.1 1.2 fusion.248
  614.2 4.2 slice_convert_fusion
  (331 shorter events, 76.8 us)
Async XLA Ops:
  0.7 8.3 %copy-start.23 = (bf16[512,768]{1,0:T(8,128)(2,1)S(1)}, bf16[512,768]{1,0:T(8,128)(2,1)}, u32[]{:S(2)}) copy-start(bf16[512,768]{1,0:T(8,128)(2,1)} %param.24) | copy-start | bytes 2359300
  4.3 116.5 %copy-start.11 = (s32[12]{0:T(128)}, s32[12]{0:T(128)S(1)}, u32[]{:S(2)}) copy-start(s32[12]{0:T(128)S(1)} %pad_add_fusion.refs_0_) | copy-start | bytes 148
  5.2 115.5 %copy-start.10 = (s32[512]{0:T(512)}, s32[512]{0:T(512)S(1)}, u32[]{:S(2)}) copy-start(s32[512]{0:T(512)S(1)} %add_select_fusion) | copy-start | bytes 6148
  6.0 3.4 copy-start.47
  6.0 3.4 copy-start.67
  6.0 4.0 copy-start.70
  6.1 4.0 copy-start.71
  6.1 4.0 copy-start.72
  6.1 4.0 copy-start.73
  6.1 4.1 copy-start.43
  7.5 2.7 copy-start.49
  9.0 2.3 copy-start.2
  9.0 2.3 copy-start.4
  93.3 4.3 copy-start.6
  93.3 4.3 copy-start.8
  97.6 1.9 copy-start.14
  99.8 11.9 %copy-start.41 = (bf16[512,768]{1,0:T(8,128)(2,1)}, bf16[512,768]{1,0:T(8,128)(2,1)S(1)}, u32[]{:S(2)}) copy-start(bf16[512,768]{1,0:T(8,128)(2,1)S(1)} %add_convert_fusion.3) | copy-start | bytes 2359300
  100.0 2.8 copy-start.45
  102.8 11.3 %copy-start.34 = (f32[512,768]{1,0:T(8,128)}, f32[512,768]{1,0:T(8,128)S(1)}, u32[]{:S(2)}) copy-start(f32[512,768]{1,0:T(8,128)S(1)} %convolution_add_fusion.4) | copy-start | bytes 4718596
  102.9 7.7 %slice-start.6 = ((s8[4718592]{0:T(1024)(128)(4,1)}), s8[4194304]{0:T(1024)(128)(4,1)S(1)}, s32[]{:S(2)}) async-start(s8[4718592]{0:T(1024)(128)(4,1)} %bitcast.358), calls=%async_computation.6 | async-start | bytes 8388608
  105.5 3.0 copy-start.80
  105.5 5.0 slice-start.7
  113.0 2.0 copy-start.15
  116.2 59.4 %copy-start.17 = (f32[512,768]{1,0:T(8,128)}, f32[512,768]{1,0:T(8,128)S(1)}, u32[]{:S(2)}) copy-start(f32[512,768]{1,0:T(8,128)S(1)} %get-tuple-element.199) | copy-start | bytes 4718596
  116.7 3.9 copy-start.69
  116.7 4.1 copy-start.3
  120.8 54.9 %copy-start.58 = (f32[768]{0:T(1024)S(1)}, f32[768]{0:T(1024)}, u32[]{:S(2)}) copy-start(f32[768]{0:T(1024)} %get-tuple-element.124) | copy-start | bytes 9220
  175.6 3.2 slice-start.2
  175.7 3.2 slice-start.3
  175.7 4.4 slice-start.4
  177.3 1.5 copy-start.46
  177.3 3.0 slice-start.5
  182.2 1.5 copy-start.40
  202.4 16.3 %copy-start.21 = (f32[512,768]{1,0:T(8,128)}, f32[512,768]{1,0:T(8,128)S(1)}, u32[]{:S(2)}) copy-start(f32[512,768]{1,0:T(8,128)S(1)} %get-tuple-element.140) | copy-start | bytes 4718596
  323.1 1.6 copy-start.27
  324.4 2.2 copy-start.25
  324.7 1.9 copy-start.18
  324.7 2.8 copy-start.30
  324.7 5.9 slice-start.8
  327.6 2.4 copy-start.22
  327.6 3.1 slice-start.9
  330.6 1.4 copy-start.35
  332.0 2.2 copy-start.81
  332.0 4.4 slice-start
  334.1 2.2 slice-start.1
  336.4 1.8 copy-start.77
  343.9 1.4 copy-start.52
  347.5 23.6 %copy-start.19 = (f32[512,768]{1,0:T(8,128)}, f32[512,768]{1,0:T(8,128)S(1)}, u32[]{:S(2)}) copy-start(f32[512,768]{1,0:T(8,128)S(1)} %get-tuple-element.144) | copy-start | bytes 4718596
  351.0 1.5 copy-start.42
  369.2 2.0 copy-start.13
  503.3 1.9 copy-start.33
  506.7 2.2 copy-start.74
  509.0 2.5 copy-start.20
  520.2 9.5 %copy-start.26 = (f32[2,192,512]{2,1,0:T(8,128)S(1)}, f32[2,192,512]{2,1,0:T(8,128)}, u32[]{:S(2)}) copy-start(f32[2,192,512]{2,1,0:T(8,128)} %copy-done.25) | copy-start | bytes 2359300
  520.2 9.5 %copy-start.28 = (f32[4,192,512]{2,1,0:T(8,128)S(1)}, f32[4,192,512]{2,1,0:T(8,128)}, u32[]{:S(2)}) copy-start(f32[4,192,512]{2,1,0:T(8,128)} %get-tuple-element.73) | copy-start | bytes 4718596
  529.7 3.2 copy-start.64
  529.7 3.2 copy-start.65
  529.7 3.2 copy-start.66
  529.7 3.2 copy-start.63
  529.7 4.0 copy-start.60
  529.7 3.9 copy-start.61
  529.8 4.0 copy-start.62
  529.8 4.0 copy-start.59
  596.6 6.3 %copy-start.29 = (bf16[2304,768]{1,0:T(8,128)(2,1)S(1)}, bf16[2304,768]{1,0:T(8,128)(2,1)}, u32[]{:S(2)}) copy-start(bf16[2304,768]{1,0:T(8,128)(2,1)} %get-tuple-element.86) | copy-start | bytes 10616836
  (28 other events, 32.2 us)

commit v6 on v5

--- a/solution.py
+++ b/solution.py
@@ -11,8 +11,9 @@
 HD = 64
 REUSE = 6
 WIN = 512
-EARLY = 4
+EARLY = 5
 CHUNK = 256
+LEAD = 3
 LAG = 2
 HOOK_FIRST, HOOK_SECOND = -3, 0
 GROUP = 3
@@ -97,9 +98,9 @@
     near, far, last = {"mp": flip(mp, 1)}, {"mp": flip(mp, 2)}, {"mp": 3 - mp}
     window = {"ctx": 1 - ctx}
     chunks = chunks_of(lead, more_rows)
-    n_chunks, n_more = len(chunks), len(more_rows)
+    n_chunks, n_more, n_lead = len(chunks), len(more_rows), LEAD * lead
     n_arrays = n_more + lead
-    early, offset = (EARLY, HOOK_FIRST) if lead else (2, HOOK_SECOND)
+    early, offset = (EARLY, HOOK_FIRST) if lead else (4, HOOK_SECOND)
     places, lo_ref, normed = take(3)
     first_values = take(3) if mixed else ()
     front, bias = (None, None) if lead else take(2)
@@ -160,14 +161,15 @@
             there = arrays[a].at[flip(mp, 2), pl.ds(start, rows)]
             return copy(c, 4, there, there, near)
 
-        across(0).start()
-        beside(0).start()
+        for c in range(n_lead):
+            across(c).start()
+            beside(c).start()
         for k in range(2 * lead):
             for way in range(3):
                 whole(k, way).start()
-        for c in range(1, early):
+        for c in range(n_lead, early):
             across(c).start()
-        for c in range(1, n_chunks):
+        for c in range(n_lead, n_chunks):
             beside(c).start()
         if lead:
             arrays[0][mp] = arrays_own[0][...]
@@ -178,8 +180,8 @@
         for late, stage in enumerate(
             ((across, widen), (widen, complete), (complete, hand_on))
         ):
-            a = step + lead - LAG * late
-            if lead <= a < n_chunks:
+            a = step + n_lead - LAG * late
+            if n_lead <= a < n_chunks:
                 stage[0](a).wait_recv()
                 stage[1](a).start()
 
@@ -202,23 +204,28 @@
             for vector in range(2):
                 for way in range(3):
                     whole(vector, way).wait_recv()
-            beside(0).wait_recv()
+            for c in range(n_lead):
+                across(c).wait_recv()
+                widen(c).start()
+            for c in range(n_lead):
+                beside(c).wait_recv()
         if lead and k == 2:
-            across(0).wait_recv()
-            widen(0).start()
-            widen(0).wait_recv()
-            complete(0).start()
-            complete(0).wait_recv()
-            hand_on(0).start()
+            for c in range(n_lead):
+                widen(c).wait_recv()
+                complete(c).start()
+            for c in range(n_lead):
+                complete(c).wait_recv()
+                hand_on(c).start()
         if lead and k == 3:
-            hand_on(0).wait_recv()
+            for c in range(n_lead):
+                hand_on(c).wait_recv()
         column = jnp.transpose(bias[slot])[: cols.shape[1], 0:1]
         cols[slot] = (dot(front[slot, : cols.shape[1]], normed[...], 1, 1) + column).astype(BF16)
         pl.when(sends_on)(lambda: pass_on(slot, {"mp": mp + 1}).start())
         pl.when(sends_window)(lambda: pass_on(slot, window).start())
     for c in range(early, n_chunks):
         across(c).start()
-    steps = n_chunks - lead + 2 * LAG
+    steps = n_chunks - n_lead + 2 * LAG
     for step in range(steps):
         if step + offset < 0:
             gather(step)
@@ -318,7 +325,7 @@
             whole(k, way).wait_send()
     for a in range(n_chunks):
         beside(a).wait_send()
-        if a >= lead:
+        if a >= n_lead:
             beside(a).wait_recv()
             hand_on(a).wait_recv()
         across(a).wait_send()
@@ -352,7 +359,7 @@
 
 
 def chunks_of(lead, more_rows):
-    chunks = [(0, 0, 3 * BAND)] * lead
+    chunks = [(0, k * BAND, BAND) for k in range(LEAD)] * lead
     for array, rows in enumerate(more_rows):
         size = CHUNK if rows % CHUNK == 0 else rows
         chunks += [(array + lead, start, size) for start in range(0, rows, size)]
@@ -409,13 +416,12 @@
 
 class Sums:
     def __init__(self, counts, rows, terms, out, refs):
-        n = len(counts)
         self.counts, self.rows, self.out = counts, rows, out
-        self.owns, self.fars, self.nears, self.lasts = (terms[k * n : k * n + n] for k in range(4))
+        self.owns, self.nears, self.fars, self.lasts = zip(*terms)
         self.from_near, self.from_last = refs[:2]
-        self.mine = self.from_near
-        self.from_y, self.from_x, self.kept, self.from_z = refs[2:6]
-        self.sems = refs[6:]
+        self.mine, self.from_y = self.from_near, out
+        self.from_x, self.kept, self.from_z = refs[2:5]
+        self.sems = refs[5:]
         self.parts = sum(counts)
         self.firsts = [sum(counts[:k]) for k in range(len(counts))]
         self.ctx, self.dp, mp = (lax.axis_index(axis) for axis in ("ctx", "dp", "mp"))
@@ -437,7 +443,6 @@
         return [
             pltpu.VMEM((total, lanes), BF16),
             pltpu.VMEM((total, lanes), BF16),
-            pltpu.VMEM((total, lanes), BF16),
             pltpu.VMEM((total // 2, lanes), BF16),
             pltpu.VMEM((total // 2, lanes), BF16),
             pltpu.VMEM((total // 2, lanes), BF16),
@@ -588,22 +593,25 @@
     lax.fori_loop(0, count, lambda i, _: (step(i), 0)[1], 0)
 
 
-def sum_kernel(counts, n_vectors, rows, *refs):
-    n = 4 * len(counts)
-    shares, terms = refs[:n], refs[n : n + n_vectors]
-    refs = refs[n + n_vectors :]
-    out, vec = refs[:2]
+def sum_kernel(arrays, places, *refs):
+    n_here, n_there = len(arrays.here), len(arrays.there)
+    here, there, refs = refs[:n_here], refs[n_here : n_here + n_there], refs[n_here + n_there :]
+    terms, out, vec = refs[: len(places)], refs[len(places)], refs[len(places) + 1]
     from_vec, v_out, v_in = refs[-3:]
-    sums = Sums(counts, rows, shares, out, refs[2:-3])
+    sums, copies = arrays.open(here, there, out, refs[len(places) + 2 : -3])
     meet(sums.partners)
-    at = 0
-    for term in terms:
-        vec[at : at + term.shape[0], : term.shape[1]] = term[...]
-        at += term.shape[0]
+    mp = lax.axis_index("mp")
+    slots = (mp, flip(mp, 1), flip(mp, 2), 3 - mp)
+    vec[...] = jnp.zeros_like(vec)
+    for term, (row, distance) in zip(terms, places, strict=True):
+        at = row if distance is None else row + slots[distance]
+        vec[pl.ds(at, 1), : term.shape[0]] = term[...].reshape(1, term.shape[0])
     for hop, partner in enumerate(sums.partners):
         copy = remote(vec, from_vec.at[hop], v_out.at[hop], v_in.at[hop], partner)
         copy.start()
         if hop == 0:
+            for own_copy in copies:
+                own_copy.wait()
             sums.start()
         copy.wait()
         vec[...] = vec[...] + from_vec[hop]
@@ -615,51 +623,87 @@
     return max(128, 32 * lax.axis_size("dp"))
 
 
-def padded(arrays):
-    rows = rows_of_part()
-    terms = [
-        [jnp.pad(v, ((0, -v.shape[0] % rows), (0, 0))) for v in part]
-        for part in zip(*arrays, strict=True)
-    ]
-    own, near, far, last = terms
-    counts = [v.shape[0] // rows for v in own]
-    bits = (lax.axis_size("dp") - 1).bit_length()
-    total = sum(counts) * rows
-    shape = jax.ShapeDtypeStruct((total, own[0].shape[1]), BF16)
-    scratch = Sums.scratch(total, sum(counts), bits, shape.shape[1])
-    return own + far, near + last, counts, bits, shape, scratch
-
-
-def unpadded(stack, arrays):
-    shares, at = [], 0
-    for own, *_ in arrays:
-        shares.append(stack[at : at + own.shape[0]])
-        at += own.shape[0] + -own.shape[0] % rows_of_part()
-    return shares
+class Arrays:
+    def __init__(self, arrays):
+        self.rows, self.bits = rows_of_part(), (lax.axis_size("dp") - 1).bit_length()
+        self.pieces = [(v[0] if isinstance(v, tuple) else v).shape[-2] for v in arrays]
+        if self.rows > 512:
+            quads = [v if isinstance(v, tuple) else by_distance(v) for v in arrays]
+            arrays = [tuple(jnp.concatenate(part) for part in zip(*quads, strict=True))]
+        self.stacked = [not isinstance(array, tuple) for array in arrays]
+        first = [array if stacked else array[0] for array, stacked in zip(arrays, self.stacked)]
+        self.sizes = [v.shape[-2] for v in first]
+        self.counts = [-(-size // self.rows) for size in self.sizes]
+        filled = [
+            tuple(self.fill(v) for v in array) if isinstance(array, tuple) else self.fill(array)
+            for array in arrays
+        ]
+        self.here = [v for array in filled if isinstance(array, tuple) for v in array[::2]]
+        self.there = []
+        for array in filled:
+            self.there += array[1::2] if isinstance(array, tuple) else [array]
+        total, lanes = sum(self.counts) * self.rows, first[0].shape[-1]
+        self.shape = jax.ShapeDtypeStruct((total, lanes), BF16)
+        self.scratch = []
+        for count, stacked in zip(self.counts, self.stacked):
+            if stacked:
+                self.scratch.append(pltpu.VMEM((2, count * self.rows, lanes), BF16))
+                self.scratch.append(pltpu.SemaphoreType.DMA((2,)))
+        self.scratch += Sums.scratch(total, sum(self.counts), self.bits, lanes)
+
+    def fill(self, value):
+        missing = -value.shape[-2] % self.rows
+        return jnp.pad(value, [(0, 0)] * (value.ndim - 2) + [(0, missing), (0, 0)])
+
+    def split(self, stack):
+        shares, at = [], 0
+        merged = len(self.pieces) > len(self.sizes)
+        for k, size in enumerate(self.pieces):
+            shares.append(stack[at : at + size])
+            at += size if merged else self.counts[k] * self.rows
+        return shares
+
+    def open(self, here, there, out, refs):
+        here, there, refs = list(here), list(there), list(refs)
+        mp = lax.axis_index("mp")
+        terms, copies = [], []
+        for stacked in self.stacked:
+            if not stacked:
+                own, far = here.pop(0), here.pop(0)
+                terms.append((own, there.pop(0), far, there.pop(0)))
+                continue
+            stack, place, sems = there.pop(0), refs.pop(0), refs.pop(0)
+            for k, slot in enumerate((mp, flip(mp, 2))):
+                copies.append(pltpu.make_async_copy(stack.at[slot], place.at[k], sems.at[k]))
+                copies[-1].start()
+            terms.append((place.at[0], stack.at[flip(mp, 1)], place.at[1], stack.at[3 - mp]))
+        return Sums(self.counts, self.rows, terms, out, refs), copies
 
 
 def sum_replicas(arrays, vectors):
-    here, there, counts, bits, shape, scratch = padded(arrays)
+    arrays = Arrays(arrays)
     place = pl.BlockSpec(memory_space=pltpu.VMEM)
     away = pl.BlockSpec(memory_space=pl.ANY)
     dma = pltpu.SemaphoreType.DMA
-    rows = sum(v.shape[0] for v in vectors)
+    hops = 3 + arrays.bits
     stack, summed = pl.pallas_call(
-        functools.partial(sum_kernel, counts, len(vectors), rows_of_part()),
-        out_shape=[shape, jax.ShapeDtypeStruct((rows, D), F32)],
-        in_specs=[place] * len(here) + [away] * len(there) + [place] * len(vectors),
+        functools.partial(sum_kernel, arrays, [v[1:] for v in vectors]),
+        out_shape=[arrays.shape, jax.ShapeDtypeStruct((len(vectors), D), F32)],
+        in_specs=[place] * len(arrays.here)
+        + [away] * len(arrays.there)
+        + [place] * len(vectors),
         out_specs=[place, place],
-        scratch_shapes=scratch
-        + [pltpu.VMEM((3 + bits, rows, D), F32), dma((3 + bits,)), dma((3 + bits,))],
+        scratch_shapes=arrays.scratch
+        + [pltpu.VMEM((hops, len(vectors), D), F32), dma((hops,)), dma((hops,))],
         compiler_params=pltpu.CompilerParams(
             collective_id=0, has_side_effects=True, vmem_limit_bytes=56 * 1024 * 1024
         ),
         name="sum_replicas",
-    )(*here, *there, *vectors)
-    return unpadded(stack, arrays), summed
-
-
-def back_kernel(mixed, counts, rows, *refs):
+    )(*arrays.here, *arrays.there, *(v[0] for v in vectors))
+    return arrays.split(stack), summed
+
+
+def back_kernel(mixed, arrays, *refs):
     refs = list(refs)
 
     def take(count):
@@ -668,14 +712,14 @@
         return taken
 
     places, flags, lo_ref = take(3)
-    shares, away = take(4 * len(counts)), take(9)
-    dq_ref, dk_ref, dv_ref = take(3)
+    here, there, away = take(len(arrays.here)), take(len(arrays.there)), take(9)
+    (dcols,) = take(1)
     if mixed:
-        dv_before, dv_earlier = take(2)
+        dv_ref, dv_before, dv_earlier = take(3)
     (out,) = take(1)
     if not mixed:
-        dv_before, dv_earlier = take(2)
-    dk_before, dk_earlier = take(2)
+        dv_ref, dv_before, dv_earlier = take(3)
+    dk_ref, dk_before, dk_earlier = take(3)
     near_k, near_v, far_k, far_v, home_k, home_v = take(6)
     values, acc_k, acc_v, acc_q = take(4)
     kv_out, kv_in = take(2)
@@ -688,12 +732,14 @@
         load.start()
     cols, before, earlier, *others, exact, grad_ref, sum_ref = fetched
     first_values, given = (others, ()) if mixed else ((), others)
-    sums = Sums(counts, rows, shares, out, refs)
+    sums, copies = arrays.open(here, there, out, refs)
 
     ctx, mp = lax.axis_index("ctx"), lax.axis_index("mp")
     sees_one = (mp >= 2) | ((mp == 0) & (ctx == 1))
     sees_two = mp == 3
     meet(sums.partners + [{"mp": 3 - mp}])
+    for copy in copies:
+        copy.wait()
     sums.start()
     keys = ((earlier, 0), (before, 0), (cols, BAND))
 
@@ -769,7 +815,7 @@
                 else:
                     pl.when(sees_one if kt >= 2 else sees_two)(functools.partial(tile, kt))
             for j in range(GROUP):
-                dq_ref[g, j * HD : (j + 1) * HD, tokens] = acc_q[j] * SCALE
+                dcols[g, j * HD : (j + 1) * HD, tokens] = (acc_q[j] * SCALE).astype(BF16)
             sums.step(2 * g + t)
         results = ((dk_earlier, dv_earlier), (dk_before, dv_before), (dk_ref, dv_ref))
         for part, (dk, dv) in enumerate(results):
@@ -819,6 +865,20 @@
 
     pl.when((mp == 1) | ((mp == 0) & (ctx == 0)))(lambda: each(4, arrive))
 
+    def round_off(g):
+        dcols[g, BAND : 2 * BAND, :] = dk_ref[g].astype(BF16)
+        if not mixed:
+            dcols[g, 2 * BAND : 3 * BAND, :] = dv_ref[g].astype(BF16)
+
+    each(4, round_off)
+    wide = BAND // 2 if mixed else BAND
+    for slot in range(4):
+        if mixed:
+            half = slice(slot % 2 * wide, (slot % 2 + 1) * wide)
+            dcols[slot, 2 * BAND : 2 * BAND + wide, :] = dv_ref[2 + slot // 2, half, :].astype(BF16)
+        rest = dcols.shape[1] - 2 * BAND - wide
+        dcols[slot, 2 * BAND + wide :, :] = jnp.zeros((rest, WIN), BF16)
+
     def sent_last(g):
         pair(g, lambda step: from_last(g, step).wait_send(), 0)
         pair(g, lambda step: from_last(g, step).wait_send(), 2)
@@ -834,7 +894,7 @@
 
 def attend_back(places, flags, low, front, firsts, given, exact, grad_heads, lse, arrays):
     mixed = bool(firsts)
-    here, there, counts, bits, shape, scratch = padded(arrays)
+    arrays = Arrays(arrays)
     place = pl.BlockSpec(memory_space=pltpu.VMEM)
     away = pl.BlockSpec(memory_space=pl.ANY)
     scalar = pl.BlockSpec(memory_space=pltpu.SMEM)
@@ -843,16 +903,20 @@
     fetched = [*front, *by_head, exact, grad_heads, lse]
     wide = jax.ShapeDtypeStruct((4, BAND, WIN), F32)
     slim = jax.ShapeDtypeStruct((4, BAND, WIN), BF16)
-    outs = [wide] * 3 + ([slim] * 2 if mixed else []) + [shape]
-    block = pltpu.VMEM((4, BAND, WIN), BF16)
+    n_cols = -(-(5 * BAND // 2 if mixed else 3 * BAND) // 128) * 128
+    outs = [jax.ShapeDtypeStruct((4, n_cols, WIN), BF16)]
+    outs += ([wide, slim, slim] if mixed else []) + [arrays.shape]
+    block, full = pltpu.VMEM((4, BAND, WIN), BF16), pltpu.VMEM((4, BAND, WIN), F32)
     results = pl.pallas_call(
-        functools.partial(back_kernel, mixed, counts, rows_of_part()),
+        functools.partial(back_kernel, mixed, arrays),
         out_shape=outs,
         in_specs=[scalar, scalar, place]
-        + [place] * len(here)
-        + [away] * (len(there) + len(fetched)),
+        + [place] * len(arrays.here)
+        + [away] * (len(arrays.there) + len(fetched)),
         out_specs=[place] * len(outs),
-        scratch_shapes=[block] * (8 if mixed else 10)
+        scratch_shapes=([] if mixed else [full, block, block])
+        + [full]
+        + [block] * 8
         + [
             pltpu.VMEM((3, BAND, WIN), BF16),
             pltpu.VMEM((TILES, BAND, TILE), F32),
@@ -863,15 +927,15 @@
         ]
         + [pltpu.VMEM(v.shape, v.dtype) for v in fetched]
         + [dma((len(fetched),))]
-        + scratch,
+        + arrays.scratch,
         compiler_params=pltpu.CompilerParams(
             collective_id=3 if mixed else 4,
             has_side_effects=True,
-            vmem_limit_bytes=60 * 1024 * 1024,
+            vmem_limit_bytes=(46 if mixed and arrays.bits < 5 else 60) * 1024 * 1024,
         ),
         name="attend_back",
-    )(places, flags, low, *here, *there, *fetched)
-    return results[:-1], unpadded(results[-1], arrays)
+    )(places, flags, low, *arrays.here, *arrays.there, *fetched)
+    return results[:-1], arrays.split(results[-1])
 
 
 def gelu(hidden):
@@ -986,89 +1050,68 @@
     grad, rounded, grad_heads, mats2, up_grads2, small2 = tail_backward(
         cotangent.astype(F32), kept2, outs2, norm_gain2, ups2, downs2
     )
-    (dq2, dk2, dv2, dv2_before, dv2_earlier), mats2 = attend_back(
+    (dcols2, dv2, dv2_before, dv2_earlier), mats2 = attend_back(
         places2, flags, low, front_kv2, front_kv1, (), exact2,
         grad_heads.reshape(4, BAND, WIN), sums2, list(zip(*mats2, strict=True)),
     )
     grad_out2 = dot(heads2.reshape(D, WIN), rounded, 1, 0).astype(BF16).reshape(4, BAND, D)
-
-    dcols2 = jnp.concatenate([dq2, dk2, dv2[2:].reshape(4, BAND // 2, WIN)], axis=1)
-    bias_grad2 = jnp.sum(dcols2, axis=2)
-    dcols2 = dcols2.astype(BF16)
-    grad_front2 = dot(dcols2.reshape(-1, WIN), normed2, 1, 0).astype(BF16).reshape(4, n_front2, D)
-    attn2 = [
-        jnp.concatenate(pair)
-        for pair in zip(by_distance(grad_out2), by_distance(grad_front2), strict=True)
-    ]
-    normed_grad = dot(dcols2.reshape(-1, WIN), front2.reshape(-1, D), 0, 0)
+    bias_grad2 = jnp.sum(dcols2.astype(F32), axis=2)
+    grad_front2 = dot(dcols2.reshape(-1, WIN), normed2, 1, 0).astype(BF16).reshape(4, -1, D)
+    normed_grad = dot(dcols2[:, :n_front2].reshape(-1, WIN), front2.reshape(-1, D), 0, 0)
     middle, gain_front2, shift_front2 = norm_back(normed_grad, unit2, scale2, norm_gain2[0])
     grad = grad + middle
 
     grad, rounded, grad_heads, mats1, up_grads1, small1 = tail_backward(
         grad, kept1, outs1, norm_gain1, ups1, downs1
     )
-    arrays = [attn2] + list(zip(*mats1, strict=True))
-    (dq1, dk1, dv1), (attn2, *mats1) = attend_back(
+    grad_out1 = dot(heads1.reshape(D, WIN), rounded, 1, 0).astype(BF16).reshape(4, BAND, D)
+    arrays = [grad_front2, jnp.concatenate([grad_out2, grad_out1], axis=1)]
+    (dcols1,), (front_sum2, out_sums, *mats1) = attend_back(
         taker, flags, low, front_kv1, (), (dv2, dv2_before, dv2_earlier), exact1,
-        grad_heads.reshape(4, BAND, WIN), sums1, arrays,
-    )
-    grad_out1 = dot(heads1.reshape(D, WIN), rounded, 1, 0).astype(BF16).reshape(4, BAND, D)
-
-    dcols1 = jnp.concatenate([dq1, dk1, dv1], axis=1)
-    bias_grad1 = jnp.sum(dcols1, axis=2)
-    dcols1 = dcols1.astype(BF16)
-    grad_front1 = dot(dcols1.reshape(-1, WIN), normed1, 1, 0).astype(BF16).reshape(4, n_front1, D)
-    attn1 = [
-        jnp.concatenate(pair)
-        for pair in zip(by_distance(grad_out1), by_distance(grad_front1), strict=True)
-    ]
-    normed_grad = dot(dcols1.reshape(-1, WIN), front1.reshape(-1, D), 0, 0)
+        grad_heads.reshape(4, BAND, WIN), sums1, arrays + list(zip(*mats1, strict=True)),
+    )
+    bias_grad1 = jnp.sum(dcols1.astype(F32), axis=2)
+    grad_front1 = dot(dcols1.reshape(-1, WIN), normed1, 1, 0).astype(BF16).reshape(4, -1, D)
+    normed_grad = dot(dcols1[:, :n_front1].reshape(-1, WIN), front1.reshape(-1, D), 0, 0)
     middle, gain_front1, shift_front1 = norm_back(normed_grad, unit1, scale1, norm_gain1[0])
     input_grad = (grad + middle).astype(BF16)
 
-    vectors = [
+    singles = [
         gain_front1, small1[0], shift_front1, small1[1], small1[2], small1[3],
         gain_front2, small2[0], shift_front2, small2[1], small2[2], small2[3],
-        bias_grad1[:, :BAND].reshape(-1), bias_grad1[:, 2 * BAND :].reshape(-1),
-        bias_grad2[:, :BAND].reshape(-1), bias_grad2[:, 2 * BAND :].reshape(-1),
-        in_order(up_grads1), in_order(up_grads2),
+        bias_grad1[:, :BAND].reshape(-1), bias_grad1[:, 2 * BAND : n_front1].reshape(-1),
+        bias_grad2[:, :BAND].reshape(-1), bias_grad2[:, 2 * BAND : n_front2].reshape(-1),
     ]
-    vectors = [vector.reshape(-1, min(D, vector.size)) for vector in vectors]
-    (attn1,), packed = sum_replicas([attn1], vectors)
-    sums, at = [], 0
-    for vector in vectors:
-        sums.append(packed[at : at + vector.shape[0]].reshape(-1)[: vector.size])
-        at += vector.shape[0]
-    me = lax.axis_index("mp")
-
-    def mine(vector):
-        return lax.dynamic_index_in_dim(vector.reshape(4, -1), me, 0, keepdims=False)
-
-    def pair(i):
-        return jnp.stack([sums[i], sums[i + 1]])
+    vectors = [(vector, row, None) for row, vector in enumerate(singles)]
+    for row, shares in ((16, up_grads1), (20, up_grads2)):
+        vectors += [(vector, row, distance) for distance, vector in enumerate(shares)]
+    (front_sum1,), sums = sum_replicas([grad_front1], vectors)
+
+    def mine(vectors):
+        return lax.dynamic_index_in_dim(vectors.reshape(4, -1), me, 0, keepdims=False)
 
     return (
         block_output,
         input_grad,
-        pair(0),
-        pair(2),
-        turned(attn1[BAND : BAND + n_front1].reshape(3, BAND, D)).astype(F32),
+        sums[0:2],
+        sums[2:4],
+        turned(front_sum1[:n_front1].reshape(3, BAND, D)).astype(F32),
         jnp.stack([mine(sums[12]), mine(sums[13])]),
-        attn1[:BAND].astype(F32),
-        pair(4),
+        out_sums[BAND:].astype(F32),
+        sums[4:6],
         mats1[0].astype(F32),
-        mine(sums[16]),
+        mine(sums[16:20]),
         mats1[1].astype(F32),
-        pair(6),
-        pair(8),
-        turned(attn2[BAND : 3 * BAND].reshape(2, BAND, D)).astype(F32),
+        sums[6:8],
+        sums[8:10],
+        turned(front_sum2[: 2 * BAND].reshape(2, BAND, D)).astype(F32),
         mine(sums[14]),
-        turned(attn2[3 * BAND : BAND + n_front2]).astype(F32),
-        mine(sums[15]),
-        attn2[:BAND].astype(F32),
-        pair(10),
+        turned(front_sum2[2 * BAND : n_front2]).astype(F32),
+        mine(sums[15, : D // 2]),
+        out_sums[:BAND].astype(F32),
+        sums[10:12],
         mats2[0].astype(F32),
-        mine(sums[17]),
+        mine(sums[20:24]),
         mats2[1].astype(F32),
     )
 

time: 626 us -> 597 us (0.954)
  local copies, waits for them, and re-layouts: 47.1 us -> 26.4 us
  other arithmetic: 46.1 us -> 37.5 us
  matrix products: 96.5 us -> 105 us
  Pallas kernels: 427 us -> 419 us
    unnamed x187 -> x149, local copies, waits for them, and re-layouts: 19.5 us -> 11.3 us
    dot_general x58, matrix products: 96.5 us -> 105 us  [dot(): lax.dot_general(left, right, (((left_dim,), (right_dim,)), ((), ())), pre...]
    concatenate x10 -> x1, other arithmetic: 8.88 us -> 1.56 us  [shards(): arrays = [grad_front2, jnp.concatenate([grad_out2, grad_out1], axis=1)]]
where the time goes in v6:
time: 597 us; the launch traced here: 590 us
  Pallas kernels  419 us (70%)
  matrix products  105 us (18%)
  other arithmetic  37.5 us (6%)
  local copies, waits for them, and re-layouts  26.4 us (4%)
    pallas_call x2, Pallas kernels, attend_back(): pl.pallas_call(functools.partial(back_kernel, mixed, arrays), out_shape=o...  238 us
    pallas_call x2, Pallas kernels, project(): pl.pallas_call(functools.partial(front_kernel, rows, int(lead), bool(firs...  128 us
    dot_general x58, matrix products, dot(): lax.dot_general(left, right, (((left_dim,), (right_dim,)), ((), ())), pre...  105 us
    pallas_call x1, Pallas kernels, sum_replicas(): pl.pallas_call(functools.partial(sum_kernel, arrays, [v[1:] for v in vect...  52.6 us

profile of v6, /device:TPU:0, one launch (start us, length us, event | category | flops | bytes accessed | tf_op | source)
XLA Modules:
  0.0 590.2 jit_solution(14135196453394024234)
XLA Ops:
  0.7 1.4 convert_reduce_fusion.6
  2.0 1.4 convert_reduce_fusion.12
  6.7 1.3 convert_reduce_fusion.2
  8.1 1.5 fusion.19
  10.8 1.1 fusion.149.refs_8_
  12.0 73.8 %front_first.1 = (bf16[4,576,512]{2,1,0:T(8,128)(2,1)}, bf16[4,384,512]{2,1,0:T(8,128)(2,1)}, bf16[4,384,512]{2,1,0:T(8,128)(2,1)}, bf16[4,192,512]{2,1,0:T(8,12...) custom-call(s32[12]{0:T(128)S(1)} %pad_add_fusion.refs_0_, ...), custom_call_target="tpu_custom_call" | custom-call | tf_op jit(solution)/shard_map/front_first/pallas_call | solution.py:390
  89.1 3.7 fusion.246
  92.8 1.8 multiply_reduce_fusion.7
  94.7 1.2 add_convert_fusion.3
  97.3 2.4 convolution_add_fusion.4
  99.7 2.7 convolution_add_fusion.5
  102.4 2.9 fusion.109
  105.3 2.1 convolution_add_fusion.6
  107.4 1.1 fusion.118
  109.8 1.1 fusion.230
  111.8 1.3 fusion.247
  117.4 54.5 %front_second.1 = (bf16[4,480,512]{2,1,0:T(8,128)(2,1)}, bf16[4,288,512]{2,1,0:T(8,128)(2,1)S(1)}, bf16[4,288,512]{2,1,0:T(8,128)(2,1)S(1)}, bf16[4,192,512]{2,1...) custom-call(s32[12]{0:T(128)S(1)} %pad_add_fusion.refs_0_, ...), custom_call_target="tpu_custom_call" | custom-call | tf_op jit(solution)/shard_map/front_second/pallas_call | solution.py:390
  174.0 1.1 copy-done.36
  181.3 2.3 fusion.232
  183.5 1.1 fusion.231
  185.4 2.1 add_convert_fusion
  187.6 2.2 fusion.254
  189.8 2.4 fusion.253
  193.7 2.2 fusion.252
  196.7 1.9 multiply_reduce_fusion
  198.7 1.3 fusion.236
  203.6 1.8 convolution_convert_fusion.15.refs_7_
  205.4 1.8 convolution_convert_fusion.14.refs_8_
  207.3 2.0 convolution_convert_fusion.13.refs_9_
  209.3 2.0 convolution_convert_fusion.12.refs_10_
  212.3 101.0 %attend_back.2 = (bf16[4,512,512]{2,1,0:T(8,128)(2,1)}, f32[4,192,512]{2,1,0:T(8,128)}, bf16[4,192,512]{2,1,0:T(8,128)(2,1)S(1)}, bf16[4,192,512]{2,1,0:T(8,128)(2,1)S(1)}, bf16[1536,768]{1,0:T(8,128)(2,1)}) custom-call(s32[12]{0:T(128)S(1)} %pad_add_fusion.refs_0_, f32[12]{0:T(128)S(1)} %convert_element_type.313.refs_1_, s32[1,512]{1,0:T(1,128)S(1)} %bitcast.290, ...), custom_call_target="tpu_custom_call" | custom-call | tf_op jit(solution)/shard_map/attend_back/pallas_call | solution.py:910
  313.3 5.9 fusion.71
  319.2 1.1 fusion.237
  320.5 3.6 fusion.251
  324.1 2.2 fusion.250
  328.1 2.2 fusion.234
  331.6 2.1 fusion.249
  334.6 1.8 multiply_reduce_fusion.1
  336.4 1.2 fusion.238
  338.1 1.8 convolution_convert_fusion.11.refs_3_
  339.9 1.8 convolution_convert_fusion.10.refs_4_
  341.8 2.0 convolution_convert_fusion.9.refs_5_
  343.7 2.0 convolution_convert_fusion.8.refs_6_
  345.7 3.5 convolution_convert_fusion.1
  350.8 1.6 pad_maximum_fusion.refs_8_
  352.3 1.8 convolution_convert_fusion.5.refs_9_
  354.1 1.8 convolution_convert_fusion.4.refs_10_
  356.0 2.0 convolution_convert_fusion.3.refs_11_
  358.0 2.0 convolution_convert_fusion.2.refs_12_
  360.0 1.7 convolution_convert_fusion.20
  361.7 137.4 %attend_back.3 = (bf16[4,640,512]{2,1,0:T(8,128)(2,1)}, bf16[2432,768]{1,0:T(8,128)(2,1)}) custom-call(s32[12]{0:T(128)} %select_reduce_fusion.1.refs_0_, f32[12]{0:T(128)} %copy-done.12, s32[1,512]{1,0:T(1,128)} %bitcast.291, bf16[768,768]{1,0:T(8,128)(2,1)} %convolution_convert_fusion.11.refs_3_, bf16[768,768]{1,0:T(8,128)(2,1)} %convolution_convert_fusion.10.refs_4_, ...), custom_call_target="tpu_custom_call" | custom-call | tf_op jit(solution)/shard_map/attend_back/pallas_call | solution.py:910
  499.1 5.8 fusion.18
  504.9 1.4 fusion.17
  507.0 4.1 convolution_convert_fusion
  514.5 52.6 %sum_replicas.1 = (bf16[640,768]{1,0:T(8,128)(2,1)}, f32[24,768]{1,0:T(8,128)}) custom-call(bf16[4,640,768]{2,1,0:T(8,128)(2,1)} %bitcast.303, f32[768]{0:T(1024)} %get-tuple-element.88.refs_1_, f32[768]{0:T(1024)} %get-tuple-element.86.refs_2_, f32[768]{0:T(1024)} %get-tuple-element.97.refs_3_, f32[768]{0:T(1024)} %get-tuple-element.96.refs_4_, ...), custom_call_target="tpu_custom_call" | custom-call | tf_op jit(solution)/shard_map/sum_replicas/pallas_call | solution.py:689
  567.1 1.5 fusion.240
  568.7 1.2 slice.199
  569.9 1.4 convert_bitcast_fusion
  572.9 2.1 slice_convert_fusion.4
  575.0 4.2 slice_convert_fusion.2
  580.6 1.3 slice.209
  581.9 1.1 convert_bitcast_fusion.1
  583.6 1.6 convert_bitcast_fusion.2
  586.6 2.5 slice_convert_fusion
  (250 shorter events, 47.1 us)
Async XLA Ops:
  5.7 3.8 copy-start.17
  5.8 206.5 %copy-start.11 = (s32[512]{0:T(512)}, s32[512]{0:T(512)S(1)}, u32[]{:S(2)}) copy-start(s32[512]{0:T(512)S(1)} %add_select_fusion) | copy-start | bytes 6148
  6.6 3.4 copy-start.37
  6.6 3.4 copy-start.50
  6.7 4.0 copy-start.53
  6.7 4.0 copy-start.54
  6.7 4.0 copy-start.55
  6.7 4.0 copy-start.56
  6.7 4.1 copy-start.33
  8.1 2.7 copy-start.39
  9.6 1.2 copy-start.43
  9.6 2.4 copy-start.2
  9.6 2.4 copy-start.4
  9.6 2.4 copy-start.5
  92.8 1.9 copy-start.15
  94.7 2.6 copy-start.41
  97.2 2.4 copy-start.31
  99.6 220.8 %copy-start.24 = (f32[512,768]{1,0:T(8,128)}, f32[512,768]{1,0:T(8,128)S(1)}, u32[]{:S(2)}) copy-start(f32[512,768]{1,0:T(8,128)S(1)} %convolution_add_fusion.4) | copy-start | bytes 4718596
  99.7 7.7 %slice-start.6 = ((s8[4718592]{0:T(1024)(128)(4,1)}), s8[4194304]{0:T(1024)(128)(4,1)S(1)}, s32[]{:S(2)}) async-start(s8[4718592]{0:T(1024)(128)(4,1)} %bitcast.321), calls=%async_computation.6 | async-start | bytes 8388608
  102.3 3.0 copy-start.62
  102.3 5.0 slice-start.7
  107.4 1.1 copy-start.60
  108.5 1.3 copy-start.28
  109.8 1.1 copy-start.58
  109.8 2.0 copy-start.16
  109.8 2.0 copy-start.46
  111.8 1.3 copy-start.47
  111.8 1.3 copy-start.48
  113.4 3.7 copy-start.52
  113.5 3.9 copy-start.3
  117.4 54.6 %copy-start.49 = (f32[768]{0:T(1024)S(1)}, f32[768]{0:T(1024)}, u32[]{:S(2)}) copy-start(f32[768]{0:T(1024)} %get-tuple-element.110) | copy-start | bytes 9220
  171.9 1.4 copy-start.1
  171.9 3.3 slice-start.2
  172.0 3.2 slice-start.3
  172.0 4.4 slice-start.4
  173.6 1.5 copy-start.36
  173.6 3.0 slice-start.5
  178.5 1.3 copy-start.26
  178.5 1.5 copy-start.30
  180.0 1.3 copy-start.27
  198.7 1.3 copy-start.57
  200.1 12.2 %copy-start.12 = (f32[12]{0:T(128)}, f32[12]{0:T(128)S(1)}, u32[]{:S(2)}) copy-start(f32[12]{0:T(128)S(1)} %convert_element_type.313.refs_1_) | copy-start | bytes 148
  313.3 5.9 %copy-start.8 = (bf16[4,192,512]{2,1,0:T(8,128)(2,1)}, bf16[4,192,512]{2,1,0:T(8,128)(2,1)S(1)}, u32[]{:S(2)}) copy-start(bf16[4,192,512]{2,1,0:T(8,128)(2,1)S(1)} %get-tuple-element.72) | copy-start | bytes 2359300
  313.3 5.9 %copy-start.9 = (bf16[4,192,512]{2,1,0:T(8,128)(2,1)}, bf16[4,192,512]{2,1,0:T(8,128)(2,1)S(1)}, u32[]{:S(2)}) copy-start(bf16[4,192,512]{2,1,0:T(8,128)(2,1)S(1)} %get-tuple-element.71) | copy-start | bytes 2359300
  313.3 10.8 %slice-start.8 = ((s8[4718592]{0:T(1024)(128)(4,1)}), s8[4194304]{0:T(1024)(128)(4,1)S(1)}, s32[]{:S(2)}) async-start(s8[4718592]{0:T(1024)(128)(4,1)} %bitcast.323), calls=%async_computation.8 | async-start | bytes 8388608
  319.2 4.9 slice-start.9
  320.5 3.6 copy-start.63
  320.5 5.8 slice-start
  324.1 2.2 slice-start.1
  326.3 1.3 copy-start.29
  326.3 1.8 copy-start.59
  330.2 1.4 copy-start.61
  336.4 1.8 copy-start.32
  343.7 2.0 copy-start.22
  345.7 3.5 copy-start.7
  356.0 2.0 copy-start.25
  358.0 2.0 copy-start.14
  361.7 137.4 %copy-start.18 = (bf16[512,768]{1,0:T(8,128)(2,1)S(1)}, bf16[512,768]{1,0:T(8,128)(2,1)}, u32[]{:S(2)}) copy-start(bf16[512,768]{1,0:T(8,128)(2,1)} %param.24) | copy-start | bytes 2359300
  361.7 137.4 %copy-start.38 = (f32[768]{0:T(1024)S(1)}, f32[768]{0:T(1024)}, u32[]{:S(2)}) copy-start(f32[768]{0:T(1024)} %copy-done.37) | copy-start | bytes 9220
  361.7 137.4 %copy-start.40 = (f32[512]{0:T(512)S(1)}, f32[512]{0:T(512)}, u32[]{:S(2)}) copy-start(f32[512]{0:T(512)} %copy-done.39) | copy-start | bytes 6148
  361.7 137.4 %copy-start.44 = (f32[512]{0:T(512)S(1)}, f32[512]{0:T(512)}, u32[]{:S(2)}) copy-start(f32[512]{0:T(512)} %copy-done.43) | copy-start | bytes 6148
  504.9 2.0 copy-start.19
  511.1 1.8 copy-start.23
  580.6 6.0 %copy-start.20 = (bf16[1536,768]{1,0:T(8,128)(2,1)S(1)}, bf16[1536,768]{1,0:T(8,128)(2,1)}, u32[]{:S(2)}) copy-start(bf16[1536,768]{1,0:T(8,128)(2,1)} %get-tuple-element.81) | copy-start | bytes 7077892
  (10 other events, 8.5 us)

commit v7 on v6

--- a/solution.py
+++ b/solution.py
@@ -172,7 +172,9 @@
         for c in range(n_lead, n_chunks):
             beside(c).start()
         if lead:
-            arrays[0][mp] = arrays_own[0][...]
+            n_front = arrays_own[0].shape[0]
+            arrays[0][mp, :n_front] = arrays_own[0][...]
+            arrays[0][:, n_front:] = jnp.zeros((4, arrays[0].shape[1] - n_front, D), BF16)
         for k in range(2 * lead):
             vectors[k][mp] = vectors_own[k][...]
 
@@ -385,6 +387,8 @@
     ] + [dma((4,))] * 4
     gathered = ([bias, small, front] if lead else []) + list(more)
     gathered = [jax.ShapeDtypeStruct((4,) + v.shape, v.dtype) for v in gathered]
+    if lead:
+        gathered[2] = jax.ShapeDtypeStruct((4, -(-n_cols // 128) * 128, D), BF16)
     rows = [v.shape[0] for v in more]
     scratch += [dma((len(chunks_of(lead, rows)), 5))] * 2 + ([dma((2, 3))] * 2 if lead else [])
     return pl.pallas_call(
@@ -397,7 +401,7 @@
         compiler_params=pltpu.CompilerParams(
             collective_id=1 if lead else 2,
             has_side_effects=True,
-            vmem_limit_bytes=48 * 1024 * 1024,
+            vmem_limit_bytes=(48 if lead else 36) * 1024 * 1024,
         ),
         name="front_first" if lead else "front_second",
     )(places, *given, *more)
@@ -415,7 +419,7 @@
 
 
 class Sums:
-    def __init__(self, counts, rows, terms, out, refs):
+    def __init__(self, counts, rows, terms, out, refs, slack):
         self.counts, self.rows, self.out = counts, rows, out
         self.owns, self.nears, self.fars, self.lasts = zip(*terms)
         self.from_near, self.from_last = refs[:2]
@@ -435,7 +439,8 @@
         self.stages = [self.join, self.spread]
         self.stages += [functools.partial(self.narrow, k) for k in range(len(self.bits))]
         self.stages += [functools.partial(self.widen, k) for k in reversed(range(len(self.bits)))]
-        self.steps = self.parts + len(self.stages) - 1
+        self.lates = [k + slack[min(k, len(slack) - 1)] for k in range(len(self.stages))]
+        self.steps = self.parts + self.lates[-1]
 
     @staticmethod
     def scratch(total, parts, bits, lanes):
@@ -562,7 +567,7 @@
             self.back_x(i).start()
 
     def step(self, i):
-        for late, stage in enumerate(self.stages):
+        for late, stage in zip(self.lates, self.stages, strict=True):
             pl.when((i >= late) & (i < self.parts + late))(functools.partial(stage, i - late))
 
     def finish(self):
@@ -663,7 +668,7 @@
             at += size if merged else self.counts[k] * self.rows
         return shares
 
-    def open(self, here, there, out, refs):
+    def open(self, here, there, out, refs, slack=(0,)):
         here, there, refs = list(here), list(there), list(refs)
         mp = lax.axis_index("mp")
         terms, copies = [], []
@@ -677,7 +682,7 @@
                 copies.append(pltpu.make_async_copy(stack.at[slot], place.at[k], sems.at[k]))
                 copies[-1].start()
             terms.append((place.at[0], stack.at[flip(mp, 1)], place.at[1], stack.at[3 - mp]))
-        return Sums(self.counts, self.rows, terms, out, refs), copies
+        return Sums(self.counts, self.rows, terms, out, refs, slack), copies
 
 
 def sum_replicas(arrays, vectors):
@@ -696,7 +701,7 @@
         scratch_shapes=arrays.scratch
         + [pltpu.VMEM((hops, len(vectors), D), F32), dma((hops,)), dma((hops,))],
         compiler_params=pltpu.CompilerParams(
-            collective_id=0, has_side_effects=True, vmem_limit_bytes=56 * 1024 * 1024
+            collective_id=0, has_side_effects=True, vmem_limit_bytes=(32 if arrays.bits > 4 else 16) * 1024 * 1024
         ),
         name="sum_replicas",
     )(*arrays.here, *arrays.there, *(v[0] for v in vectors))
@@ -732,7 +737,8 @@
         load.start()
     cols, before, earlier, *others, exact, grad_ref, sum_ref = fetched
     first_values, given = (others, ()) if mixed else ((), others)
-    sums, copies = arrays.open(here, there, out, refs)
+    slack = (0, 1, 1, 1, 1, 2) if mixed else (0, 2)
+    sums, copies = arrays.open(here, there, out, refs, slack)
 
     ctx, mp = lax.axis_index("ctx"), lax.axis_index("mp")
     sees_one = (mp >= 2) | ((mp == 0) & (ctx == 1))
@@ -931,7 +937,7 @@
         compiler_params=pltpu.CompilerParams(
             collective_id=3 if mixed else 4,
             has_side_effects=True,
-            vmem_limit_bytes=(46 if mixed and arrays.bits < 5 else 60) * 1024 * 1024,
+            vmem_limit_bytes=(60 if arrays.bits > 4 else 38 if mixed else 48) * 1024 * 1024,
         ),
         name="attend_back",
     )(places, flags, low, *arrays.here, *arrays.there, *fetched)
@@ -1038,7 +1044,6 @@
     )
     ups2, downs2 = ([up_weight2] + by_distance(up2)[1:], [down_weight2] + by_distance(down2)[1:])
     outs2 = lax.dynamic_update_index_in_dim(outs2, out_weight2, me, 0).reshape(D, D)
-    front2 = front2[:, :n_front2]
 
     front_kv2 = (cols2, before2, earlier2)
     stream2, kept2 = tail_forward(
@@ -1057,7 +1062,7 @@
     grad_out2 = dot(heads2.reshape(D, WIN), rounded, 1, 0).astype(BF16).reshape(4, BAND, D)
     bias_grad2 = jnp.sum(dcols2.astype(F32), axis=2)
     grad_front2 = dot(dcols2.reshape(-1, WIN), normed2, 1, 0).astype(BF16).reshape(4, -1, D)
-    normed_grad = dot(dcols2[:, :n_front2].reshape(-1, WIN), front2.reshape(-1, D), 0, 0)
+    normed_grad = dot(dcols2.reshape(-1, WIN), front2.reshape(-1, D), 0, 0)
     middle, gain_front2, shift_front2 = norm_back(normed_grad, unit2, scale2, norm_gain2[0])
     grad = grad + middle
 
@@ -1072,7 +1077,7 @@
     )
     bias_grad1 = jnp.sum(dcols1.astype(F32), axis=2)
     grad_front1 = dot(dcols1.reshape(-1, WIN), normed1, 1, 0).astype(BF16).reshape(4, -1, D)
-    normed_grad = dot(dcols1[:, :n_front1].reshape(-1, WIN), front1.reshape(-1, D), 0, 0)
+    normed_grad = dot(dcols1.reshape(-1, WIN), front1.reshape(-1, D), 0, 0)
     middle, gain_front1, shift_front1 = norm_back(normed_grad, unit1, scale1, norm_gain1[0])
     input_grad = (grad + middle).astype(BF16)
 

time: 597 us -> 562 us (0.941)
  Pallas kernels: 419 us -> 405 us
  matrix products: 105 us -> 92 us
    pallas_call x2, Pallas kernels: 238 us -> 223 us  [attend_back(): pl.pallas_call(functools.partial(back_kernel, mixed, arrays), out_shape=o...]
    dot_general x58, matrix products: 105 us -> 92 us  [dot(): lax.dot_general(left, right, (((left_dim,), (right_dim,)), ((), ())), pre...]
    unnamed x149 -> x121, local copies, waits for them, and re-layouts: 11.3 us -> 14.5 us
where the time goes in v7:
time: 562 us; the launch traced here: 555 us
  Pallas kernels  405 us (72%)
  matrix products  92 us (16%)
  other arithmetic  35 us (6%)
  local copies, waits for them, and re-layouts  20.5 us (4%)
    pallas_call x2, Pallas kernels, attend_back(): pl.pallas_call(functools.partial(back_kernel, mixed, arrays), out_shape=o...  223 us
    pallas_call x2, Pallas kernels, project(): pl.pallas_call(functools.partial(front_kernel, rows, int(lead), bool(firs...  125 us
    dot_general x58, matrix products, dot(): lax.dot_general(left, right, (((left_dim,), (right_dim,)), ((), ())), pre...  92 us
    pallas_call x1, Pallas kernels, sum_replicas(): pl.pallas_call(functools.partial(sum_kernel, arrays, [v[1:] for v in vect...  57.5 us
    unnamed x121, local copies, waits for them, and re-layouts  14.5 us

profile of v7, /device:TPU:0, one launch (start us, length us, event | category | flops | bytes accessed | tf_op | source)
XLA Modules:
  0.0 555.0 jit_solution(9878950401849170427)
XLA Ops:
  4.6 0.8 convert_reduce_fusion.10
  5.5 1.3 convert_reduce_fusion.2
  6.9 1.5 fusion.14
  9.0 1.2 fusion.144.refs_8_
  10.3 73.8 %front_first.1 = (bf16[4,576,512]{2,1,0:T(8,128)(2,1)}, bf16[4,384,512]{2,1,0:T(8,128)(2,1)}, bf16[4,384,512]{2,1,0:T(8,128)(2,1)}, bf16[4,192,512]{2,1,0:T(8,12...) custom-call(s32[12]{0:T(128)S(1)} %pad_add_fusion.refs_0_, ...), custom_call_target="tpu_custom_call" | custom-call | tf_op jit(solution)/shard_map/front_first/pallas_call | solution.py:394
  84.1 0.9 copy-done.13
  85.0 1.0 copy-done.15
  86.7 3.7 fusion.241
  90.4 1.8 multiply_reduce_fusion.7
  92.8 2.2 convolution_add_fusion.4
  95.0 2.7 convolution_add_fusion.5
  97.7 2.9 fusion.104
  100.6 2.1 convolution_add_fusion.6
  102.7 1.1 fusion.113
  105.7 1.1 fusion.225
  107.7 1.4 fusion.242
  109.8 1.0 bitcast_dynamic-update-slice_fusion.refs_6_
  112.1 50.9 %front_second.1 = (bf16[4,480,512]{2,1,0:T(8,128)(2,1)S(1)}, bf16[4,288,512]{2,1,0:T(8,128)(2,1)S(1)}, bf16[4,288,512]{2,1,0:T(8,128)(2,1)S(1)}, bf16[4,192,512]...) custom-call(s32[12]{0:T(128)S(1)} %pad_add_fusion.refs_0_, ...), custom_call_target="tpu_custom_call" | custom-call | tf_op jit(solution)/shard_map/front_second/pallas_call | solution.py:394
  163.1 0.9 fusion.243
  165.5 1.0 slice-done.2
  168.2 1.1 fusion.84
  170.1 1.1 fusion.90
  172.6 1.7 fusion.227
  174.2 1.1 fusion.226
  176.1 2.2 add_convert_fusion
  178.3 1.6 fusion.249
  179.9 1.7 fusion.248
  183.3 1.6 fusion.247
  185.6 1.5 multiply_reduce_fusion
  189.6 0.9 convolution_convert_fusion.17.refs_5_
  190.6 0.9 convolution_convert_fusion.16.refs_6_
  193.7 0.9 convolution_convert_fusion.13.refs_9_
  194.7 0.9 convolution_convert_fusion.12.refs_10_
  195.6 1.0 convolution_convert_fusion.21
  196.7 94.0 %attend_back.2 = (bf16[4,512,512]{2,1,0:T(8,128)(2,1)}, f32[4,192,512]{2,1,0:T(8,128)S(1)}, bf16[4,192,512]{2,1,0:T(8,128)(2,1)S(1)}, bf16[4,192,512]{2,1,0:T(8,128)(2,1)S(1)}, bf16[1536,768]{1,0:T(8,128)(2,1)}) custom-call(s32[12]{0:T(128)S(1)} %pad_add_fusion.refs_0_, f32[12]{0:T(128)S(1)} %convert_element_type.313.refs_1_, s32[1,512]{1,0:T(1,128)S(1)} %bitcast.302, ...), custom_call_target="tpu_custom_call" | custom-call | tf_op jit(solution)/shard_map/attend_back/pallas_call | solution.py:916
  290.7 5.4 fusion.66
  296.9 1.3 copy-done.28
  298.2 3.0 fusion.246
  301.2 2.9 fusion.245
  305.6 1.6 fusion.229
  308.6 2.8 fusion.244
  312.3 1.5 multiply_reduce_fusion.1
  316.5 0.9 convolution_convert_fusion.9.refs_5_
  317.5 2.0 convolution_convert_fusion.8.refs_6_
  319.4 3.5 convolution_convert_fusion.1
  324.5 1.6 pad_maximum_fusion.refs_8_
  326.0 1.8 convolution_convert_fusion.5.refs_9_
  327.9 1.8 convolution_convert_fusion.4.refs_10_
  329.7 2.0 convolution_convert_fusion.3.refs_11_
  331.7 2.0 convolution_convert_fusion.2.refs_12_
  334.5 128.9 %attend_back.3 = (bf16[4,640,512]{2,1,0:T(8,128)(2,1)}, bf16[2432,768]{1,0:T(8,128)(2,1)}) custom-call(s32[12]{0:T(128)S(1)} %select_reduce_fusion.1.refs_0_, f32[12]{0:T(128)S(1)} %convert_element_type.313.refs_1_, s32[1,512]{1,0:T(1,128)S(1)} %bitcast.303, bf16[768,768]{1,0:T(8,128)(2,1)S(1)} %convolution_convert_fusion.11.refs_3_, ...), custom_call_target="tpu_custom_call" | custom-call | tf_op jit(solution)/shard_map/attend_back/pallas_call | solution.py:916
  463.4 4.5 fusion.13
  468.0 1.5 fusion.12
  470.0 4.1 convolution_convert_fusion
  474.6 1.9 convert_reduce_fusion.1
  476.8 2.1 copy-done.3
  478.9 57.5 %sum_replicas.1 = (bf16[640,768]{1,0:T(8,128)(2,1)S(1)}, f32[24,768]{1,0:T(8,128)S(1)}) custom-call(bf16[4,640,768]{2,1,0:T(8,128)(2,1)S(1)} %bitcast.291, f32[768]{0:T(1024)S(1)} %get-tuple-element.88.refs_1_, f32[768]{0:T(1024)S(1)} %get-tuple-element.86.refs_2_, f32[768]{0:T(1024)S(1)} %get-tuple-element.97.refs_3_, f32[768]{0:T(1024)S(1)} %get-tuple-element.96.refs_4_, ...), custom_call_target="tpu_custom_call" | custom-call | tf_op jit(solution)/shard_map/sum_replicas/pallas_call | solution.py:694
  537.1 1.4 convert_bitcast_fusion
  539.2 2.1 slice_convert_fusion.4
  541.4 4.2 slice_convert_fusion.2
  546.2 1.3 slice.197
  547.4 1.1 convert_bitcast_fusion.1
  549.2 1.6 convert_bitcast_fusion.2
  551.4 2.5 slice_convert_fusion
  (221 shorter events, 38.5 us)
Async XLA Ops:
  4.6 3.8 copy-start.21
  5.4 3.3 copy-start.37
  5.5 3.4 copy-start.38
  5.5 3.4 copy-start.39
  5.5 3.4 copy-start.40
  5.5 3.4 copy-start.41
  5.5 3.5 copy-start.34
  8.4 1.8 copy-start.9
  8.4 1.8 copy-start.11
  8.4 1.8 copy-start.12
  84.1 0.9 copy-start.13
  84.9 1.0 copy-start.15
  90.4 1.9 copy-start.17
  92.6 8.0 %copy-start.31 = (bf16[512,768]{1,0:T(8,128)(2,1)}, bf16[512,768]{1,0:T(8,128)(2,1)S(1)}, u32[]{:S(2)}) copy-start(bf16[512,768]{1,0:T(8,128)(2,1)S(1)} %add_convert_fusion.3) | copy-start | bytes 2359300
  95.0 11.9 %copy-start.27 = (f32[512,768]{1,0:T(8,128)}, f32[512,768]{1,0:T(8,128)S(1)}, u32[]{:S(2)}) copy-start(f32[512,768]{1,0:T(8,128)S(1)} %convolution_add_fusion.4) | copy-start | bytes 4718596
  95.0 7.7 %slice-start.6 = ((s8[4718592]{0:T(1024)(128)(4,1)}), s8[4194304]{0:T(1024)(128)(4,1)S(1)}, s32[]{:S(2)}) async-start(s8[4718592]{0:T(1024)(128)(4,1)} %bitcast.324), calls=%async_computation.6 | async-start | bytes 8388608
  97.6 2.9 copy-start.48
  97.7 5.0 slice-start.7
  102.7 1.2 copy-start.46
  102.7 1.7 copy-start.32
  104.4 1.3 copy-start.29
  105.7 1.2 copy-start.44
  105.7 2.0 copy-start.18
  107.7 1.4 copy-start.35
  107.7 1.4 copy-start.36
  107.7 2.2 copy-start.25
  107.7 3.4 copy-start.7
  107.7 3.4 copy-start.8
  107.7 3.4 copy-start.10
  109.2 1.9 copy-start.2
  109.5 2.2 copy-start
  109.5 2.6 copy-start.1
  163.0 1.3 copy-start.4
  163.0 1.8 copy-start.5
  163.0 3.5 slice-start.2
  163.1 3.5 slice-start.3
  163.1 4.8 slice-start.4
  165.1 3.0 slice-start.5
  170.0 13.2 %copy-start.50 = (f32[512,768]{1,0:T(8,128)}, f32[512,768]{1,0:T(8,128)S(1)}, u32[]{:S(2)}) copy-start(f32[512,768]{1,0:T(8,128)S(1)} %convolution_add_fusion.2) | copy-start | bytes 4718596
  170.0 1.7 copy-start.30
  187.1 0.7 copy-start.43
  187.9 7.8 %copy-start.19 = (f32[512,768]{1,0:T(8,128)}, f32[512,768]{1,0:T(8,128)S(1)}, u32[]{:S(2)}) copy-start(f32[512,768]{1,0:T(8,128)S(1)} %get-tuple-element.126) | copy-start | bytes 4718596
  192.3 1.4 copy-start.51
  290.7 5.5 copy-start.6
  290.7 5.5 copy-start.20
  296.8 1.4 copy-start.28
  298.2 3.0 copy-start.49
  298.2 5.9 %slice-start = ((s8[4718592]{0:T(1024)(128)(4,1)}), s8[4194304]{0:T(1024)(128)(4,1)S(1)}, s32[]{:S(2)}) async-start(s8[4718592]{0:T(1024)(128)(4,1)} %bitcast.318), calls=%async_computation | async-start | bytes 8388608
  301.2 2.9 slice-start.1
  304.2 1.4 copy-start.45
  307.2 1.4 copy-start.47
  313.7 1.1 copy-start.33
  317.5 2.0 copy-start.26
  319.4 3.5 copy-start.14
  331.7 2.0 copy-start.16
  334.5 129.0 %copy-start.22 = (bf16[512,768]{1,0:T(8,128)(2,1)S(1)}, bf16[512,768]{1,0:T(8,128)(2,1)}, u32[]{:S(2)}) copy-start(bf16[512,768]{1,0:T(8,128)(2,1)} %param.24) | copy-start | bytes 2359300
  334.5 129.0 %copy-start.42 = (bf16[4,640,768]{2,1,0:T(8,128)(2,1)S(1)}, bf16[4,640,768]{2,1,0:T(8,128)(2,1)}, u32[]{:S(2)}) copy-start(bf16[4,640,768]{2,1,0:T(8,128)(2,1)} %get-tuple-element.77) | copy-start | bytes 11796484
  467.9 2.0 copy-start.23
  476.8 2.1 copy-start.3
  546.2 5.3 copy-start.24

commit v8 on v7

--- a/solution.py
+++ b/solution.py
@@ -14,8 +14,8 @@
 EARLY = 5
 CHUNK = 256
 LEAD = 3
-LAG = 2
-HOOK_FIRST, HOOK_SECOND = -3, 0
+LAG_FIRST, LAG_SECOND = 3, 2
+HOOK_FIRST, HOOK_SECOND = -2, 0
 GROUP = 3
 BAND = GROUP * HD
 TILE = 256
@@ -101,6 +101,7 @@
     n_chunks, n_more, n_lead = len(chunks), len(more_rows), LEAD * lead
     n_arrays = n_more + lead
     early, offset = (EARLY, HOOK_FIRST) if lead else (4, HOOK_SECOND)
+    lag = LAG_FIRST if lead else LAG_SECOND
     places, lo_ref, normed = take(3)
     first_values = take(3) if mixed else ()
     front, bias = (None, None) if lead else take(2)
@@ -182,7 +183,7 @@
         for late, stage in enumerate(
             ((across, widen), (widen, complete), (complete, hand_on))
         ):
-            a = step + n_lead - LAG * late
+            a = step + n_lead - lag * late
             if n_lead <= a < n_chunks:
                 stage[0](a).wait_recv()
                 stage[1](a).start()
@@ -227,7 +228,7 @@
         pl.when(sends_window)(lambda: pass_on(slot, window).start())
     for c in range(early, n_chunks):
         across(c).start()
-    steps = n_chunks - n_lead + 2 * LAG
+    steps = n_chunks - n_lead + 2 * lag
     for step in range(steps):
         if step + offset < 0:
             gather(step)
@@ -611,16 +612,21 @@
     for term, (row, distance) in zip(terms, places, strict=True):
         at = row if distance is None else row + slots[distance]
         vec[pl.ds(at, 1), : term.shape[0]] = term[...].reshape(1, term.shape[0])
-    for hop, partner in enumerate(sums.partners):
-        copy = remote(vec, from_vec.at[hop], v_out.at[hop], v_in.at[hop], partner)
-        copy.start()
-        if hop == 0:
-            for own_copy in copies:
-                own_copy.wait()
-            sums.start()
-        copy.wait()
-        vec[...] = vec[...] + from_vec[hop]
-    each(sums.steps, sums.step)
+    hops = [
+        remote(vec, from_vec.at[hop], v_out.at[hop], v_in.at[hop], partner)
+        for hop, partner in enumerate(sums.partners)
+    ]
+    hops[0].start()
+    for own_copy in copies:
+        own_copy.wait()
+    sums.start()
+    for i in range(max(sums.steps, len(hops))):
+        sums.step(i)
+        if i < len(hops):
+            hops[i].wait()
+            vec[...] = vec[...] + from_vec[i]
+        if i + 1 < len(hops):
+            hops[i + 1].start()
     sums.finish()
 
 
@@ -937,7 +943,7 @@
         compiler_params=pltpu.CompilerParams(
             collective_id=3 if mixed else 4,
             has_side_effects=True,
-            vmem_limit_bytes=(60 if arrays.bits > 4 else 38 if mixed else 48) * 1024 * 1024,
+            vmem_limit_bytes=(60 if arrays.bits > 4 else 38 if mixed else 43) * 1024 * 1024,
         ),
         name="attend_back",
     )(places, flags, low, *arrays.here, *arrays.there, *fetched)
@@ -1070,8 +1076,8 @@
         grad, kept1, outs1, norm_gain1, ups1, downs1
     )
     grad_out1 = dot(heads1.reshape(D, WIN), rounded, 1, 0).astype(BF16).reshape(4, BAND, D)
-    arrays = [grad_front2, jnp.concatenate([grad_out2, grad_out1], axis=1)]
-    (dcols1,), (front_sum2, out_sums, *mats1) = attend_back(
+    arrays = [grad_front2]
+    (dcols1,), (front_sum2, *mats1) = attend_back(
         taker, flags, low, front_kv1, (), (dv2, dv2_before, dv2_earlier), exact1,
         grad_heads.reshape(4, BAND, WIN), sums1, arrays + list(zip(*mats1, strict=True)),
     )
@@ -1090,7 +1096,8 @@
     vectors = [(vector, row, None) for row, vector in enumerate(singles)]
     for row, shares in ((16, up_grads1), (20, up_grads2)):
         vectors += [(vector, row, distance) for distance, vector in enumerate(shares)]
-    (front_sum1,), sums = sum_replicas([grad_front1], vectors)
+    grad_outs = jnp.concatenate([grad_out2, grad_out1], axis=1)
+    (out_sums, front_sum1), sums = sum_replicas([grad_outs, grad_front1], vectors)
 
     def mine(vectors):
         return lax.dynamic_index_in_dim(vectors.reshape(4, -1), me, 0, keepdims=False)

time: 562 us -> 547 us (0.973)
  Pallas kernels: 405 us -> 393 us
    pallas_call x2, Pallas kernels: 223 us -> 203 us  [attend_back(): pl.pallas_call(functools.partial(back_kernel, mixed, arrays), out_shape=o...]
    pallas_call x1, Pallas kernels: 57.5 us -> 66.5 us  [sum_replicas(): pl.pallas_call(functools.partial(sum_kernel, arrays, [v[1:] for v in vect...]
    unnamed x121 -> x119, local copies, waits for them, and re-layouts: 14.5 us -> 16.3 us
where the time goes in v8:
time: 547 us; the launch traced here: 541 us
  Pallas kernels  393 us (72%)
  matrix products  89.3 us (16%)
  other arithmetic  33.6 us (6%)
  local copies, waits for them, and re-layouts  22.4 us (4%)
    pallas_call x2, Pallas kernels, attend_back(): pl.pallas_call(functools.partial(back_kernel, mixed, arrays), out_shape=o...  203 us
    pallas_call x2, Pallas kernels, project(): pl.pallas_call(functools.partial(front_kernel, rows, int(lead), bool(firs...  124 us
    dot_general x58, matrix products, dot(): lax.dot_general(left, right, (((left_dim,), (right_dim,)), ((), ())), pre...  89.3 us
    pallas_call x1, Pallas kernels, sum_replicas(): pl.pallas_call(functools.partial(sum_kernel, arrays, [v[1:] for v in vect...  66.5 us
    unnamed x119, local copies, waits for them, and re-layouts  16.3 us

profile of v8, /device:TPU:0, one launch (start us, length us, event | category | flops | bytes accessed | tf_op | source)
XLA Modules:
  0.0 540.8 jit_solution(11236460948494139950)
XLA Ops:
  3.7 0.8 reduce-window.8
  4.6 0.8 convert_reduce_fusion.10
  5.5 1.3 convert_reduce_fusion.2
  6.9 1.5 fusion.14
  9.0 1.2 fusion.144.refs_8_
  10.3 70.0 %front_first.1 = (bf16[4,576,512]{2,1,0:T(8,128)(2,1)}, bf16[4,384,512]{2,1,0:T(8,128)(2,1)}, bf16[4,384,512]{2,1,0:T(8,128)(2,1)}, bf16[4,192,512]{2,1,0:T(8,12...) custom-call(s32[12]{0:T(128)S(1)} %pad_add_fusion.refs_0_, ...), custom_call_target="tpu_custom_call" | custom-call | tf_op jit(solution)/shard_map/front_first/pallas_call | solution.py:395
  80.3 0.9 copy-done.14
  81.2 1.0 copy-done.16
  82.9 3.7 fusion.241
  86.6 1.8 multiply_reduce_fusion.7
  89.0 2.2 convolution_add_fusion.4
  91.2 2.7 convolution_add_fusion.5
  93.9 2.9 fusion.104
  96.9 2.1 convolution_add_fusion.6
  99.0 1.1 fusion.113
  101.4 1.1 fusion.225
  103.4 1.3 fusion.242
  105.5 1.0 bitcast_dynamic-update-slice_fusion.refs_6_
  108.2 53.6 %front_second.1 = (bf16[4,480,512]{2,1,0:T(8,128)(2,1)S(1)}, bf16[4,288,512]{2,1,0:T(8,128)(2,1)S(1)}, bf16[4,288,512]{2,1,0:T(8,128)(2,1)S(1)}, bf16[4,192,512]...) custom-call(s32[12]{0:T(128)S(1)} %pad_add_fusion.refs_0_, ...), custom_call_target="tpu_custom_call" | custom-call | tf_op jit(solution)/shard_map/front_second/pallas_call | solution.py:395
  161.9 0.9 fusion.243
  164.3 1.0 slice-done.2
  166.9 1.1 fusion.84
  168.8 1.1 fusion.90
  170.7 1.7 fusion.227
  172.4 1.1 fusion.226
  174.3 2.2 add_convert_fusion
  176.5 1.6 fusion.249
  178.1 1.8 fusion.248
  179.9 0.8 fusion.86
  181.5 1.6 fusion.247
  183.9 1.5 multiply_reduce_fusion
  187.9 1.0 convolution_convert_fusion.17.refs_5_
  188.9 1.0 convolution_convert_fusion.16.refs_6_
  191.5 1.0 convolution_convert_fusion.13.refs_9_
  192.4 1.0 convolution_convert_fusion.12.refs_10_
  193.4 1.0 convolution_convert_fusion.21
  194.4 91.3 %attend_back.2 = (bf16[4,512,512]{2,1,0:T(8,128)(2,1)}, f32[4,192,512]{2,1,0:T(8,128)S(1)}, bf16[4,192,512]{2,1,0:T(8,128)(2,1)S(1)}, bf16[4,192,512]{2,1,0:T(8,128)(2,1)S(1)}, bf16[1536,768]{1,0:T(8,128)(2,1)}) custom-call(s32[12]{0:T(128)S(1)} %pad_add_fusion.refs_0_, f32[12]{0:T(128)S(1)} %convert_element_type.313.refs_1_, s32[1,512]{1,0:T(1,128)S(1)} %bitcast.302, ...), custom_call_target="tpu_custom_call" | custom-call | tf_op jit(solution)/shard_map/attend_back/pallas_call | solution.py:922
  285.8 5.4 %fusion.66 = (f32[768]{0:T(1024)S(1)}, f32[512]{0:T(512)S(1)}, f32[512]{0:T(512)S(1)}, f32[768]{0:T(1024)S(1)}, f32[512,768,1]{1,0,2:T(8,128)S(1)}) fusion(f32[512,768]{1,0:T(8,128)S(1)} %copy-done.22, f32[512]{0:T(512)S(1)} %add_rsqrt_fusion.1, f32[512]{0:T(512)S(1)} %broadcast_multiply_fusion.9, f32[768]{0:T(1024)S(1)} %get-tuple-element.191, ...), kind=kOutput, calls=%fused_computation.99 | convolution fusion | flops 1614149120 | bytes 8406016 | tf_op jit(solution)/shard_map/dot_general | solution.py:65
  291.9 1.3 copy-done.30
  293.2 3.0 fusion.246
  296.3 2.9 fusion.245
  301.0 1.6 fusion.229
  303.9 2.8 fusion.244
  308.2 1.5 multiply_reduce_fusion.1
  312.5 0.9 convolution_convert_fusion.9.refs_5_
  313.5 0.9 convolution_convert_fusion.8.refs_6_
  315.1 3.5 convolution_convert_fusion.1
  320.1 0.9 convolution_convert_fusion.5.refs_10_
  321.1 2.0 convolution_convert_fusion.4.refs_11_
  323.9 111.9 %attend_back.3 = (bf16[4,640,512]{2,1,0:T(8,128)(2,1)}, bf16[2048,768]{1,0:T(8,128)(2,1)}) custom-call(s32[12]{0:T(128)S(1)} %select_reduce_fusion.1.refs_0_, f32[12]{0:T(128)S(1)} %convert_element_type.313.refs_1_, s32[1,512]{1,0:T(1,128)S(1)} %bitcast.303, bf16[768,768]{1,0:T(8,128)(2,1)S(1)} %convolution_convert_fusion.11.refs_3_, ...), custom_call_target="tpu_custom_call" | custom-call | tf_op jit(solution)/shard_map/attend_back/pallas_call | solution.py:922
  435.8 5.7 %fusion.13 = (f32[768]{0:T(1024)S(1)}, f32[512]{0:T(512)S(1)}, f32[512]{0:T(512)S(1)}, f32[768]{0:T(1024)S(1)}, f32[512,768,1]{1,0,2:T(8,128)S(1)}) fusion(bf16[512,768]{1,0:T(8,128)(2,1)S(1)} %copy-done.24, f32[512]{0:T(512)S(1)} %add_rsqrt_fusion.3, f32[512]{0:T(512)S(1)} %broadcast_multiply_fusion.11, f32[768]{0:T(1024)S(1)} %get-tuple-element.189, ...), kind=kOutput, calls=%fused_computation.40 | convolution fusion | flops 2017195520 | bytes 8930304 | tf_op jit(solution)/shard_map/dot_general | solution.py:65
  441.5 1.5 fusion.12
  444.7 1.6 copy-done.25
  446.3 4.1 convolution_convert_fusion
  451.0 1.9 convert_reduce_fusion.1
  453.1 2.1 copy-done.3
  455.2 66.5 %sum_replicas.1 = (bf16[1024,768]{1,0:T(8,128)(2,1)S(1)}, f32[24,768]{1,0:T(8,128)S(1)}) custom-call(bf16[4,384,768]{2,1,0:T(8,128)(2,1)S(1)} %pad_maximum_fusion.refs_0_, bf16[4,640,768]{2,1,0:T(8,128)(2,1)S(1)} %bitcast.291, f32[768]{0:T(1024)S(1)} %get-tuple-element.88.refs_2_, f32[768]{0:T(1024)S(1)} %get-tuple-element.86.refs_3_, ...), custom_call_target="tpu_custom_call" | custom-call | tf_op jit(solution)/shard_map/sum_replicas/pallas_call | solution.py:700
  522.9 1.4 convert_bitcast_fusion
  525.0 2.1 slice_convert_fusion.4
  527.2 4.2 slice_convert_fusion.2
  532.0 1.3 slice.199
  533.2 1.1 convert_bitcast_fusion.1
  534.9 1.6 convert_bitcast_fusion.2
  537.2 2.5 slice_convert_fusion
  (219 shorter events, 38.9 us)
Async XLA Ops:
  4.6 3.8 copy-start.23
  5.4 3.3 copy-start.39
  5.5 3.4 copy-start.40
  5.5 3.4 copy-start.41
  5.5 3.4 copy-start.42
  5.5 3.4 copy-start.43
  5.5 3.5 copy-start.36
  8.4 1.8 copy-start.10
  8.4 1.8 copy-start.12
  8.4 1.8 copy-start.13
  80.3 0.9 copy-start.14
  81.2 1.0 copy-start.16
  86.6 1.9 copy-start.18
  88.8 11.3 %copy-start.34 = (bf16[512,768]{1,0:T(8,128)(2,1)}, bf16[512,768]{1,0:T(8,128)(2,1)S(1)}, u32[]{:S(2)}) copy-start(bf16[512,768]{1,0:T(8,128)(2,1)S(1)} %add_convert_fusion.3) | copy-start | bytes 2359300
  91.2 11.4 %copy-start.29 = (f32[512,768]{1,0:T(8,128)}, f32[512,768]{1,0:T(8,128)S(1)}, u32[]{:S(2)}) copy-start(f32[512,768]{1,0:T(8,128)S(1)} %convolution_add_fusion.4) | copy-start | bytes 4718596
  91.2 7.7 %slice-start.6 = ((s8[4718592]{0:T(1024)(128)(4,1)}), s8[4194304]{0:T(1024)(128)(4,1)S(1)}, s32[]{:S(2)}) async-start(s8[4718592]{0:T(1024)(128)(4,1)} %bitcast.324), calls=%async_computation.6 | async-start | bytes 8388608
  93.9 3.0 copy-start.49
  93.9 5.0 slice-start.7
  99.0 1.2 copy-start.47
  100.1 1.3 copy-start.31
  101.4 1.2 copy-start.45
  101.4 2.0 copy-start.19
  103.4 1.4 copy-start.37
  103.4 1.4 copy-start.38
  103.4 2.1 copy-start.27
  103.4 3.3 copy-start.8
  103.4 3.3 copy-start.9
  103.4 3.3 copy-start.11
  104.7 57.1 %copy-start.21 = (f32[512,768]{1,0:T(8,128)}, f32[512,768]{1,0:T(8,128)S(1)}, u32[]{:S(2)}) copy-start(f32[512,768]{1,0:T(8,128)S(1)} %get-tuple-element.169) | copy-start | bytes 4718596
  104.8 2.3 copy-start.2
  105.1 2.6 copy-start
  105.1 3.1 copy-start.1
  161.8 1.3 copy-start.4
  161.8 1.8 copy-start.5
  161.8 3.5 slice-start.2
  161.8 3.5 slice-start.3
  161.9 4.8 slice-start.4
  163.9 3.0 slice-start.5
  168.8 1.1 copy-start.33
  185.4 0.7 copy-start.44
  194.4 91.3 %copy-start.22 = (f32[512,768]{1,0:T(8,128)S(1)}, f32[512,768]{1,0:T(8,128)}, u32[]{:S(2)}) copy-start(f32[512,768]{1,0:T(8,128)} %copy-done.21) | copy-start | bytes 4718596
  285.7 5.5 %copy-start.6 = (f32[4,192,512]{2,1,0:T(8,128)}, f32[4,192,512]{2,1,0:T(8,128)S(1)}, u32[]{:S(2)}) copy-start(f32[4,192,512]{2,1,0:T(8,128)S(1)} %get-tuple-element.73) | copy-start | bytes 4718596
  291.8 1.4 copy-start.30
  293.2 3.0 copy-start.50
  293.2 5.9 %slice-start = ((s8[4718592]{0:T(1024)(128)(4,1)}), s8[4194304]{0:T(1024)(128)(4,1)S(1)}, s32[]{:S(2)}) async-start(s8[4718592]{0:T(1024)(128)(4,1)} %bitcast.318), calls=%async_computation | async-start | bytes 8388608
  296.2 2.9 slice-start.1
  299.2 1.3 copy-start.32
  299.2 1.8 copy-start.46
  302.5 1.4 copy-start.48
  306.8 1.4 copy-start.20
  309.7 1.1 copy-start.35
  313.5 1.6 copy-start.28
  321.1 2.0 copy-start.17
  323.9 111.9 %copy-start.24 = (bf16[512,768]{1,0:T(8,128)(2,1)S(1)}, bf16[512,768]{1,0:T(8,128)(2,1)}, u32[]{:S(2)}) copy-start(bf16[512,768]{1,0:T(8,128)(2,1)} %param.24) | copy-start | bytes 2359300
  441.5 1.5 copy-start.15
  444.5 1.7 copy-start.25
  453.1 2.1 copy-start.3
  521.7 1.2 copy-start.7
  531.9 5.3 copy-start.26

commit v9 on v8

--- a/solution.py
+++ b/solution.py
@@ -402,7 +402,7 @@
         compiler_params=pltpu.CompilerParams(
             collective_id=1 if lead else 2,
             has_side_effects=True,
-            vmem_limit_bytes=(48 if lead else 36) * 1024 * 1024,
+            vmem_limit_bytes=(48 if lead else 28) * 1024 * 1024,
         ),
         name="front_first" if lead else "front_second",
     )(places, *given, *more)
@@ -943,7 +943,7 @@
         compiler_params=pltpu.CompilerParams(
             collective_id=3 if mixed else 4,
             has_side_effects=True,
-            vmem_limit_bytes=(60 if arrays.bits > 4 else 38 if mixed else 43) * 1024 * 1024,
+            vmem_limit_bytes=(60 if arrays.bits > 4 else 36 if mixed else 43) * 1024 * 1024,
         ),
         name="attend_back",
     )(places, flags, low, *arrays.here, *arrays.there, *fetched)

time: 547 us -> 545 us (level)
    unnamed x119 -> x133, local copies, waits for them, and re-layouts: 16.3 us -> 17.9 us
where the time goes in v9:
time: 545 us; the launch traced here: 538 us
  Pallas kernels  392 us (72%)
  matrix products  87.1 us (16%)
  other arithmetic  32.5 us (6%)
  local copies, waits for them, and re-layouts  24 us (4%)
    pallas_call x2, Pallas kernels, attend_back(): pl.pallas_call(functools.partial(back_kernel, mixed, arrays), out_shape=o...  204 us
    pallas_call x2, Pallas kernels, project(): pl.pallas_call(functools.partial(front_kernel, rows, int(lead), bool(firs...  122 us
    dot_general x58, matrix products, dot(): lax.dot_general(left, right, (((left_dim,), (right_dim,)), ((), ())), pre...  87.1 us
    pallas_call x1, Pallas kernels, sum_replicas(): pl.pallas_call(functools.partial(sum_kernel, arrays, [v[1:] for v in vect...  66.3 us
    unnamed x133, local copies, waits for them, and re-layouts  17.9 us

profile of v9, /device:TPU:0, one launch (start us, length us, event | category | flops | bytes accessed | tf_op | source)
XLA Modules:
  0.0 538.0 jit_solution(14715815434425436707)
XLA Ops:
  3.7 0.8 reduce-window.8
  4.6 0.8 convert_reduce_fusion.10
  5.5 1.3 convert_reduce_fusion.2
  6.9 1.5 fusion.14
  9.0 1.2 fusion.144.refs_8_
  10.3 70.0 %front_first.1 = (bf16[4,576,512]{2,1,0:T(8,128)(2,1)}, bf16[4,384,512]{2,1,0:T(8,128)(2,1)}, bf16[4,384,512]{2,1,0:T(8,128)(2,1)}, bf16[4,192,512]{2,1,0:T(8,12...) custom-call(s32[12]{0:T(128)S(1)} %pad_add_fusion.refs_0_, ...), custom_call_target="tpu_custom_call" | custom-call | tf_op jit(solution)/shard_map/front_first/pallas_call | solution.py:395
  80.3 0.9 copy-done.18
  81.2 1.0 copy-done.22
  82.9 3.7 fusion.241
  86.6 1.8 multiply_reduce_fusion.7
  89.0 2.2 convolution_add_fusion.4
  91.2 2.7 convolution_add_fusion.5
  93.9 2.9 fusion.104
  96.9 2.1 convolution_add_fusion.6
  99.0 1.1 fusion.113
  101.4 1.1 fusion.225
  103.4 1.4 fusion.242
  108.5 52.0 %front_second.1 = (bf16[4,480,512]{2,1,0:T(8,128)(2,1)S(1)}, bf16[4,288,512]{2,1,0:T(8,128)(2,1)S(1)}, bf16[4,288,512]{2,1,0:T(8,128)(2,1)S(1)}, bf16[4,192,512]...) custom-call(s32[12]{0:T(128)S(1)} %pad_add_fusion.refs_0_, ...), custom_call_target="tpu_custom_call" | custom-call | tf_op jit(solution)/shard_map/front_second/pallas_call | solution.py:395
  160.6 0.9 fusion.243
  165.0 1.1 fusion.84
  166.9 1.1 fusion.90
  168.8 1.7 fusion.227
  170.5 1.1 fusion.226
  172.4 2.1 add_convert_fusion
  174.5 1.6 fusion.249
  176.1 1.8 fusion.248
  177.9 0.8 fusion.86
  179.5 1.6 fusion.247
  182.0 1.4 multiply_reduce_fusion
  185.1 0.8 convolution_convert_fusion.18.refs_4_
  185.9 1.0 convolution_convert_fusion.17.refs_5_
  186.8 1.0 convolution_convert_fusion.16.refs_6_
  189.4 1.0 convolution_convert_fusion.13.refs_9_
  190.4 0.9 convolution_convert_fusion.12.refs_10_
  191.4 1.0 convolution_convert_fusion.21
  192.6 91.6 %attend_back.2 = (bf16[4,512,512]{2,1,0:T(8,128)(2,1)}, f32[4,192,512]{2,1,0:T(8,128)S(1)}, bf16[4,192,512]{2,1,0:T(8,128)(2,1)S(1)}, bf16[4,192,512]{2,1,0:T(8,128)(2,1)S(1)}, bf16[1536,768]{1,0:T(8,128)(2,1)}) custom-call(s32[12]{0:T(128)S(1)} %pad_add_fusion.refs_0_, f32[12]{0:T(128)S(1)} %convert_element_type.313.refs_1_, s32[1,512]{1,0:T(1,128)S(1)} %bitcast.302, ...), custom_call_target="tpu_custom_call" | custom-call | tf_op jit(solution)/shard_map/attend_back/pallas_call | solution.py:922
  284.2 4.5 fusion.66
  289.5 1.3 copy-done.38
  290.8 3.0 fusion.246
  293.8 2.9 fusion.245
  298.5 1.6 fusion.229
  301.5 2.9 fusion.244
  305.8 1.5 multiply_reduce_fusion.1
  309.2 0.8 convolution_convert_fusion.10.refs_4_
  310.1 1.0 convolution_convert_fusion.9.refs_5_
  311.0 1.0 convolution_convert_fusion.8.refs_6_
  312.6 3.5 convolution_convert_fusion.1
  317.7 1.0 convolution_convert_fusion.5.refs_10_
  318.7 2.0 convolution_convert_fusion.4.refs_11_
  321.5 112.0 %attend_back.3 = (bf16[4,640,512]{2,1,0:T(8,128)(2,1)}, bf16[2048,768]{1,0:T(8,128)(2,1)}) custom-call(s32[12]{0:T(128)S(1)} %select_reduce_fusion.1.refs_0_, f32[12]{0:T(128)S(1)} %convert_element_type.313.refs_1_, s32[1,512]{1,0:T(1,128)S(1)} %bitcast.303, bf16[768,768]{1,0:T(8,128)(2,1)S(1)} %convolution_convert_fusion.11.refs_3_, ...), custom_call_target="tpu_custom_call" | custom-call | tf_op jit(solution)/shard_map/attend_back/pallas_call | solution.py:922
  433.5 4.5 fusion.13
  438.0 1.5 fusion.12
  442.1 1.6 copy-done.33
  443.7 4.1 convolution_convert_fusion
  448.4 1.9 convert_reduce_fusion.1
  450.5 2.1 copy-done.3
  452.6 66.3 %sum_replicas.1 = (bf16[1024,768]{1,0:T(8,128)(2,1)S(1)}, f32[24,768]{1,0:T(8,128)S(1)}) custom-call(bf16[4,384,768]{2,1,0:T(8,128)(2,1)S(1)} %pad_maximum_fusion.refs_0_, bf16[4,640,768]{2,1,0:T(8,128)(2,1)S(1)} %bitcast.291, f32[768]{0:T(1024)S(1)} %get-tuple-element.88.refs_2_, f32[768]{0:T(1024)S(1)} %get-tuple-element.86.refs_3_, ...), custom_call_target="tpu_custom_call" | custom-call | tf_op jit(solution)/shard_map/sum_replicas/pallas_call | solution.py:700
  520.1 1.4 convert_bitcast_fusion
  522.2 2.1 slice_convert_fusion.4
  524.4 4.2 slice_convert_fusion.2
  529.2 1.3 slice.199
  530.4 1.1 convert_bitcast_fusion.1
  532.2 1.6 convert_bitcast_fusion.2
  534.4 2.5 slice_convert_fusion
  (232 shorter events, 39.8 us)
Async XLA Ops:
  4.6 3.8 copy-start.31
  5.4 3.3 copy-start.47
  5.5 3.4 copy-start.48
  5.5 3.4 copy-start.49
  5.5 3.4 copy-start.50
  5.5 3.4 copy-start.51
  5.5 3.5 copy-start.44
  8.4 1.8 copy-start.13
  8.4 1.8 copy-start.15
  8.4 1.8 copy-start.17
  81.2 1.0 copy-start.22
  86.6 1.9 copy-start.24
  88.8 11.2 %copy-start.42 = (bf16[512,768]{1,0:T(8,128)(2,1)}, bf16[512,768]{1,0:T(8,128)(2,1)S(1)}, u32[]{:S(2)}) copy-start(bf16[512,768]{1,0:T(8,128)(2,1)S(1)} %add_convert_fusion.3) | copy-start | bytes 2359300
  91.2 11.3 %copy-start.37 = (f32[512,768]{1,0:T(8,128)}, f32[512,768]{1,0:T(8,128)S(1)}, u32[]{:S(2)}) copy-start(f32[512,768]{1,0:T(8,128)S(1)} %convolution_add_fusion.4) | copy-start | bytes 4718596
  91.2 7.7 %slice-start.4 = ((s8[4718592]{0:T(1024)(128)(4,1)}), s8[4194304]{0:T(1024)(128)(4,1)S(1)}, s32[]{:S(2)}) async-start(s8[4718592]{0:T(1024)(128)(4,1)} %bitcast.322), calls=%async_computation.4 | async-start | bytes 8388608
  93.9 3.0 copy-start.58
  93.9 5.0 slice-start.5
  98.9 1.1 copy-start.56
  100.1 1.3 copy-start.39
  101.4 1.2 copy-start.54
  101.4 2.0 copy-start.25
  103.3 1.4 copy-start.45
  103.3 1.5 copy-start.46
  103.3 2.2 copy-start.4
  103.3 2.2 copy-start.35
  103.4 2.5 copy-start.9
  103.4 3.3 copy-start.10
  103.4 3.3 copy-start.14
  104.8 55.8 %copy-start.27 = (f32[512,768]{1,0:T(8,128)}, f32[512,768]{1,0:T(8,128)S(1)}, u32[]{:S(2)}) copy-start(f32[512,768]{1,0:T(8,128)S(1)} %get-tuple-element.169) | copy-start | bytes 4718596
  104.9 2.6 copy-start.2
  105.2 2.9 copy-start
  105.2 3.3 copy-start.1
  160.5 1.3 copy-start.5
  160.5 1.8 copy-start.6
  160.6 2.3 copy-start.11
  160.6 2.7 copy-start.20
  160.6 4.2 slice-start.2
  163.6 1.4 slice-start.3
  166.9 1.1 copy-start.41
  184.1 104.6 %copy-start.29 = (f32[512,768]{1,0:T(8,128)}, f32[512,768]{1,0:T(8,128)S(1)}, u32[]{:S(2)}) copy-start(f32[512,768]{1,0:T(8,128)S(1)} %get-tuple-element.126) | copy-start | bytes 4718596
  191.3 1.3 copy-start.12
  192.6 91.6 %copy-start.28 = (f32[512,768]{1,0:T(8,128)S(1)}, f32[512,768]{1,0:T(8,128)}, u32[]{:S(2)}) copy-start(f32[512,768]{1,0:T(8,128)} %copy-done.27) | copy-start | bytes 4718596
  284.2 4.5 copy-start.7
  289.4 1.4 copy-start.38
  290.8 3.0 copy-start.59
  290.8 6.0 %slice-start = ((s8[4718592]{0:T(1024)(128)(4,1)}), s8[4194304]{0:T(1024)(128)(4,1)S(1)}, s32[]{:S(2)}) async-start(s8[4718592]{0:T(1024)(128)(4,1)} %bitcast.318), calls=%async_computation | async-start | bytes 8388608
  293.8 2.9 slice-start.1
  296.7 1.3 copy-start.40
  296.8 1.8 copy-start.55
  298.5 1.6 copy-start.16
  300.1 1.4 copy-start.57
  304.4 1.4 copy-start.26
  307.3 1.1 copy-start.43
  311.0 1.6 copy-start.36
  318.7 2.0 copy-start.23
  321.5 112.0 %copy-start.32 = (bf16[512,768]{1,0:T(8,128)(2,1)S(1)}, bf16[512,768]{1,0:T(8,128)(2,1)}, u32[]{:S(2)}) copy-start(bf16[512,768]{1,0:T(8,128)(2,1)} %param.24) | copy-start | bytes 2359300
  321.5 112.0 %copy-start.52 = (bf16[4,640,768]{2,1,0:T(8,128)(2,1)S(1)}, bf16[4,640,768]{2,1,0:T(8,128)(2,1)}, u32[]{:S(2)}) copy-start(bf16[4,640,768]{2,1,0:T(8,128)(2,1)} %get-tuple-element.77) | copy-start | bytes 11796484
  438.0 1.5 copy-start.19
  439.5 1.1 copy-start.21
  439.5 1.7 copy-start.30
  441.9 1.7 copy-start.33
  450.5 2.1 copy-start.3
  518.9 1.2 copy-start.8
  529.2 5.3 copy-start.34
  (2 other events, 1.6 us)
